TPU v7x, 256 devices: a whole 4x4x8 slice. The times are simulated.
256 devices in a mesh: pop: 32 (over x_hi, z, core), wa: 8 (over x_lo, y).
Axes of the slice: x: 4 (x_hi: 2, x_lo: 2; x = x_hi * 2 + x_lo), y: 4, z: 8, core: 2. Of those that a mesh axis runs over, the one named last changes fastest.
Arguments:
- inputs: bfloat16 [8192, 24, 4096], P('pop', 'wa'), may hold values from -6 to 6
- weight: bfloat16 [2048, 4096], P(None, 'wa'), may hold values from -0.09375 to 0.09375
- factor_in: bfloat16 [8192, 4096], P('pop'), may hold values from -0.09375 to 0.09375
- factor_out: bfloat16 [8192, 2048], P('pop'), may hold values from -6 to 6
- readout: float32 [2048], replicated, may hold values from -0.125 to 0.125
Outputs:
- weight_step: float32 [2048, 4096], P('pop', 'wa')
- utilities: float32 [8192], P('pop')
All inputs are finite; a program needn't handle non-finite values.
Results may differ from a plain program's by a relative error of at most 0.0029.
Values may be sent and summed in bfloat16 or wider, within the bound.
No kernel may reach another device: no remote copies, remote signals or barrier semaphores. Data moves between devices by JAX's collectives and lax.ppermute only.
A program may use at most 128 MiB of HBM per device.

v0:
```python
import jax
import jax.numpy as jnp
from jax import lax
from jax.sharding import PartitionSpec as P

perturb_scale = 0.5
epsilon = 1e-05


def shards(inputs, weight, factor_in, factor_out, readout):
    members_here, rows_here, width = inputs.shape
    out_width, block_width = weight.shape
    flat = inputs.reshape(members_here * rows_here, width)
    proj = lax.dot_general(
        flat,
        lax.all_gather(weight, "wa", axis=1, tiled=True),
        (((1,), (1,)), ((), ())),
        preferred_element_type=jnp.float32,
    )
    low = jnp.einsum("mrd,md->mr", inputs, factor_in, preferred_element_type=jnp.float32)
    pert = (
        proj.reshape(members_here, rows_here, out_width)
        + perturb_scale * low[:, :, None] * factor_out.astype(jnp.float32)[:, None, :]
    )
    row_count = rows_here * lax.axis_size("wa")
    partial_fit = jnp.sum(jnp.tanh(pert) * readout, axis=(1, 2)) / row_count
    fitness = lax.psum(partial_fit, "wa")
    member_count = members_here * lax.axis_size("pop")
    total = lax.psum(jnp.sum(fitness), "pop")
    mean = total / member_count
    spread = lax.psum(jnp.sum((fitness - mean) ** 2), "pop") / member_count
    utilities = (fitness - mean) / jnp.sqrt(spread + epsilon)
    scaled = (utilities[:, None] * factor_out.astype(jnp.float32)).astype(jnp.bfloat16)
    feature_start = lax.axis_index("wa") * block_width
    in_block = lax.dynamic_slice_in_dim(factor_in, feature_start, block_width, 1)
    summed = lax.psum_scatter(
        lax.dot_general(
            scaled, in_block, (((0,), (0,)), ((), ())), preferred_element_type=jnp.float32
        ),
        "pop",
        scatter_dimension=0,
        tiled=True,
    )
    weight_step = summed / jnp.sqrt(jnp.float32(member_count))
    return (weight_step, utilities)


def solution(mesh):
    placed = (P("pop", "wa", None), P(None, "wa"), P("pop", None), P("pop", None), P())
    return jax.shard_map(
        shards, mesh=mesh, in_specs=placed, out_specs=(P("pop", "wa"), P("pop")), check_vma=False
    )
```

profile of v0, /device:TPU:1, one launch (start us, length us, event | category | flops | bytes accessed | tf_op | source)
XLA Modules:
  0.0 484.9 jit_solution(12404838927739926441)
XLA Ops:
  7.2 0.0 copy-start
  7.2 0.0 all-gather.2.cloned.1.call-start
  7.2 0.7 all-gather.2.cloned.1.call-update
  7.9 0.0 reduce-scatter.2.cloned.1.call-start
  8.0 2.8 convert_element_type.7
  10.8 0.0 copy-done
  10.8 0.0 copy-start.3
  10.8 14.9 %fusion.2 = f32[256,1,3]{2,1,0:T(1,128)S(1)} fusion(bf16[256,3,4096]{2,0,1:T(8,128)(2,1)} %param.5, bf16[256,4096,1]{1,0,2:T(8,128)(2,1)S(1)} %bitcast.9), kind=kOutput, calls=%fused_computation.2 | convolution fusion | flops 6291456 | bytes 8391680 | tf_op jit(solution)/shard_map/mrd,md->mr/dot_general | solution.py:20
  25.7 0.1 copy.9
  25.8 160.9 %all-gather.2.cloned.1.call-done = bf16[2048,4096]{1,0:T(8,128)(2,1)} async-done(((bf16[2048,512]{1,0:T(8,128)(2,1)}), bf16[2048,4096]{1,0:T(8,128)(2,1)}) %all-gather.2.cloned.1.call-update) | async-done | bytes 16777232 | tf_op jit(solution)/shard_map/all_gather | solution.py:16
  186.7 0.0 copy-done.3
  186.7 19.3 %multiply_reduce_fusion = f32[256]{0:T(256)S(1)} fusion(bf16[256,3,4096]{2,0,1:T(8,128)(2,1)} %param.5, bf16[2048,4096]{1,0:T(8,128)(2,1)} %all-gather.2.cloned.1.call-done, f32[2048]{0:T(1024)S(1)} %copy-done.3, f32[256,2048]{1,0:T(8,128)} %convert_element_type.7, f32[256,3]{0,1:T(4,128)S(1)} %bitcast_multiply_fusion), kind=kOutput, calls=%fused_computation.4 | convolution fusion | flops 12891193344 | bytes 25178112 | tf_op jit(solution)/shard_map/dot_general | solution.py:14
  206.0 13.0 %psum.21 = f32[256]{0:T(256)S(1)} all-reduce(f32[256]{0:T(256)S(1)} %broadcast_multiply_fusion.1), channel_id=1, replica_groups=mesh['pop'=32,'wa'=8] {'wa'}, use_global_device_ids=true, to_apply=%region_1.0 | all-reduce | flops 256 | bytes 2048 | tf_op jit(solution)/shard_map/psum | solution.py:27
  219.0 0.6 reduce_sum.28
  219.6 69.6 %psum.22 = f32[]{:T(128)} all-reduce(f32[]{:T(128)} %reduce_sum.28), channel_id=1, replica_groups=mesh['pop'=32,'wa'=8] {'pop'}, use_global_device_ids=true, to_apply=%region_3.0 | all-reduce | flops 1 | bytes 8 | tf_op jit(solution)/shard_map/psum | solution.py:29
  289.9 0.6 multiply_reduce_fusion.1
  290.5 66.5 %psum.23 = f32[]{:T(128)} all-reduce(f32[]{:T(128)} %multiply_reduce_fusion.1), channel_id=1, replica_groups=mesh['pop'=32,'wa'=8] {'pop'}, use_global_device_ids=true, to_apply=%region_5.0 | all-reduce | flops 1 | bytes 8 | tf_op jit(solution)/shard_map/psum | solution.py:31
  357.8 0.0 copy-done.1
  357.8 0.0 copy-start.2
  357.8 2.8 fusion.7
  360.6 0.0 reduce-scatter.2.cloned.1.call-update
  360.6 0.0 copy-done.2
  360.6 115.9 %reduce-scatter.2.cloned.1.call-done = f32[64,512]{1,0:T(8,128)} async-done(((f32[2048,512]{1,0:T(8,128)}), f32[64,512]{1,0:T(8,128)}) %reduce-scatter.2.cloned.1.call-update) | async-done | bytes 131088 | tf_op jit(solution)/shard_map/reduce_scatter | solution.py:36
  476.5 1.6 broadcast_multiply_fusion
  (4 shorter events, 0.0 us)
Async XLA Ops:
  7.2 3.6 copy-start
  7.2 179.6 %all-gather.2.cloned.1.call-start = ((), (), s32[]{:S(2)}) async-start(), calls=%async_computation.1 | async-start | bytes 18874368 | tf_op jit(solution)/shard_map/all_gather | solution.py:16
  7.9 468.6 %reduce-scatter.2.cloned.1.call-start = ((), (), s32[]{:S(2)}) async-start(), calls=%async_computation.2 | async-start | bytes 4325376 | tf_op jit(solution)/shard_map/reduce_scatter | solution.py:36
  10.8 175.9 %copy-start.3 = (f32[2048]{0:T(1024)S(1)}, f32[2048]{0:T(1024)}, u32[]{:S(2)}) copy-start(f32[2048]{0:T(1024)} %param.9) | copy-start | bytes 24580
  25.8 331.9 %copy-start.1 = (bf16[256,2048]{1,0:T(8,128)(2,1)S(1)}, bf16[256,2048]{1,0:T(8,128)(2,1)}, u32[]{:S(2)}) copy-start(bf16[256,2048]{1,0:T(8,128)(2,1)} %param.8) | copy-start | bytes 3145732
  357.8 2.8 copy-start.2
Sparse Core Ops, SparseCore 0:
  9.8 176.8 all-gather.1
  360.7 115.7 reduce-scatter.1
where the time goes:
time: 489 us; the launch traced here: 485 us
  waiting for transfers between devices  278 us (57%)
  blocking collectives  149 us (30%)
  matrix products  37 us (8%)
  between operations  15.4 us (3%)
  other arithmetic  5.62 us (1%)
    all_gather x1, waiting for transfers between devices, shards(): lax.all_gather(weight, 'wa', axis=1, tiled=True)  161 us
    reduce_scatter x1, waiting for transfers between devices, shards(): lax.psum_scatter(lax.dot_general(scaled, in_block, (((0,), (0,)), ((), ()...  116 us
    psum x1, blocking collectives, shards(): total = lax.psum(jnp.sum(fitness), 'pop')  69.6 us
    psum x1, blocking collectives, shards(): spread = lax.psum(jnp.sum((fitness - mean) ** 2), 'pop') / member_count  66.5 us
    dot_general x1, matrix products, shards(): lax.dot_general(flat, lax.all_gather(weight, 'wa', axis=1, tiled=True), (...  19.3 us
    dot_general x1, matrix products, shards(): jnp.einsum('mrd,md->mr', inputs, factor_in, preferred_element_type=jnp.fl...  14.9 us
    psum x1, blocking collectives, shards(): fitness = lax.psum(partial_fit, 'wa')  13 us
  transfers between devices with their start and end apart: 2, of which 2 were waited for; matrix products, arithmetic and copies ran while one was open for 4% of the time, Pallas kernels for 0%

commit v1 on v0

v1 whole, which is shorter than its diff:
```python
import functools

import jax
import jax.numpy as jnp
import numpy as np
from jax import lax
from jax.experimental import pallas as pl
from jax.experimental.pallas import tpu as pltpu
from jax.sharding import Mesh, PartitionSpec as P

perturb_scale = 0.5
epsilon = 1e-05

XH, Z, CORE, XL, Y = 2, 8, 2, 2, 4
AXES = ("xh", "z", "core", "xl", "y")
SIZES = (XH, Z, CORE, XL, Y)
WA = XL * Y
ROWS_ALL = 24
VMEM_BYTES = 48 * 1024 * 1024


def permutation(move):
    pairs = []
    for i in range(int(np.prod(SIZES))):
        at = [int(v) for v in np.unravel_index(i, SIZES)]
        to = move(*at)
        pairs.append((i, int(np.ravel_multi_index(to, SIZES))))
    return pairs


def go_y(step):
    def move(xh, z, c, xl, y):
        s = step if c == 0 else -step
        return (xh, z, c, xl, (y + s) % Y)

    return permutation(move)


def go_x():
    def move(xh, z, c, xl, y):
        x = xh * 2 + xl
        if c == 0:
            x = x ^ 1
        else:
            x = (x + 1) % 4 if x % 2 else (x - 1) % 4
        return (x // 2, z, c, x % 2, y)

    return permutation(move)


def go_core():
    return permutation(lambda xh, z, c, xl, y: (xh, z, 1 - c, xl, y))


def nt_dot(a, b):
    return lax.dot_general(a, b, (((1,), (1,)), ((), ())), preferred_element_type=jnp.float32)


def group_kernel(count, has_acc, kidx, *refs):
    x_own = refs[:count]
    x_oth = refs[count : 2 * count]
    ws = refs[2 * count : 3 * count]
    rest = refs[3 * count :]
    acc_in = rest[0] if has_acc else None
    out = rest[-1]
    tile = out.shape[2]
    width = out.shape[3]
    for side, xs in ((0, x_own), (1, x_oth)):
        total = None
        for x, w in zip(xs, ws):
            part = nt_dot(x[...].reshape(3 * tile, x.shape[2]), w[...])
            total = part if total is None else total + part
        total = total.reshape(3, tile, width)
        if has_acc:
            total = total + acc_in[side]
        out[side] = total


def group_matmul(kidx, x_own, x_oth, ws, acc, tile=128):
    count = len(ws)
    members = x_own.shape[1]
    block = ws[0].shape[1]
    width = ws[0].shape[0]

    def x_spec(s):
        return pl.BlockSpec((3, tile, block), lambda i, k, s=s: (0, i, k[s]))

    specs = [x_spec(s) for s in range(count)] * 2
    specs += [pl.BlockSpec((width, block), lambda i, k: (0, 0))] * count
    acc_spec = pl.BlockSpec((2, 3, tile, width), lambda i, k: (0, 0, i, 0))
    args = [x_own] * count + [x_oth] * count + list(ws)
    alias = {}
    if acc is not None:
        specs.append(acc_spec)
        args.append(acc)
        alias = {len(args): 0}
    flops = 2 * 2 * 3 * members * width * block * count
    return pl.pallas_call(
        functools.partial(group_kernel, count, acc is not None),
        out_shape=jax.ShapeDtypeStruct((2, 3, members, width), jnp.float32),
        grid_spec=pltpu.PrefetchScalarGridSpec(
            num_scalar_prefetch=1,
            grid=(members // tile,),
            in_specs=specs,
            out_specs=acc_spec,
        ),
        input_output_aliases=alias,
        compiler_params=pltpu.CompilerParams(vmem_limit_bytes=VMEM_BYTES),
        cost_estimate=pl.CostEstimate(flops=flops, bytes_accessed=16 * 1024 * 1024, transcendentals=0),
    )(kidx, *args)


def last_kernel(kidx, x_own, x_oth, w, acc, low, fout, readout, out):
    tile = acc.shape[2]
    width = acc.shape[3]
    chunk = 256
    ones = jnp.ones((8, 128), jnp.float32)
    for side, x in ((0, x_own), (1, x_oth)):
        total = jnp.zeros((tile, 128), jnp.float32)
        flat = x[...].reshape(3 * tile, x.shape[2])
        for j in range(0, width, chunk):
            cols = pl.ds(j, chunk)
            part = nt_dot(flat, w[cols, :]).reshape(3, tile, chunk)
            shift = fout[side, :, cols].astype(jnp.float32)
            read = readout[:, cols]
            summed = None
            for r in range(3):
                pert = part[r] + acc[side, r, :, cols] + low[side, r] * shift
                term = jnp.tanh(pert)
                summed = term if summed is None else summed + term
            summed = summed * read
            for h in range(0, chunk, 128):
                total = total + summed[:, h : h + 128]
        out[side] = lax.dot_general(
            ones,
            total,
            (((1,), (1,)), ((), ())),
            preferred_element_type=jnp.float32,
            precision=lax.Precision.HIGHEST,
        )


def last_matmul(kidx, x_own, x_oth, w, acc, low, fout, readout, tile=128):
    members = x_own.shape[1]
    width, block = w.shape
    x_spec = pl.BlockSpec((3, tile, block), lambda i, k: (0, i, k[0]))
    return pl.pallas_call(
        last_kernel,
        out_shape=jax.ShapeDtypeStruct((2, 8, members), jnp.float32),
        grid_spec=pltpu.PrefetchScalarGridSpec(
            num_scalar_prefetch=1,
            grid=(members // tile,),
            in_specs=[
                x_spec,
                x_spec,
                pl.BlockSpec((width, block), lambda i, k: (0, 0)),
                pl.BlockSpec((2, 3, tile, width), lambda i, k: (0, 0, i, 0)),
                pl.BlockSpec((2, 3, tile, 1), lambda i, k: (0, 0, i, 0)),
                pl.BlockSpec((2, tile, width), lambda i, k: (0, i, 0)),
                pl.BlockSpec((1, width), lambda i, k: (0, 0)),
            ],
            out_specs=pl.BlockSpec((2, 8, tile), lambda i, k: (0, 0, i)),
        ),
        compiler_params=pltpu.CompilerParams(vmem_limit_bytes=VMEM_BYTES),
        cost_estimate=pl.CostEstimate(
            flops=2 * 6 * members * width * block,
            bytes_accessed=12 * 1024 * 1024,
            transcendentals=6 * members * width,
        ),
    )(kidx, x_own, x_oth, w, acc, low, fout, readout)


def step_kernel(place, fit, fout_t, fin, part, util):
    values = fit[...]
    count = values.shape[0] * values.shape[1]
    mean = jnp.sum(values) / count
    spread = jnp.sum((values - mean) ** 2) / count
    root = jnp.sqrt(jnp.full((1, 1), spread + epsilon, jnp.float32))
    xh, z, c = place[0], place[1], place[2]
    util[...] = (fit[pl.ds(xh * 16 + z * 2 + c, 1), :] - mean) / root
    total = None
    members = fin.shape[1]
    for k in range(Z):
        row = (fit[pl.ds(xh * 16 + k * 2 + c, 1), :] - mean) / root
        scaled = (fout_t[:, k * members : (k + 1) * members].astype(jnp.float32) * row).astype(jnp.bfloat16)
        one = jnp.dot(scaled, fin[k], preferred_element_type=jnp.float32)
        total = one if total is None else total + one
    part[...] = total * (1.0 / np.sqrt(float(count)))


def weight_part(place, fit, fout_t, fin):
    rows = fout_t.shape[0]
    members, cols = fin.shape[1], fin.shape[2]
    vmem = pl.BlockSpec(memory_space=pltpu.VMEM)
    return pl.pallas_call(
        step_kernel,
        out_shape=(
            jax.ShapeDtypeStruct((rows, cols), jnp.float32),
            jax.ShapeDtypeStruct((1, members), jnp.float32),
        ),
        in_specs=[pl.BlockSpec(memory_space=pltpu.SMEM), vmem, vmem, vmem],
        out_specs=(vmem, vmem),
        compiler_params=pltpu.CompilerParams(vmem_limit_bytes=VMEM_BYTES),
        cost_estimate=pl.CostEstimate(
            flops=2 * rows * Z * members * cols, bytes_accessed=4 * 1024 * 1024, transcendentals=0
        ),
    )(place, fit, fout_t, fin)


def share(x, axes, count):
    return lax.all_to_all(jnp.broadcast_to(x[None], (count,) + x.shape), axes, 0, 0, tiled=True)


def shards(inputs, weight, factor_in, factor_out, readout):
    members, rows_here, width = inputs.shape
    out_width, block = weight.shape
    half = out_width // 2
    xh, z, c, xl, y = (lax.axis_index(a) for a in AXES)
    wa = xl * Y + y
    sign = 1 - 2 * c
    y_fwd, y_bwd, x_go, core_go = go_y(1), go_y(-1), go_x(), go_core()

    def send(v, pairs):
        return lax.ppermute(v, AXES, pairs)

    def col(xl_at, off):
        return xl_at * Y + lax.rem(y + off + Y, Y)

    xo = 1 - xl
    k_own, k_a, k_b, k_c = col(xl, 0), col(xl, -sign), col(xl, sign), col(xl, 2)
    k_d, k_e, k_f, k_g = col(xo, 0), col(xo, -sign), col(xo, sign), col(xo, 2)

    x_own = inputs.transpose(1, 0, 2)
    w_own = lax.dynamic_slice_in_dim(weight, c * half, half, 0)

    w_a = send(w_own, y_fwd)
    w_d = send(w_own, x_go)
    x_oth = send(x_own, core_go)

    fin_here = lax.dynamic_slice_in_dim(factor_in, wa * block, block, 1)
    fin_all = lax.all_gather(fin_here, "z", axis=0)
    m_slice = members // WA
    fout_here = lax.dynamic_slice_in_dim(factor_out, wa * m_slice, m_slice, 0)
    pieces = fout_here.reshape(m_slice, XH, Z, CORE, out_width // (XH * Z * CORE))
    pieces = pieces.transpose(2, 0, 1, 3, 4).reshape(Z, m_slice, out_width // Z)
    pieces = lax.all_to_all(pieces, "z", 0, 0, tiled=True)
    fout_all = lax.all_gather(pieces, ("xl", "y"), axis=0)
    fout_t = fout_all.transpose(3, 1, 0, 2).reshape(out_width // Z, Z * members)

    low_own = perturb_scale * jnp.sum(
        x_own.astype(jnp.float32) * factor_in.astype(jnp.float32)[None], axis=-1
    )
    read_mine = lax.dynamic_slice_in_dim(readout, c * half, half, 0)[None]
    fout_mine = lax.dynamic_slice_in_dim(factor_out, c * half, half, 1)
    fout_theirs = lax.dynamic_slice_in_dim(factor_out, (1 - c) * half, half, 1)
    low_oth = send(low_own, core_go)
    fout_oth = send(fout_theirs, core_go)
    low = jnp.stack([low_own, low_oth])[..., None]
    fout = jnp.stack([fout_mine, fout_oth])

    def idx(*ks):
        return jnp.stack(ks).astype(jnp.int32)

    w_b = send(w_own, y_bwd)
    w_e = send(w_a, x_go)
    acc = group_matmul(idx(k_own, k_a, k_d), x_own, x_oth, [w_own, w_a, w_d], None)
    w_f = send(w_b, x_go)
    w_c = send(w_a, y_fwd)
    acc = group_matmul(idx(k_b, k_e), x_own, x_oth, [w_b, w_e], acc)
    quarter = half // 2
    w_g0 = send(w_c[:quarter], x_go)
    w_g1 = send(w_e[quarter:], y_fwd)
    acc = group_matmul(idx(k_f, k_c), x_own, x_oth, [w_f, w_c], acc)
    w_g = jnp.concatenate([w_g0, w_g1], axis=0)
    partial = last_matmul(idx(k_g), x_own, x_oth, w_g, acc, low, fout, read_mine)[:, 0, :]

    by_core = jnp.where(c == 0, partial, partial[::-1])
    spread_out = share(by_core.reshape(2 * members), ("core", "xl", "y"), CORE * WA)
    fit_chip = jnp.sum(spread_out.reshape(CORE * WA, 2 * members), axis=0) / ROWS_ALL
    fit = share(fit_chip, ("xh", "z"), XH * Z).reshape(XH * Z * CORE, members)

    part, util = weight_part(idx(xh, z, c), fit, fout_t, fin_all)
    out_rows = part.shape[0] // (XH * CORE)
    swapped = lax.all_to_all(part.reshape(XH * CORE, out_rows, block), ("xh", "core"), 0, 0, tiled=True)
    return jnp.sum(swapped, axis=0), util.reshape(members)


def solution(mesh):
    fine = Mesh(mesh.devices.reshape(SIZES), AXES)
    pop, wa = ("xh", "z", "core"), ("xl", "y")
    placed = (P(pop, wa, None), P(None, wa), P(pop, None), P(pop, None), P())
    return jax.shard_map(
        shards, mesh=fine, in_specs=placed, out_specs=(P(pop, wa), P(pop)), check_vma=False
    )
```

time: 489 us -> 182 us (0.37)
  waiting for transfers between devices: 278 us -> 43.2 us
  blocking collectives: 149 us -> 13.4 us
  starting transfers between devices: 0.08 us -> 43.3 us
  matrix products: 37 us -> 0 us
  Pallas kernels: 0 us -> 35.2 us
  local copies, waits for them, and re-layouts: 0.11 us -> 18.5 us
  other arithmetic: 5.62 us -> 13.2 us
    all_gather x1 -> x2, waiting for transfers between devices: 161 us -> 0.02 us  [the longest x1 0.02 us: shards(): fin_all = lax.all_gather(fin_here, 'z', axis=0)]
    psum x3 -> x0, blocking collectives: 149 us -> none  [the longest x1 69.6 us: shards(): total = lax.psum(jnp.sum(fitness), 'pop')]
    reduce_scatter x1 -> x0, waiting for transfers between devices: 116 us -> none  [shards(): lax.psum_scatter(lax.dot_general(scaled, in_block, (((0,), (0,)), ((), ()...]
    dot_general x3 -> x0, matrix products: 37 us -> none  [the longest x1 19.3 us: shards(): lax.dot_general(flat, lax.all_gather(weight, 'wa', axis=1, tiled=True), (...]
    pallas_call x0 -> x5, Pallas kernels: none -> 35.2 us  [the longest x3 27.8 us: group_matmul(): pl.pallas_call(functools.partial(group_kernel, count, acc is not None), o...]
    ppermute x0 -> x11, starting transfers between devices: none -> 28.6 us  [send(): return lax.ppermute(v, AXES, pairs)]
    ppermute x0 -> x11, waiting for transfers between devices: none -> 24 us  [send(): return lax.ppermute(v, AXES, pairs)]
    all_to_all x0 -> x3, waiting for transfers between devices: none -> 19.1 us  [the longest x2 10.8 us: share(): lax.all_to_all(jnp.broadcast_to(x[None], (count,) + x.shape), axes, 0, 0,...]
  transfers between devices with their start and end apart: 2 -> 16, of which waited for: 2 -> 7; matrix products, arithmetic and copies ran while one was open for 4% -> 16% of each run, Pallas kernels for 0% -> 18%
where the time goes in v1:
time: 182 us; the launch traced here: 181 us
  starting transfers between devices  43.3 us (24%)
  waiting for transfers between devices  43.2 us (24%)
  Pallas kernels  35.2 us (19%)
  local copies, waits for them, and re-layouts  18.5 us (10%)
  between operations  14.2 us (8%)
  blocking collectives  13.4 us (7%)
  other arithmetic  13.2 us (7%)
    ppermute x11, starting transfers between devices, send(): return lax.ppermute(v, AXES, pairs)  28.6 us
    pallas_call x3, Pallas kernels, group_matmul(): pl.pallas_call(functools.partial(group_kernel, count, acc is not None), o...  27.8 us
    ppermute x11, waiting for transfers between devices, send(): return lax.ppermute(v, AXES, pairs)  24 us
    all_to_all x1, blocking collectives, shards(): lax.all_to_all(part.reshape(XH * CORE, out_rows, block), ('xh', 'core'),...  13.4 us
    all_to_all x2, waiting for transfers between devices, share(): lax.all_to_all(jnp.broadcast_to(x[None], (count,) + x.shape), axes, 0, 0,...  10.8 us
    all_to_all x1, waiting for transfers between devices, shards(): pieces = lax.all_to_all(pieces, 'z', 0, 0, tiled=True)  8.31 us
    all_to_all x2, starting transfers between devices, share(): lax.all_to_all(jnp.broadcast_to(x[None], (count,) + x.shape), axes, 0, 0,...  8.26 us
    all_to_all x1, starting transfers between devices, shards(): pieces = lax.all_to_all(pieces, 'z', 0, 0, tiled=True)  6.45 us
  transfers between devices with their start and end apart: 16, of which 7 were waited for; matrix products, arithmetic and copies ran while one was open for 16% of the time, Pallas kernels for 18%

profile of v1, /device:TPU:1, one launch (start us, length us, event | category | flops | bytes accessed | tf_op | source)
XLA Modules:
  0.0 181.1 jit_solution(11300741839783178964)
XLA Ops:
  7.2 3.3 %collective-permute-start = (bf16[3,256,4096]{2,1,0:T(8,128)(2,1)}, bf16[3,256,4096]{2,1,0:T(8,128)(2,1)}, u32[]{:S(2)}, u32[]{:S(2)}) collective-permute-start(bf16[3,256,4096]{2,1,0:T(8,128)(2,1)} %bitcast.40), channel_id=1, source_target_pairs={{0,8},{1,9},{2,10},{3,11},{4,12},{5,13},{6,14},{7,15},{8,0},{9,1},... | collective-permute-start | bytes 18874376 | tf_op jit(solution)/shard_map/ppermute | solution.py:224
  12.7 6.5 %all-to-all-start.2 = ((bf16[8,32,256]{2,1,0:T(8,128)(2,1)}), bf16[8,32,256]{2,1,0:T(8,128)(2,1)S(1)}, u32[]{:S(2)}, u32[]{:S(2)}) async-start(bf16[8,32,256]{2,1,0:T(8,128)(2,1)} %reshape.52), calls=%async_computation.2 | async-start | bytes 262144 | tf_op jit(solution)/shard_map/all_to_all | solution.py:246
  19.2 8.3 %all-to-all-done.2 = bf16[8,32,256]{2,1,0:T(8,128)(2,1)S(1)} async-done(((bf16[8,32,256]{2,1,0:T(8,128)(2,1)}), bf16[8,32,256]{2,1,0:T(8,128)(2,1)S(1)}, u32[]{:S(2)}, u32[]{:S(2)}) %all-to-all-start.2) | async-done | bytes 131104 | tf_op jit(solution)/shard_map/all_to_all | solution.py:246
  28.4 2.8 %collective-permute-start.1 = (bf16[1024,512]{1,0:T(8,128)(2,1)S(1)}, bf16[1024,512]{1,0:T(8,128)(2,1)}, u32[]{:S(2)}, u32[]{:S(2)}) collective-permute-start(bf16[1024,512]{1,0:T(8,128)(2,1)S(1)} %constant_dynamic-slice_fusion.3.refs_6_), channel_id=1, source_target_pairs={{0,1},{1,2},{2,3},{3,0},{4,5},{5,6},{6,7},{7,4},{8,11},{9,8},{10,9... | collective-permute-start | bytes 3145736 | tf_op jit(solution)/shard_map/ppermute | solution.py:224
  31.2 15.1 %collective-permute-done.1.refs_7_ = bf16[1024,512]{1,0:T(8,128)(2,1)} collective-permute-done((bf16[1024,512]{1,0:T(8,128)(2,1)S(1)}, bf16[1024,512]{1,0:T(8,128)(2,1)}, u32[]{:S(2)}, u32[]{:S(2)}) %collective-permute-start.1) | collective-permute-done | bytes 1048608 | tf_op jit(solution)/shard_map/ppermute | solution.py:224
  46.3 2.3 %collective-permute-start.4 = (bf16[1024,512]{1,0:T(8,128)(2,1)}, bf16[1024,512]{1,0:T(8,128)(2,1)}, u32[]{:S(2)}, u32[]{:S(2)}) collective-permute-start(bf16[1024,512]{1,0:T(8,128)(2,1)} %collective-permute-done.1.refs_7_), channel_id=1, source_target_pairs={{0,4},{1,5},{2,6},{3,7},{4,0},{5,1},{6,2},{7,3},{8,140},{9,141},{1... | collective-permute-start | bytes 3145736 | tf_op jit(solution)/shard_map/ppermute | solution.py:224
  50.3 3.6 %collective-permute-start.2 = (bf16[1024,512]{1,0:T(8,128)(2,1)}, bf16[1024,512]{1,0:T(8,128)(2,1)}, u32[]{:S(2)}, u32[]{:S(2)}) collective-permute-start(bf16[1024,512]{1,0:T(8,128)(2,1)} %collective-permute-done.1.refs_7_), channel_id=1, source_target_pairs={{0,1},{1,2},{2,3},{3,0},{4,5},{5,6},{6,7},{7,4},{8,11},{9,8},{10,9... | collective-permute-start | bytes 3145736 | tf_op jit(solution)/shard_map/ppermute | solution.py:224
  54.3 4.1 %convert_element_type.7 = f32[256,4096]{1,0:T(8,128)} convert(bf16[256,4096]{1,0:T(8,128)(2,1)} %param.7) | non-fusion elementwise | flops 1048576 | bytes 6291456 | tf_op jit(solution)/shard_map/convert_element_type | solution.py:251
  58.4 2.2 %dynamic-slice_bitcast_fusion = (bf16[1,256,1024]{2,1,0:T(8,128)(2,1)}, bf16[256,1024]{1,0:T(8,128)(2,1)}) fusion(bf16[256,2048]{1,0:T(8,128)(2,1)} %param.8, s32[]{:T(128)S(6)} %select_n.23, s32[]{:T(128)S(6)} %select_n.24), kind=kLoop, calls=%fused_computation.3 | loop fusion | bytes 2097160 | tf_op jit(solution)/shard_map/stack | solution.py:259
  61.8 7.4 %collective-permute-start.10 = (bf16[256,1024]{1,0:T(8,128)(2,1)}, bf16[256,1024]{1,0:T(8,128)(2,1)}, u32[]{:S(2)}, u32[]{:S(2)}) collective-permute-start(bf16[256,1024]{1,0:T(8,128)(2,1)} %get-tuple-element.7), channel_id=1, source_target_pairs={{0,8},{1,9},{2,10},{3,11},{4,12},{5,13},{6,14},{7,15},{8,0},{9,1},... | collective-permute-start | bytes 1572872 | tf_op jit(solution)/shard_map/ppermute | solution.py:224
  69.1 5.4 %multiply_reduce_fusion = f32[3,256]{1,0:T(4,128)S(1)} fusion(f32[256,4096]{1,0:T(8,128)} %convert_element_type.7, bf16[256,3,4096]{2,0,1:T(8,128)(2,1)} %param.5), kind=kLoop, calls=%fused_computation | loop fusion | flops 9436416 | bytes 10488832 | tf_op jit(solution)/shard_map/reduce_sum | solution.py:250
  74.5 3.6 %collective-permute-done.2.refs_5_ = bf16[1024,512]{1,0:T(8,128)(2,1)} collective-permute-done((bf16[1024,512]{1,0:T(8,128)(2,1)}, bf16[1024,512]{1,0:T(8,128)(2,1)}, u32[]{:S(2)}, u32[]{:S(2)}) %collective-permute-start.2) | collective-permute-done | bytes 1048608 | tf_op jit(solution)/shard_map/ppermute | solution.py:224
  78.1 5.8 %collective-permute-start.9 = (f32[3,256]{1,0:T(4,128)S(1)}, f32[3,256]{1,0:T(4,128)S(1)}, u32[]{:S(2)}, u32[]{:S(2)}) collective-permute-start(f32[3,256]{1,0:T(4,128)S(1)} %get-tuple-element.9), channel_id=1, source_target_pairs={{0,8},{1,9},{2,10},{3,11},{4,12},{5,13},{6,14},{7,15},{8,0},{9,1},... | collective-permute-start | bytes 9224 | tf_op jit(solution)/shard_map/ppermute | solution.py:224
  93.4 4.1 %collective-permute-done.3 = bf16[512,512]{1,0:T(8,128)(2,1)} collective-permute-done((bf16[512,512]{1,0:T(8,128)(2,1)}, bf16[512,512]{1,0:T(8,128)(2,1)}, u32[]{:S(2)}, u32[]{:S(2)}) %collective-permute-start.3) | collective-permute-done | bytes 524320 | tf_op jit(solution)/shard_map/ppermute | solution.py:224
  98.9 9.9 %shard_map.68.refs_6_ = f32[2,3,256,1024]{3,2,1,0:T(8,128)} custom-call(s32[3]{0:T(128)S(1)} %pad_add_fusion.3.kidx, bf16[3,256,4096]{2,1,0:T(8,128)(2,1)} %bitcast.41, bf16[3,256,4096]{2,1,0:T(8,128)(2,1)} %bitcast.42, bf16[3,256,4096]{2,1,0:T(8,128)(2,1)} %bitcast.43, bf16[3,256,4096]{2,1,0:T(8,128)(2,1)} %collective-permute-done.refs_3_.refs_4_.refs_5_.refs_2_.x_oth, ...), custom_call_target="tpu_custom_call" | custom-call | flops 4831838208 | bytes 16777216 | tf_op jit(solution)/shard_map/pallas_call | solution.py:98
  108.8 8.9 %shard_map.69.refs_6_ = f32[2,3,256,1024]{3,2,1,0:T(8,128)} custom-call(s32[2]{0:T(128)S(1)} %pad_add_fusion.2.kidx, bf16[3,256,4096]{2,1,0:T(8,128)(2,1)} %bitcast.44, bf16[3,256,4096]{2,1,0:T(8,128)(2,1)} %bitcast.45, bf16[3,256,4096]{2,1,0:T(8,128)(2,1)} %collective-permute-done.refs_3_.refs_4_.refs_5_.refs_2_.x_oth, ...), custom_call_target="tpu_custom_call", output_to_operand_aliasing={{}: (7, {})} | custom-call | flops 3221225472 | bytes 16777216 | tf_op jit(solution)/shard_map/pallas_call | solution.py:98
  117.7 8.9 %shard_map.70.acc = f32[2,3,256,1024]{3,2,1,0:T(8,128)} custom-call(s32[2]{0:T(128)S(1)} %pad_add_fusion.1.kidx, bf16[3,256,4096]{2,1,0:T(8,128)(2,1)} %bitcast.46, bf16[3,256,4096]{2,1,0:T(8,128)(2,1)} %bitcast.47, bf16[3,256,4096]{2,1,0:T(8,128)(2,1)} %collective-permute-done.refs_3_.refs_4_.refs_5_.refs_2_.x_oth, ...), custom_call_target="tpu_custom_call", output_to_operand_aliasing={{}: (7, {})} | custom-call | flops 3221225472 | bytes 16777216 | tf_op jit(solution)/shard_map/pallas_call | solution.py:98
  126.7 5.5 %shard_map.71 = f32[2,8,256]{2,1,0:T(8,128)S(1)} custom-call(s32[1]{0:T(128)} %bitcast.3.kidx, bf16[3,256,4096]{2,1,0:T(8,128)(2,1)} %bitcast.48, bf16[3,256,4096]{2,1,0:T(8,128)(2,1)} %collective-permute-done.refs_3_.refs_4_.refs_5_.refs_2_.x_oth, bf16[1024,512]{1,0:T(8,128)(2,1)S(1)} %pad_maximum_fusion.w, f32[2,3,256,1024]{3,2,1,0:T(8,128)} %shard_map.70.acc, ...), custom_call_target="tpu_custom_call" | custom-call | flops 1610612736 | bytes 12582912 | tf_op jit(solution)/shard_map/pallas_call | solution.py:147
  133.0 4.2 %all-to-all-start = ((f32[16,1,512]{2,1,0:T(1,128)}), f32[16,1,512]{2,1,0:T(1,128)S(1)}, u32[]{:S(2)}, u32[]{:S(2)}) async-start(f32[16,1,512]{2,1,0:T(1,128)} %broadcast_in_dim.23), calls=%async_computation | async-start | bytes 65536 | tf_op jit(solution)/shard_map/all_to_all | solution.py:211
  137.2 5.8 %all-to-all-done = f32[16,1,512]{2,1,0:T(1,128)S(1)} async-done(((f32[16,1,512]{2,1,0:T(1,128)}), f32[16,1,512]{2,1,0:T(1,128)S(1)}, u32[]{:S(2)}, u32[]{:S(2)}) %all-to-all-start) | async-done | bytes 32800 | tf_op jit(solution)/shard_map/all_to_all | solution.py:211
  143.7 4.0 %all-to-all-start.1 = ((f32[16,1,512]{2,1,0:T(1,128)}), f32[16,1,512]{2,1,0:T(1,128)S(1)}, u32[]{:S(2)}, u32[]{:S(2)}) async-start(f32[16,1,512]{2,1,0:T(1,128)} %broadcast_in_dim.24), calls=%async_computation.1 | async-start | bytes 65536 | tf_op jit(solution)/shard_map/all_to_all | solution.py:211
  147.8 2.3 %copy.32 = bf16[256,8,8,32]{0,3,2,1:T(8,128)(2,1)} copy(bf16[256,8,8,32]{0,3,1,2:T(8,128)(2,1)} %bitcast.50) | data formatting | bytes 2097152 | tf_op jit(solution)/shard_map/transpose | solution.py:248
  151.6 5.0 %all-to-all-done.1 = f32[16,1,512]{2,1,0:T(1,128)S(1)} async-done(((f32[16,1,512]{2,1,0:T(1,128)}), f32[16,1,512]{2,1,0:T(1,128)S(1)}, u32[]{:S(2)}, u32[]{:S(2)}) %all-to-all-start.1) | async-done | bytes 32800 | tf_op jit(solution)/shard_map/all_to_all | solution.py:211
  160.2 13.4 %all_to_all.22 = f32[4,64,512]{2,1,0:T(8,128)S(1)} all-to-all(f32[4,64,512]{2,1,0:T(8,128)S(1)} %bitcast.38), channel_id=1, replica_groups=mesh['xh'=2,'z'=8,'core'=2,'xl'=2,'y'=4] {'xh','core'}, dimensions={0} | all-to-all | bytes 1048576 | tf_op jit(solution)/shard_map/all_to_all | solution.py:284
  (63 shorter events, 24.2 us)
Async XLA Ops:
  7.2 21.1 %copy-start = (bf16[2048,512]{1,0:T(8,128)(2,1)S(1)}, bf16[2048,512]{1,0:T(8,128)(2,1)}, u32[]{:S(2)}) copy-start(bf16[2048,512]{1,0:T(8,128)(2,1)} %param.6) | copy-start | bytes 6291460
  7.2 91.7 %collective-permute-start = (bf16[3,256,4096]{2,1,0:T(8,128)(2,1)}, bf16[3,256,4096]{2,1,0:T(8,128)(2,1)}, u32[]{:S(2)}, u32[]{:S(2)}) collective-permute-start(bf16[3,256,4096]{2,1,0:T(8,128)(2,1)} %bitcast.40), channel_id=1, source_target_pairs={{0,8},{1,9},{2,10},{3,11},{4,12},{5,13},{6,14},{7,15},{8,0},{9,1},... | collective-permute-start | bytes 18874376 | tf_op jit(solution)/shard_map/ppermute | solution.py:224
  12.7 14.8 %all-to-all-start.2 = ((bf16[8,32,256]{2,1,0:T(8,128)(2,1)}), bf16[8,32,256]{2,1,0:T(8,128)(2,1)S(1)}, u32[]{:S(2)}, u32[]{:S(2)}) async-start(bf16[8,32,256]{2,1,0:T(8,128)(2,1)} %reshape.52), calls=%async_computation.2 | async-start | bytes 262144 | tf_op jit(solution)/shard_map/all_to_all | solution.py:246
  19.2 128.6 %all-gather.5.cloned.1.call-start = ((), (), s32[]{:S(2)}) async-start(), calls=%async_computation.4 | async-start | bytes 1179648 | tf_op jit(solution)/shard_map/all_gather | solution.py:247
  27.5 0.7 copy-start.3
  28.2 128.4 %all-gather.7.cloned.1.call-start = ((), (), s32[]{:S(2)}) async-start(), calls=%async_computation.5 | async-start | bytes 2359296 | tf_op jit(solution)/shard_map/all_gather | solution.py:241
  28.4 17.9 %collective-permute-start.1 = (bf16[1024,512]{1,0:T(8,128)(2,1)S(1)}, bf16[1024,512]{1,0:T(8,128)(2,1)}, u32[]{:S(2)}, u32[]{:S(2)}) collective-permute-start(bf16[1024,512]{1,0:T(8,128)(2,1)S(1)} %constant_dynamic-slice_fusion.3.refs_6_), channel_id=1, source_target_pairs={{0,1},{1,2},{2,3},{3,0},{4,5},{5,6},{6,7},{7,4},{8,11},{9,8},{10,9... | collective-permute-start | bytes 3145736 | tf_op jit(solution)/shard_map/ppermute | solution.py:224
  46.3 15.5 %collective-permute-start.4 = (bf16[1024,512]{1,0:T(8,128)(2,1)}, bf16[1024,512]{1,0:T(8,128)(2,1)}, u32[]{:S(2)}, u32[]{:S(2)}) collective-permute-start(bf16[1024,512]{1,0:T(8,128)(2,1)} %collective-permute-done.1.refs_7_), channel_id=1, source_target_pairs={{0,4},{1,5},{2,6},{3,7},{4,0},{5,1},{6,2},{7,3},{8,140},{9,141},{1... | collective-permute-start | bytes 3145736 | tf_op jit(solution)/shard_map/ppermute | solution.py:224
  50.3 27.9 %collective-permute-start.2 = (bf16[1024,512]{1,0:T(8,128)(2,1)}, bf16[1024,512]{1,0:T(8,128)(2,1)}, u32[]{:S(2)}, u32[]{:S(2)}) collective-permute-start(bf16[1024,512]{1,0:T(8,128)(2,1)} %collective-permute-done.1.refs_7_), channel_id=1, source_target_pairs={{0,1},{1,2},{2,3},{3,0},{4,5},{5,6},{6,7},{7,4},{8,11},{9,8},{10,9... | collective-permute-start | bytes 3145736 | tf_op jit(solution)/shard_map/ppermute | solution.py:224
  53.9 45.0 %collective-permute-start.8 = (bf16[1024,512]{1,0:T(8,128)(2,1)S(1)}, bf16[1024,512]{1,0:T(8,128)(2,1)}, u32[]{:S(2)}, u32[]{:S(2)}) collective-permute-start(bf16[1024,512]{1,0:T(8,128)(2,1)S(1)} %constant_dynamic-slice_fusion.3.refs_6_), channel_id=1, source_target_pairs={{0,4},{1,5},{2,6},{3,7},{4,0},{5,1},{6,2},{7,3},{8,140},{9,141},{1... | collective-permute-start | bytes 3145736 | tf_op jit(solution)/shard_map/ppermute | solution.py:224
  54.3 34.8 %collective-permute-start.6 = (bf16[1024,512]{1,0:T(8,128)(2,1)S(1)}, bf16[1024,512]{1,0:T(8,128)(2,1)}, u32[]{:S(2)}, u32[]{:S(2)}) collective-permute-start(bf16[1024,512]{1,0:T(8,128)(2,1)S(1)} %constant_dynamic-slice_fusion.3.refs_6_), channel_id=1, source_target_pairs={{0,3},{1,0},{2,1},{3,2},{4,7},{5,4},{6,5},{7,6},{8,9},{9,10},{10,1... | collective-permute-start | bytes 3145736 | tf_op jit(solution)/shard_map/ppermute | solution.py:224
  61.8 27.1 %copy-start.4 = (f32[2048]{0:T(1024)S(1)}, f32[2048]{0:T(1024)}, u32[]{:S(2)}) copy-start(f32[2048]{0:T(1024)} %param.9) | copy-start | bytes 24580
  61.8 27.0 %collective-permute-start.10 = (bf16[256,1024]{1,0:T(8,128)(2,1)}, bf16[256,1024]{1,0:T(8,128)(2,1)}, u32[]{:S(2)}, u32[]{:S(2)}) collective-permute-start(bf16[256,1024]{1,0:T(8,128)(2,1)} %get-tuple-element.7), channel_id=1, source_target_pairs={{0,8},{1,9},{2,10},{3,11},{4,12},{5,13},{6,14},{7,15},{8,0},{9,1},... | collective-permute-start | bytes 1572872 | tf_op jit(solution)/shard_map/ppermute | solution.py:224
  78.1 9.6 %collective-permute-start.9 = (f32[3,256]{1,0:T(4,128)S(1)}, f32[3,256]{1,0:T(4,128)S(1)}, u32[]{:S(2)}, u32[]{:S(2)}) collective-permute-start(f32[3,256]{1,0:T(4,128)S(1)} %get-tuple-element.9), channel_id=1, source_target_pairs={{0,8},{1,9},{2,10},{3,11},{4,12},{5,13},{6,14},{7,15},{8,0},{9,1},... | collective-permute-start | bytes 9224 | tf_op jit(solution)/shard_map/ppermute | solution.py:224
  87.7 9.9 %collective-permute-start.3 = (bf16[512,512]{1,0:T(8,128)(2,1)}, bf16[512,512]{1,0:T(8,128)(2,1)}, u32[]{:S(2)}, u32[]{:S(2)}) collective-permute-start(bf16[512,512]{1,0:T(8,128)(2,1)} %slice.12), channel_id=1, source_target_pairs={{0,4},{1,5},{2,6},{3,7},{4,0},{5,1},{6,2},{7,3},{8,140},{9,141},{1... | collective-permute-start | bytes 1572872 | tf_op jit(solution)/shard_map/ppermute | solution.py:224
  88.8 8.8 %collective-permute-start.5 = (bf16[512,512]{1,0:T(8,128)(2,1)}, bf16[512,512]{1,0:T(8,128)(2,1)}, u32[]{:S(2)}, u32[]{:S(2)}) collective-permute-start(bf16[512,512]{1,0:T(8,128)(2,1)} %slice.13), channel_id=1, source_target_pairs={{0,1},{1,2},{2,3},{3,0},{4,5},{5,6},{6,7},{7,4},{8,11},{9,8},{10,9... | collective-permute-start | bytes 1572872 | tf_op jit(solution)/shard_map/ppermute | solution.py:224
  89.1 28.7 %collective-permute-start.7 = (bf16[1024,512]{1,0:T(8,128)(2,1)}, bf16[1024,512]{1,0:T(8,128)(2,1)}, u32[]{:S(2)}, u32[]{:S(2)}) collective-permute-start(bf16[1024,512]{1,0:T(8,128)(2,1)} %collective-permute-done.6.refs_4_), channel_id=1, source_target_pairs={{0,4},{1,5},{2,6},{3,7},{4,0},{5,1},{6,2},{7,3},{8,140},{9,141},{1... | collective-permute-start | bytes 3145736 | tf_op jit(solution)/shard_map/ppermute | solution.py:224
  117.7 9.0 %copy-start.1 = (f32[2,3,256,1]{3,2,1,0:T(8,128)S(1)}, f32[2,3,256,1]{3,2,1,0:T(8,128)}, u32[]{:S(2)}) copy-start(f32[2,3,256,1]{3,2,1,0:T(8,128)} %copy.29.low) | copy-start | bytes 18436
  133.0 10.0 %all-to-all-start = ((f32[16,1,512]{2,1,0:T(1,128)}), f32[16,1,512]{2,1,0:T(1,128)S(1)}, u32[]{:S(2)}, u32[]{:S(2)}) async-start(f32[16,1,512]{2,1,0:T(1,128)} %broadcast_in_dim.23), calls=%async_computation | async-start | bytes 65536 | tf_op jit(solution)/shard_map/all_to_all | solution.py:211
  143.7 12.9 %all-to-all-start.1 = ((f32[16,1,512]{2,1,0:T(1,128)}), f32[16,1,512]{2,1,0:T(1,128)S(1)}, u32[]{:S(2)}, u32[]{:S(2)}) async-start(f32[16,1,512]{2,1,0:T(1,128)} %broadcast_in_dim.24), calls=%async_computation.1 | async-start | bytes 65536 | tf_op jit(solution)/shard_map/all_to_all | solution.py:211
  156.7 1.6 copy-start.2
Sparse Core Ops, SparseCore 0:
  28.3 34.7 all-gather.4
  64.9 42.8 all-gather.6

commit v2 on v1

v2 whole, which is shorter than its diff:
```python
import functools

import jax
import jax.numpy as jnp
import numpy as np
from jax import lax
from jax.experimental import pallas as pl
from jax.experimental.pallas import tpu as pltpu
from jax.sharding import Mesh, PartitionSpec as P

perturb_scale = 0.5
epsilon = 1e-05

XH, Z, CORE, XL, Y = 2, 8, 2, 2, 4
AXES = ("xh", "z", "core", "xl", "y")
SIZES = (XH, Z, CORE, XL, Y)
WA = XL * Y
ROWS_ALL = 24
VMEM_BYTES = 24 * 1024 * 1024


def permutation(move):
    pairs = []
    for i in range(int(np.prod(SIZES))):
        at = [int(v) for v in np.unravel_index(i, SIZES)]
        to = move(*at)
        pairs.append((i, int(np.ravel_multi_index(to, SIZES))))
    return pairs


def go_y(step):
    def move(xh, z, c, xl, y):
        s = step if c == 0 else -step
        return (xh, z, c, xl, (y + s) % Y)

    return permutation(move)


def go_x():
    def move(xh, z, c, xl, y):
        x = xh * 2 + xl
        if c == 0:
            x = x ^ 1
        else:
            x = (x + 1) % 4 if x % 2 else (x - 1) % 4
        return (x // 2, z, c, x % 2, y)

    return permutation(move)


def go_core():
    return permutation(lambda xh, z, c, xl, y: (xh, z, 1 - c, xl, y))


def go_xh():
    return permutation(lambda xh, z, c, xl, y: (1 - xh, z, c, xl, y))


def nt_dot(a, b):
    return lax.dot_general(a, b, (((1,), (1,)), ((), ())), preferred_element_type=jnp.float32)


def fetch_columns(kidx, count, block, sources, buffers, sems):
    copies = []
    for s in range(count):
        cols = pl.ds(pl.multiple_of(kidx[s] * block, block), block)
        for side in range(2):
            copy = pltpu.make_async_copy(
                sources[side].at[:, :, cols], buffers.at[s, side], sems.at[s, side]
            )
            copy.start()
            copies.append(copy)
    return copies


def group_kernel(count, has_acc, kidx, x_own, x_oth, *refs):
    ws = refs[:count]
    acc_in = refs[count] if has_acc else None
    out, token, buffers, sems = refs[-4:]
    members, width = out.shape[2], out.shape[3]
    block = ws[0].shape[1]
    copies = fetch_columns(kidx, count, block, (x_own, x_oth), buffers, sems)
    token[...] = jnp.zeros_like(token)
    chunk = 512
    for side in range(2):
        for s in range(count):
            copies[2 * s + side].wait()
        for j in range(0, width, chunk):
            cols = pl.ds(j, chunk)
            total = None
            for s, w in enumerate(ws):
                part = nt_dot(buffers[s, side].reshape(3 * members, block), w[cols, :])
                total = part if total is None else total + part
            total = total.reshape(3, members, chunk)
            if has_acc:
                total = total + acc_in[side, :, :, cols]
            out[side, :, :, cols] = total


def group_matmul(kidx, x_own, x_oth, ws, acc):
    count = len(ws)
    members = x_own.shape[1]
    width, block = ws[0].shape
    smem = pl.BlockSpec(memory_space=pltpu.SMEM)
    vmem = pl.BlockSpec(memory_space=pltpu.VMEM)
    hbm = pl.BlockSpec(memory_space=pl.ANY)
    args = [x_own, x_oth] + list(ws)
    specs = [smem, hbm, hbm] + [vmem] * count
    alias = {}
    if acc is not None:
        specs.append(vmem)
        args.append(acc)
        alias = {len(args): 0}
    flops = 2 * 2 * 3 * members * width * block * count
    return pl.pallas_call(
        functools.partial(group_kernel, count, acc is not None),
        out_shape=(
            jax.ShapeDtypeStruct((2, 3, members, width), jnp.float32),
            jax.ShapeDtypeStruct((8, 128), jnp.float32),
        ),
        in_specs=specs,
        out_specs=(vmem, vmem),
        scratch_shapes=[
            pltpu.VMEM((count, 2, 3, members, block), jnp.bfloat16),
            pltpu.SemaphoreType.DMA((count, 2)),
        ],
        input_output_aliases=alias,
        compiler_params=pltpu.CompilerParams(vmem_limit_bytes=VMEM_BYTES),
        cost_estimate=pl.CostEstimate(flops=flops, bytes_accessed=16 * 1024 * 1024, transcendentals=0),
    )(kidx, *args)


def last_kernel(kidx, x_own, x_oth, w, acc, low_own, low_oth, fout_own, fout_oth, readout, out, buffers, sems):
    members, width = acc.shape[2], acc.shape[3]
    block = w.shape[1]
    copies = fetch_columns(kidx, 1, block, (x_own, x_oth), buffers, sems)
    chunk = 256
    ones = jnp.ones((8, 128), jnp.float32)
    for side, low, fout in ((0, low_own, fout_own), (1, low_oth, fout_oth)):
        copies[side].wait()
        total = jnp.zeros((members, 128), jnp.float32)
        for j in range(0, width, chunk):
            cols = pl.ds(j, chunk)
            part = nt_dot(buffers[0, side].reshape(3 * members, block), w[cols, :])
            part = part.reshape(3, members, chunk)
            shift = fout[:, cols].astype(jnp.float32)
            summed = None
            for r in range(3):
                pert = part[r] + acc[side, r, :, cols] + low[r] * shift
                term = jnp.tanh(pert)
                summed = term if summed is None else summed + term
            summed = summed * readout[:, cols]
            for h in range(0, chunk, 128):
                total = total + summed[:, h : h + 128]
        row = lax.dot_general(
            ones,
            total,
            (((1,), (1,)), ((), ())),
            preferred_element_type=jnp.float32,
            precision=lax.Precision.HIGHEST,
        )
        out[jnp.bitwise_xor(kidx[1], side)] = row


def last_matmul(kidx, x_own, x_oth, w, acc, low_own, low_oth, fout_own, fout_oth, readout):
    members = x_own.shape[1]
    width, block = w.shape
    smem = pl.BlockSpec(memory_space=pltpu.SMEM)
    vmem = pl.BlockSpec(memory_space=pltpu.VMEM)
    hbm = pl.BlockSpec(memory_space=pl.ANY)
    return pl.pallas_call(
        last_kernel,
        out_shape=jax.ShapeDtypeStruct((2, 8, members), jnp.float32),
        in_specs=[smem, hbm, hbm] + [vmem] * 7,
        out_specs=vmem,
        scratch_shapes=[
            pltpu.VMEM((1, 2, 3, members, block), jnp.bfloat16),
            pltpu.SemaphoreType.DMA((1, 2)),
        ],
        compiler_params=pltpu.CompilerParams(vmem_limit_bytes=VMEM_BYTES),
        cost_estimate=pl.CostEstimate(
            flops=2 * 6 * members * width * block,
            bytes_accessed=12 * 1024 * 1024,
            transcendentals=6 * members * width,
        ),
    )(kidx, x_own, x_oth, w, acc, low_own, low_oth, fout_own, fout_oth, readout)


def low_kernel(x, fin, out):
    width = fin.shape[1]
    chunk = 128
    totals = [None] * 3
    for j in range(0, width, chunk):
        cols = pl.ds(j, chunk)
        f = fin[:, cols].astype(jnp.float32)
        for r in range(3):
            term = x[r, :, cols].astype(jnp.float32) * f
            totals[r] = term if totals[r] is None else totals[r] + term
    for r in range(3):
        out[r] = perturb_scale * jnp.sum(totals[r], axis=1, keepdims=True)


def low_term(x, fin):
    rows, members, width = x.shape
    tile = 64
    return pl.pallas_call(
        low_kernel,
        out_shape=jax.ShapeDtypeStruct((rows, members, 1), jnp.float32),
        grid=(members // tile,),
        in_specs=[
            pl.BlockSpec((rows, tile, width), lambda i: (0, i, 0)),
            pl.BlockSpec((tile, width), lambda i: (i, 0)),
        ],
        out_specs=pl.BlockSpec((rows, tile, 1), lambda i: (0, i, 0)),
        compiler_params=pltpu.CompilerParams(vmem_limit_bytes=VMEM_BYTES),
        cost_estimate=pl.CostEstimate(
            flops=2 * rows * members * width, bytes_accessed=9 * 1024 * 1024, transcendentals=0
        ),
    )(x, fin)


def step_kernel(place, fit, fout_t, fin, keep, give, util):
    values = fit[...]
    count = values.shape[0] * values.shape[1]
    mean = jnp.sum(values) / count
    spread = jnp.sum((values - mean) ** 2) / count
    root = jnp.sqrt(jnp.full((1, 1), spread + epsilon, jnp.float32))
    xh, z, c = place[0], place[1], place[2]
    util[...] = (fit[pl.ds(xh * 16 + z * 2 + c, 1), :] - mean) / root
    total = None
    members = fin.shape[1]
    for k in range(Z):
        row = (fit[pl.ds(xh * 16 + k * 2 + c, 1), :] - mean) / root
        scaled = (fout_t[:, k * members : (k + 1) * members].astype(jnp.float32) * row).astype(jnp.bfloat16)
        one = jnp.dot(scaled, fin[k], preferred_element_type=jnp.float32)
        total = one if total is None else total + one
    total = total * (1.0 / np.sqrt(float(count)))
    rows = keep.shape[1]
    total = total.reshape(XH, CORE, rows, total.shape[1])
    for h in range(XH):
        at = jnp.bitwise_xor(xh, h)
        keep[at] = jnp.where(c == 0, total[h, 0], total[h, 1])
        give[at] = jnp.where(c == 0, total[h, 1], total[h, 0])


def weight_part(place, fit, fout_t, fin):
    rows = fout_t.shape[0]
    members, cols = fin.shape[1], fin.shape[2]
    vmem = pl.BlockSpec(memory_space=pltpu.VMEM)
    return pl.pallas_call(
        step_kernel,
        out_shape=(
            jax.ShapeDtypeStruct((XH, rows // (XH * CORE), cols), jnp.float32),
            jax.ShapeDtypeStruct((XH, rows // (XH * CORE), cols), jnp.float32),
            jax.ShapeDtypeStruct((1, members), jnp.float32),
        ),
        in_specs=[pl.BlockSpec(memory_space=pltpu.SMEM), vmem, vmem, vmem],
        out_specs=(vmem, vmem, vmem),
        compiler_params=pltpu.CompilerParams(vmem_limit_bytes=VMEM_BYTES),
        cost_estimate=pl.CostEstimate(
            flops=2 * rows * Z * members * cols, bytes_accessed=4 * 1024 * 1024, transcendentals=0
        ),
    )(place, fit, fout_t, fin)


def share(x, axes, count):
    return lax.all_to_all(jnp.broadcast_to(x[None], (count,) + x.shape), axes, 0, 0, tiled=True)


def shards(inputs, weight, factor_in, factor_out, readout):
    members, rows_here, width = inputs.shape
    out_width, block = weight.shape
    half = out_width // 2
    xh, z, c, xl, y = (lax.axis_index(a) for a in AXES)
    wa = xl * Y + y
    sign = 1 - 2 * c
    y_fwd, y_bwd, x_go, core_go = go_y(1), go_y(-1), go_x(), go_core()

    def send(v, pairs):
        return lax.ppermute(v, AXES, pairs)

    def col(xl_at, off):
        return xl_at * Y + lax.rem(y + off + Y, Y)

    xo = 1 - xl
    k_own, k_a, k_b, k_c = col(xl, 0), col(xl, -sign), col(xl, sign), col(xl, 2)
    k_d, k_e, k_f, k_g = col(xo, 0), col(xo, -sign), col(xo, sign), col(xo, 2)

    x_own = inputs.transpose(1, 0, 2)
    w_own = lax.dynamic_slice_in_dim(weight, c * half, half, 0)

    def idx(*ks):
        return jnp.stack(ks).astype(jnp.int32)

    def after(values, *done):
        return lax.optimization_barrier((tuple(values), done))[0]

    w_a = send(w_own, y_fwd)
    w_d = send(w_own, x_go)
    x_oth = send(x_own, core_go)

    fin_here = lax.dynamic_slice_in_dim(factor_in, wa * block, block, 1)
    fin_all = lax.all_gather(fin_here, "z", axis=0)
    rows_out = out_width // (XH * Z * CORE)
    pieces = factor_out.reshape(members, XH, Z, CORE, rows_out)
    pieces = pieces.transpose(2, 0, 1, 3, 4).reshape(Z, members, out_width // Z)
    pieces = lax.all_to_all(pieces, "z", 0, 0, tiled=True)

    w_a, w_d, w_own2 = after((w_a, w_d, w_own))
    w_b = send(w_own2, y_bwd)
    w_e = send(w_a, x_go)
    acc, token = group_matmul(idx(k_own, k_a, k_d), x_own, x_oth, [w_own, w_a, w_d], None)

    x_low, fin_low, fout_low = after((x_own, factor_in, factor_out), w_a, w_d)
    low_own = low_term(x_low, fin_low)
    read_mine = lax.dynamic_slice_in_dim(readout, c * half, half, 0)[None]
    fout_mine = lax.dynamic_slice_in_dim(fout_low, c * half, half, 1)
    fout_theirs = lax.dynamic_slice_in_dim(fout_low, (1 - c) * half, half, 1)
    fout_oth = send(fout_theirs, core_go)

    w_a3, w_b3 = after((w_a, w_b), w_e, token)
    w_f = send(w_b3, x_go)
    w_c = send(w_a3, y_fwd)
    low_oth = send(low_own, core_go)
    acc, token = group_matmul(idx(k_b, k_e), x_own, x_oth, [w_b, w_e], acc)

    quarter = half // 2
    w_c4, w_e4 = after((w_c, w_e), w_f, token)
    w_g0 = send(w_c4[:quarter], x_go)
    w_g1 = send(w_e4[quarter:], y_fwd)
    acc, token = group_matmul(idx(k_f, k_c), x_own, x_oth, [w_f, w_c], acc)
    w_g = jnp.concatenate([w_g0, w_g1], axis=0)
    partial = last_matmul(
        idx(k_g, c), x_own, x_oth, w_g, acc, low_own, low_oth, fout_mine, fout_oth, read_mine
    )[:, 0, :]

    spread_out = share(partial.reshape(2 * members), ("core", "xl", "y"), CORE * WA)
    fit_chip = jnp.sum(spread_out.reshape(CORE * WA, 2 * members), axis=0) / ROWS_ALL
    fit = share(fit_chip, ("xh", "z"), XH * Z).reshape(XH * Z * CORE, members)

    pieces = after((pieces,), partial)[0]
    fout_t = pieces.transpose(2, 0, 1).reshape(out_width // Z, Z * members)
    keep, give, util = weight_part(idx(xh, z, c), fit, fout_t, fin_all)
    summed = keep + send(give, core_go)
    weight_step = summed[0] + send(summed[1], go_xh())
    return weight_step, util.reshape(members)


def solution(mesh):
    fine = Mesh(mesh.devices.reshape(SIZES), AXES)
    pop, wa = ("xh", "z", "core"), ("xl", "y")
    placed = (P(pop, wa, None), P(None, wa), P(pop, None), P(pop, None), P())
    return jax.shard_map(
        shards, mesh=fine, in_specs=placed, out_specs=(P(pop, wa), P(pop)), check_vma=False
    )
```

time: 182 us -> 180 us (0.989)
  waiting for transfers between devices: 43.2 us -> 86.8 us
  blocking collectives: 13.4 us -> 0 us
  starting transfers between devices: 43.3 us -> 32.5 us
  other arithmetic: 13.2 us -> 2.5 us
  Pallas kernels: 35.2 us -> 25.5 us
    ppermute x11 -> x13, waiting for transfers between devices: 24 us -> 46.8 us  [send(): return lax.ppermute(v, AXES, pairs)]
    all_to_all x1, waiting for transfers between devices: 8.31 us -> 29.3 us  [shards(): pieces = lax.all_to_all(pieces, 'z', 0, 0, tiled=True)]
    ppermute x11 -> x13, starting transfers between devices: 28.6 us -> 15.2 us  [send(): return lax.ppermute(v, AXES, pairs)]
    all_to_all x1 -> x0, blocking collectives: 13.4 us -> none  [shards(): lax.all_to_all(part.reshape(XH * CORE, out_rows, block), ('xh', 'core'),...]
    pallas_call x3, Pallas kernels: 27.8 us -> 17.7 us  [group_matmul(): pl.pallas_call(functools.partial(group_kernel, count, acc is not None), o...]
    unnamed x12 -> x23, local copies, waits for them, and re-layouts: 2.26 us -> 9.49 us
    reduce_sum x2 -> x0, other arithmetic: 6.05 us -> none  [the longest x1 5.36 us: shards(): jnp.sum(x_own.astype(jnp.float32) * factor_in.astype(jnp.float32)[None],...]
    convert_element_type x1 -> x0, other arithmetic: 4.15 us -> none  [shards(): factor_in.astype(jnp.float32)[None]]
  transfers between devices with their start and end apart: 16 -> 17, of which waited for: 7 -> 12; matrix products, arithmetic and copies ran while one was open for 16% -> 6% of each run, Pallas kernels for 18% -> 13%
where the time goes in v2:
time: 180 us; the launch traced here: 179 us
  waiting for transfers between devices  86.8 us (48%)
  starting transfers between devices  32.5 us (18%)
  Pallas kernels  25.5 us (14%)
  local copies, waits for them, and re-layouts  17.7 us (10%)
  between operations  14.2 us (8%)
  other arithmetic  2.5 us (1%)
    ppermute x13, waiting for transfers between devices, send(): return lax.ppermute(v, AXES, pairs)  46.8 us
    all_to_all x1, waiting for transfers between devices, shards(): pieces = lax.all_to_all(pieces, 'z', 0, 0, tiled=True)  29.3 us
    pallas_call x3, Pallas kernels, group_matmul(): pl.pallas_call(functools.partial(group_kernel, count, acc is not None), o...  17.7 us
    ppermute x13, starting transfers between devices, send(): return lax.ppermute(v, AXES, pairs)  15.2 us
    all_to_all x2, waiting for transfers between devices, share(): lax.all_to_all(jnp.broadcast_to(x[None], (count,) + x.shape), axes, 0, 0,...  10.7 us
    all_to_all x2, starting transfers between devices, share(): lax.all_to_all(jnp.broadcast_to(x[None], (count,) + x.shape), axes, 0, 0,...  9.99 us
    unnamed x23, local copies, waits for them, and re-layouts  9.49 us
    all_to_all x1, starting transfers between devices, shards(): pieces = lax.all_to_all(pieces, 'z', 0, 0, tiled=True)  7.32 us
  transfers between devices with their start and end apart: 17, of which 12 were waited for; matrix products, arithmetic and copies ran while one was open for 6% of the time, Pallas kernels for 13%

profile of v2, /device:TPU:1, one launch (start us, length us, event | category | flops | bytes accessed | tf_op | source)
XLA Modules:
  0.0 179.3 jit_solution(7474912177993059731)
XLA Ops:
  7.2 3.3 %collective-permute-start = (bf16[3,256,4096]{2,1,0:T(8,128)(2,1)}, bf16[3,256,4096]{2,1,0:T(8,128)(2,1)}, u32[]{:S(2)}, u32[]{:S(2)}) collective-permute-start(bf16[3,256,4096]{2,1,0:T(8,128)(2,1)} %bitcast.29), channel_id=1, source_target_pairs={{0,8},{1,9},{2,10},{3,11},{4,12},{5,13},{6,14},{7,15},{8,0},{9,1},... | collective-permute-start | bytes 18874376 | tf_op jit(solution)/shard_map/ppermute | solution.py:280
  12.5 2.5 %collective-permute-start.2 = (bf16[1024,512]{1,0:T(8,128)(2,1)S(1)}, bf16[1024,512]{1,0:T(8,128)(2,1)S(1)}, u32[]{:S(2)}, u32[]{:S(2)}) collective-permute-start(bf16[1024,512]{1,0:T(8,128)(2,1)S(1)} %constant_dynamic-slice_fusion.3.refs_0_), channel_id=1, source_target_pairs={{0,4},{1,5},{2,6},{3,7},{4,0},{5,1},{6,2},{7,3},{8,140},{9,141},{1... | collective-permute-start | bytes 3145736 | tf_op jit(solution)/shard_map/ppermute | solution.py:280
  15.0 9.8 %collective-permute-done.1.refs_1_ = bf16[1024,512]{1,0:T(8,128)(2,1)} collective-permute-done((bf16[1024,512]{1,0:T(8,128)(2,1)S(1)}, bf16[1024,512]{1,0:T(8,128)(2,1)}, u32[]{:S(2)}, u32[]{:S(2)}) %collective-permute-start.1) | collective-permute-done | bytes 1048608 | tf_op jit(solution)/shard_map/ppermute | solution.py:280
  24.8 3.0 %collective-permute-done.2.refs_2_ = bf16[1024,512]{1,0:T(8,128)(2,1)S(1)} collective-permute-done((bf16[1024,512]{1,0:T(8,128)(2,1)S(1)}, bf16[1024,512]{1,0:T(8,128)(2,1)S(1)}, u32[]{:S(2)}, u32[]{:S(2)}) %collective-permute-start.2) | collective-permute-done | bytes 1048608 | tf_op jit(solution)/shard_map/ppermute | solution.py:280
  28.7 2.1 %collective-permute-start.4 = (bf16[1024,512]{1,0:T(8,128)(2,1)}, bf16[1024,512]{1,0:T(8,128)(2,1)S(1)}, u32[]{:S(2)}, u32[]{:S(2)}) collective-permute-start(bf16[1024,512]{1,0:T(8,128)(2,1)} %collective-permute-done.1.refs_1_), channel_id=1, source_target_pairs={{0,4},{1,5},{2,6},{3,7},{4,0},{5,1},{6,2},{7,3},{8,140},{9,141},{1... | collective-permute-start | bytes 3145736 | tf_op jit(solution)/shard_map/ppermute | solution.py:280
  31.8 12.0 %collective-permute-done.4.refs_1_ = bf16[1024,512]{1,0:T(8,128)(2,1)S(1)} collective-permute-done((bf16[1024,512]{1,0:T(8,128)(2,1)}, bf16[1024,512]{1,0:T(8,128)(2,1)S(1)}, u32[]{:S(2)}, u32[]{:S(2)}) %collective-permute-start.4) | collective-permute-done | bytes 1048608 | tf_op jit(solution)/shard_map/ppermute | solution.py:280
  43.8 2.0 %collective-permute-done.3.refs_0_ = bf16[1024,512]{1,0:T(8,128)(2,1)} collective-permute-done((bf16[1024,512]{1,0:T(8,128)(2,1)S(1)}, bf16[1024,512]{1,0:T(8,128)(2,1)}, u32[]{:S(2)}, u32[]{:S(2)}) %collective-permute-start.3) | collective-permute-done | bytes 1048608 | tf_op jit(solution)/shard_map/ppermute | solution.py:280
  48.5 11.6 %collective-permute-done.5.refs_1_ = bf16[1024,512]{1,0:T(8,128)(2,1)} collective-permute-done((bf16[1024,512]{1,0:T(8,128)(2,1)}, bf16[1024,512]{1,0:T(8,128)(2,1)}, u32[]{:S(2)}, u32[]{:S(2)}) %collective-permute-start.5) | collective-permute-done | bytes 1048608 | tf_op jit(solution)/shard_map/ppermute | solution.py:280
  61.0 1.9 %slice.15 = bf16[512,512]{1,0:T(8,128)(2,1)} slice(bf16[1024,512]{1,0:T(8,128)(2,1)} %collective-permute-done.5.refs_1_), slice={[0:512], [0:512]} | slice | bytes 1048576 | tf_op jit(solution)/shard_map/slice | solution.py:329
  64.9 2.8 %copy-done.1 = bf16[256,3,4096]{2,0,1:T(8,128)(2,1)S(1)} copy-done((bf16[256,3,4096]{2,0,1:T(8,128)(2,1)S(1)}, bf16[256,3,4096]{2,0,1:T(8,128)(2,1)}, u32[]{:S(2)}) %copy-start.1) | copy-done | bytes 6291480
  69.4 2.2 %shard_map.71.low_own = f32[3,256,1]{2,1,0:T(8,128)S(1)} custom-call(bf16[3,256,4096]{2,1,0:T(8,128)(2,1)S(1)} %bitcast.30, bf16[256,4096]{1,0:T(8,128)(2,1)S(1)} %copy-done.3), custom_call_target="tpu_custom_call" | custom-call | flops 6291456 | bytes 9437184 | tf_op jit(solution)/shard_map/pallas_call | solution.py:206
  74.6 6.9 %shard_map.68 = (f32[2,3,256,1024]{3,2,1,0:T(8,128)S(1)}, f32[8,128]{1,0:T(8,128)}) custom-call(s32[3]{0:T(128)S(1)} %pad_add_fusion.4.kidx, bf16[3,256,4096]{2,1,0:T(8,128)(2,1)S(1)} %bitcast.31, bf16[3,256,4096]{2,1,0:T(8,128)(2,1)} %collective-permute-done.x_oth, bf16[1024,512]{1,0:T(8,128)(2,1)S(1)} %copy-done.6, ...), custom_call_target="tpu_custom_call" | custom-call | flops 4831838208 | bytes 16777216 | tf_op jit(solution)/shard_map/pallas_call | solution.py:115
  81.5 5.2 %shard_map.69 = (f32[2,3,256,1024]{3,2,1,0:T(8,128)S(1)}, f32[8,128]{1,0:T(8,128)}) custom-call(s32[2]{0:T(128)S(1)} %pad_add_fusion.3.kidx, bf16[3,256,4096]{2,1,0:T(8,128)(2,1)S(1)} %bitcast.32, bf16[3,256,4096]{2,1,0:T(8,128)(2,1)} %collective-permute-done.x_oth, ...), custom_call_target="tpu_custom_call", output_to_operand_aliasing={{0}: (5, {})} | custom-call | flops 3221225472 | bytes 16777216 | tf_op jit(solution)/shard_map/pallas_call | solution.py:115
  86.8 5.5 %shard_map.70 = (f32[2,3,256,1024]{3,2,1,0:T(8,128)S(1)}, f32[8,128]{1,0:T(8,128)}) custom-call(s32[2]{0:T(128)S(1)} %pad_add_fusion.2.kidx, bf16[3,256,4096]{2,1,0:T(8,128)(2,1)S(1)} %bitcast.33, bf16[3,256,4096]{2,1,0:T(8,128)(2,1)} %collective-permute-done.x_oth, ...), custom_call_target="tpu_custom_call", output_to_operand_aliasing={{0}: (5, {})} | custom-call | flops 3221225472 | bytes 16777216 | tf_op jit(solution)/shard_map/pallas_call | solution.py:115
  92.3 3.7 %shard_map.72 = f32[2,8,256]{2,1,0:T(8,128)S(1)} custom-call(s32[2]{0:T(128)S(1)} %pad_add_fusion.1.kidx, bf16[3,256,4096]{2,1,0:T(8,128)(2,1)S(1)} %bitcast.34, bf16[3,256,4096]{2,1,0:T(8,128)(2,1)} %collective-permute-done.x_oth, bf16[1024,512]{1,0:T(8,128)(2,1)S(1)} %pad_maximum_fusion.w, f32[2,3,256,1024]{3,2,1,0:T(8,128)S(1)} %get-tuple-element.27.acc, ...), custom_call_target="tpu_custom_call" | custom-call | flops 1610612736 | bytes 12582912 | tf_op jit(solution)/shard_map/pallas_call | solution.py:171
  96.7 6.2 %all-to-all-start = ((f32[16,1,512]{2,1,0:T(1,128)}), f32[16,1,512]{2,1,0:T(1,128)S(1)}, u32[]{:S(2)}, u32[]{:S(2)}) async-start(f32[16,1,512]{2,1,0:T(1,128)} %broadcast_in_dim.18), calls=%async_computation | async-start | bytes 65536 | tf_op jit(solution)/shard_map/all_to_all | solution.py:267
  105.4 3.3 %all-to-all-done = f32[16,1,512]{2,1,0:T(1,128)S(1)} async-done(((f32[16,1,512]{2,1,0:T(1,128)}), f32[16,1,512]{2,1,0:T(1,128)S(1)}, u32[]{:S(2)}, u32[]{:S(2)}) %all-to-all-start) | async-done | bytes 32800 | tf_op jit(solution)/shard_map/all_to_all | solution.py:267
  108.7 7.3 %all-to-all-start.2 = ((bf16[8,256,256]{1,2,0:T(8,128)(2,1)}), bf16[8,256,256]{1,2,0:T(8,128)(2,1)}, u32[]{:S(2)}, u32[]{:S(2)}) async-start(bf16[8,256,256]{1,2,0:T(8,128)(2,1)} %bitcast.16), calls=%async_computation.2 | async-start | bytes 2097152 | tf_op jit(solution)/shard_map/all_to_all | solution.py:307
  116.1 29.3 %all-to-all-done.2 = bf16[8,256,256]{1,2,0:T(8,128)(2,1)} async-done(((bf16[8,256,256]{1,2,0:T(8,128)(2,1)}), bf16[8,256,256]{1,2,0:T(8,128)(2,1)}, u32[]{:S(2)}, u32[]{:S(2)}) %all-to-all-start.2) | async-done | bytes 1048608 | tf_op jit(solution)/shard_map/all_to_all | solution.py:307
  146.0 3.8 %all-to-all-start.1 = ((f32[16,1,512]{2,1,0:T(1,128)}), f32[16,1,512]{2,1,0:T(1,128)S(1)}, u32[]{:S(2)}, u32[]{:S(2)}) async-start(f32[16,1,512]{2,1,0:T(1,128)} %broadcast_in_dim.19), calls=%async_computation.1 | async-start | bytes 65536 | tf_op jit(solution)/shard_map/all_to_all | solution.py:267
  151.3 7.4 %all-to-all-done.1 = f32[16,1,512]{2,1,0:T(1,128)S(1)} async-done(((f32[16,1,512]{2,1,0:T(1,128)}), f32[16,1,512]{2,1,0:T(1,128)S(1)}, u32[]{:S(2)}, u32[]{:S(2)}) %all-to-all-start.1) | async-done | bytes 32800 | tf_op jit(solution)/shard_map/all_to_all | solution.py:267
  160.4 1.9 %shard_map.73 = (f32[2,64,512]{2,1,0:T(8,128)S(1)}, f32[2,64,512]{2,1,0:T(8,128)S(1)}, f32[1,256]{1,0:T(1,128)}) custom-call(s32[3]{0:T(128)S(1)} %pad_add_fusion.place, f32[32,256]{1,0:T(8,128)S(1)} %reshape.37.fit, bf16[256,2048]{1,0:T(8,128)(2,1)S(1)} %bitcast.35, bf16[8,256,512]{2,1,0:T(8,128)(2,1)S(1)} %bitcast.36), custom_call_target="tpu_custom_call" | custom-call | flops 536870912 | bytes 4194304 | tf_op jit(solution)/shard_map/pallas_call | solution.py:250
  162.3 1.9 %collective-permute-start.11 = (f32[2,64,512]{2,1,0:T(8,128)S(1)}, f32[2,64,512]{2,1,0:T(8,128)S(1)}, u32[]{:S(2)}, u32[]{:S(2)}) collective-permute-start(f32[2,64,512]{2,1,0:T(8,128)S(1)} %get-tuple-element.32), channel_id=1, source_target_pairs={{0,8},{1,9},{2,10},{3,11},{4,12},{5,13},{6,14},{7,15},{8,0},{9,1},... | collective-permute-start | bytes 786440 | tf_op jit(solution)/shard_map/ppermute | solution.py:280
  165.9 5.9 %collective-permute-done.12 = f32[64,512]{1,0:T(8,128)S(1)} collective-permute-done((f32[64,512]{1,0:T(8,128)S(1)}, f32[64,512]{1,0:T(8,128)S(1)}, u32[]{:S(2)}, u32[]{:S(2)}) %collective-permute-start.12) | collective-permute-done | bytes 131104 | tf_op jit(solution)/shard_map/ppermute | solution.py:280
  (64 shorter events, 23.5 us)
Async XLA Ops:
  7.2 3.4 %copy-start = (bf16[2048,512]{1,0:T(8,128)(2,1)S(1)}, bf16[2048,512]{1,0:T(8,128)(2,1)}, u32[]{:S(2)}) copy-start(bf16[2048,512]{1,0:T(8,128)(2,1)} %param.6) | copy-start | bytes 6291460
  7.2 151.6 %all-gather.3.cloned.1.call-start = ((), (), s32[]{:S(2)}) async-start(), calls=%async_computation.3 | async-start | bytes 2359296 | tf_op jit(solution)/shard_map/all_gather | solution.py:303
  7.2 67.3 %collective-permute-start = (bf16[3,256,4096]{2,1,0:T(8,128)(2,1)}, bf16[3,256,4096]{2,1,0:T(8,128)(2,1)}, u32[]{:S(2)}, u32[]{:S(2)}) collective-permute-start(bf16[3,256,4096]{2,1,0:T(8,128)(2,1)} %bitcast.29), channel_id=1, source_target_pairs={{0,8},{1,9},{2,10},{3,11},{4,12},{5,13},{6,14},{7,15},{8,0},{9,1},... | collective-permute-start | bytes 18874376 | tf_op jit(solution)/shard_map/ppermute | solution.py:280
  10.6 54.2 %copy-start.10 = (f32[2048]{0:T(1024)S(1)}, f32[2048]{0:T(1024)}, u32[]{:S(2)}) copy-start(f32[2048]{0:T(1024)} %param.9) | copy-start | bytes 24580
  10.6 14.1 %collective-permute-start.1 = (bf16[1024,512]{1,0:T(8,128)(2,1)S(1)}, bf16[1024,512]{1,0:T(8,128)(2,1)}, u32[]{:S(2)}, u32[]{:S(2)}) collective-permute-start(bf16[1024,512]{1,0:T(8,128)(2,1)S(1)} %constant_dynamic-slice_fusion.3.refs_0_), channel_id=1, source_target_pairs={{0,1},{1,2},{2,3},{3,0},{4,5},{5,6},{6,7},{7,4},{8,11},{9,8},{10,9... | collective-permute-start | bytes 3145736 | tf_op jit(solution)/shard_map/ppermute | solution.py:280
  12.5 15.3 %collective-permute-start.2 = (bf16[1024,512]{1,0:T(8,128)(2,1)S(1)}, bf16[1024,512]{1,0:T(8,128)(2,1)S(1)}, u32[]{:S(2)}, u32[]{:S(2)}) collective-permute-start(bf16[1024,512]{1,0:T(8,128)(2,1)S(1)} %constant_dynamic-slice_fusion.3.refs_0_), channel_id=1, source_target_pairs={{0,4},{1,5},{2,6},{3,7},{4,0},{5,1},{6,2},{7,3},{8,140},{9,141},{1... | collective-permute-start | bytes 3145736 | tf_op jit(solution)/shard_map/ppermute | solution.py:280
  28.7 15.1 %collective-permute-start.4 = (bf16[1024,512]{1,0:T(8,128)(2,1)}, bf16[1024,512]{1,0:T(8,128)(2,1)S(1)}, u32[]{:S(2)}, u32[]{:S(2)}) collective-permute-start(bf16[1024,512]{1,0:T(8,128)(2,1)} %collective-permute-done.1.refs_1_), channel_id=1, source_target_pairs={{0,4},{1,5},{2,6},{3,7},{4,0},{5,1},{6,2},{7,3},{8,140},{9,141},{1... | collective-permute-start | bytes 3145736 | tf_op jit(solution)/shard_map/ppermute | solution.py:280
  30.8 15.0 %collective-permute-start.3 = (bf16[1024,512]{1,0:T(8,128)(2,1)S(1)}, bf16[1024,512]{1,0:T(8,128)(2,1)}, u32[]{:S(2)}, u32[]{:S(2)}) collective-permute-start(bf16[1024,512]{1,0:T(8,128)(2,1)S(1)} %constant_dynamic-slice_fusion.3.refs_0_), channel_id=1, source_target_pairs={{0,3},{1,0},{2,1},{3,2},{4,7},{5,4},{6,5},{7,6},{8,9},{9,10},{10,1... | collective-permute-start | bytes 3145736 | tf_op jit(solution)/shard_map/ppermute | solution.py:280
  45.8 14.3 %collective-permute-start.5 = (bf16[1024,512]{1,0:T(8,128)(2,1)}, bf16[1024,512]{1,0:T(8,128)(2,1)}, u32[]{:S(2)}, u32[]{:S(2)}) collective-permute-start(bf16[1024,512]{1,0:T(8,128)(2,1)} %collective-permute-done.1.refs_1_), channel_id=1, source_target_pairs={{0,1},{1,2},{2,3},{3,0},{4,5},{5,6},{6,7},{7,4},{8,11},{9,8},{10,9... | collective-permute-start | bytes 3145736 | tf_op jit(solution)/shard_map/ppermute | solution.py:280
  45.8 15.2 %collective-permute-start.6 = (bf16[1024,512]{1,0:T(8,128)(2,1)}, bf16[1024,512]{1,0:T(8,128)(2,1)}, u32[]{:S(2)}, u32[]{:S(2)}) collective-permute-start(bf16[1024,512]{1,0:T(8,128)(2,1)} %collective-permute-done.3.refs_0_), channel_id=1, source_target_pairs={{0,4},{1,5},{2,6},{3,7},{4,0},{5,1},{6,2},{7,3},{8,140},{9,141},{1... | collective-permute-start | bytes 3145736 | tf_op jit(solution)/shard_map/ppermute | solution.py:280
  62.8 9.9 %collective-permute-start.7 = (bf16[512,512]{1,0:T(8,128)(2,1)}, bf16[512,512]{1,0:T(8,128)(2,1)}, u32[]{:S(2)}, u32[]{:S(2)}) collective-permute-start(bf16[512,512]{1,0:T(8,128)(2,1)} %slice.15), channel_id=1, source_target_pairs={{0,4},{1,5},{2,6},{3,7},{4,0},{5,1},{6,2},{7,3},{8,140},{9,141},{1... | collective-permute-start | bytes 1572872 | tf_op jit(solution)/shard_map/ppermute | solution.py:280
  64.6 8.6 %collective-permute-start.8 = (bf16[512,512]{1,0:T(8,128)(2,1)}, bf16[512,512]{1,0:T(8,128)(2,1)}, u32[]{:S(2)}, u32[]{:S(2)}) collective-permute-start(bf16[512,512]{1,0:T(8,128)(2,1)} %slice.16), channel_id=1, source_target_pairs={{0,1},{1,2},{2,3},{3,0},{4,5},{5,6},{6,7},{7,4},{8,11},{9,8},{10,9... | collective-permute-start | bytes 1572872 | tf_op jit(solution)/shard_map/ppermute | solution.py:280
  64.9 2.8 %copy-start.1 = (bf16[256,3,4096]{2,0,1:T(8,128)(2,1)S(1)}, bf16[256,3,4096]{2,0,1:T(8,128)(2,1)}, u32[]{:S(2)}) copy-start(bf16[256,3,4096]{2,0,1:T(8,128)(2,1)} %param.5) | copy-start | bytes 18874372
  69.4 3.0 %copy-start.9 = (bf16[256,2048]{1,0:T(8,128)(2,1)S(1)}, bf16[256,2048]{1,0:T(8,128)(2,1)}, u32[]{:S(2)}) copy-start(bf16[256,2048]{1,0:T(8,128)(2,1)} %param.8) | copy-start | bytes 3145732
  69.4 5.2 %copy-start.2 = (bf16[256,3,4096]{2,0,1:T(8,128)(2,1)S(1)}, bf16[256,3,4096]{2,0,1:T(8,128)(2,1)}, u32[]{:S(2)}) copy-start(bf16[256,3,4096]{2,0,1:T(8,128)(2,1)} %param.5) | copy-start | bytes 18874372
  71.5 3.0 %copy-start.6 = (bf16[1024,512]{1,0:T(8,128)(2,1)S(1)}, bf16[1024,512]{1,0:T(8,128)(2,1)}, u32[]{:S(2)}) copy-start(bf16[1024,512]{1,0:T(8,128)(2,1)} %copy-done.5) | copy-start | bytes 3145732
  71.5 3.1 %copy-start.8 = (bf16[1024,512]{1,0:T(8,128)(2,1)S(1)}, bf16[1024,512]{1,0:T(8,128)(2,1)}, u32[]{:S(2)}) copy-start(bf16[1024,512]{1,0:T(8,128)(2,1)} %copy-done.7) | copy-start | bytes 3145732
  71.5 20.8 %collective-permute-start.9 = (f32[3,256,1]{2,1,0:T(8,128)S(1)}, f32[3,256,1]{2,1,0:T(8,128)S(1)}, u32[]{:S(2)}, u32[]{:S(2)}) collective-permute-start(f32[3,256,1]{2,1,0:T(8,128)S(1)} %shard_map.71.low_own), channel_id=1, source_target_pairs={{0,8},{1,9},{2,10},{3,11},{4,12},{5,13},{6,14},{7,15},{8,0},{9,1},... | collective-permute-start | bytes 9224 | tf_op jit(solution)/shard_map/ppermute | solution.py:280
  72.5 19.9 %collective-permute-start.10 = (bf16[256,1024]{1,0:T(8,128)(2,1)S(1)}, bf16[256,1024]{1,0:T(8,128)(2,1)S(1)}, u32[]{:S(2)}, u32[]{:S(2)}) collective-permute-start(bf16[256,1024]{1,0:T(8,128)(2,1)S(1)} %get-tuple-element.34), channel_id=1, source_target_pairs={{0,8},{1,9},{2,10},{3,11},{4,12},{5,13},{6,14},{7,15},{8,0},{9,1},... | collective-permute-start | bytes 1572872 | tf_op jit(solution)/shard_map/ppermute | solution.py:280
  96.7 12.0 %all-to-all-start = ((f32[16,1,512]{2,1,0:T(1,128)}), f32[16,1,512]{2,1,0:T(1,128)S(1)}, u32[]{:S(2)}, u32[]{:S(2)}) async-start(f32[16,1,512]{2,1,0:T(1,128)} %broadcast_in_dim.18), calls=%async_computation | async-start | bytes 65536 | tf_op jit(solution)/shard_map/all_to_all | solution.py:267
  108.7 36.7 %all-to-all-start.2 = ((bf16[8,256,256]{1,2,0:T(8,128)(2,1)}), bf16[8,256,256]{1,2,0:T(8,128)(2,1)}, u32[]{:S(2)}, u32[]{:S(2)}) async-start(bf16[8,256,256]{1,2,0:T(8,128)(2,1)} %bitcast.16), calls=%async_computation.2 | async-start | bytes 2097152 | tf_op jit(solution)/shard_map/all_to_all | solution.py:307
  146.0 12.7 %all-to-all-start.1 = ((f32[16,1,512]{2,1,0:T(1,128)}), f32[16,1,512]{2,1,0:T(1,128)S(1)}, u32[]{:S(2)}, u32[]{:S(2)}) async-start(f32[16,1,512]{2,1,0:T(1,128)} %broadcast_in_dim.19), calls=%async_computation.1 | async-start | bytes 65536 | tf_op jit(solution)/shard_map/all_to_all | solution.py:267
  162.3 3.1 %collective-permute-start.11 = (f32[2,64,512]{2,1,0:T(8,128)S(1)}, f32[2,64,512]{2,1,0:T(8,128)S(1)}, u32[]{:S(2)}, u32[]{:S(2)}) collective-permute-start(f32[2,64,512]{2,1,0:T(8,128)S(1)} %get-tuple-element.32), channel_id=1, source_target_pairs={{0,8},{1,9},{2,10},{3,11},{4,12},{5,13},{6,14},{7,15},{8,0},{9,1},... | collective-permute-start | bytes 786440 | tf_op jit(solution)/shard_map/ppermute | solution.py:280
  165.5 6.3 %collective-permute-start.12 = (f32[64,512]{1,0:T(8,128)S(1)}, f32[64,512]{1,0:T(8,128)S(1)}, u32[]{:S(2)}, u32[]{:S(2)}) collective-permute-start(f32[64,512]{1,0:T(8,128)S(1)} %slice_bitcast_fusion), channel_id=1, source_target_pairs={{0,128},{1,129},{2,130},{3,131},{4,132},{5,133},{6,134},{7,135},{8... | collective-permute-start | bytes 393224 | tf_op jit(solution)/shard_map/ppermute | solution.py:280
  (4 other events, 5.2 us)
Sparse Core Ops, SparseCore 0:
  48.6 38.9 all-gather.2

commit v3 on v2

v3 whole, which is shorter than its diff:
```python
import functools

import jax
import jax.numpy as jnp
import numpy as np
from jax import lax
from jax.experimental import pallas as pl
from jax.experimental.pallas import tpu as pltpu
from jax.sharding import Mesh, PartitionSpec as P

perturb_scale = 0.5
epsilon = 1e-05

XH, Z, CORE, XL, Y = 2, 8, 2, 2, 4
AXES = ("xh", "z", "core", "xl", "y")
SIZES = (XH, Z, CORE, XL, Y)
WA = XL * Y
CHAINS = 2
ROWS_ALL = 24
VMEM_BYTES = 55 * 1024 * 1024
SMALL_BYTES = 1024 * 1024


def permutation(move):
    pairs = []
    for i in range(int(np.prod(SIZES))):
        at = [int(v) for v in np.unravel_index(i, SIZES)]
        to = move(*at)
        pairs.append((i, int(np.ravel_multi_index(to, SIZES))))
    return pairs


def go_y(step):
    def move(xh, z, c, xl, y):
        s = step if c == 0 else -step
        return (xh, z, c, xl, (y + s) % Y)

    return permutation(move)


def go_x():
    def move(xh, z, c, xl, y):
        x = xh * 2 + xl
        if c == 0:
            x = x ^ 1
        else:
            x = (x + 1) % 4 if x % 2 else (x - 1) % 4
        return (x // 2, z, c, x % 2, y)

    return permutation(move)


def go_core():
    return permutation(lambda xh, z, c, xl, y: (xh, z, 1 - c, xl, y))


def go_xh():
    return permutation(lambda xh, z, c, xl, y: (1 - xh, z, c, xl, y))


def nt_dot(a, b):
    return lax.dot_general(a, b, (((1,), (1,)), ((), ())), preferred_element_type=jnp.float32)


def fetch_columns(kidx, count, block, sources, buffers, sems):
    copies = []
    for s in range(count):
        cols = pl.ds(pl.multiple_of(kidx[s] * block, block), block)
        for side in range(2):
            copy = pltpu.make_async_copy(
                sources[side].at[:, :, cols], buffers.at[s, side], sems.at[s, side]
            )
            copy.start()
            copies.append(copy)
    return copies


def fetch_weights(sent, ws, sems):
    copies = []
    for s, w in enumerate(sent):
        copy = pltpu.make_async_copy(w, ws.at[s], sems.at[s])
        copy.start()
        copies.append(copy)
    return copies


def group_kernel(count, has_acc, extra, kidx, x_own, x_oth, *refs):
    refs = refs[extra:]
    sent = refs[:count]
    acc_in = refs[count] if has_acc else None
    out, token, ws, w_sems, buffers, sems = refs[-6:]
    members, width = out.shape[2], out.shape[3]
    block = sent[0].shape[1]
    copies = fetch_columns(kidx, count, block, (x_own, x_oth), buffers, sems)
    fetched = fetch_weights(sent, ws, w_sems)
    token[...] = jnp.zeros_like(token)
    chunk = 512
    for side in range(2):
        for s in range(count):
            copies[2 * s + side].wait()
            if side == 0:
                fetched[s].wait()
        for j in range(0, width, chunk):
            cols = pl.ds(j, chunk)
            total = None
            for s in range(count):
                part = nt_dot(buffers[s, side].reshape(3 * members, block), ws[s, cols, :])
                total = part if total is None else total + part
            total = total.reshape(3, members, chunk)
            if has_acc:
                total = total + acc_in[side, :, :, cols]
            out[side, :, :, cols] = total


def group_matmul(kidx, x_own, x_oth, ws, acc, extra=()):
    count = len(ws)
    members = x_own.shape[1]
    width, block = ws[0].shape
    smem = pl.BlockSpec(memory_space=pltpu.SMEM)
    vmem = pl.BlockSpec(memory_space=pltpu.VMEM)
    hbm = pl.BlockSpec(memory_space=pltpu.HBM)
    args = [x_own, x_oth, *extra] + list(ws)
    specs = [smem, hbm, hbm] + [hbm] * len(extra) + [hbm] * count
    alias = {}
    if acc is not None:
        specs.append(vmem)
        args.append(acc)
        alias = {len(args): 0}
    flops = 2 * 2 * 3 * members * width * block * count
    return pl.pallas_call(
        functools.partial(group_kernel, count, acc is not None, len(extra)),
        out_shape=(
            jax.ShapeDtypeStruct((2, 3, members, width), jnp.float32),
            jax.ShapeDtypeStruct((8, 128), jnp.float32),
        ),
        in_specs=specs,
        out_specs=(vmem, vmem),
        scratch_shapes=[
            pltpu.VMEM((count, width, block), jnp.bfloat16),
            pltpu.SemaphoreType.DMA((count,)),
            pltpu.VMEM((count, 2, 3, members, block), jnp.bfloat16),
            pltpu.SemaphoreType.DMA((count, 2)),
        ],
        input_output_aliases=alias,
        compiler_params=pltpu.CompilerParams(vmem_limit_bytes=VMEM_BYTES),
        cost_estimate=pl.CostEstimate(flops=flops, bytes_accessed=16 * 1024 * 1024, transcendentals=0),
    )(kidx, *args)


def last_kernel(first, kidx, x_own, x_oth, sent, pieces, acc, low_own, low_oth, fout_own, fout_oth, readout, *refs):
    before = refs[0] if len(refs) == 6 else None
    out, w, w_sems, buffers, sems = refs[-5:]
    members, width = acc.shape[2], acc.shape[3]
    block = sent.shape[1]
    fetched = fetch_weights([sent], w, w_sems)
    copies = fetch_columns(kidx, 1, block, (x_own, x_oth), buffers, sems)
    fetched[0].wait()
    chunk = 256
    ones = jnp.ones((8, 128), jnp.float32)
    for side, low, fout in ((0, low_own, fout_own), (1, low_oth, fout_oth)):
        copies[side].wait()
        total = jnp.zeros((members, 128), jnp.float32)
        for j in range(0, width, chunk):
            cols = pl.ds(j, chunk)
            part = nt_dot(buffers[0, side].reshape(3 * members, block), w[0, cols, :])
            part = part.reshape(3, members, chunk)
            shift = fout[:, pl.ds(first + j, chunk)].astype(jnp.float32)
            summed = None
            for r in range(3):
                pert = part[r] + acc[side, r, :, cols] + low[r] * shift
                term = jnp.tanh(pert)
                summed = term if summed is None else summed + term
            summed = summed * readout[:, pl.ds(first + j, chunk)]
            for h in range(0, chunk, 128):
                total = total + summed[:, h : h + 128]
        row = lax.dot_general(
            ones,
            total,
            (((1,), (1,)), ((), ())),
            preferred_element_type=jnp.float32,
            precision=lax.Precision.HIGHEST,
        )[0:1]
        at = pl.ds(pl.multiple_of(jnp.bitwise_xor(kidx[1], side) * members, members), members)
        if before is not None:
            row = row + before[0, :, at]
        for k in range(out.shape[0]):
            out[k, :, at] = row


def last_matmul(first, kidx, x_own, x_oth, w, pieces, acc, low_own, low_oth, fout_own, fout_oth, readout, before):
    members = x_own.shape[1]
    width, block = w.shape
    smem = pl.BlockSpec(memory_space=pltpu.SMEM)
    vmem = pl.BlockSpec(memory_space=pltpu.VMEM)
    hbm = pl.BlockSpec(memory_space=pltpu.HBM)
    args = [acc, low_own, low_oth, fout_own, fout_oth, readout]
    if before is not None:
        args.append(before)
    return pl.pallas_call(
        functools.partial(last_kernel, first),
        out_shape=jax.ShapeDtypeStruct((CORE * WA, 1, 2 * members), jnp.float32),
        in_specs=[smem, hbm, hbm, hbm, hbm] + [vmem] * len(args),
        out_specs=vmem,
        scratch_shapes=[
            pltpu.VMEM((1, width, block), jnp.bfloat16),
            pltpu.SemaphoreType.DMA((1,)),
            pltpu.VMEM((1, 2, 3, members, block), jnp.bfloat16),
            pltpu.SemaphoreType.DMA((1, 2)),
        ],
        compiler_params=pltpu.CompilerParams(vmem_limit_bytes=VMEM_BYTES),
        cost_estimate=pl.CostEstimate(
            flops=2 * 6 * members * width * block,
            bytes_accessed=6 * 1024 * 1024,
            transcendentals=6 * members * width,
        ),
    )(kidx, x_own, x_oth, w, pieces, *args)


def after_kernel(*refs):
    pass


def after(values, *done):
    hbm = pl.BlockSpec(memory_space=pltpu.HBM)
    count = len(values)
    return pl.pallas_call(
        after_kernel,
        out_shape=tuple(jax.ShapeDtypeStruct(v.shape, v.dtype) for v in values),
        in_specs=[hbm] * (count + len(done)),
        out_specs=(hbm,) * count,
        input_output_aliases={i: i for i in range(count)},
        compiler_params=pltpu.CompilerParams(vmem_limit_bytes=SMALL_BYTES),
    )(*values, *done)


def sum_kernel(got, out):
    out[...] = jnp.broadcast_to(jnp.sum(got[...], axis=0, keepdims=True) / ROWS_ALL, out.shape)


def sum_and_copy(got):
    vmem = pl.BlockSpec(memory_space=pltpu.VMEM)
    return pl.pallas_call(
        sum_kernel,
        out_shape=jax.ShapeDtypeStruct((XH * Z,) + got.shape[1:], jnp.float32),
        in_specs=[vmem],
        out_specs=vmem,
        compiler_params=pltpu.CompilerParams(vmem_limit_bytes=SMALL_BYTES),
    )(got)


def low_kernel(x, fin, out, x_buf, f_buf, sems):
    tiles, rows, tile, width = x_buf.shape
    copies = []
    for t in range(tiles):
        span = pl.ds(t * tile, tile)
        pair = (
            pltpu.make_async_copy(x.at[:, span, :], x_buf.at[t], sems.at[t, 0]),
            pltpu.make_async_copy(fin.at[span, :], f_buf.at[t], sems.at[t, 1]),
        )
        for copy in pair:
            copy.start()
        copies.append(pair)
    chunk = 128
    for t in range(tiles):
        for copy in copies[t]:
            copy.wait()
        totals = [None] * rows
        for j in range(0, width, chunk):
            cols = pl.ds(j, chunk)
            f = f_buf[t, :, cols].astype(jnp.float32)
            for r in range(rows):
                term = x_buf[t, r, :, cols].astype(jnp.float32) * f
                totals[r] = term if totals[r] is None else totals[r] + term
        for r in range(rows):
            out[r, pl.ds(t * tile, tile), :] = perturb_scale * jnp.sum(totals[r], axis=1, keepdims=True)


def low_term(x, fin):
    rows, members, width = x.shape
    tile = 64
    tiles = members // tile
    hbm = pl.BlockSpec(memory_space=pltpu.HBM)
    return pl.pallas_call(
        low_kernel,
        out_shape=jax.ShapeDtypeStruct((rows, members, 1), jnp.float32),
        in_specs=[hbm, hbm],
        out_specs=pl.BlockSpec(memory_space=pltpu.VMEM),
        scratch_shapes=[
            pltpu.VMEM((tiles, rows, tile, width), jnp.bfloat16),
            pltpu.VMEM((tiles, tile, width), jnp.bfloat16),
            pltpu.SemaphoreType.DMA((tiles, 2)),
        ],
        compiler_params=pltpu.CompilerParams(vmem_limit_bytes=VMEM_BYTES),
        cost_estimate=pl.CostEstimate(
            flops=2 * rows * members * width, bytes_accessed=9 * 1024 * 1024, transcendentals=0
        ),
    )(x, fin)


def step_kernel(place, fit, fout, fin, keep, give, util, rows_ref):
    values = fit[...]
    members = fin.shape[1]
    count = values.shape[0] * values.shape[2]
    mean = jnp.sum(values) / count
    spread = jnp.sum((values - mean) ** 2) / count
    root = jnp.sqrt(jnp.full((1, 1), spread + epsilon, jnp.float32))
    xh, z, c = place[0], place[1], place[2]
    at = pl.ds(pl.multiple_of(c * members, members), members)
    util[...] = (fit[xh * Z + z, :, at] - mean) / root
    for k in range(Z):
        rows_ref[k : k + 1, :] = fit[xh * Z + k, :, at]
    columns = (jnp.transpose(rows_ref[...]) - mean) / root
    total = None
    for k in range(Z):
        scaled = (fout[k].astype(jnp.float32) * columns[:, k : k + 1]).astype(jnp.bfloat16)
        one = lax.dot_general(
            scaled, fin[k], (((0,), (0,)), ((), ())), preferred_element_type=jnp.float32
        )
        total = one if total is None else total + one
    total = total * (1.0 / np.sqrt(float(count)))
    rows = keep.shape[1]
    total = total.reshape(XH, CORE, rows, total.shape[1])
    for h in range(XH):
        to = jnp.bitwise_xor(xh, h)
        keep[to] = jnp.where(c == 0, total[h, 0], total[h, 1])
        give[to] = jnp.where(c == 0, total[h, 1], total[h, 0])


def weight_part(place, fit, fout, fin):
    members, rows = fout.shape[1], fout.shape[2]
    cols = fin.shape[2]
    vmem = pl.BlockSpec(memory_space=pltpu.VMEM)
    block = jax.ShapeDtypeStruct((XH, rows // (XH * CORE), cols), jnp.float32)
    return pl.pallas_call(
        step_kernel,
        out_shape=(block, block, jax.ShapeDtypeStruct((1, members), jnp.float32)),
        in_specs=[pl.BlockSpec(memory_space=pltpu.SMEM), vmem, vmem, vmem],
        out_specs=(vmem, vmem, vmem),
        scratch_shapes=[pltpu.VMEM((Z, members), jnp.float32)],
        compiler_params=pltpu.CompilerParams(vmem_limit_bytes=VMEM_BYTES),
        cost_estimate=pl.CostEstimate(
            flops=2 * rows * Z * members * cols, bytes_accessed=4 * 1024 * 1024, transcendentals=0
        ),
    )(place, fit, fout, fin)


def share(x, axes):
    return lax.all_to_all(x, axes, 0, 0, tiled=True)


def shards(inputs, weight, factor_in, factor_out, readout):
    members, rows_here, width = inputs.shape
    out_width, block = weight.shape
    half = out_width // 2
    xh, z, c, xl, y = (lax.axis_index(a) for a in AXES)
    wa = xl * Y + y
    sign = 1 - 2 * c
    y_fwd, y_bwd, x_go, core_go = go_y(1), go_y(-1), go_x(), go_core()

    def send(v, pairs):
        return lax.ppermute(v, AXES, pairs)

    def col(xl_at, off):
        return xl_at * Y + lax.rem(y + off + Y, Y)

    xo = 1 - xl
    k_own, k_a, k_b, k_c = col(xl, 0), col(xl, -sign), col(xl, sign), col(xl, 2)
    k_d, k_e, k_f, k_g = col(xo, 0), col(xo, -sign), col(xo, sign), col(xo, 2)

    x_own = inputs.transpose(1, 0, 2)
    def col(xl_at, off):
        return xl_at * Y + lax.rem(y + off + Y, Y)

    xo = 1 - xl
    k_own, k_a, k_b, k_c = col(xl, 0), col(xl, -sign), col(xl, sign), col(xl, 2)
    k_d, k_e, k_f, k_g = col(xo, 0), col(xo, -sign), col(xo, sign), col(xo, 2)

    x_own = inputs.transpose(1, 0, 2)
    w_own = lax.dynamic_slice_in_dim(weight, c * half, half, 0)

    def idx(*ks):
        return jnp.stack(ks).astype(jnp.int32)

    fin_here = lax.dynamic_slice_in_dim(factor_in, wa * block, block, 1)
    fin_all = lax.all_gather(fin_here, "z", axis=0)
    rows_out = out_width // (XH * Z * CORE)
    pieces = factor_out.reshape(members, XH, Z, CORE, rows_out)
    pieces = pieces.transpose(2, 0, 1, 3, 4).reshape(Z, members, out_width // Z)
    pieces = lax.all_to_all(pieces, "z", 0, 0, tiled=True)

    part = half // CHAINS
    chains = range(CHAINS)
    starts = [c * half + h * part for h in chains]
    own = [lax.dynamic_slice_in_dim(weight, at, part, 0) for at in starts]
    w_a = [send(w, y_fwd) for w in own]
    w_d = [send(w, x_go) for w in own]
    x_oth = send(x_own, core_go)

    low_own = low_term(x_own, factor_in)
    low_oth = send(low_own, core_go)
    fout_theirs = lax.dynamic_slice_in_dim(factor_out, (1 - c) * half, half, 1)
    fout_got = send(fout_theirs, core_go)
    fout_mine = lax.dynamic_slice_in_dim(factor_out, c * half, half, 1)
    read_mine = lax.dynamic_slice_in_dim(readout, c * half, half, 0)[None]

    w_b, w_e, w_c, w_f, acc, token = ([None] * CHAINS for _ in range(6))
    for h in chains:
        own[h], w_a[h], w_d[h] = after((own[h], w_a[h], w_d[h]))
        w_b[h] = send(own[h], y_bwd)
        w_e[h] = send(w_a[h], x_go)
        acc[h], token[h] = group_matmul(
            idx(k_own, k_a, k_d), x_own, x_oth, [own[h], w_a[h], w_d[h]], None, (low_own, fout_mine)
        )
    for h in chains:
        w_a[h], w_b[h], w_e[h] = after((w_a[h], w_b[h], w_e[h]), token[h])
        w_c[h] = send(w_a[h], y_fwd)
        w_f[h] = send(w_b[h], x_go)
        acc[h], token[h] = group_matmul(
            idx(k_b, k_e), x_own, x_oth, [w_b[h], w_e[h]], acc[h], (low_oth, fout_got)
        )
    w_g = [None] * CHAINS
    for h in chains:
        w_c[h], w_f[h], w_e[h] = after((w_c[h], w_f[h], w_e[h]), token[h])
        w_g[h] = send(w_c[h], x_go) if h == 0 else send(w_e[h], y_fwd)
        acc[h], token[h] = group_matmul(
            idx(k_f, k_c), x_own, x_oth, [w_f[h], w_c[h]], acc[h]
        )
    partial = None
    for h in chains:
        partial = last_matmul(
            h * part, idx(k_g, c), x_own, x_oth, w_g[h], pieces if h == 1 else w_g[h], acc[h],
            low_own, low_oth, fout_mine, fout_got, read_mine, partial,
        )

    fit = share(sum_and_copy(share(partial, ("core", "xl", "y"))), ("xh", "z"))

    keep, give, util = weight_part(idx(xh, z, c), fit, pieces, fin_all)
    summed = keep + send(give, core_go)
    weight_step = summed[0] + send(summed[1], go_xh())
    return weight_step, util.reshape(members)


def solution(mesh):
    fine = Mesh(mesh.devices.reshape(SIZES), AXES)
    pop, wa = ("xh", "z", "core"), ("xl", "y")
    placed = (P(pop, wa, None), P(None, wa), P(pop, None), P(pop, None), P())
    return jax.shard_map(
        shards, mesh=fine, in_specs=placed, out_specs=(P(pop, wa), P(pop)), check_vma=False
    )
```

time: 180 us -> 178 us (0.989)
  waiting for transfers between devices: 86.8 us -> 27.8 us
  Pallas kernels: 25.5 us -> 70.4 us
  starting transfers between devices: 32.5 us -> 42.6 us
  other arithmetic: 2.5 us -> 4.96 us
    pallas_call x5 -> x16, Pallas kernels: 23.3 us -> 65.6 us  [the longest x6 48 us: group_matmul(): pl.pallas_call(functools.partial(group_kernel, count, acc is not None, le...]
    ppermute x13 -> x19, waiting for transfers between devices: 46.8 us -> 13.8 us  [send(): return lax.ppermute(v, AXES, pairs)]
    all_to_all x1, waiting for transfers between devices: 29.3 us -> 0.01 us  [shards(): pieces = lax.all_to_all(pieces, 'z', 0, 0, tiled=True)]
    ppermute x13 -> x19, starting transfers between devices: 15.2 us -> 22.7 us  [send(): return lax.ppermute(v, AXES, pairs)]
    all_to_all x2, waiting for transfers between devices: 10.7 us -> 13.9 us  [share(): return lax.all_to_all(x, axes, 0, 0, tiled=True)]
    another operation x5, other arithmetic: 0.38 us -> 3.29 us  [idx(): return jnp.stack(ks).astype(jnp.int32)]
    slice x3 -> x0, local copies, waits for them, and re-layouts: 2.71 us -> none  [the longest x1 1.89 us: shards(): w_g0 = send(w_c4[:quarter], x_go)]
    pallas_call x1, Pallas kernels: 2.17 us -> 4.8 us  [low_term(): pl.pallas_call(low_kernel, out_shape=jax.ShapeDtypeStruct((rows, members,...]
  transfers between devices with their start and end apart: 17 -> 23, of which waited for: 12 -> 6; matrix products, arithmetic and copies ran while one was open for 6% -> 8% of each run, Pallas kernels for 13% -> 37%
where the time goes in v3:
time: 178 us
  Pallas kernels  70.4 us (40%)
  starting transfers between devices  42.6 us (24%)
  waiting for transfers between devices  27.8 us (16%)
  local copies, waits for them, and re-layouts  17.4 us (10%)
  between operations  14.4 us (8%)
  other arithmetic  4.96 us (3%)
    pallas_call x6, Pallas kernels, group_matmul(): pl.pallas_call(functools.partial(group_kernel, count, acc is not None, le...  48 us
    ppermute x19, starting transfers between devices, send(): return lax.ppermute(v, AXES, pairs)  22.7 us
    all_to_all x2, waiting for transfers between devices, share(): return lax.all_to_all(x, axes, 0, 0, tiled=True)  13.9 us
    ppermute x19, waiting for transfers between devices, send(): return lax.ppermute(v, AXES, pairs)  13.8 us
    pallas_call x2, Pallas kernels, last_matmul(): pl.pallas_call(functools.partial(last_kernel, first), out_shape=jax.Shape...  12.7 us
    all_to_all x2, starting transfers between devices, share(): return lax.all_to_all(x, axes, 0, 0, tiled=True)  11.7 us
    all_to_all x1, starting transfers between devices, shards(): pieces = lax.all_to_all(pieces, 'z', 0, 0, tiled=True)  8.2 us
    unnamed x47, local copies, waits for them, and re-layouts  8.13 us
  transfers between devices with their start and end apart: 23, of which 6 were waited for; matrix products, arithmetic and copies ran while one was open for 8% of the time, Pallas kernels for 37%

profile of v3, /device:TPU:1, one launch (start us, length us, event | category | flops | bytes accessed | tf_op | source)
XLA Modules:
  0.0 177.5 jit_solution(16939408320344209190)
XLA Ops:
  7.2 3.3 %collective-permute-start = (bf16[3,256,4096]{2,1,0:T(8,128)(2,1)}, bf16[3,256,4096]{2,1,0:T(8,128)(2,1)}, u32[]{:S(2)}, u32[]{:S(2)}) collective-permute-start(bf16[3,256,4096]{2,1,0:T(8,128)(2,1)} %bitcast.25), channel_id=1, source_target_pairs={{0,8},{1,9},{2,10},{3,11},{4,12},{5,13},{6,14},{7,15},{8,0},{9,1},... | collective-permute-start | bytes 18874376 | tf_op jit(solution)/shard_map/ppermute | solution.py:361
  14.6 2.5 %collective-permute-start.11 = (bf16[512,512]{1,0:T(8,128)(2,1)S(1)}, bf16[512,512]{1,0:T(8,128)(2,1)S(1)}, u32[]{:S(2)}, u32[]{:S(2)}) collective-permute-start(bf16[512,512]{1,0:T(8,128)(2,1)S(1)} %get-tuple-element.62.refs_0_), channel_id=1, source_target_pairs={{0,4},{1,5},{2,6},{3,7},{4,0},{5,1},{6,2},{7,3},{8,140},{9,141},{1... | collective-permute-start | bytes 1572872 | tf_op jit(solution)/shard_map/ppermute | solution.py:361
  17.8 4.3 %collective-permute-done.10.refs_1_ = bf16[512,512]{1,0:T(8,128)(2,1)} collective-permute-done((bf16[512,512]{1,0:T(8,128)(2,1)S(1)}, bf16[512,512]{1,0:T(8,128)(2,1)}, u32[]{:S(2)}, u32[]{:S(2)}) %collective-permute-start.10) | collective-permute-done | bytes 524320 | tf_op jit(solution)/shard_map/ppermute | solution.py:361
  25.1 2.5 %collective-permute-start.13 = (bf16[512,512]{1,0:T(8,128)(2,1)}, bf16[512,512]{1,0:T(8,128)(2,1)S(1)}, u32[]{:S(2)}, u32[]{:S(2)}) collective-permute-start(bf16[512,512]{1,0:T(8,128)(2,1)} %get-tuple-element.46.refs_3_.refs_0_), channel_id=1, source_target_pairs={{0,4},{1,5},{2,6},{3,7},{4,0},{5,1},{6,2},{7,3},{8,140},{9,141},{1... | collective-permute-start | bytes 1572872 | tf_op jit(solution)/shard_map/ppermute | solution.py:361
  27.5 2.3 %copy.30 = bf16[256,2048]{0,1:T(8,128)(2,1)} copy(bf16[256,2048]{1,0:T(8,128)(2,1)} %param.8) | data formatting | bytes 2097152 | tf_op args[3]
  29.8 2.3 %copy.31 = bf16[8,256,2,2,64]{1,4,3,2,0:T(8,128)(2,1)} copy(bf16[8,256,2,2,64]{1,4,3,0,2:T(8,128)(2,1)} %bitcast.36) | data formatting | bytes 2097152 | tf_op jit(solution)/shard_map/transpose | solution.py:388
  34.4 8.2 %all-to-all-start = ((bf16[8,256,256]{2,1,0:T(8,128)(2,1)}), bf16[8,256,256]{2,1,0:T(8,128)(2,1)}, u32[]{:S(2)}, u32[]{:S(2)}) async-start(bf16[8,256,256]{2,1,0:T(8,128)(2,1)} %copy.32), calls=%async_computation | async-start | bytes 2097152 | tf_op jit(solution)/shard_map/all_to_all | solution.py:389
  42.6 4.8 %shard_map.69.refs_0_.low_own = f32[3,256,1]{2,1,0:T(8,128)} custom-call(bf16[3,256,4096]{2,1,0:T(8,128)(2,1)} %bitcast.26, bf16[256,4096]{1,0:T(8,128)(2,1)} %fin.1), custom_call_target="tpu_custom_call" | custom-call | flops 6291456 | bytes 9437184 | tf_op jit(solution)/shard_map/pallas_call | solution.py:283
  51.0 8.2 %shard_map.76 = (f32[2,3,256,512]{3,2,1,0:T(8,128)}, f32[8,128]{1,0:T(8,128)}) custom-call(s32[3]{0:T(128)} %pad_add_fusion.2.kidx, bf16[3,256,4096]{2,1,0:T(8,128)(2,1)} %bitcast.27, bf16[3,256,4096]{2,1,0:T(8,128)(2,1)} %collective-permute-done.x_oth, f32[3,256,1]{2,1,0:T(8,128)} %shard_map.69.refs_0_.low_own, ...), custom_call_target="tpu_custom_call" | custom-call | flops 2415919104 | bytes 16777216 | tf_op jit(solution)/shard_map/pallas_call | solution.py:130
  61.8 8.1 %shard_map.70 = (f32[2,3,256,512]{3,2,1,0:T(8,128)}, f32[8,128]{1,0:T(8,128)}) custom-call(s32[3]{0:T(128)} %pad_add_fusion.2.kidx, bf16[3,256,4096]{2,1,0:T(8,128)(2,1)} %bitcast.28, bf16[3,256,4096]{2,1,0:T(8,128)(2,1)} %collective-permute-done.x_oth, f32[3,256,1]{2,1,0:T(8,128)} %shard_map.69.refs_0_.low_own, ...), custom_call_target="tpu_custom_call" | custom-call | flops 2415919104 | bytes 16777216 | tf_op jit(solution)/shard_map/pallas_call | solution.py:130
  69.9 2.5 %collective-permute-start.15 = (bf16[512,512]{1,0:T(8,128)(2,1)S(1)}, bf16[512,512]{1,0:T(8,128)(2,1)S(1)}, u32[]{:S(2)}, u32[]{:S(2)}) collective-permute-start(bf16[512,512]{1,0:T(8,128)(2,1)S(1)} %get-tuple-element.51.refs_2_), channel_id=1, source_target_pairs={{0,4},{1,5},{2,6},{3,7},{4,0},{5,1},{6,2},{7,3},{8,140},{9,141},{1... | collective-permute-start | bytes 1572872 | tf_op jit(solution)/shard_map/ppermute | solution.py:361
  76.3 7.9 %shard_map.78 = (f32[2,3,256,512]{3,2,1,0:T(8,128)}, f32[8,128]{1,0:T(8,128)}) custom-call(s32[2]{0:T(128)} %pad_add_fusion.3.kidx, bf16[3,256,4096]{2,1,0:T(8,128)(2,1)} %bitcast.29, bf16[3,256,4096]{2,1,0:T(8,128)(2,1)} %collective-permute-done.x_oth, f32[3,256,1]{2,1,0:T(8,128)} %copy-done.17, ...), custom_call_target="tpu_custom_call", output_to_operand_aliasing={{0}: (7, {})} | custom-call | flops 1610612736 | bytes 16777216 | tf_op jit(solution)/shard_map/pallas_call | solution.py:130
  84.2 8.0 %shard_map.72 = (f32[2,3,256,512]{3,2,1,0:T(8,128)}, f32[8,128]{1,0:T(8,128)}) custom-call(s32[2]{0:T(128)} %pad_add_fusion.3.kidx, bf16[3,256,4096]{2,1,0:T(8,128)(2,1)} %bitcast.30, bf16[3,256,4096]{2,1,0:T(8,128)(2,1)} %collective-permute-done.x_oth, f32[3,256,1]{2,1,0:T(8,128)} %copy-done.17, ...), custom_call_target="tpu_custom_call", output_to_operand_aliasing={{0}: (7, {})} | custom-call | flops 1610612736 | bytes 16777216 | tf_op jit(solution)/shard_map/pallas_call | solution.py:130
  92.3 2.6 %collective-permute-start.16 = (bf16[512,512]{1,0:T(8,128)(2,1)S(1)}, bf16[512,512]{1,0:T(8,128)(2,1)S(1)}, u32[]{:S(2)}, u32[]{:S(2)}) collective-permute-start(bf16[512,512]{1,0:T(8,128)(2,1)S(1)} %get-tuple-element.55.refs_1_), channel_id=1, source_target_pairs={{0,4},{1,5},{2,6},{3,7},{4,0},{5,1},{6,2},{7,3},{8,140},{9,141},{1... | collective-permute-start | bytes 1572872 | tf_op jit(solution)/shard_map/ppermute | solution.py:361
  97.6 7.9 %shard_map.80 = (f32[2,3,256,512]{3,2,1,0:T(8,128)}, f32[8,128]{1,0:T(8,128)}) custom-call(s32[2]{0:T(128)} %pad_add_fusion.4.kidx, bf16[3,256,4096]{2,1,0:T(8,128)(2,1)} %bitcast.31, bf16[3,256,4096]{2,1,0:T(8,128)(2,1)} %collective-permute-done.x_oth, bf16[512,512]{1,0:T(8,128)(2,1)} %copy-done.10, ...), custom_call_target="tpu_custom_call", output_to_operand_aliasing={{0}: (5, {})} | custom-call | flops 1610612736 | bytes 16777216 | tf_op jit(solution)/shard_map/pallas_call | solution.py:130
  105.5 7.9 %shard_map.74 = (f32[2,3,256,512]{3,2,1,0:T(8,128)}, f32[8,128]{1,0:T(8,128)}) custom-call(s32[2]{0:T(128)} %pad_add_fusion.4.kidx, bf16[3,256,4096]{2,1,0:T(8,128)(2,1)} %bitcast.32, bf16[3,256,4096]{2,1,0:T(8,128)(2,1)} %collective-permute-done.x_oth, bf16[512,512]{1,0:T(8,128)(2,1)} %get-tuple-element.42.refs_0_, ...), custom_call_target="tpu_custom_call", output_to_operand_aliasing={{0}: (5, {})} | custom-call | flops 1610612736 | bytes 16777216 | tf_op jit(solution)/shard_map/pallas_call | solution.py:130
  114.2 6.3 %shard_map.81.refs_0_ = f32[16,1,512]{2,1,0:T(1,128)} custom-call(s32[2]{0:T(128)} %pad_add_fusion.1.kidx, bf16[3,256,4096]{2,1,0:T(8,128)(2,1)} %bitcast.33, bf16[3,256,4096]{2,1,0:T(8,128)(2,1)} %collective-permute-done.x_oth, bf16[512,512]{1,0:T(8,128)(2,1)} %copy-done.19, bf16[512,512]{1,0:T(8,128)(2,1)} %copy-done.19, ...), custom_call_target="tpu_custom_call" | custom-call | flops 805306368 | bytes 6291456 | tf_op jit(solution)/shard_map/pallas_call | solution.py:199
  121.3 6.3 %shard_map.82 = f32[16,1,512]{2,1,0:T(1,128)} custom-call(s32[2]{0:T(128)} %pad_add_fusion.1.kidx, bf16[3,256,4096]{2,1,0:T(8,128)(2,1)} %bitcast.34, bf16[3,256,4096]{2,1,0:T(8,128)(2,1)} %collective-permute-done.x_oth, bf16[512,512]{1,0:T(8,128)(2,1)} %copy-done.20, bf16[8,256,256]{2,1,0:T(8,128)(2,1)} %all-to-all-done.pieces.fout, ...), custom_call_target="tpu_custom_call" | custom-call | flops 805306368 | bytes 6291456 | tf_op jit(solution)/shard_map/pallas_call | solution.py:199
  127.7 3.4 %all-to-all-start.1 = ((f32[16,1,512]{2,1,0:T(1,128)}), f32[16,1,512]{2,1,0:T(1,128)S(1)}, u32[]{:S(2)}, u32[]{:S(2)}) async-start(f32[16,1,512]{2,1,0:T(1,128)} %shard_map.82), calls=%async_computation.1 | async-start | bytes 65536 | tf_op jit(solution)/shard_map/all_to_all | solution.py:348
  131.1 5.7 %all-to-all-done.1.got = f32[16,1,512]{2,1,0:T(1,128)S(1)} async-done(((f32[16,1,512]{2,1,0:T(1,128)}), f32[16,1,512]{2,1,0:T(1,128)S(1)}, u32[]{:S(2)}, u32[]{:S(2)}) %all-to-all-start.1) | async-done | bytes 32800 | tf_op jit(solution)/shard_map/all_to_all | solution.py:348
  137.4 8.3 %all-to-all-start.2 = ((f32[16,1,512]{2,1,0:T(1,128)}), f32[16,1,512]{2,1,0:T(1,128)S(1)}, u32[]{:S(2)}, u32[]{:S(2)}) async-start(f32[16,1,512]{2,1,0:T(1,128)} %shard_map.83), calls=%async_computation.2 | async-start | bytes 65536 | tf_op jit(solution)/shard_map/all_to_all | solution.py:348
  146.4 8.2 %all-to-all-done.2.fit = f32[16,1,512]{2,1,0:T(1,128)S(1)} async-done(((f32[16,1,512]{2,1,0:T(1,128)}), f32[16,1,512]{2,1,0:T(1,128)S(1)}, u32[]{:S(2)}, u32[]{:S(2)}) %all-to-all-start.2) | async-done | bytes 32800 | tf_op jit(solution)/shard_map/all_to_all | solution.py:348
  155.3 4.3 %shard_map.84 = (f32[2,64,512]{2,1,0:T(8,128)}, f32[2,64,512]{2,1,0:T(8,128)}, f32[1,256]{1,0:T(1,128)}) custom-call(s32[3]{0:T(128)} %pad_add_fusion.place, f32[16,1,512]{2,1,0:T(1,128)} %copy-done.21, bf16[8,256,256]{2,1,0:T(8,128)(2,1)} %all-to-all-done.pieces.fout, bf16[8,256,512]{2,1,0:T(8,128)(2,1)} %bitcast.37), custom_call_target="tpu_custom_call" | custom-call | flops 536870912 | bytes 4194304 | tf_op jit(solution)/shard_map/pallas_call | solution.py:334
  164.1 5.9 %collective-permute-done.18 = f32[64,512]{1,0:T(8,128)S(1)} collective-permute-done((f32[64,512]{1,0:T(8,128)S(1)}, f32[64,512]{1,0:T(8,128)S(1)}, u32[]{:S(2)}, u32[]{:S(2)}) %collective-permute-start.18) | collective-permute-done | bytes 131104 | tf_op jit(solution)/shard_map/ppermute | solution.py:361
  (101 shorter events, 31.3 us)
Async XLA Ops:
  7.2 139.2 %all-gather.3.cloned.1.call-start = ((), (), s32[]{:S(2)}) async-start(), calls=%async_computation.3 | async-start | bytes 2359296 | tf_op jit(solution)/shard_map/all_gather | solution.py:385
  7.2 42.3 %collective-permute-start = (bf16[3,256,4096]{2,1,0:T(8,128)(2,1)}, bf16[3,256,4096]{2,1,0:T(8,128)(2,1)}, u32[]{:S(2)}, u32[]{:S(2)}) collective-permute-start(bf16[3,256,4096]{2,1,0:T(8,128)(2,1)} %bitcast.25), channel_id=1, source_target_pairs={{0,8},{1,9},{2,10},{3,11},{4,12},{5,13},{6,14},{7,15},{8,0},{9,1},... | collective-permute-start | bytes 18874376 | tf_op jit(solution)/shard_map/ppermute | solution.py:361
  13.5 8.5 %collective-permute-start.10 = (bf16[512,512]{1,0:T(8,128)(2,1)S(1)}, bf16[512,512]{1,0:T(8,128)(2,1)}, u32[]{:S(2)}, u32[]{:S(2)}) collective-permute-start(bf16[512,512]{1,0:T(8,128)(2,1)S(1)} %get-tuple-element.62.refs_0_), channel_id=1, source_target_pairs={{0,1},{1,2},{2,3},{3,0},{4,5},{5,6},{6,7},{7,4},{8,11},{9,8},{10,9... | collective-permute-start | bytes 1572872 | tf_op jit(solution)/shard_map/ppermute | solution.py:361
  14.6 9.6 %collective-permute-start.11 = (bf16[512,512]{1,0:T(8,128)(2,1)S(1)}, bf16[512,512]{1,0:T(8,128)(2,1)S(1)}, u32[]{:S(2)}, u32[]{:S(2)}) collective-permute-start(bf16[512,512]{1,0:T(8,128)(2,1)S(1)} %get-tuple-element.62.refs_0_), channel_id=1, source_target_pairs={{0,4},{1,5},{2,6},{3,7},{4,0},{5,1},{6,2},{7,3},{8,140},{9,141},{1... | collective-permute-start | bytes 1572872 | tf_op jit(solution)/shard_map/ppermute | solution.py:361
  17.1 31.4 %collective-permute-start.1 = (bf16[512,512]{1,0:T(8,128)(2,1)S(1)}, bf16[512,512]{1,0:T(8,128)(2,1)}, u32[]{:S(2)}, u32[]{:S(2)}) collective-permute-start(bf16[512,512]{1,0:T(8,128)(2,1)S(1)} %get-tuple-element.63.refs_0_), channel_id=1, source_target_pairs={{0,1},{1,2},{2,3},{3,0},{4,5},{5,6},{6,7},{7,4},{8,11},{9,8},{10,9... | collective-permute-start | bytes 1572872 | tf_op jit(solution)/shard_map/ppermute | solution.py:361
  17.6 31.0 %collective-permute-start.2 = (bf16[512,512]{1,0:T(8,128)(2,1)S(1)}, bf16[512,512]{1,0:T(8,128)(2,1)S(1)}, u32[]{:S(2)}, u32[]{:S(2)}) collective-permute-start(bf16[512,512]{1,0:T(8,128)(2,1)S(1)} %get-tuple-element.63.refs_0_), channel_id=1, source_target_pairs={{0,4},{1,5},{2,6},{3,7},{4,0},{5,1},{6,2},{7,3},{8,140},{9,141},{1... | collective-permute-start | bytes 1572872 | tf_op jit(solution)/shard_map/ppermute | solution.py:361
  25.1 34.2 %collective-permute-start.13 = (bf16[512,512]{1,0:T(8,128)(2,1)}, bf16[512,512]{1,0:T(8,128)(2,1)S(1)}, u32[]{:S(2)}, u32[]{:S(2)}) collective-permute-start(bf16[512,512]{1,0:T(8,128)(2,1)} %get-tuple-element.46.refs_3_.refs_0_), channel_id=1, source_target_pairs={{0,4},{1,5},{2,6},{3,7},{4,0},{5,1},{6,2},{7,3},{8,140},{9,141},{1... | collective-permute-start | bytes 1572872 | tf_op jit(solution)/shard_map/ppermute | solution.py:361
  27.5 31.8 %collective-permute-start.12 = (bf16[512,512]{1,0:T(8,128)(2,1)S(1)}, bf16[512,512]{1,0:T(8,128)(2,1)S(1)}, u32[]{:S(2)}, u32[]{:S(2)}) collective-permute-start(bf16[512,512]{1,0:T(8,128)(2,1)S(1)} %get-tuple-element.47.refs_2_), channel_id=1, source_target_pairs={{0,3},{1,0},{2,1},{3,2},{4,7},{5,4},{6,5},{7,6},{8,9},{9,10},{10,1... | collective-permute-start | bytes 1572872 | tf_op jit(solution)/shard_map/ppermute | solution.py:361
  34.4 86.1 %all-to-all-start = ((bf16[8,256,256]{2,1,0:T(8,128)(2,1)}), bf16[8,256,256]{2,1,0:T(8,128)(2,1)}, u32[]{:S(2)}, u32[]{:S(2)}) async-start(bf16[8,256,256]{2,1,0:T(8,128)(2,1)} %copy.32), calls=%async_computation | async-start | bytes 2097152 | tf_op jit(solution)/shard_map/all_to_all | solution.py:389
  48.5 21.4 %collective-permute-start.4 = (bf16[512,512]{1,0:T(8,128)(2,1)}, bf16[512,512]{1,0:T(8,128)(2,1)S(1)}, u32[]{:S(2)}, u32[]{:S(2)}) collective-permute-start(bf16[512,512]{1,0:T(8,128)(2,1)} %get-tuple-element.32.refs_3_.refs_0_), channel_id=1, source_target_pairs={{0,4},{1,5},{2,6},{3,7},{4,0},{5,1},{6,2},{7,3},{8,140},{9,141},{1... | collective-permute-start | bytes 1572872 | tf_op jit(solution)/shard_map/ppermute | solution.py:361
  48.8 23.7 %collective-permute-start.3 = (bf16[512,512]{1,0:T(8,128)(2,1)S(1)}, bf16[512,512]{1,0:T(8,128)(2,1)}, u32[]{:S(2)}, u32[]{:S(2)}) collective-permute-start(bf16[512,512]{1,0:T(8,128)(2,1)S(1)} %get-tuple-element.33.refs_2_), channel_id=1, source_target_pairs={{0,3},{1,0},{2,1},{3,2},{4,7},{5,4},{6,5},{7,6},{8,9},{9,10},{10,1... | collective-permute-start | bytes 1572872 | tf_op jit(solution)/shard_map/ppermute | solution.py:361
  49.5 26.8 %collective-permute-start.8 = (bf16[256,1024]{1,0:T(8,128)(2,1)}, bf16[256,1024]{1,0:T(8,128)(2,1)}, u32[]{:S(2)}, u32[]{:S(2)}) collective-permute-start(bf16[256,1024]{1,0:T(8,128)(2,1)} %get-tuple-element.64), channel_id=1, source_target_pairs={{0,8},{1,9},{2,10},{3,11},{4,12},{5,13},{6,14},{7,15},{8,0},{9,1},... | collective-permute-start | bytes 1572872 | tf_op jit(solution)/shard_map/ppermute | solution.py:361
  59.2 15.4 %collective-permute-start.7 = (f32[3,256,1]{2,1,0:T(8,128)S(1)}, f32[3,256,1]{2,1,0:T(8,128)S(1)}, u32[]{:S(2)}, u32[]{:S(2)}) collective-permute-start(f32[3,256,1]{2,1,0:T(8,128)S(1)} %copy-done.16), channel_id=1, source_target_pairs={{0,8},{1,9},{2,10},{3,11},{4,12},{5,13},{6,14},{7,15},{8,0},{9,1},... | collective-permute-start | bytes 9224 | tf_op jit(solution)/shard_map/ppermute | solution.py:361
  60.1 32.2 %collective-permute-start.14 = (bf16[512,512]{1,0:T(8,128)(2,1)}, bf16[512,512]{1,0:T(8,128)(2,1)S(1)}, u32[]{:S(2)}, u32[]{:S(2)}) collective-permute-start(bf16[512,512]{1,0:T(8,128)(2,1)} %get-tuple-element.50), channel_id=1, source_target_pairs={{0,1},{1,2},{2,3},{3,0},{4,5},{5,6},{6,7},{7,4},{8,11},{9,8},{10,9... | collective-permute-start | bytes 1572872 | tf_op jit(solution)/shard_map/ppermute | solution.py:361
  69.9 22.3 %collective-permute-start.15 = (bf16[512,512]{1,0:T(8,128)(2,1)S(1)}, bf16[512,512]{1,0:T(8,128)(2,1)S(1)}, u32[]{:S(2)}, u32[]{:S(2)}) collective-permute-start(bf16[512,512]{1,0:T(8,128)(2,1)S(1)} %get-tuple-element.51.refs_2_), channel_id=1, source_target_pairs={{0,4},{1,5},{2,6},{3,7},{4,0},{5,1},{6,2},{7,3},{8,140},{9,141},{1... | collective-permute-start | bytes 1572872 | tf_op jit(solution)/shard_map/ppermute | solution.py:361
  73.2 11.0 %copy-start.2 = (bf16[512,512]{1,0:T(8,128)(2,1)}, bf16[512,512]{1,0:T(8,128)(2,1)S(1)}, u32[]{:S(2)}) copy-start(bf16[512,512]{1,0:T(8,128)(2,1)S(1)} %get-tuple-element.38.refs_3_.refs_2_) | copy-start | bytes 1572868
  73.2 21.7 %collective-permute-start.5 = (bf16[512,512]{1,0:T(8,128)(2,1)}, bf16[512,512]{1,0:T(8,128)(2,1)S(1)}, u32[]{:S(2)}, u32[]{:S(2)}) collective-permute-start(bf16[512,512]{1,0:T(8,128)(2,1)} %get-tuple-element.36), channel_id=1, source_target_pairs={{0,1},{1,2},{2,3},{3,0},{4,5},{5,6},{6,7},{7,4},{8,11},{9,8},{10,9... | collective-permute-start | bytes 1572872 | tf_op jit(solution)/shard_map/ppermute | solution.py:361
  75.4 19.4 %collective-permute-start.6 = (bf16[512,512]{1,0:T(8,128)(2,1)}, bf16[512,512]{1,0:T(8,128)(2,1)}, u32[]{:S(2)}, u32[]{:S(2)}) collective-permute-start(bf16[512,512]{1,0:T(8,128)(2,1)} %get-tuple-element.37.refs_2_), channel_id=1, source_target_pairs={{0,4},{1,5},{2,6},{3,7},{4,0},{5,1},{6,2},{7,3},{8,140},{9,141},{1... | collective-permute-start | bytes 1572872 | tf_op jit(solution)/shard_map/ppermute | solution.py:361
  92.3 21.1 %collective-permute-start.16 = (bf16[512,512]{1,0:T(8,128)(2,1)S(1)}, bf16[512,512]{1,0:T(8,128)(2,1)S(1)}, u32[]{:S(2)}, u32[]{:S(2)}) collective-permute-start(bf16[512,512]{1,0:T(8,128)(2,1)S(1)} %get-tuple-element.55.refs_1_), channel_id=1, source_target_pairs={{0,4},{1,5},{2,6},{3,7},{4,0},{5,1},{6,2},{7,3},{8,140},{9,141},{1... | collective-permute-start | bytes 1572872 | tf_op jit(solution)/shard_map/ppermute | solution.py:361
  95.6 25.0 %collective-permute-start.9 = (bf16[512,512]{1,0:T(8,128)(2,1)S(1)}, bf16[512,512]{1,0:T(8,128)(2,1)S(1)}, u32[]{:S(2)}, u32[]{:S(2)}) collective-permute-start(bf16[512,512]{1,0:T(8,128)(2,1)S(1)} %get-tuple-element.41), channel_id=1, source_target_pairs={{0,1},{1,2},{2,3},{3,0},{4,5},{5,6},{6,7},{7,4},{8,11},{9,8},{10,9... | collective-permute-start | bytes 1572872 | tf_op jit(solution)/shard_map/ppermute | solution.py:361
  127.7 9.1 %all-to-all-start.1 = ((f32[16,1,512]{2,1,0:T(1,128)}), f32[16,1,512]{2,1,0:T(1,128)S(1)}, u32[]{:S(2)}, u32[]{:S(2)}) async-start(f32[16,1,512]{2,1,0:T(1,128)} %shard_map.82), calls=%async_computation.1 | async-start | bytes 65536 | tf_op jit(solution)/shard_map/all_to_all | solution.py:348
  137.4 17.2 %all-to-all-start.2 = ((f32[16,1,512]{2,1,0:T(1,128)}), f32[16,1,512]{2,1,0:T(1,128)S(1)}, u32[]{:S(2)}, u32[]{:S(2)}) async-start(f32[16,1,512]{2,1,0:T(1,128)} %shard_map.83), calls=%async_computation.2 | async-start | bytes 65536 | tf_op jit(solution)/shard_map/all_to_all | solution.py:348
  159.5 3.2 %collective-permute-start.17 = (f32[2,64,512]{2,1,0:T(8,128)}, f32[2,64,512]{2,1,0:T(8,128)S(1)}, u32[]{:S(2)}, u32[]{:S(2)}) collective-permute-start(f32[2,64,512]{2,1,0:T(8,128)} %get-tuple-element.60), channel_id=1, source_target_pairs={{0,8},{1,9},{2,10},{3,11},{4,12},{5,13},{6,14},{7,15},{8,0},{9,1},... | collective-permute-start | bytes 786440 | tf_op jit(solution)/shard_map/ppermute | solution.py:361
  163.7 6.3 %collective-permute-start.18 = (f32[64,512]{1,0:T(8,128)S(1)}, f32[64,512]{1,0:T(8,128)S(1)}, u32[]{:S(2)}, u32[]{:S(2)}) collective-permute-start(f32[64,512]{1,0:T(8,128)S(1)} %slice_bitcast_fusion), channel_id=1, source_target_pairs={{0,128},{1,129},{2,130},{3,131},{4,132},{5,133},{6,134},{7,135},{8... | collective-permute-start | bytes 393224 | tf_op jit(solution)/shard_map/ppermute | solution.py:361
  (22 other events, 120.8 us)
Sparse Core Ops, SparseCore 0:
  12.4 48.1 all-gather.2

commit v4 on v3

--- a/solution.py
+++ b/solution.py
@@ -17,7 +17,7 @@
 WA = XL * Y
 CHAINS = 2
 ROWS_ALL = 24
-VMEM_BYTES = 55 * 1024 * 1024
+VMEM_BYTES = 46 * 1024 * 1024
 SMALL_BYTES = 1024 * 1024
 
 
@@ -62,10 +62,10 @@
     return lax.dot_general(a, b, (((1,), (1,)), ((), ())), preferred_element_type=jnp.float32)
 
 
-def fetch_columns(kidx, count, block, sources, buffers, sems):
+def fetch_columns(kidx, base, count, block, sources, buffers, sems):
     copies = []
     for s in range(count):
-        cols = pl.ds(pl.multiple_of(kidx[s] * block, block), block)
+        cols = pl.ds(pl.multiple_of(kidx[base + s] * block, block), block)
         for side in range(2):
             copy = pltpu.make_async_copy(
                 sources[side].at[:, :, cols], buffers.at[s, side], sems.at[s, side]
@@ -84,14 +84,14 @@
     return copies
 
 
-def group_kernel(count, has_acc, extra, kidx, x_own, x_oth, *refs):
+def group_kernel(base, count, has_acc, extra, kidx, x_own, x_oth, *refs):
     refs = refs[extra:]
     sent = refs[:count]
     acc_in = refs[count] if has_acc else None
     out, token, ws, w_sems, buffers, sems = refs[-6:]
     members, width = out.shape[2], out.shape[3]
     block = sent[0].shape[1]
-    copies = fetch_columns(kidx, count, block, (x_own, x_oth), buffers, sems)
+    copies = fetch_columns(kidx, base, count, block, (x_own, x_oth), buffers, sems)
     fetched = fetch_weights(sent, ws, w_sems)
     token[...] = jnp.zeros_like(token)
     chunk = 512
@@ -112,7 +112,7 @@
             out[side, :, :, cols] = total
 
 
-def group_matmul(kidx, x_own, x_oth, ws, acc, extra=()):
+def group_matmul(base, kidx, x_own, x_oth, ws, acc, extra=()):
     count = len(ws)
     members = x_own.shape[1]
     width, block = ws[0].shape
@@ -128,7 +128,7 @@
         alias = {len(args): 0}
     flops = 2 * 2 * 3 * members * width * block * count
     return pl.pallas_call(
-        functools.partial(group_kernel, count, acc is not None, len(extra)),
+        functools.partial(group_kernel, base, count, acc is not None, len(extra)),
         out_shape=(
             jax.ShapeDtypeStruct((2, 3, members, width), jnp.float32),
             jax.ShapeDtypeStruct((8, 128), jnp.float32),
@@ -153,7 +153,7 @@
     members, width = acc.shape[2], acc.shape[3]
     block = sent.shape[1]
     fetched = fetch_weights([sent], w, w_sems)
-    copies = fetch_columns(kidx, 1, block, (x_own, x_oth), buffers, sems)
+    copies = fetch_columns(kidx, 7, 1, block, (x_own, x_oth), buffers, sems)
     fetched[0].wait()
     chunk = 256
     ones = jnp.ones((8, 128), jnp.float32)
@@ -180,7 +180,7 @@
             preferred_element_type=jnp.float32,
             precision=lax.Precision.HIGHEST,
         )[0:1]
-        at = pl.ds(pl.multiple_of(jnp.bitwise_xor(kidx[1], side) * members, members), members)
+        at = pl.ds(pl.multiple_of(jnp.bitwise_xor(kidx[8], side) * members, members), members)
         if before is not None:
             row = row + before[0, :, at]
         for k in range(out.shape[0]):
@@ -221,7 +221,7 @@
 
 
 def after(values, *done):
-    hbm = pl.BlockSpec(memory_space=pltpu.HBM)
+    hbm = pl.BlockSpec(memory_space=pl.ANY)
     count = len(values)
     return pl.pallas_call(
         after_kernel,
@@ -248,7 +248,37 @@
     )(got)
 
 
-def low_kernel(x, fin, out, x_buf, f_buf, sems):
+def take_kernel(place, weight, fin, *refs):
+    parts, fin_here, sems = refs[:-2], refs[-2], refs[-1]
+    rows, block = parts[0].shape
+    copies = []
+    for h, out in enumerate(parts):
+        at = pl.ds(pl.multiple_of(place[8] * (rows * len(parts)) + h * rows, rows), rows)
+        copies.append(pltpu.make_async_copy(weight.at[at, :], out, sems.at[h]))
+    cols = pl.ds(pl.multiple_of(place[0] * block, block), block)
+    copies.append(pltpu.make_async_copy(fin.at[:, cols], fin_here, sems.at[len(parts)]))
+    for copy in copies:
+        copy.start()
+    for copy in copies:
+        copy.wait()
+
+
+def take_blocks(place, weight, fin, part):
+    block = weight.shape[1]
+    hbm = pl.BlockSpec(memory_space=pl.ANY)
+    shapes = [jax.ShapeDtypeStruct((part, block), weight.dtype)] * CHAINS
+    shapes.append(jax.ShapeDtypeStruct((fin.shape[0], block), fin.dtype))
+    return pl.pallas_call(
+        take_kernel,
+        out_shape=tuple(shapes),
+        in_specs=[pl.BlockSpec(memory_space=pltpu.SMEM), hbm, hbm],
+        out_specs=(hbm,) * len(shapes),
+        scratch_shapes=[pltpu.SemaphoreType.DMA((len(shapes),))],
+        compiler_params=pltpu.CompilerParams(vmem_limit_bytes=VMEM_BYTES),
+    )(place, weight, fin)
+
+
+def low_kernel(place, x, fin, fout, readout, out, pieces, mine, theirs, read, x_buf, f_buf, sems, out_sems):
     tiles, rows, tile, width = x_buf.shape
     copies = []
     for t in range(tiles):
@@ -260,6 +290,20 @@
         for copy in pair:
             copy.start()
         copies.append(pair)
+    half = mine.shape[1]
+    moves = []
+    for at, to in ((place[8], mine), (1 - place[8], theirs)):
+        cols = pl.ds(pl.multiple_of(at * half, half), half)
+        moves.append((fout.at[:, cols], to))
+    run = pieces.shape[2] // XH
+    for h in range(XH):
+        for k in range(Z):
+            cols = pl.ds(h * half + k * run, run)
+            moves.append((fout.at[:, cols], pieces.at[k, :, pl.ds(h * run, run)]))
+    moved = [pltpu.make_async_copy(a, b, out_sems.at[i]) for i, (a, b) in enumerate(moves)]
+    for copy in moved:
+        copy.start()
+    read[...] = readout[:, pl.ds(pl.multiple_of(place[8] * half, half), half)]
     chunk = 128
     for t in range(tiles):
         for copy in copies[t]:
@@ -273,28 +317,40 @@
                 totals[r] = term if totals[r] is None else totals[r] + term
         for r in range(rows):
             out[r, pl.ds(t * tile, tile), :] = perturb_scale * jnp.sum(totals[r], axis=1, keepdims=True)
-
-
-def low_term(x, fin):
+    for copy in moved:
+        copy.wait()
+
+
+def low_term(place, x, fin, fout, readout):
     rows, members, width = x.shape
+    out_width = fout.shape[1]
+    half = out_width // CORE
     tile = 64
     tiles = members // tile
-    hbm = pl.BlockSpec(memory_space=pltpu.HBM)
+    hbm = pl.BlockSpec(memory_space=pl.ANY)
+    vmem = pl.BlockSpec(memory_space=pltpu.VMEM)
     return pl.pallas_call(
         low_kernel,
-        out_shape=jax.ShapeDtypeStruct((rows, members, 1), jnp.float32),
-        in_specs=[hbm, hbm],
-        out_specs=pl.BlockSpec(memory_space=pltpu.VMEM),
+        out_shape=(
+            jax.ShapeDtypeStruct((rows, members, 1), jnp.float32),
+            jax.ShapeDtypeStruct((Z, members, out_width // Z), fout.dtype),
+            jax.ShapeDtypeStruct((members, half), fout.dtype),
+            jax.ShapeDtypeStruct((members, half), fout.dtype),
+            jax.ShapeDtypeStruct((1, half), readout.dtype),
+        ),
+        in_specs=[pl.BlockSpec(memory_space=pltpu.SMEM), hbm, hbm, hbm, vmem],
+        out_specs=(vmem, hbm, hbm, hbm, vmem),
         scratch_shapes=[
             pltpu.VMEM((tiles, rows, tile, width), jnp.bfloat16),
             pltpu.VMEM((tiles, tile, width), jnp.bfloat16),
             pltpu.SemaphoreType.DMA((tiles, 2)),
+            pltpu.SemaphoreType.DMA((2 + XH * Z,)),
         ],
         compiler_params=pltpu.CompilerParams(vmem_limit_bytes=VMEM_BYTES),
         cost_estimate=pl.CostEstimate(
             flops=2 * rows * members * width, bytes_accessed=9 * 1024 * 1024, transcendentals=0
         ),
-    )(x, fin)
+    )(place, x, fin, fout, readout)
 
 
 def step_kernel(place, fit, fout, fin, keep, give, util, rows_ref):
@@ -304,7 +360,7 @@
     mean = jnp.sum(values) / count
     spread = jnp.sum((values - mean) ** 2) / count
     root = jnp.sqrt(jnp.full((1, 1), spread + epsilon, jnp.float32))
-    xh, z, c = place[0], place[1], place[2]
+    c, xh, z = place[8], place[9], place[10]
     at = pl.ds(pl.multiple_of(c * members, members), members)
     util[...] = (fit[xh * Z + z, :, at] - mean) / root
     for k in range(Z):
@@ -378,63 +434,55 @@
     x_own = inputs.transpose(1, 0, 2)
     w_own = lax.dynamic_slice_in_dim(weight, c * half, half, 0)
 
-    def idx(*ks):
-        return jnp.stack(ks).astype(jnp.int32)
-
-    fin_here = lax.dynamic_slice_in_dim(factor_in, wa * block, block, 1)
-    fin_all = lax.all_gather(fin_here, "z", axis=0)
-    rows_out = out_width // (XH * Z * CORE)
-    pieces = factor_out.reshape(members, XH, Z, CORE, rows_out)
-    pieces = pieces.transpose(2, 0, 1, 3, 4).reshape(Z, members, out_width // Z)
-    pieces = lax.all_to_all(pieces, "z", 0, 0, tiled=True)
+    places = jnp.stack([k_own, k_a, k_d, k_b, k_e, k_f, k_c, k_g, c, xh, z]).astype(jnp.int32)
 
     part = half // CHAINS
     chains = range(CHAINS)
-    starts = [c * half + h * part for h in chains]
-    own = [lax.dynamic_slice_in_dim(weight, at, part, 0) for at in starts]
+    *own, fin_here = take_blocks(places, weight, factor_in, part)
     w_a = [send(w, y_fwd) for w in own]
     w_d = [send(w, x_go) for w in own]
     x_oth = send(x_own, core_go)
 
-    low_own = low_term(x_own, factor_in)
+    low_own, pieces_here, fout_mine, fout_theirs, read_mine = low_term(
+        places, x_own, factor_in, factor_out, readout[None]
+    )
+    fin_all = lax.all_gather(fin_here, "z", axis=0)
+    pieces = lax.all_to_all(pieces_here, "z", 0, 0, tiled=True)
     low_oth = send(low_own, core_go)
-    fout_theirs = lax.dynamic_slice_in_dim(factor_out, (1 - c) * half, half, 1)
     fout_got = send(fout_theirs, core_go)
-    fout_mine = lax.dynamic_slice_in_dim(factor_out, c * half, half, 1)
-    read_mine = lax.dynamic_slice_in_dim(readout, c * half, half, 0)[None]
 
     w_b, w_e, w_c, w_f, acc, token = ([None] * CHAINS for _ in range(6))
     for h in chains:
-        own[h], w_a[h], w_d[h] = after((own[h], w_a[h], w_d[h]))
+        own[h], w_a[h], w_d[h] = after((own[h], w_a[h], w_d[h]), low_own)
         w_b[h] = send(own[h], y_bwd)
         w_e[h] = send(w_a[h], x_go)
         acc[h], token[h] = group_matmul(
-            idx(k_own, k_a, k_d), x_own, x_oth, [own[h], w_a[h], w_d[h]], None, (low_own, fout_mine)
+            0, places, x_own, x_oth, [own[h], w_a[h], w_d[h]], None
         )
     for h in chains:
         w_a[h], w_b[h], w_e[h] = after((w_a[h], w_b[h], w_e[h]), token[h])
         w_c[h] = send(w_a[h], y_fwd)
         w_f[h] = send(w_b[h], x_go)
         acc[h], token[h] = group_matmul(
-            idx(k_b, k_e), x_own, x_oth, [w_b[h], w_e[h]], acc[h], (low_oth, fout_got)
+            3, places, x_own, x_oth, [w_b[h], w_e[h]], acc[h], (low_oth, fout_got)
         )
     w_g = [None] * CHAINS
     for h in chains:
         w_c[h], w_f[h], w_e[h] = after((w_c[h], w_f[h], w_e[h]), token[h])
         w_g[h] = send(w_c[h], x_go) if h == 0 else send(w_e[h], y_fwd)
         acc[h], token[h] = group_matmul(
-            idx(k_f, k_c), x_own, x_oth, [w_f[h], w_c[h]], acc[h]
+            5, places, x_own, x_oth, [w_f[h], w_c[h]], acc[h]
         )
     partial = None
     for h in chains:
         partial = last_matmul(
-            h * part, idx(k_g, c), x_own, x_oth, w_g[h], pieces if h == 1 else w_g[h], acc[h],
+            h * part, places, x_own, x_oth, w_g[h], pieces if h == 1 else w_g[h], acc[h],
             low_own, low_oth, fout_mine, fout_got, read_mine, partial,
         )
 
     fit = share(sum_and_copy(share(partial, ("core", "xl", "y"))), ("xh", "z"))
 
-    keep, give, util = weight_part(idx(xh, z, c), fit, pieces, fin_all)
+    keep, give, util = weight_part(places, fit, pieces, fin_all)
     summed = keep + send(give, core_go)
     weight_step = summed[0] + send(summed[1], go_xh())
     return weight_step, util.reshape(members)

time: 178 us -> 144 us (0.81)
  Pallas kernels: 70.4 us -> 46.6 us
  blocking collectives: 0 us -> 10.2 us
  waiting for transfers between devices: 27.8 us -> 18.2 us
  other arithmetic: 4.96 us -> 0.72 us
  local copies, waits for them, and re-layouts: 17.4 us -> 13.4 us
  starting transfers between devices: 42.6 us -> 39.5 us
    pallas_call x7 -> x8, Pallas kernels: 52.8 us -> 35.3 us  [the longest x6 29.7 us: group_matmul(): pl.pallas_call(functools.partial(group_kernel, base, count, acc is not No...]
    all_to_all x0 -> x1, blocking collectives: none -> 10.2 us  [share(): return lax.all_to_all(x, axes, 0, 0, tiled=True)]
    unnamed x47 -> x36, local copies, waits for them, and re-layouts: 8.13 us -> 13.3 us
    all_to_all x2 -> x1, waiting for transfers between devices: 13.9 us -> 8.83 us  [share(): return lax.all_to_all(x, axes, 0, 0, tiled=True)]
    pallas_call x2, Pallas kernels: 12.7 us -> 7.66 us  [last_matmul(): pl.pallas_call(functools.partial(last_kernel, first), out_shape=jax.Shape...]
    dynamic_slice x4 -> x0, local copies, waits for them, and re-layouts: 4.65 us -> none  [the longest x1 1.69 us: shards(): fin_here = lax.dynamic_slice_in_dim(factor_in, wa * block, block, 1)]
    ppermute x19, waiting for transfers between devices: 13.8 us -> 9.36 us  [send(): return lax.ppermute(v, AXES, pairs)]
    another operation x5 -> x0, other arithmetic: 3.29 us -> none  [idx(): return jnp.stack(ks).astype(jnp.int32)]
  transfers between devices with their start and end apart: 23 -> 22, of which waited for: 6 -> 5; matrix products, arithmetic and copies ran while one was open for 8% -> 0% of each run, Pallas kernels for 37% -> 31%
where the time goes in v4:
time: 144 us; the launch traced here: 143 us
  Pallas kernels  46.6 us (32%)
  starting transfers between devices  39.5 us (27%)
  waiting for transfers between devices  18.2 us (13%)
  between operations  14.4 us (10%)
  local copies, waits for them, and re-layouts  13.4 us (9%)
  blocking collectives  10.2 us (7%)
    pallas_call x6, Pallas kernels, group_matmul(): pl.pallas_call(functools.partial(group_kernel, base, count, acc is not No...  29.7 us
    ppermute x19, starting transfers between devices, send(): return lax.ppermute(v, AXES, pairs)  22.5 us
    unnamed x36, local copies, waits for them, and re-layouts  13.3 us
    all_to_all x1, blocking collectives, share(): return lax.all_to_all(x, axes, 0, 0, tiled=True)  10.2 us
    ppermute x19, waiting for transfers between devices, send(): return lax.ppermute(v, AXES, pairs)  9.36 us
    all_to_all x1, waiting for transfers between devices, share(): return lax.all_to_all(x, axes, 0, 0, tiled=True)  8.83 us
    all_to_all x1, starting transfers between devices, share(): return lax.all_to_all(x, axes, 0, 0, tiled=True)  8.81 us
    all_to_all x1, starting transfers between devices, shards(): pieces = lax.all_to_all(pieces_here, 'z', 0, 0, tiled=True)  8.19 us
  transfers between devices with their start and end apart: 22, of which 5 were waited for; matrix products, arithmetic and copies ran while one was open for 0% of the time, Pallas kernels for 31%

profile of v4, /device:TPU:1, one launch (start us, length us, event | category | flops | bytes accessed | tf_op | source)
XLA Modules:
  0.0 143.0 jit_solution(746635286052850791)
XLA Ops:
  7.2 3.3 %collective-permute-start = (bf16[3,256,4096]{2,1,0:T(8,128)(2,1)}, bf16[3,256,4096]{2,1,0:T(8,128)(2,1)}, u32[]{:S(2)}, u32[]{:S(2)}) collective-permute-start(bf16[3,256,4096]{2,1,0:T(8,128)(2,1)} %bitcast.23), channel_id=1, source_target_pairs={{0,8},{1,9},{2,10},{3,11},{4,12},{5,13},{6,14},{7,15},{8,0},{9,1},... | collective-permute-start | bytes 18874376 | tf_op jit(solution)/shard_map/ppermute | solution.py:417
  10.6 1.6 %copy-done.2 = bf16[256,4096]{1,0:T(8,128)(2,1)S(1)} copy-done((bf16[256,4096]{1,0:T(8,128)(2,1)S(1)}, bf16[256,4096]{1,0:T(8,128)(2,1)}, u32[]{:S(2)}) %copy-start.2) | copy-done | bytes 2097176
  16.3 2.5 %collective-permute-start.11 = (bf16[512,512]{1,0:T(8,128)(2,1)S(1)}, bf16[512,512]{1,0:T(8,128)(2,1)}, u32[]{:S(2)}, u32[]{:S(2)}) collective-permute-start(bf16[512,512]{1,0:T(8,128)(2,1)S(1)} %get-tuple-element.60.refs_0_), channel_id=1, source_target_pairs={{0,4},{1,5},{2,6},{3,7},{4,0},{5,1},{6,2},{7,3},{8,140},{9,141},{1... | collective-permute-start | bytes 1572872 | tf_op jit(solution)/shard_map/ppermute | solution.py:417
  20.6 4.3 %shard_map.69 = (f32[3,256,1]{2,1,0:T(8,128)S(1)}, bf16[8,256,256]{2,1,0:T(8,128)(2,1)S(1)}, bf16[256,1024]{1,0:T(8,128)(2,1)S(1)}, bf16[256,1024]{1,0:T(8,128)(2,1)}, f32[1,1024]{1,0:T(1,128)S(1)}) custom-call(s32[11]{0:T(128)S(1)} %stack.47.place.kidx, bf16[3,256,4096]{2,1,0:T(8,128)(2,1)} %bitcast.24, bf16[256,4096]{1,0:T(8,128)(2,1)S(1)} %copy-done.3, ...), custom_call_target="tpu_custom_call" | custom-call | flops 6291456 | bytes 9437184 | tf_op jit(solution)/shard_map/pallas_call | solution.py:332
  26.7 8.2 %all-to-all-start = ((bf16[8,256,256]{2,1,0:T(8,128)(2,1)}), bf16[8,256,256]{2,1,0:T(8,128)(2,1)}, u32[]{:S(2)}, u32[]{:S(2)}) async-start(bf16[8,256,256]{2,1,0:T(8,128)(2,1)} %copy-done.13), calls=%async_computation | async-start | bytes 2097152 | tf_op jit(solution)/shard_map/all_to_all | solution.py:450
  36.0 2.5 %collective-permute-start.13 = (bf16[512,512]{1,0:T(8,128)(2,1)}, bf16[512,512]{1,0:T(8,128)(2,1)S(1)}, u32[]{:S(2)}, u32[]{:S(2)}) collective-permute-start(bf16[512,512]{1,0:T(8,128)(2,1)} %get-tuple-element.61.refs_1_.refs_0_), channel_id=1, source_target_pairs={{0,4},{1,5},{2,6},{3,7},{4,0},{5,1},{6,2},{7,3},{8,140},{9,141},{1... | collective-permute-start | bytes 1572872 | tf_op jit(solution)/shard_map/ppermute | solution.py:417
  38.9 6.1 %shard_map.77 = (f32[2,3,256,512]{3,2,1,0:T(8,128)S(1)}, f32[8,128]{1,0:T(8,128)S(1)}) custom-call(s32[11]{0:T(128)S(1)} %stack.47.place.kidx, bf16[3,256,4096]{2,1,0:T(8,128)(2,1)} %bitcast.25, bf16[3,256,4096]{2,1,0:T(8,128)(2,1)} %collective-permute-done.x_oth, bf16[512,512]{1,0:T(8,128)(2,1)S(1)} %get-tuple-element.62.refs_0_, ...), custom_call_target="tpu_custom_call" | custom-call | flops 2415919104 | bytes 16777216 | tf_op jit(solution)/shard_map/pallas_call | solution.py:130
  45.9 2.4 %collective-permute-start.14 = (bf16[512,512]{1,0:T(8,128)(2,1)}, bf16[512,512]{1,0:T(8,128)(2,1)S(1)}, u32[]{:S(2)}, u32[]{:S(2)}) collective-permute-start(bf16[512,512]{1,0:T(8,128)(2,1)} %get-tuple-element.65), channel_id=1, source_target_pairs={{0,1},{1,2},{2,3},{3,0},{4,5},{5,6},{6,7},{7,4},{8,11},{9,8},{10,9... | collective-permute-start | bytes 1572872 | tf_op jit(solution)/shard_map/ppermute | solution.py:417
  48.2 2.0 %collective-permute-done.3.refs_1_ = bf16[512,512]{1,0:T(8,128)(2,1)S(1)} collective-permute-done((bf16[512,512]{1,0:T(8,128)(2,1)S(1)}, bf16[512,512]{1,0:T(8,128)(2,1)S(1)}, u32[]{:S(2)}, u32[]{:S(2)}) %collective-permute-start.3) | collective-permute-done | bytes 524320 | tf_op jit(solution)/shard_map/ppermute | solution.py:417
  50.3 2.5 %collective-permute-start.15 = (bf16[512,512]{1,0:T(8,128)(2,1)S(1)}, bf16[512,512]{1,0:T(8,128)(2,1)S(1)}, u32[]{:S(2)}, u32[]{:S(2)}) collective-permute-start(bf16[512,512]{1,0:T(8,128)(2,1)S(1)} %get-tuple-element.66.refs_2_), channel_id=1, source_target_pairs={{0,4},{1,5},{2,6},{3,7},{4,0},{5,1},{6,2},{7,3},{8,140},{9,141},{1... | collective-permute-start | bytes 1572872 | tf_op jit(solution)/shard_map/ppermute | solution.py:417
  53.8 6.1 %shard_map.71 = (f32[2,3,256,512]{3,2,1,0:T(8,128)S(1)}, f32[8,128]{1,0:T(8,128)S(1)}) custom-call(s32[11]{0:T(128)S(1)} %stack.47.place.kidx, bf16[3,256,4096]{2,1,0:T(8,128)(2,1)} %bitcast.26, bf16[3,256,4096]{2,1,0:T(8,128)(2,1)} %collective-permute-done.x_oth, bf16[512,512]{1,0:T(8,128)(2,1)S(1)} %copy-done.12, ...), custom_call_target="tpu_custom_call" | custom-call | flops 2415919104 | bytes 16777216 | tf_op jit(solution)/shard_map/pallas_call | solution.py:130
  60.4 4.3 %shard_map.79 = (f32[2,3,256,512]{3,2,1,0:T(8,128)S(1)}, f32[8,128]{1,0:T(8,128)S(1)}) custom-call(s32[11]{0:T(128)S(1)} %stack.47.place.kidx, bf16[3,256,4096]{2,1,0:T(8,128)(2,1)} %bitcast.27, bf16[3,256,4096]{2,1,0:T(8,128)(2,1)} %collective-permute-done.x_oth, ...), custom_call_target="tpu_custom_call", output_to_operand_aliasing={{0}: (7, {})} | custom-call | flops 1610612736 | bytes 16777216 | tf_op jit(solution)/shard_map/pallas_call | solution.py:130
  64.7 2.6 %collective-permute-start.16 = (bf16[512,512]{1,0:T(8,128)(2,1)S(1)}, bf16[512,512]{1,0:T(8,128)(2,1)S(1)}, u32[]{:S(2)}, u32[]{:S(2)}) collective-permute-start(bf16[512,512]{1,0:T(8,128)(2,1)S(1)} %get-tuple-element.70.refs_1_), channel_id=1, source_target_pairs={{0,4},{1,5},{2,6},{3,7},{4,0},{5,1},{6,2},{7,3},{8,140},{9,141},{1... | collective-permute-start | bytes 1572872 | tf_op jit(solution)/shard_map/ppermute | solution.py:417
  67.2 4.7 %shard_map.73 = (f32[2,3,256,512]{3,2,1,0:T(8,128)S(1)}, f32[8,128]{1,0:T(8,128)S(1)}) custom-call(s32[11]{0:T(128)S(1)} %stack.47.place.kidx, bf16[3,256,4096]{2,1,0:T(8,128)(2,1)} %bitcast.28, bf16[3,256,4096]{2,1,0:T(8,128)(2,1)} %collective-permute-done.x_oth, ...), custom_call_target="tpu_custom_call", output_to_operand_aliasing={{0}: (7, {})} | custom-call | flops 1610612736 | bytes 16777216 | tf_op jit(solution)/shard_map/pallas_call | solution.py:130
  72.3 4.3 %shard_map.81 = (f32[2,3,256,512]{3,2,1,0:T(8,128)S(1)}, f32[8,128]{1,0:T(8,128)}) custom-call(s32[11]{0:T(128)S(1)} %stack.47.place.kidx, bf16[3,256,4096]{2,1,0:T(8,128)(2,1)} %bitcast.29, bf16[3,256,4096]{2,1,0:T(8,128)(2,1)} %collective-permute-done.x_oth, bf16[512,512]{1,0:T(8,128)(2,1)S(1)} %get-tuple-element.71.refs_0_, ...), custom_call_target="tpu_custom_call", output_to_operand_aliasing={{0}: (5, {})} | custom-call | flops 1610612736 | bytes 16777216 | tf_op jit(solution)/shard_map/pallas_call | solution.py:130
  76.6 4.3 %shard_map.75 = (f32[2,3,256,512]{3,2,1,0:T(8,128)S(1)}, f32[8,128]{1,0:T(8,128)}) custom-call(s32[11]{0:T(128)S(1)} %stack.47.place.kidx, bf16[3,256,4096]{2,1,0:T(8,128)(2,1)} %bitcast.30, bf16[3,256,4096]{2,1,0:T(8,128)(2,1)} %collective-permute-done.x_oth, bf16[512,512]{1,0:T(8,128)(2,1)S(1)} %get-tuple-element.54.refs_0_, ...), custom_call_target="tpu_custom_call", output_to_operand_aliasing={{0}: (5, {})} | custom-call | flops 1610612736 | bytes 16777216 | tf_op jit(solution)/shard_map/pallas_call | solution.py:130
  80.9 3.8 %shard_map.82.refs_0_ = f32[16,1,512]{2,1,0:T(1,128)S(1)} custom-call(s32[11]{0:T(128)S(1)} %stack.47.place.kidx, bf16[3,256,4096]{2,1,0:T(8,128)(2,1)} %bitcast.31, bf16[3,256,4096]{2,1,0:T(8,128)(2,1)} %collective-permute-done.x_oth, bf16[512,512]{1,0:T(8,128)(2,1)S(1)} %collective-permute-done.16.sent.pieces, ...), custom_call_target="tpu_custom_call" | custom-call | flops 805306368 | bytes 6291456 | tf_op jit(solution)/shard_map/pallas_call | solution.py:199
  89.1 3.9 %shard_map.83 = f32[16,1,512]{2,1,0:T(1,128)S(1)} custom-call(s32[11]{0:T(128)S(1)} %stack.47.place.kidx, bf16[3,256,4096]{2,1,0:T(8,128)(2,1)} %bitcast.32, bf16[3,256,4096]{2,1,0:T(8,128)(2,1)} %collective-permute-done.x_oth, bf16[512,512]{1,0:T(8,128)(2,1)} %collective-permute-done.9.sent, bf16[8,256,256]{2,1,0:T(8,128)(2,1)} %all-to-all-done.pieces.fout, ...), custom_call_target="tpu_custom_call" | custom-call | flops 805306368 | bytes 6291456 | tf_op jit(solution)/shard_map/pallas_call | solution.py:199
  93.0 10.2 %all_to_all.15.got = f32[16,1,512]{2,1,0:T(1,128)S(1)} all-to-all(f32[16,1,512]{2,1,0:T(1,128)S(1)} %shard_map.83), channel_id=1, replica_groups=mesh['xh'=2,'z'=8,'core'=2,'xl'=2,'y'=4] {'core','xl','y'}, dimensions={0} | all-to-all | bytes 65536 | tf_op jit(solution)/shard_map/all_to_all | solution.py:404
  103.8 8.8 %all-to-all-start.2 = ((f32[16,1,512]{2,1,0:T(1,128)}), f32[16,1,512]{2,1,0:T(1,128)S(1)}, u32[]{:S(2)}, u32[]{:S(2)}) async-start(f32[16,1,512]{2,1,0:T(1,128)} %shard_map.84), calls=%async_computation.2 | async-start | bytes 65536 | tf_op jit(solution)/shard_map/all_to_all | solution.py:404
  112.7 8.8 %all-to-all-done.2.fit = f32[16,1,512]{2,1,0:T(1,128)S(1)} async-done(((f32[16,1,512]{2,1,0:T(1,128)}), f32[16,1,512]{2,1,0:T(1,128)S(1)}, u32[]{:S(2)}, u32[]{:S(2)}) %all-to-all-start.2) | async-done | bytes 32800 | tf_op jit(solution)/shard_map/all_to_all | solution.py:404
  123.1 3.0 %shard_map.85 = (f32[2,64,512]{2,1,0:T(8,128)S(1)}, f32[2,64,512]{2,1,0:T(8,128)S(1)}, f32[1,256]{1,0:T(1,128)}) custom-call(s32[11]{0:T(128)S(1)} %stack.47.place.kidx, f32[16,1,512]{2,1,0:T(1,128)S(1)} %all-to-all-done.2.fit, bf16[8,256,256]{2,1,0:T(8,128)(2,1)} %all-to-all-done.pieces.fout, bf16[8,256,512]{2,1,0:T(8,128)(2,1)S(1)} %bitcast.21), custom_call_target="tpu_custom_call" | custom-call | flops 536870912 | bytes 4194304 | tf_op jit(solution)/shard_map/pallas_call | solution.py:390
  126.1 1.8 %collective-permute-start.17 = (f32[2,64,512]{2,1,0:T(8,128)S(1)}, f32[2,64,512]{2,1,0:T(8,128)S(1)}, u32[]{:S(2)}, u32[]{:S(2)}) collective-permute-start(f32[2,64,512]{2,1,0:T(8,128)S(1)} %get-tuple-element.76), channel_id=1, source_target_pairs={{0,8},{1,9},{2,10},{3,11},{4,12},{5,13},{6,14},{7,15},{8,0},{9,1},... | collective-permute-start | bytes 786440 | tf_op jit(solution)/shard_map/ppermute | solution.py:417
  129.6 5.9 %collective-permute-done.18 = f32[64,512]{1,0:T(8,128)S(1)} collective-permute-done((f32[64,512]{1,0:T(8,128)S(1)}, f32[64,512]{1,0:T(8,128)S(1)}, u32[]{:S(2)}, u32[]{:S(2)}) %collective-permute-start.18) | collective-permute-done | bytes 131104 | tf_op jit(solution)/shard_map/ppermute | solution.py:417
  (80 shorter events, 21.0 us)
Async XLA Ops:
  7.2 105.5 %all-gather.3.cloned.1.call-start = ((), (), s32[]{:S(2)}) async-start(), calls=%async_computation.3 | async-start | bytes 2359296 | tf_op jit(solution)/shard_map/all_gather | solution.py:449
  7.2 31.7 %collective-permute-start = (bf16[3,256,4096]{2,1,0:T(8,128)(2,1)}, bf16[3,256,4096]{2,1,0:T(8,128)(2,1)}, u32[]{:S(2)}, u32[]{:S(2)}) collective-permute-start(bf16[3,256,4096]{2,1,0:T(8,128)(2,1)} %bitcast.23), channel_id=1, source_target_pairs={{0,8},{1,9},{2,10},{3,11},{4,12},{5,13},{6,14},{7,15},{8,0},{9,1},... | collective-permute-start | bytes 18874376 | tf_op jit(solution)/shard_map/ppermute | solution.py:417
  15.2 19.7 %collective-permute-start.10 = (bf16[512,512]{1,0:T(8,128)(2,1)S(1)}, bf16[512,512]{1,0:T(8,128)(2,1)}, u32[]{:S(2)}, u32[]{:S(2)}) collective-permute-start(bf16[512,512]{1,0:T(8,128)(2,1)S(1)} %get-tuple-element.60.refs_0_), channel_id=1, source_target_pairs={{0,1},{1,2},{2,3},{3,0},{4,5},{5,6},{6,7},{7,4},{8,11},{9,8},{10,9... | collective-permute-start | bytes 1572872 | tf_op jit(solution)/shard_map/ppermute | solution.py:417
  16.3 18.6 %collective-permute-start.11 = (bf16[512,512]{1,0:T(8,128)(2,1)S(1)}, bf16[512,512]{1,0:T(8,128)(2,1)}, u32[]{:S(2)}, u32[]{:S(2)}) collective-permute-start(bf16[512,512]{1,0:T(8,128)(2,1)S(1)} %get-tuple-element.60.refs_0_), channel_id=1, source_target_pairs={{0,4},{1,5},{2,6},{3,7},{4,0},{5,1},{6,2},{7,3},{8,140},{9,141},{1... | collective-permute-start | bytes 1572872 | tf_op jit(solution)/shard_map/ppermute | solution.py:417
  18.8 19.7 %collective-permute-start.1 = (bf16[512,512]{1,0:T(8,128)(2,1)S(1)}, bf16[512,512]{1,0:T(8,128)(2,1)}, u32[]{:S(2)}, u32[]{:S(2)}) collective-permute-start(bf16[512,512]{1,0:T(8,128)(2,1)S(1)} %get-tuple-element.40.refs_0_), channel_id=1, source_target_pairs={{0,1},{1,2},{2,3},{3,0},{4,5},{5,6},{6,7},{7,4},{8,11},{9,8},{10,9... | collective-permute-start | bytes 1572872 | tf_op jit(solution)/shard_map/ppermute | solution.py:417
  19.2 19.3 %collective-permute-start.2 = (bf16[512,512]{1,0:T(8,128)(2,1)S(1)}, bf16[512,512]{1,0:T(8,128)(2,1)}, u32[]{:S(2)}, u32[]{:S(2)}) collective-permute-start(bf16[512,512]{1,0:T(8,128)(2,1)S(1)} %get-tuple-element.40.refs_0_), channel_id=1, source_target_pairs={{0,4},{1,5},{2,6},{3,7},{4,0},{5,1},{6,2},{7,3},{8,140},{9,141},{1... | collective-permute-start | bytes 1572872 | tf_op jit(solution)/shard_map/ppermute | solution.py:417
  26.7 58.6 %all-to-all-start = ((bf16[8,256,256]{2,1,0:T(8,128)(2,1)}), bf16[8,256,256]{2,1,0:T(8,128)(2,1)}, u32[]{:S(2)}, u32[]{:S(2)}) async-start(bf16[8,256,256]{2,1,0:T(8,128)(2,1)} %copy-done.13), calls=%async_computation | async-start | bytes 2097152 | tf_op jit(solution)/shard_map/all_to_all | solution.py:450
  34.9 10.1 %collective-permute-start.12 = (bf16[512,512]{1,0:T(8,128)(2,1)S(1)}, bf16[512,512]{1,0:T(8,128)(2,1)S(1)}, u32[]{:S(2)}, u32[]{:S(2)}) collective-permute-start(bf16[512,512]{1,0:T(8,128)(2,1)S(1)} %get-tuple-element.62.refs_0_), channel_id=1, source_target_pairs={{0,3},{1,0},{2,1},{3,2},{4,7},{5,4},{6,5},{7,6},{8,9},{9,10},{10,1... | collective-permute-start | bytes 1572872 | tf_op jit(solution)/shard_map/ppermute | solution.py:417
  36.0 9.9 %collective-permute-start.13 = (bf16[512,512]{1,0:T(8,128)(2,1)}, bf16[512,512]{1,0:T(8,128)(2,1)S(1)}, u32[]{:S(2)}, u32[]{:S(2)}) collective-permute-start(bf16[512,512]{1,0:T(8,128)(2,1)} %get-tuple-element.61.refs_1_.refs_0_), channel_id=1, source_target_pairs={{0,4},{1,5},{2,6},{3,7},{4,0},{5,1},{6,2},{7,3},{8,140},{9,141},{1... | collective-permute-start | bytes 1572872 | tf_op jit(solution)/shard_map/ppermute | solution.py:417
  38.5 11.8 %collective-permute-start.3 = (bf16[512,512]{1,0:T(8,128)(2,1)S(1)}, bf16[512,512]{1,0:T(8,128)(2,1)S(1)}, u32[]{:S(2)}, u32[]{:S(2)}) collective-permute-start(bf16[512,512]{1,0:T(8,128)(2,1)S(1)} %get-tuple-element.43.refs_0_), channel_id=1, source_target_pairs={{0,3},{1,0},{2,1},{3,2},{4,7},{5,4},{6,5},{7,6},{8,9},{9,10},{10,1... | collective-permute-start | bytes 1572872 | tf_op jit(solution)/shard_map/ppermute | solution.py:417
  38.7 21.3 %collective-permute-start.4 = (bf16[512,512]{1,0:T(8,128)(2,1)}, bf16[512,512]{1,0:T(8,128)(2,1)}, u32[]{:S(2)}, u32[]{:S(2)}) collective-permute-start(bf16[512,512]{1,0:T(8,128)(2,1)} %get-tuple-element.42.refs_1_.refs_0_), channel_id=1, source_target_pairs={{0,4},{1,5},{2,6},{3,7},{4,0},{5,1},{6,2},{7,3},{8,140},{9,141},{1... | collective-permute-start | bytes 1572872 | tf_op jit(solution)/shard_map/ppermute | solution.py:417
  38.9 21.5 %collective-permute-start.8 = (bf16[256,1024]{1,0:T(8,128)(2,1)}, bf16[256,1024]{1,0:T(8,128)(2,1)S(1)}, u32[]{:S(2)}, u32[]{:S(2)}) collective-permute-start(bf16[256,1024]{1,0:T(8,128)(2,1)} %get-tuple-element.49), channel_id=1, source_target_pairs={{0,8},{1,9},{2,10},{3,11},{4,12},{5,13},{6,14},{7,15},{8,0},{9,1},... | collective-permute-start | bytes 1572872 | tf_op jit(solution)/shard_map/ppermute | solution.py:417
  45.0 15.0 %collective-permute-start.7 = (f32[3,256,1]{2,1,0:T(8,128)S(1)}, f32[3,256,1]{2,1,0:T(8,128)S(1)}, u32[]{:S(2)}, u32[]{:S(2)}) collective-permute-start(f32[3,256,1]{2,1,0:T(8,128)S(1)} %get-tuple-element.41.refs_3_.low_own), channel_id=1, source_target_pairs={{0,8},{1,9},{2,10},{3,11},{4,12},{5,13},{6,14},{7,15},{8,0},{9,1},... | collective-permute-start | bytes 9224 | tf_op jit(solution)/shard_map/ppermute | solution.py:417
  45.9 18.8 %collective-permute-start.14 = (bf16[512,512]{1,0:T(8,128)(2,1)}, bf16[512,512]{1,0:T(8,128)(2,1)S(1)}, u32[]{:S(2)}, u32[]{:S(2)}) collective-permute-start(bf16[512,512]{1,0:T(8,128)(2,1)} %get-tuple-element.65), channel_id=1, source_target_pairs={{0,1},{1,2},{2,3},{3,0},{4,5},{5,6},{6,7},{7,4},{8,11},{9,8},{10,9... | collective-permute-start | bytes 1572872 | tf_op jit(solution)/shard_map/ppermute | solution.py:417
  50.3 14.4 %collective-permute-start.15 = (bf16[512,512]{1,0:T(8,128)(2,1)S(1)}, bf16[512,512]{1,0:T(8,128)(2,1)S(1)}, u32[]{:S(2)}, u32[]{:S(2)}) collective-permute-start(bf16[512,512]{1,0:T(8,128)(2,1)S(1)} %get-tuple-element.66.refs_2_), channel_id=1, source_target_pairs={{0,4},{1,5},{2,6},{3,7},{4,0},{5,1},{6,2},{7,3},{8,140},{9,141},{1... | collective-permute-start | bytes 1572872 | tf_op jit(solution)/shard_map/ppermute | solution.py:417
  60.0 11.9 %collective-permute-start.5 = (bf16[512,512]{1,0:T(8,128)(2,1)}, bf16[512,512]{1,0:T(8,128)(2,1)S(1)}, u32[]{:S(2)}, u32[]{:S(2)}) collective-permute-start(bf16[512,512]{1,0:T(8,128)(2,1)} %get-tuple-element.46), channel_id=1, source_target_pairs={{0,1},{1,2},{2,3},{3,0},{4,5},{5,6},{6,7},{7,4},{8,11},{9,8},{10,9... | collective-permute-start | bytes 1572872 | tf_op jit(solution)/shard_map/ppermute | solution.py:417
  60.1 20.8 %copy-start.4 = (f32[3,256,1]{2,1,0:T(8,128)}, f32[3,256,1]{2,1,0:T(8,128)S(1)}, u32[]{:S(2)}) copy-start(f32[3,256,1]{2,1,0:T(8,128)S(1)} %collective-permute-done.7.refs_0_.low_oth) | copy-start | bytes 9220
  60.1 11.8 %collective-permute-start.6 = (bf16[512,512]{1,0:T(8,128)(2,1)S(1)}, bf16[512,512]{1,0:T(8,128)(2,1)S(1)}, u32[]{:S(2)}, u32[]{:S(2)}) collective-permute-start(bf16[512,512]{1,0:T(8,128)(2,1)S(1)} %get-tuple-element.47.refs_2_), channel_id=1, source_target_pairs={{0,4},{1,5},{2,6},{3,7},{4,0},{5,1},{6,2},{7,3},{8,140},{9,141},{1... | collective-permute-start | bytes 1572872 | tf_op jit(solution)/shard_map/ppermute | solution.py:417
  60.3 20.5 %copy-start = (bf16[256,1024]{1,0:T(8,128)(2,1)}, bf16[256,1024]{1,0:T(8,128)(2,1)S(1)}, u32[]{:S(2)}) copy-start(bf16[256,1024]{1,0:T(8,128)(2,1)S(1)} %collective-permute-done.8.refs_1_.fout_oth) | copy-start | bytes 1572868
  64.7 16.2 %collective-permute-start.16 = (bf16[512,512]{1,0:T(8,128)(2,1)S(1)}, bf16[512,512]{1,0:T(8,128)(2,1)S(1)}, u32[]{:S(2)}, u32[]{:S(2)}) collective-permute-start(bf16[512,512]{1,0:T(8,128)(2,1)S(1)} %get-tuple-element.70.refs_1_), channel_id=1, source_target_pairs={{0,4},{1,5},{2,6},{3,7},{4,0},{5,1},{6,2},{7,3},{8,140},{9,141},{1... | collective-permute-start | bytes 1572872 | tf_op jit(solution)/shard_map/ppermute | solution.py:417
  71.9 13.4 %collective-permute-start.9 = (bf16[512,512]{1,0:T(8,128)(2,1)}, bf16[512,512]{1,0:T(8,128)(2,1)}, u32[]{:S(2)}, u32[]{:S(2)}) collective-permute-start(bf16[512,512]{1,0:T(8,128)(2,1)} %get-tuple-element.52), channel_id=1, source_target_pairs={{0,1},{1,2},{2,3},{3,0},{4,5},{5,6},{6,7},{7,4},{8,11},{9,8},{10,9... | collective-permute-start | bytes 1572872 | tf_op jit(solution)/shard_map/ppermute | solution.py:417
  103.8 17.7 %all-to-all-start.2 = ((f32[16,1,512]{2,1,0:T(1,128)}), f32[16,1,512]{2,1,0:T(1,128)S(1)}, u32[]{:S(2)}, u32[]{:S(2)}) async-start(f32[16,1,512]{2,1,0:T(1,128)} %shard_map.84), calls=%async_computation.2 | async-start | bytes 65536 | tf_op jit(solution)/shard_map/all_to_all | solution.py:404
  126.1 3.0 %collective-permute-start.17 = (f32[2,64,512]{2,1,0:T(8,128)S(1)}, f32[2,64,512]{2,1,0:T(8,128)S(1)}, u32[]{:S(2)}, u32[]{:S(2)}) collective-permute-start(f32[2,64,512]{2,1,0:T(8,128)S(1)} %get-tuple-element.76), channel_id=1, source_target_pairs={{0,8},{1,9},{2,10},{3,11},{4,12},{5,13},{6,14},{7,15},{8,0},{9,1},... | collective-permute-start | bytes 786440 | tf_op jit(solution)/shard_map/ppermute | solution.py:417
  129.2 6.3 %collective-permute-start.18 = (f32[64,512]{1,0:T(8,128)S(1)}, f32[64,512]{1,0:T(8,128)S(1)}, u32[]{:S(2)}, u32[]{:S(2)}) collective-permute-start(f32[64,512]{1,0:T(8,128)S(1)} %slice_bitcast_fusion), channel_id=1, source_target_pairs={{0,128},{1,129},{2,130},{3,131},{4,132},{5,133},{6,134},{7,135},{8... | collective-permute-start | bytes 393224 | tf_op jit(solution)/shard_map/ppermute | solution.py:417
  (16 other events, 42.0 us)
Sparse Core Ops, SparseCore 0:
  15.3 58.8 all-gather.2

commit v5 on v4

--- a/solution.py
+++ b/solution.py
@@ -17,8 +17,10 @@
 WA = XL * Y
 CHAINS = 2
 ROWS_ALL = 24
-VMEM_BYTES = 46 * 1024 * 1024
+VMEM_BYTES = 41 * 1024 * 1024
+LAST_BYTES = 41 * 1024 * 1024
 SMALL_BYTES = 1024 * 1024
+LARGE_BYTES = 58 * 1024 * 1024
 
 
 def permutation(move):
@@ -62,44 +64,59 @@
     return lax.dot_general(a, b, (((1,), (1,)), ((), ())), preferred_element_type=jnp.float32)
 
 
-def fetch_columns(kidx, base, count, block, sources, buffers, sems):
-    copies = []
-    for s in range(count):
-        cols = pl.ds(pl.multiple_of(kidx[base + s] * block, block), block)
-        for side in range(2):
-            copy = pltpu.make_async_copy(
-                sources[side].at[:, :, cols], buffers.at[s, side], sems.at[s, side]
-            )
-            copy.start()
-            copies.append(copy)
-    return copies
-
-
-def fetch_weights(sent, ws, sems):
-    copies = []
-    for s, w in enumerate(sent):
-        copy = pltpu.make_async_copy(w, ws.at[s], sems.at[s])
+def fetch(kidx, base, x_own, x_oth, sent, ws, w_sems, buffers, sems):
+    count, part, block = len(sent), sent[0][0].shape[0], sent[0][0].shape[1]
+    waits = [[], []]
+
+    def start(source, to, sem, side):
+        copy = pltpu.make_async_copy(source, to, sem)
         copy.start()
-        copies.append(copy)
-    return copies
-
-
-def group_kernel(base, count, has_acc, extra, kidx, x_own, x_oth, *refs):
-    refs = refs[extra:]
-    sent = refs[:count]
-    acc_in = refs[count] if has_acc else None
+        waits[side].append(copy)
+
+    for side, x in ((0, x_own), (1, x_oth)):
+        for s in range(count):
+            if side == 0:
+                for h in range(CHAINS):
+                    start(sent[s][h], ws.at[s, pl.ds(h * part, part), :], w_sems.at[s, h], side)
+            cols = pl.ds(pl.multiple_of(kidx[base + s] * block, block), block)
+            start(x.at[:, :, cols], buffers.at[s, side], sems.at[s, side], side)
+    return waits
+
+
+def fetch_scratch(count, members, width, block):
+    return [
+        pltpu.VMEM((count, width, block), jnp.bfloat16),
+        pltpu.SemaphoreType.DMA((count, CHAINS)),
+        pltpu.VMEM((count, 2, 3, members, block), jnp.bfloat16),
+        pltpu.SemaphoreType.DMA((count, 2)),
+    ]
+
+
+def pairs(refs):
+    return [refs[i : i + CHAINS] for i in range(0, len(refs), CHAINS)]
+
+
+def group_kernel(base, count, has_acc, ahead, kidx, x_own, x_oth, *refs):
+    sent = pairs(refs[: count * CHAINS])
+    acc_in = refs[count * CHAINS] if has_acc else None
+    if ahead:
+        *refs, x_last, ws, w_sems, buffers, sems, last_sems = refs
+        refs = (*refs, ws, w_sems, buffers, sems)
     out, token, ws, w_sems, buffers, sems = refs[-6:]
     members, width = out.shape[2], out.shape[3]
-    block = sent[0].shape[1]
-    copies = fetch_columns(kidx, base, count, block, (x_own, x_oth), buffers, sems)
-    fetched = fetch_weights(sent, ws, w_sems)
+    block = ws.shape[2]
+    waits = fetch(kidx, base, x_own, x_oth, sent, ws, w_sems, buffers, sems)
+    early = []
+    if ahead:
+        cols = pl.ds(pl.multiple_of(kidx[base + count] * block, block), block)
+        for side, x in ((0, x_own), (1, x_oth)):
+            early.append(pltpu.make_async_copy(x.at[:, :, cols], x_last.at[side], last_sems.at[side]))
+            early[-1].start()
     token[...] = jnp.zeros_like(token)
     chunk = 512
     for side in range(2):
-        for s in range(count):
-            copies[2 * s + side].wait()
-            if side == 0:
-                fetched[s].wait()
+        for copy in waits[side]:
+            copy.wait()
         for j in range(0, width, chunk):
             cols = pl.ds(j, chunk)
             total = None
@@ -110,17 +127,20 @@
             if has_acc:
                 total = total + acc_in[side, :, :, cols]
             out[side, :, :, cols] = total
-
-
-def group_matmul(base, kidx, x_own, x_oth, ws, acc, extra=()):
-    count = len(ws)
+    for copy in early:
+        copy.wait()
+
+
+def group_matmul(base, kidx, x_own, x_oth, sent, acc, ahead=False):
+    count = len(sent)
     members = x_own.shape[1]
-    width, block = ws[0].shape
+    part, block = sent[0][0].shape
+    width = part * CHAINS
     smem = pl.BlockSpec(memory_space=pltpu.SMEM)
     vmem = pl.BlockSpec(memory_space=pltpu.VMEM)
-    hbm = pl.BlockSpec(memory_space=pltpu.HBM)
-    args = [x_own, x_oth, *extra] + list(ws)
-    specs = [smem, hbm, hbm] + [hbm] * len(extra) + [hbm] * count
+    hbm = pl.BlockSpec(memory_space=pl.ANY)
+    args = [x_own, x_oth] + [w for ws in sent for w in ws]
+    specs = [smem] + [hbm] * len(args)
     alias = {}
     if acc is not None:
         specs.append(vmem)
@@ -128,49 +148,50 @@
         alias = {len(args): 0}
     flops = 2 * 2 * 3 * members * width * block * count
     return pl.pallas_call(
-        functools.partial(group_kernel, base, count, acc is not None, len(extra)),
+        functools.partial(group_kernel, base, count, acc is not None, ahead),
         out_shape=(
             jax.ShapeDtypeStruct((2, 3, members, width), jnp.float32),
             jax.ShapeDtypeStruct((8, 128), jnp.float32),
-        ),
+        )
+        + ((jax.ShapeDtypeStruct((2, 3, members, block), x_own.dtype),) if ahead else ()),
         in_specs=specs,
-        out_specs=(vmem, vmem),
-        scratch_shapes=[
-            pltpu.VMEM((count, width, block), jnp.bfloat16),
-            pltpu.SemaphoreType.DMA((count,)),
-            pltpu.VMEM((count, 2, 3, members, block), jnp.bfloat16),
-            pltpu.SemaphoreType.DMA((count, 2)),
-        ],
+        out_specs=(vmem,) * (3 if ahead else 2),
+        scratch_shapes=fetch_scratch(count, members, width, block)
+        + ([pltpu.SemaphoreType.DMA((2,))] if ahead else []),
         input_output_aliases=alias,
         compiler_params=pltpu.CompilerParams(vmem_limit_bytes=VMEM_BYTES),
-        cost_estimate=pl.CostEstimate(flops=flops, bytes_accessed=16 * 1024 * 1024, transcendentals=0),
+        cost_estimate=pl.CostEstimate(flops=flops, bytes_accessed=8 * 1024 * 1024, transcendentals=0),
     )(kidx, *args)
 
 
-def last_kernel(first, kidx, x_own, x_oth, sent, pieces, acc, low_own, low_oth, fout_own, fout_oth, readout, *refs):
-    before = refs[0] if len(refs) == 6 else None
-    out, w, w_sems, buffers, sems = refs[-5:]
+def last_kernel(kidx, *refs):
+    sent = refs[:CHAINS]
+    x, acc, low_own, low_oth, fout_own, fout_oth, readout, out, ws, w_sems = refs[CHAINS:]
     members, width = acc.shape[2], acc.shape[3]
-    block = sent.shape[1]
-    fetched = fetch_weights([sent], w, w_sems)
-    copies = fetch_columns(kidx, 7, 1, block, (x_own, x_oth), buffers, sems)
-    fetched[0].wait()
+    block = ws.shape[1]
+    part_rows = sent[0].shape[0]
+    copies = []
+    for h in range(CHAINS):
+        to = ws.at[pl.ds(h * part_rows, part_rows), :]
+        copies.append(pltpu.make_async_copy(sent[h], to, w_sems.at[h]))
+        copies[-1].start()
+    for copy in copies:
+        copy.wait()
     chunk = 256
     ones = jnp.ones((8, 128), jnp.float32)
     for side, low, fout in ((0, low_own, fout_own), (1, low_oth, fout_oth)):
-        copies[side].wait()
         total = jnp.zeros((members, 128), jnp.float32)
         for j in range(0, width, chunk):
             cols = pl.ds(j, chunk)
-            part = nt_dot(buffers[0, side].reshape(3 * members, block), w[0, cols, :])
+            part = nt_dot(x[side].reshape(3 * members, block), ws[cols, :])
             part = part.reshape(3, members, chunk)
-            shift = fout[:, pl.ds(first + j, chunk)].astype(jnp.float32)
+            shift = fout[:, cols].astype(jnp.float32)
             summed = None
             for r in range(3):
                 pert = part[r] + acc[side, r, :, cols] + low[r] * shift
                 term = jnp.tanh(pert)
                 summed = term if summed is None else summed + term
-            summed = summed * readout[:, pl.ds(first + j, chunk)]
+            summed = summed * readout[:, cols]
             for h in range(0, chunk, 128):
                 total = total + summed[:, h : h + 128]
         row = lax.dot_general(
@@ -181,39 +202,33 @@
             precision=lax.Precision.HIGHEST,
         )[0:1]
         at = pl.ds(pl.multiple_of(jnp.bitwise_xor(kidx[8], side) * members, members), members)
-        if before is not None:
-            row = row + before[0, :, at]
         for k in range(out.shape[0]):
             out[k, :, at] = row
 
 
-def last_matmul(first, kidx, x_own, x_oth, w, pieces, acc, low_own, low_oth, fout_own, fout_oth, readout, before):
-    members = x_own.shape[1]
-    width, block = w.shape
+def last_matmul(kidx, sent, x, acc, low_own, low_oth, fout_own, fout_oth, readout):
+    members = x.shape[2]
+    part, block = sent[0].shape
+    width = part * CHAINS
     smem = pl.BlockSpec(memory_space=pltpu.SMEM)
     vmem = pl.BlockSpec(memory_space=pltpu.VMEM)
-    hbm = pl.BlockSpec(memory_space=pltpu.HBM)
-    args = [acc, low_own, low_oth, fout_own, fout_oth, readout]
-    if before is not None:
-        args.append(before)
-    return pl.pallas_call(
-        functools.partial(last_kernel, first),
+    hbm = pl.BlockSpec(memory_space=pl.ANY)
+    return pl.pallas_call(
+        last_kernel,
         out_shape=jax.ShapeDtypeStruct((CORE * WA, 1, 2 * members), jnp.float32),
-        in_specs=[smem, hbm, hbm, hbm, hbm] + [vmem] * len(args),
+        in_specs=[smem] + [hbm] * CHAINS + [vmem] * 7,
         out_specs=vmem,
         scratch_shapes=[
-            pltpu.VMEM((1, width, block), jnp.bfloat16),
-            pltpu.SemaphoreType.DMA((1,)),
-            pltpu.VMEM((1, 2, 3, members, block), jnp.bfloat16),
-            pltpu.SemaphoreType.DMA((1, 2)),
+            pltpu.VMEM((width, block), jnp.bfloat16),
+            pltpu.SemaphoreType.DMA((CHAINS,)),
         ],
-        compiler_params=pltpu.CompilerParams(vmem_limit_bytes=VMEM_BYTES),
+        compiler_params=pltpu.CompilerParams(vmem_limit_bytes=LAST_BYTES),
         cost_estimate=pl.CostEstimate(
             flops=2 * 6 * members * width * block,
             bytes_accessed=6 * 1024 * 1024,
             transcendentals=6 * members * width,
         ),
-    )(kidx, x_own, x_oth, w, pieces, *args)
+    )(kidx, *sent, x, acc, low_own, low_oth, fout_own, fout_oth, readout)
 
 
 def after_kernel(*refs):
@@ -274,7 +289,7 @@
         in_specs=[pl.BlockSpec(memory_space=pltpu.SMEM), hbm, hbm],
         out_specs=(hbm,) * len(shapes),
         scratch_shapes=[pltpu.SemaphoreType.DMA((len(shapes),))],
-        compiler_params=pltpu.CompilerParams(vmem_limit_bytes=VMEM_BYTES),
+        compiler_params=pltpu.CompilerParams(vmem_limit_bytes=LARGE_BYTES),
     )(place, weight, fin)
 
 
@@ -346,14 +361,23 @@
             pltpu.SemaphoreType.DMA((tiles, 2)),
             pltpu.SemaphoreType.DMA((2 + XH * Z,)),
         ],
-        compiler_params=pltpu.CompilerParams(vmem_limit_bytes=VMEM_BYTES),
+        compiler_params=pltpu.CompilerParams(vmem_limit_bytes=LARGE_BYTES),
         cost_estimate=pl.CostEstimate(
             flops=2 * rows * members * width, bytes_accessed=9 * 1024 * 1024, transcendentals=0
         ),
     )(place, x, fin, fout, readout)
 
 
-def step_kernel(place, fit, fout, fin, keep, give, util, rows_ref):
+def step_kernel(place, fit, fout_all, fin_all, keep, give, util, rows_ref, fout, fin, sems):
+    copies = []
+    for k in range(Z):
+        pair = (
+            pltpu.make_async_copy(fout_all.at[k], fout.at[k], sems.at[k, 0]),
+            pltpu.make_async_copy(fin_all.at[k], fin.at[k], sems.at[k, 1]),
+        )
+        for copy in pair:
+            copy.start()
+        copies.append(pair)
     values = fit[...]
     members = fin.shape[1]
     count = values.shape[0] * values.shape[2]
@@ -368,6 +392,8 @@
     columns = (jnp.transpose(rows_ref[...]) - mean) / root
     total = None
     for k in range(Z):
+        for copy in copies[k]:
+            copy.wait()
         scaled = (fout[k].astype(jnp.float32) * columns[:, k : k + 1]).astype(jnp.bfloat16)
         one = lax.dot_general(
             scaled, fin[k], (((0,), (0,)), ((), ())), preferred_element_type=jnp.float32
@@ -386,14 +412,20 @@
     members, rows = fout.shape[1], fout.shape[2]
     cols = fin.shape[2]
     vmem = pl.BlockSpec(memory_space=pltpu.VMEM)
+    hbm = pl.BlockSpec(memory_space=pl.ANY)
     block = jax.ShapeDtypeStruct((XH, rows // (XH * CORE), cols), jnp.float32)
     return pl.pallas_call(
         step_kernel,
         out_shape=(block, block, jax.ShapeDtypeStruct((1, members), jnp.float32)),
-        in_specs=[pl.BlockSpec(memory_space=pltpu.SMEM), vmem, vmem, vmem],
+        in_specs=[pl.BlockSpec(memory_space=pltpu.SMEM), vmem, hbm, hbm],
         out_specs=(vmem, vmem, vmem),
-        scratch_shapes=[pltpu.VMEM((Z, members), jnp.float32)],
-        compiler_params=pltpu.CompilerParams(vmem_limit_bytes=VMEM_BYTES),
+        scratch_shapes=[
+            pltpu.VMEM((Z, members), jnp.float32),
+            pltpu.VMEM(fout.shape, fout.dtype),
+            pltpu.VMEM(fin.shape, fin.dtype),
+            pltpu.SemaphoreType.DMA((Z, 2)),
+        ],
+        compiler_params=pltpu.CompilerParams(vmem_limit_bytes=LARGE_BYTES),
         cost_estimate=pl.CostEstimate(
             flops=2 * rows * Z * members * cols, bytes_accessed=4 * 1024 * 1024, transcendentals=0
         ),
@@ -451,34 +483,25 @@
     low_oth = send(low_own, core_go)
     fout_got = send(fout_theirs, core_go)
 
-    w_b, w_e, w_c, w_f, acc, token = ([None] * CHAINS for _ in range(6))
+    w_b, w_e, w_c, w_f, w_g = ([None] * CHAINS for _ in range(5))
     for h in chains:
         own[h], w_a[h], w_d[h] = after((own[h], w_a[h], w_d[h]), low_own)
         w_b[h] = send(own[h], y_bwd)
         w_e[h] = send(w_a[h], x_go)
-        acc[h], token[h] = group_matmul(
-            0, places, x_own, x_oth, [own[h], w_a[h], w_d[h]], None
-        )
+    acc, token = group_matmul(0, places, x_own, x_oth, [own, w_a, w_d], None)
     for h in chains:
-        w_a[h], w_b[h], w_e[h] = after((w_a[h], w_b[h], w_e[h]), token[h])
+        w_a[h], w_b[h], w_e[h] = after((w_a[h], w_b[h], w_e[h]), token)
         w_c[h] = send(w_a[h], y_fwd)
         w_f[h] = send(w_b[h], x_go)
-        acc[h], token[h] = group_matmul(
-            3, places, x_own, x_oth, [w_b[h], w_e[h]], acc[h], (low_oth, fout_got)
-        )
-    w_g = [None] * CHAINS
+    acc, token = group_matmul(3, places, x_own, x_oth, [w_b, w_e], acc)
     for h in chains:
-        w_c[h], w_f[h], w_e[h] = after((w_c[h], w_f[h], w_e[h]), token[h])
+        w_c[h], w_f[h], w_e[h] = after((w_c[h], w_f[h], w_e[h]), token)
         w_g[h] = send(w_c[h], x_go) if h == 0 else send(w_e[h], y_fwd)
-        acc[h], token[h] = group_matmul(
-            5, places, x_own, x_oth, [w_f[h], w_c[h]], acc[h]
-        )
-    partial = None
-    for h in chains:
-        partial = last_matmul(
-            h * part, places, x_own, x_oth, w_g[h], pieces if h == 1 else w_g[h], acc[h],
-            low_own, low_oth, fout_mine, fout_got, read_mine, partial,
-        )
+    acc, token, x_last = group_matmul(5, places, x_own, x_oth, [w_f, w_c], acc, ahead=True)
+    partial = last_matmul(
+        places, w_g, x_last, acc, low_own, low_oth, fout_mine, fout_got, read_mine
+    )
+    (partial,) = after((partial,), pieces)
 
     fit = share(sum_and_copy(share(partial, ("core", "xl", "y"))), ("xh", "z"))
 

time: 144 us -> 227 us (1.58)
  Pallas kernels: 46.6 us -> 137 us
  local copies, waits for them, and re-layouts: 13.4 us -> 3.31 us
  waiting for transfers between devices: 18.2 us -> 21.8 us
    pallas_call x1, Pallas kernels: 4.27 us -> 66.4 us  [low_term(): pl.pallas_call(low_kernel, out_shape=(jax.ShapeDtypeStruct((rows, members...]
    pallas_call x1, Pallas kernels: 1.35 us -> 41.5 us  [take_blocks(): pl.pallas_call(take_kernel, out_shape=tuple(shapes), in_specs=[pl.BlockSp...]
    unnamed x36 -> x22, local copies, waits for them, and re-layouts: 13.3 us -> 2.62 us
    pallas_call x6 -> x3, Pallas kernels: 29.7 us -> 20.6 us  [group_matmul(): pl.pallas_call(functools.partial(group_kernel, base, count, acc is not No...]
    pallas_call x2 -> x1, Pallas kernels: 7.66 us -> 3.45 us  [last_matmul(): pl.pallas_call(last_kernel, out_shape=jax.ShapeDtypeStruct((CORE * WA, 1,...]
    ppermute x19, waiting for transfers between devices: 9.36 us -> 12.9 us  [send(): return lax.ppermute(v, AXES, pairs)]
  transfers between devices with their start and end apart: 22 -> 22, of which waited for: 5 -> 7; matrix products, arithmetic and copies ran while one was open for 0% -> 0% of each run, Pallas kernels for 31% -> 58%
where the time goes in v5:
time: 227 us
  Pallas kernels  137 us (60%)
  starting transfers between devices  40.1 us (18%)
  waiting for transfers between devices  21.8 us (10%)
  between operations  14.3 us (6%)
  blocking collectives  8.49 us (4%)
  local copies, waits for them, and re-layouts  3.31 us (1%)
    pallas_call x1, Pallas kernels, low_term(): pl.pallas_call(low_kernel, out_shape=(jax.ShapeDtypeStruct((rows, members...  66.4 us
    pallas_call x1, Pallas kernels, take_blocks(): pl.pallas_call(take_kernel, out_shape=tuple(shapes), in_specs=[pl.BlockSp...  41.5 us
    ppermute x19, starting transfers between devices, send(): return lax.ppermute(v, AXES, pairs)  22.8 us
    pallas_call x3, Pallas kernels, group_matmul(): pl.pallas_call(functools.partial(group_kernel, base, count, acc is not No...  20.6 us
    ppermute x19, waiting for transfers between devices, send(): return lax.ppermute(v, AXES, pairs)  12.9 us
    all_to_all x1, starting transfers between devices, share(): return lax.all_to_all(x, axes, 0, 0, tiled=True)  8.98 us
    all_to_all x1, waiting for transfers between devices, share(): return lax.all_to_all(x, axes, 0, 0, tiled=True)  8.83 us
    all_to_all x1, blocking collectives, share(): return lax.all_to_all(x, axes, 0, 0, tiled=True)  8.49 us
  transfers between devices with their start and end apart: 22, of which 7 were waited for; matrix products, arithmetic and copies ran while one was open for 0% of the time, Pallas kernels for 58%

profile of v5, /device:TPU:1, one launch (start us, length us, event | category | flops | bytes accessed | tf_op | source)
XLA Modules:
  0.0 226.8 jit_solution(10406969982669560838)
XLA Ops:
  7.2 3.3 %collective-permute-start.4 = (bf16[3,256,4096]{2,1,0:T(8,128)(2,1)}, bf16[3,256,4096]{2,1,0:T(8,128)(2,1)}, u32[]{:S(2)}, u32[]{:S(2)}) collective-permute-start(bf16[3,256,4096]{2,1,0:T(8,128)(2,1)} %bitcast.21), channel_id=1, source_target_pairs={{0,8},{1,9},{2,10},{3,11},{4,12},{5,13},{6,14},{7,15},{8,0},{9,1},... | collective-permute-start | bytes 18874376 | tf_op jit(solution)/shard_map/ppermute | solution.py:449
  11.2 41.5 %shard_map.68 = (bf16[512,512]{1,0:T(8,128)(2,1)}, bf16[512,512]{1,0:T(8,128)(2,1)}, bf16[256,512]{1,0:T(8,128)(2,1)}) custom-call(s32[11]{0:T(128)} %stack.47.place.kidx, bf16[2048,512]{1,0:T(8,128)(2,1)} %weight.1, bf16[256,4096]{1,0:T(8,128)(2,1)} %fin.3), custom_call_target="tpu_custom_call" | custom-call | tf_op jit(solution)/shard_map/pallas_call | solution.py:286
  52.8 1.1 collective-permute-start.5
  53.8 2.5 %collective-permute-start.6 = (bf16[512,512]{1,0:T(8,128)(2,1)}, bf16[512,512]{1,0:T(8,128)(2,1)}, u32[]{:S(2)}, u32[]{:S(2)}) collective-permute-start(bf16[512,512]{1,0:T(8,128)(2,1)} %get-tuple-element.40.refs_0_), channel_id=1, source_target_pairs={{0,4},{1,5},{2,6},{3,7},{4,0},{5,1},{6,2},{7,3},{8,140},{9,141},{1... | collective-permute-start | bytes 1572872 | tf_op jit(solution)/shard_map/ppermute | solution.py:449
  57.0 66.4 %shard_map.69 = (f32[3,256,1]{2,1,0:T(8,128)}, bf16[8,256,256]{2,1,0:T(8,128)(2,1)}, bf16[256,1024]{1,0:T(8,128)(2,1)}, bf16[256,1024]{1,0:T(8,128)(2,1)}, f32[1,1024]{1,0:T(1,128)}) custom-call(s32[11]{0:T(128)} %stack.47.place.kidx, bf16[3,256,4096]{2,1,0:T(8,128)(2,1)} %bitcast.22, bf16[256,4096]{1,0:T(8,128)(2,1)} %fin.3, bf16[256,2048]{1,0:T(8,128)(2,1)} %fout.1, ...), custom_call_target="tpu_custom_call" | custom-call | flops 6291456 | bytes 9437184 | tf_op jit(solution)/shard_map/pallas_call | solution.py:347
  123.4 8.2 %all-to-all-start = ((bf16[8,256,256]{2,1,0:T(8,128)(2,1)}), bf16[8,256,256]{2,1,0:T(8,128)(2,1)S(1)}, u32[]{:S(2)}, u32[]{:S(2)}) async-start(bf16[8,256,256]{2,1,0:T(8,128)(2,1)} %get-tuple-element.65), calls=%async_computation | async-start | bytes 2097152 | tf_op jit(solution)/shard_map/all_to_all | solution.py:482
  132.6 2.5 %collective-permute-start.10 = (bf16[512,512]{1,0:T(8,128)(2,1)S(1)}, bf16[512,512]{1,0:T(8,128)(2,1)S(1)}, u32[]{:S(2)}, u32[]{:S(2)}) collective-permute-start(bf16[512,512]{1,0:T(8,128)(2,1)S(1)} %get-tuple-element.42.refs_3_.refs_0_), channel_id=1, source_target_pairs={{0,4},{1,5},{2,6},{3,7},{4,0},{5,1},{6,2},{7,3},{8,140},{9,141},{1... | collective-permute-start | bytes 1572872 | tf_op jit(solution)/shard_map/ppermute | solution.py:449
  135.1 1.0 collective-permute-start.9
  137.4 8.4 %shard_map.72 = (f32[2,3,256,1024]{3,2,1,0:T(8,128)S(1)}, f32[8,128]{1,0:T(8,128)S(1)}) custom-call(s32[11]{0:T(128)S(1)} %copy-done.7, bf16[3,256,4096]{2,1,0:T(8,128)(2,1)} %bitcast.23, bf16[3,256,4096]{2,1,0:T(8,128)(2,1)} %collective-permute-done.4.x_oth, bf16[512,512]{1,0:T(8,128)(2,1)S(1)} %get-tuple-element.39.refs_0_, ...), custom_call_target="tpu_custom_call" | custom-call | flops 4831838208 | bytes 8388608 | tf_op jit(solution)/shard_map/pallas_call | solution.py:150
  145.8 2.7 %collective-permute-start.12 = (bf16[512,512]{1,0:T(8,128)(2,1)S(1)}, bf16[512,512]{1,0:T(8,128)(2,1)S(1)}, u32[]{:S(2)}, u32[]{:S(2)}) collective-permute-start(bf16[512,512]{1,0:T(8,128)(2,1)S(1)} %get-tuple-element.54), channel_id=1, source_target_pairs={{0,1},{1,2},{2,3},{3,0},{4,5},{5,6},{6,7},{7,4},{8,11},{9,8},{10,9... | collective-permute-start | bytes 1572872 | tf_op jit(solution)/shard_map/ppermute | solution.py:449
  148.6 2.5 %collective-permute-start.13 = (bf16[512,512]{1,0:T(8,128)(2,1)S(1)}, bf16[512,512]{1,0:T(8,128)(2,1)S(1)}, u32[]{:S(2)}, u32[]{:S(2)}) collective-permute-start(bf16[512,512]{1,0:T(8,128)(2,1)S(1)} %get-tuple-element.49.refs_1_), channel_id=1, source_target_pairs={{0,4},{1,5},{2,6},{3,7},{4,0},{5,1},{6,2},{7,3},{8,140},{9,141},{1... | collective-permute-start | bytes 1572872 | tf_op jit(solution)/shard_map/ppermute | solution.py:449
  151.7 5.8 %shard_map.75 = (f32[2,3,256,1024]{3,2,1,0:T(8,128)S(1)}, f32[8,128]{1,0:T(8,128)S(1)}) custom-call(s32[11]{0:T(128)S(1)} %copy-done.7, bf16[3,256,4096]{2,1,0:T(8,128)(2,1)} %bitcast.24, bf16[3,256,4096]{2,1,0:T(8,128)(2,1)} %collective-permute-done.4.x_oth, bf16[512,512]{1,0:T(8,128)(2,1)S(1)} %get-tuple-element.47.refs_0_, ...), custom_call_target="tpu_custom_call", output_to_operand_aliasing={{0}: (7, {})} | custom-call | flops 3221225472 | bytes 8388608 | tf_op jit(solution)/shard_map/pallas_call | solution.py:150
  158.9 1.4 collective-permute-done.7.refs_0_
  160.3 3.4 %collective-permute-done.8.refs_1_ = bf16[512,512]{1,0:T(8,128)(2,1)S(1)} collective-permute-done((bf16[512,512]{1,0:T(8,128)(2,1)S(1)}, bf16[512,512]{1,0:T(8,128)(2,1)S(1)}, u32[]{:S(2)}, u32[]{:S(2)}) %collective-permute-start.8) | collective-permute-done | bytes 524320 | tf_op jit(solution)/shard_map/ppermute | solution.py:449
  163.7 2.5 %collective-permute-start.11 = (bf16[512,512]{1,0:T(8,128)(2,1)S(1)}, bf16[512,512]{1,0:T(8,128)(2,1)S(1)}, u32[]{:S(2)}, u32[]{:S(2)}) collective-permute-start(bf16[512,512]{1,0:T(8,128)(2,1)S(1)} %get-tuple-element.53.refs_2_), channel_id=1, source_target_pairs={{0,4},{1,5},{2,6},{3,7},{4,0},{5,1},{6,2},{7,3},{8,140},{9,141},{1... | collective-permute-start | bytes 1572872 | tf_op jit(solution)/shard_map/ppermute | solution.py:449
  166.3 6.4 %shard_map.78 = (f32[2,3,256,1024]{3,2,1,0:T(8,128)S(1)}, f32[8,128]{1,0:T(8,128)}, bf16[2,3,256,512]{3,2,1,0:T(8,128)(2,1)S(1)}) custom-call(s32[11]{0:T(128)S(1)} %copy-done.7, bf16[3,256,4096]{2,1,0:T(8,128)(2,1)} %bitcast.25, bf16[3,256,4096]{2,1,0:T(8,128)(2,1)} %collective-permute-done.4.x_oth, ...), custom_call_target="tpu_custom_call", output_to_operand_aliasing={{0}: (7, {})} | custom-call | flops 3221225472 | bytes 8388608 | tf_op jit(solution)/shard_map/pallas_call | solution.py:150
  173.0 3.5 %shard_map.79.refs_0_ = f32[16,1,512]{2,1,0:T(1,128)S(1)} custom-call(s32[11]{0:T(128)S(1)} %copy-done.7, bf16[512,512]{1,0:T(8,128)(2,1)S(1)} %collective-permute-done.11.refs_0_, bf16[512,512]{1,0:T(8,128)(2,1)S(1)} %collective-permute-done.14.refs_1_, bf16[2,3,256,512]{3,2,1,0:T(8,128)(2,1)S(1)} %get-tuple-element.60.refs_2_, ...), custom_call_target="tpu_custom_call" | custom-call | flops 1610612736 | bytes 6291456 | tf_op jit(solution)/shard_map/pallas_call | solution.py:216
  176.5 8.5 %all_to_all.15.got = f32[16,1,512]{2,1,0:T(1,128)S(1)} all-to-all(f32[16,1,512]{2,1,0:T(1,128)S(1)} %shard_map.80), channel_id=1, replica_groups=mesh['xh'=2,'z'=8,'core'=2,'xl'=2,'y'=4] {'core','xl','y'}, dimensions={0} | all-to-all | bytes 65536 | tf_op jit(solution)/shard_map/all_to_all | solution.py:436
  185.6 9.0 %all-to-all-start.2 = ((f32[16,1,512]{2,1,0:T(1,128)}), f32[16,1,512]{2,1,0:T(1,128)S(1)}, u32[]{:S(2)}, u32[]{:S(2)}) async-start(f32[16,1,512]{2,1,0:T(1,128)} %shard_map.81), calls=%async_computation.2 | async-start | bytes 65536 | tf_op jit(solution)/shard_map/all_to_all | solution.py:436
  194.6 8.8 %all-to-all-done.2.fit = f32[16,1,512]{2,1,0:T(1,128)S(1)} async-done(((f32[16,1,512]{2,1,0:T(1,128)}), f32[16,1,512]{2,1,0:T(1,128)S(1)}, u32[]{:S(2)}, u32[]{:S(2)}) %all-to-all-start.2) | async-done | bytes 32800 | tf_op jit(solution)/shard_map/all_to_all | solution.py:436
  204.1 4.6 %shard_map.82 = (f32[2,64,512]{2,1,0:T(8,128)}, f32[2,64,512]{2,1,0:T(8,128)}, f32[1,256]{1,0:T(1,128)}) custom-call(s32[11]{0:T(128)} %stack.47.place.kidx, f32[16,1,512]{2,1,0:T(1,128)} %copy-done.9, bf16[8,256,256]{2,1,0:T(8,128)(2,1)} %copy-done, bf16[8,256,512]{2,1,0:T(8,128)(2,1)} %bitcast.26), custom_call_target="tpu_custom_call" | custom-call | flops 536870912 | bytes 4194304 | tf_op jit(solution)/shard_map/pallas_call | solution.py:417
  208.7 1.9 collective-permute-start.17
  210.6 1.4 collective-permute-done.17
  213.4 5.9 %collective-permute-done.18 = f32[64,512]{1,0:T(8,128)S(1)} collective-permute-done((f32[64,512]{1,0:T(8,128)S(1)}, f32[64,512]{1,0:T(8,128)S(1)}, u32[]{:S(2)}, u32[]{:S(2)}) %collective-permute-start.18) | collective-permute-done | bytes 131104 | tf_op jit(solution)/shard_map/ppermute | solution.py:449
  (63 shorter events, 9.4 us)
Async XLA Ops:
  7.2 187.4 %all-gather.3.cloned.1.call-start = ((), (), s32[]{:S(2)}) async-start(), calls=%async_computation.3 | async-start | bytes 2359296 | tf_op jit(solution)/shard_map/all_gather | solution.py:481
  7.2 130.1 %collective-permute-start.4 = (bf16[3,256,4096]{2,1,0:T(8,128)(2,1)}, bf16[3,256,4096]{2,1,0:T(8,128)(2,1)}, u32[]{:S(2)}, u32[]{:S(2)}) collective-permute-start(bf16[3,256,4096]{2,1,0:T(8,128)(2,1)} %bitcast.21), channel_id=1, source_target_pairs={{0,8},{1,9},{2,10},{3,11},{4,12},{5,13},{6,14},{7,15},{8,0},{9,1},... | collective-permute-start | bytes 18874376 | tf_op jit(solution)/shard_map/ppermute | solution.py:449
  52.8 78.9 %collective-permute-start.5 = (bf16[512,512]{1,0:T(8,128)(2,1)}, bf16[512,512]{1,0:T(8,128)(2,1)S(1)}, u32[]{:S(2)}, u32[]{:S(2)}) collective-permute-start(bf16[512,512]{1,0:T(8,128)(2,1)} %get-tuple-element.40.refs_0_), channel_id=1, source_target_pairs={{0,1},{1,2},{2,3},{3,0},{4,5},{5,6},{6,7},{7,4},{8,11},{9,8},{10,9... | collective-permute-start | bytes 1572872 | tf_op jit(solution)/shard_map/ppermute | solution.py:449
  53.8 77.8 %collective-permute-start.6 = (bf16[512,512]{1,0:T(8,128)(2,1)}, bf16[512,512]{1,0:T(8,128)(2,1)}, u32[]{:S(2)}, u32[]{:S(2)}) collective-permute-start(bf16[512,512]{1,0:T(8,128)(2,1)} %get-tuple-element.40.refs_0_), channel_id=1, source_target_pairs={{0,4},{1,5},{2,6},{3,7},{4,0},{5,1},{6,2},{7,3},{8,140},{9,141},{1... | collective-permute-start | bytes 1572872 | tf_op jit(solution)/shard_map/ppermute | solution.py:449
  56.3 79.8 %collective-permute-start = (bf16[512,512]{1,0:T(8,128)(2,1)}, bf16[512,512]{1,0:T(8,128)(2,1)S(1)}, u32[]{:S(2)}, u32[]{:S(2)}) collective-permute-start(bf16[512,512]{1,0:T(8,128)(2,1)} %get-tuple-element.36.refs_0_), channel_id=1, source_target_pairs={{0,1},{1,2},{2,3},{3,0},{4,5},{5,6},{6,7},{7,4},{8,11},{9,8},{10,9... | collective-permute-start | bytes 1572872 | tf_op jit(solution)/shard_map/ppermute | solution.py:449
  56.8 79.4 %collective-permute-start.1 = (bf16[512,512]{1,0:T(8,128)(2,1)}, bf16[512,512]{1,0:T(8,128)(2,1)}, u32[]{:S(2)}, u32[]{:S(2)}) collective-permute-start(bf16[512,512]{1,0:T(8,128)(2,1)} %get-tuple-element.36.refs_0_), channel_id=1, source_target_pairs={{0,4},{1,5},{2,6},{3,7},{4,0},{5,1},{6,2},{7,3},{8,140},{9,141},{1... | collective-permute-start | bytes 1572872 | tf_op jit(solution)/shard_map/ppermute | solution.py:449
  57.0 79.2 %copy-start.5 = (bf16[512,512]{1,0:T(8,128)(2,1)S(1)}, bf16[512,512]{1,0:T(8,128)(2,1)}, u32[]{:S(2)}) copy-start(bf16[512,512]{1,0:T(8,128)(2,1)} %get-tuple-element.36.refs_0_) | copy-start | bytes 1572868
  57.0 80.4 %copy-start.7 = (s32[11]{0:T(128)S(1)}, s32[11]{0:T(128)}, u32[]{:S(2)}) copy-start(s32[11]{0:T(128)} %stack.47.place.kidx) | copy-start | bytes 136
  123.4 53.0 %all-to-all-start = ((bf16[8,256,256]{2,1,0:T(8,128)(2,1)}), bf16[8,256,256]{2,1,0:T(8,128)(2,1)S(1)}, u32[]{:S(2)}, u32[]{:S(2)}) async-start(bf16[8,256,256]{2,1,0:T(8,128)(2,1)} %get-tuple-element.65), calls=%async_computation | async-start | bytes 2097152 | tf_op jit(solution)/shard_map/all_to_all | solution.py:482
  132.6 13.1 %collective-permute-start.10 = (bf16[512,512]{1,0:T(8,128)(2,1)S(1)}, bf16[512,512]{1,0:T(8,128)(2,1)S(1)}, u32[]{:S(2)}, u32[]{:S(2)}) collective-permute-start(bf16[512,512]{1,0:T(8,128)(2,1)S(1)} %get-tuple-element.42.refs_3_.refs_0_), channel_id=1, source_target_pairs={{0,4},{1,5},{2,6},{3,7},{4,0},{5,1},{6,2},{7,3},{8,140},{9,141},{1... | collective-permute-start | bytes 1572872 | tf_op jit(solution)/shard_map/ppermute | solution.py:449
  135.1 10.7 %collective-permute-start.9 = (bf16[512,512]{1,0:T(8,128)(2,1)S(1)}, bf16[512,512]{1,0:T(8,128)(2,1)S(1)}, u32[]{:S(2)}, u32[]{:S(2)}) collective-permute-start(bf16[512,512]{1,0:T(8,128)(2,1)S(1)} %get-tuple-element.41.refs_1_), channel_id=1, source_target_pairs={{0,3},{1,0},{2,1},{3,2},{4,7},{5,4},{6,5},{7,6},{8,9},{9,10},{10,1... | collective-permute-start | bytes 1572872 | tf_op jit(solution)/shard_map/ppermute | solution.py:449
  137.1 13.9 %collective-permute-start.2 = (bf16[512,512]{1,0:T(8,128)(2,1)S(1)}, bf16[512,512]{1,0:T(8,128)(2,1)S(1)}, u32[]{:S(2)}, u32[]{:S(2)}) collective-permute-start(bf16[512,512]{1,0:T(8,128)(2,1)S(1)} %get-tuple-element.39.refs_0_), channel_id=1, source_target_pairs={{0,3},{1,0},{2,1},{3,2},{4,7},{5,4},{6,5},{7,6},{8,9},{9,10},{10,1... | collective-permute-start | bytes 1572872 | tf_op jit(solution)/shard_map/ppermute | solution.py:449
  137.2 13.9 %collective-permute-start.3 = (bf16[512,512]{1,0:T(8,128)(2,1)S(1)}, bf16[512,512]{1,0:T(8,128)(2,1)S(1)}, u32[]{:S(2)}, u32[]{:S(2)}) collective-permute-start(bf16[512,512]{1,0:T(8,128)(2,1)S(1)} %get-tuple-element.38.refs_2_.refs_0_), channel_id=1, source_target_pairs={{0,4},{1,5},{2,6},{3,7},{4,0},{5,1},{6,2},{7,3},{8,140},{9,141},{1... | collective-permute-start | bytes 1572872 | tf_op jit(solution)/shard_map/ppermute | solution.py:449
  145.8 11.7 %collective-permute-start.12 = (bf16[512,512]{1,0:T(8,128)(2,1)S(1)}, bf16[512,512]{1,0:T(8,128)(2,1)S(1)}, u32[]{:S(2)}, u32[]{:S(2)}) collective-permute-start(bf16[512,512]{1,0:T(8,128)(2,1)S(1)} %get-tuple-element.54), channel_id=1, source_target_pairs={{0,1},{1,2},{2,3},{3,0},{4,5},{5,6},{6,7},{7,4},{8,11},{9,8},{10,9... | collective-permute-start | bytes 1572872 | tf_op jit(solution)/shard_map/ppermute | solution.py:449
  148.6 9.5 %collective-permute-start.13 = (bf16[512,512]{1,0:T(8,128)(2,1)S(1)}, bf16[512,512]{1,0:T(8,128)(2,1)S(1)}, u32[]{:S(2)}, u32[]{:S(2)}) collective-permute-start(bf16[512,512]{1,0:T(8,128)(2,1)S(1)} %get-tuple-element.49.refs_1_), channel_id=1, source_target_pairs={{0,4},{1,5},{2,6},{3,7},{4,0},{5,1},{6,2},{7,3},{8,140},{9,141},{1... | collective-permute-start | bytes 1572872 | tf_op jit(solution)/shard_map/ppermute | solution.py:449
  151.1 9.2 %collective-permute-start.7 = (bf16[512,512]{1,0:T(8,128)(2,1)S(1)}, bf16[512,512]{1,0:T(8,128)(2,1)S(1)}, u32[]{:S(2)}, u32[]{:S(2)}) collective-permute-start(bf16[512,512]{1,0:T(8,128)(2,1)S(1)} %get-tuple-element.46), channel_id=1, source_target_pairs={{0,1},{1,2},{2,3},{3,0},{4,5},{5,6},{6,7},{7,4},{8,11},{9,8},{10,9... | collective-permute-start | bytes 1572872 | tf_op jit(solution)/shard_map/ppermute | solution.py:449
  151.5 12.2 %collective-permute-start.8 = (bf16[512,512]{1,0:T(8,128)(2,1)S(1)}, bf16[512,512]{1,0:T(8,128)(2,1)S(1)}, u32[]{:S(2)}, u32[]{:S(2)}) collective-permute-start(bf16[512,512]{1,0:T(8,128)(2,1)S(1)} %get-tuple-element.47.refs_0_), channel_id=1, source_target_pairs={{0,4},{1,5},{2,6},{3,7},{4,0},{5,1},{6,2},{7,3},{8,140},{9,141},{1... | collective-permute-start | bytes 1572872 | tf_op jit(solution)/shard_map/ppermute | solution.py:449
  151.7 20.9 %collective-permute-start.16 = (bf16[256,1024]{1,0:T(8,128)(2,1)S(1)}, bf16[256,1024]{1,0:T(8,128)(2,1)S(1)}, u32[]{:S(2)}, u32[]{:S(2)}) collective-permute-start(bf16[256,1024]{1,0:T(8,128)(2,1)S(1)} %copy-done.10), channel_id=1, source_target_pairs={{0,8},{1,9},{2,10},{3,11},{4,12},{5,13},{6,14},{7,15},{8,0},{9,1},... | collective-permute-start | bytes 1572872 | tf_op jit(solution)/shard_map/ppermute | solution.py:449
  158.1 14.6 %collective-permute-start.14 = (bf16[512,512]{1,0:T(8,128)(2,1)S(1)}, bf16[512,512]{1,0:T(8,128)(2,1)S(1)}, u32[]{:S(2)}, u32[]{:S(2)}) collective-permute-start(bf16[512,512]{1,0:T(8,128)(2,1)S(1)} %get-tuple-element.55), channel_id=1, source_target_pairs={{0,1},{1,2},{2,3},{3,0},{4,5},{5,6},{6,7},{7,4},{8,11},{9,8},{10,9... | collective-permute-start | bytes 1572872 | tf_op jit(solution)/shard_map/ppermute | solution.py:449
  163.7 9.2 %collective-permute-start.11 = (bf16[512,512]{1,0:T(8,128)(2,1)S(1)}, bf16[512,512]{1,0:T(8,128)(2,1)S(1)}, u32[]{:S(2)}, u32[]{:S(2)}) collective-permute-start(bf16[512,512]{1,0:T(8,128)(2,1)S(1)} %get-tuple-element.53.refs_2_), channel_id=1, source_target_pairs={{0,4},{1,5},{2,6},{3,7},{4,0},{5,1},{6,2},{7,3},{8,140},{9,141},{1... | collective-permute-start | bytes 1572872 | tf_op jit(solution)/shard_map/ppermute | solution.py:449
  166.2 6.4 %collective-permute-start.15 = (f32[3,256,1]{2,1,0:T(8,128)S(1)}, f32[3,256,1]{2,1,0:T(8,128)S(1)}, u32[]{:S(2)}, u32[]{:S(2)}) collective-permute-start(f32[3,256,1]{2,1,0:T(8,128)S(1)} %copy-done.3), channel_id=1, source_target_pairs={{0,8},{1,9},{2,10},{3,11},{4,12},{5,13},{6,14},{7,15},{8,0},{9,1},... | collective-permute-start | bytes 9224 | tf_op jit(solution)/shard_map/ppermute | solution.py:449
  185.6 17.8 %all-to-all-start.2 = ((f32[16,1,512]{2,1,0:T(1,128)}), f32[16,1,512]{2,1,0:T(1,128)S(1)}, u32[]{:S(2)}, u32[]{:S(2)}) async-start(f32[16,1,512]{2,1,0:T(1,128)} %shard_map.81), calls=%async_computation.2 | async-start | bytes 65536 | tf_op jit(solution)/shard_map/all_to_all | solution.py:436
  208.7 3.3 %collective-permute-start.17 = (f32[2,64,512]{2,1,0:T(8,128)}, f32[2,64,512]{2,1,0:T(8,128)S(1)}, u32[]{:S(2)}, u32[]{:S(2)}) collective-permute-start(f32[2,64,512]{2,1,0:T(8,128)} %get-tuple-element.68), channel_id=1, source_target_pairs={{0,8},{1,9},{2,10},{3,11},{4,12},{5,13},{6,14},{7,15},{8,0},{9,1},... | collective-permute-start | bytes 786440 | tf_op jit(solution)/shard_map/ppermute | solution.py:449
  213.0 6.3 %collective-permute-start.18 = (f32[64,512]{1,0:T(8,128)S(1)}, f32[64,512]{1,0:T(8,128)S(1)}, u32[]{:S(2)}, u32[]{:S(2)}) collective-permute-start(f32[64,512]{1,0:T(8,128)S(1)} %slice_bitcast_fusion), channel_id=1, source_target_pairs={{0,128},{1,129},{2,130},{3,131},{4,132},{5,133},{6,134},{7,135},{8... | collective-permute-start | bytes 393224 | tf_op jit(solution)/shard_map/ppermute | solution.py:449
  (9 other events, 150.8 us)
Sparse Core Ops, SparseCore 0:
  52.9 77.7 all-gather.2

commit v6 on v5

--- a/solution.py
+++ b/solution.py
@@ -287,13 +287,15 @@
         take_kernel,
         out_shape=tuple(shapes),
         in_specs=[pl.BlockSpec(memory_space=pltpu.SMEM), hbm, hbm],
-        out_specs=(hbm,) * len(shapes),
+        out_specs=(pl.BlockSpec(memory_space=pltpu.VMEM),) * len(shapes),
         scratch_shapes=[pltpu.SemaphoreType.DMA((len(shapes),))],
         compiler_params=pltpu.CompilerParams(vmem_limit_bytes=LARGE_BYTES),
     )(place, weight, fin)
 
 
-def low_kernel(place, x, fin, fout, readout, out, pieces, mine, theirs, read, x_buf, f_buf, sems, out_sems):
+def low_kernel(place, x, fin, fout_all, readout, out, pieces, mine, theirs, read, x_buf, f_buf, fout, sems, out_sems):
+    whole = pltpu.make_async_copy(fout_all, fout, out_sems.at[0])
+    whole.start()
     tiles, rows, tile, width = x_buf.shape
     copies = []
     for t in range(tiles):
@@ -315,7 +317,8 @@
         for k in range(Z):
             cols = pl.ds(h * half + k * run, run)
             moves.append((fout.at[:, cols], pieces.at[k, :, pl.ds(h * run, run)]))
-    moved = [pltpu.make_async_copy(a, b, out_sems.at[i]) for i, (a, b) in enumerate(moves)]
+    moved = [pltpu.make_async_copy(a, b, out_sems.at[i + 1]) for i, (a, b) in enumerate(moves)]
+    whole.wait()
     for copy in moved:
         copy.start()
     read[...] = readout[:, pl.ds(pl.multiple_of(place[8] * half, half), half)]
@@ -358,8 +361,9 @@
         scratch_shapes=[
             pltpu.VMEM((tiles, rows, tile, width), jnp.bfloat16),
             pltpu.VMEM((tiles, tile, width), jnp.bfloat16),
+            pltpu.VMEM(fout.shape, fout.dtype),
             pltpu.SemaphoreType.DMA((tiles, 2)),
-            pltpu.SemaphoreType.DMA((2 + XH * Z,)),
+            pltpu.SemaphoreType.DMA((3 + XH * Z,)),
         ],
         compiler_params=pltpu.CompilerParams(vmem_limit_bytes=LARGE_BYTES),
         cost_estimate=pl.CostEstimate(
@@ -485,7 +489,7 @@
 
     w_b, w_e, w_c, w_f, w_g = ([None] * CHAINS for _ in range(5))
     for h in chains:
-        own[h], w_a[h], w_d[h] = after((own[h], w_a[h], w_d[h]), low_own)
+        own[h], w_a[h], w_d[h] = after((own[h], w_a[h], w_d[h]), read_mine)
         w_b[h] = send(own[h], y_bwd)
         w_e[h] = send(w_a[h], x_go)
     acc, token = group_matmul(0, places, x_own, x_oth, [own, w_a, w_d], None)

time: 227 us -> 129 us (0.57)
  Pallas kernels: 137 us -> 39.5 us
    pallas_call x1, Pallas kernels: 66.4 us -> 7.1 us  [low_term(): pl.pallas_call(low_kernel, out_shape=(jax.ShapeDtypeStruct((rows, members...]
    pallas_call x1, Pallas kernels: 41.5 us -> 3.03 us  [take_blocks(): pl.pallas_call(take_kernel, out_shape=tuple(shapes), in_specs=[pl.BlockSp...]
  transfers between devices with their start and end apart: 22 -> 22, of which waited for: 7 -> 7; matrix products, arithmetic and copies ran while one was open for 0% -> 1% of each run, Pallas kernels for 58% -> 27%
where the time goes in v6:
time: 129 us
  starting transfers between devices  40.8 us (32%)
  Pallas kernels  39.5 us (31%)
  waiting for transfers between devices  21.3 us (17%)
  between operations  14.3 us (11%)
  blocking collectives  8.36 us (6%)
  local copies, waits for them, and re-layouts  2.7 us (2%)
  other arithmetic  1.67 us (1%)
    ppermute x19, starting transfers between devices, send(): return lax.ppermute(v, AXES, pairs)  23.5 us
    pallas_call x3, Pallas kernels, group_matmul(): pl.pallas_call(functools.partial(group_kernel, base, count, acc is not No...  20.6 us
    ppermute x19, waiting for transfers between devices, send(): return lax.ppermute(v, AXES, pairs)  12.5 us
    all_to_all x1, starting transfers between devices, share(): return lax.all_to_all(x, axes, 0, 0, tiled=True)  9.12 us
    all_to_all x1, waiting for transfers between devices, share(): return lax.all_to_all(x, axes, 0, 0, tiled=True)  8.83 us
    all_to_all x1, blocking collectives, share(): return lax.all_to_all(x, axes, 0, 0, tiled=True)  8.36 us
    all_to_all x1, starting transfers between devices, shards(): pieces = lax.all_to_all(pieces_here, 'z', 0, 0, tiled=True)  8.2 us
    pallas_call x1, Pallas kernels, low_term(): pl.pallas_call(low_kernel, out_shape=(jax.ShapeDtypeStruct((rows, members...  7.1 us
  transfers between devices with their start and end apart: 22, of which 7 were waited for; matrix products, arithmetic and copies ran while one was open for 1% of the time, Pallas kernels for 27%

profile of v6, /device:TPU:1, one launch (start us, length us, event | category | flops | bytes accessed | tf_op | source)
XLA Modules:
  0.0 128.6 jit_solution(13198722466300243287)
XLA Ops:
  7.2 3.3 %collective-permute-start.4 = (bf16[3,256,4096]{2,1,0:T(8,128)(2,1)}, bf16[3,256,4096]{2,1,0:T(8,128)(2,1)}, u32[]{:S(2)}, u32[]{:S(2)}) collective-permute-start(bf16[3,256,4096]{2,1,0:T(8,128)(2,1)} %bitcast.21), channel_id=1, source_target_pairs={{0,8},{1,9},{2,10},{3,11},{4,12},{5,13},{6,14},{7,15},{8,0},{9,1},... | collective-permute-start | bytes 18874376 | tf_op jit(solution)/shard_map/ppermute | solution.py:453
  11.2 3.0 %shard_map.68 = (bf16[512,512]{1,0:T(8,128)(2,1)}, bf16[512,512]{1,0:T(8,128)(2,1)}, bf16[256,512]{1,0:T(8,128)(2,1)}) custom-call(s32[11]{0:T(128)} %stack.47.place.kidx, bf16[2048,512]{1,0:T(8,128)(2,1)} %weight.1, bf16[256,4096]{1,0:T(8,128)(2,1)} %fin.3), custom_call_target="tpu_custom_call" | custom-call | tf_op jit(solution)/shard_map/pallas_call | solution.py:286
  14.3 1.1 collective-permute-start.5
  15.4 2.5 %collective-permute-start.6 = (bf16[512,512]{1,0:T(8,128)(2,1)}, bf16[512,512]{1,0:T(8,128)(2,1)}, u32[]{:S(2)}, u32[]{:S(2)}) collective-permute-start(bf16[512,512]{1,0:T(8,128)(2,1)} %get-tuple-element.40.refs_0_), channel_id=1, source_target_pairs={{0,4},{1,5},{2,6},{3,7},{4,0},{5,1},{6,2},{7,3},{8,140},{9,141},{1... | collective-permute-start | bytes 1572872 | tf_op jit(solution)/shard_map/ppermute | solution.py:453
  18.5 7.1 %shard_map.69 = (f32[3,256,1]{2,1,0:T(8,128)}, bf16[8,256,256]{2,1,0:T(8,128)(2,1)}, bf16[256,1024]{1,0:T(8,128)(2,1)}, bf16[256,1024]{1,0:T(8,128)(2,1)}, f32[1,1024]{1,0:T(1,128)}) custom-call(s32[11]{0:T(128)} %stack.47.place.kidx, bf16[3,256,4096]{2,1,0:T(8,128)(2,1)} %bitcast.22, bf16[256,4096]{1,0:T(8,128)(2,1)} %fin.3, bf16[256,2048]{1,0:T(8,128)(2,1)} %fout_all.1, ...), custom_call_target="tpu_custom_call" | custom-call | flops 6291456 | bytes 9437184 | tf_op jit(solution)/shard_map/pallas_call | solution.py:350
  25.6 8.2 %all-to-all-start = ((bf16[8,256,256]{2,1,0:T(8,128)(2,1)}), bf16[8,256,256]{2,1,0:T(8,128)(2,1)S(1)}, u32[]{:S(2)}, u32[]{:S(2)}) async-start(bf16[8,256,256]{2,1,0:T(8,128)(2,1)} %get-tuple-element.65), calls=%async_computation | async-start | bytes 2097152 | tf_op jit(solution)/shard_map/all_to_all | solution.py:486
  34.5 2.5 %collective-permute-start.10 = (bf16[512,512]{1,0:T(8,128)(2,1)S(1)}, bf16[512,512]{1,0:T(8,128)(2,1)S(1)}, u32[]{:S(2)}, u32[]{:S(2)}) collective-permute-start(bf16[512,512]{1,0:T(8,128)(2,1)S(1)} %get-tuple-element.42.refs_3_.refs_0_), channel_id=1, source_target_pairs={{0,4},{1,5},{2,6},{3,7},{4,0},{5,1},{6,2},{7,3},{8,140},{9,141},{1... | collective-permute-start | bytes 1572872 | tf_op jit(solution)/shard_map/ppermute | solution.py:453
  37.0 1.0 collective-permute-start.9
  38.9 8.4 %shard_map.72 = (f32[2,3,256,1024]{3,2,1,0:T(8,128)S(1)}, f32[8,128]{1,0:T(8,128)S(1)}) custom-call(s32[11]{0:T(128)S(1)} %copy-done.8, bf16[3,256,4096]{2,1,0:T(8,128)(2,1)} %bitcast.23, bf16[3,256,4096]{2,1,0:T(8,128)(2,1)} %collective-permute-done.4.x_oth, bf16[512,512]{1,0:T(8,128)(2,1)S(1)} %get-tuple-element.39.refs_0_, ...), custom_call_target="tpu_custom_call" | custom-call | flops 4831838208 | bytes 8388608 | tf_op jit(solution)/shard_map/pallas_call | solution.py:150
  47.4 2.8 %collective-permute-start.12 = (bf16[512,512]{1,0:T(8,128)(2,1)S(1)}, bf16[512,512]{1,0:T(8,128)(2,1)S(1)}, u32[]{:S(2)}, u32[]{:S(2)}) collective-permute-start(bf16[512,512]{1,0:T(8,128)(2,1)S(1)} %get-tuple-element.54), channel_id=1, source_target_pairs={{0,1},{1,2},{2,3},{3,0},{4,5},{5,6},{6,7},{7,4},{8,11},{9,8},{10,9... | collective-permute-start | bytes 1572872 | tf_op jit(solution)/shard_map/ppermute | solution.py:453
  50.2 2.5 %collective-permute-start.13 = (bf16[512,512]{1,0:T(8,128)(2,1)S(1)}, bf16[512,512]{1,0:T(8,128)(2,1)S(1)}, u32[]{:S(2)}, u32[]{:S(2)}) collective-permute-start(bf16[512,512]{1,0:T(8,128)(2,1)S(1)} %get-tuple-element.49.refs_1_), channel_id=1, source_target_pairs={{0,4},{1,5},{2,6},{3,7},{4,0},{5,1},{6,2},{7,3},{8,140},{9,141},{1... | collective-permute-start | bytes 1572872 | tf_op jit(solution)/shard_map/ppermute | solution.py:453
  53.5 5.8 %shard_map.75 = (f32[2,3,256,1024]{3,2,1,0:T(8,128)S(1)}, f32[8,128]{1,0:T(8,128)S(1)}) custom-call(s32[11]{0:T(128)S(1)} %copy-done.8, bf16[3,256,4096]{2,1,0:T(8,128)(2,1)} %bitcast.24, bf16[3,256,4096]{2,1,0:T(8,128)(2,1)} %collective-permute-done.4.x_oth, bf16[512,512]{1,0:T(8,128)(2,1)S(1)} %get-tuple-element.47.refs_0_, ...), custom_call_target="tpu_custom_call", output_to_operand_aliasing={{0}: (7, {})} | custom-call | flops 3221225472 | bytes 8388608 | tf_op jit(solution)/shard_map/pallas_call | solution.py:150
  59.8 1.3 collective-permute-start.14
  61.9 3.4 %collective-permute-done.8.refs_1_ = bf16[512,512]{1,0:T(8,128)(2,1)S(1)} collective-permute-done((bf16[512,512]{1,0:T(8,128)(2,1)S(1)}, bf16[512,512]{1,0:T(8,128)(2,1)S(1)}, u32[]{:S(2)}, u32[]{:S(2)}) %collective-permute-start.8) | collective-permute-done | bytes 524320 | tf_op jit(solution)/shard_map/ppermute | solution.py:453
  65.3 2.6 %collective-permute-start.11 = (bf16[512,512]{1,0:T(8,128)(2,1)S(1)}, bf16[512,512]{1,0:T(8,128)(2,1)S(1)}, u32[]{:S(2)}, u32[]{:S(2)}) collective-permute-start(bf16[512,512]{1,0:T(8,128)(2,1)S(1)} %get-tuple-element.53.refs_2_), channel_id=1, source_target_pairs={{0,4},{1,5},{2,6},{3,7},{4,0},{5,1},{6,2},{7,3},{8,140},{9,141},{1... | collective-permute-start | bytes 1572872 | tf_op jit(solution)/shard_map/ppermute | solution.py:453
  68.0 6.4 %shard_map.78 = (f32[2,3,256,1024]{3,2,1,0:T(8,128)S(1)}, f32[8,128]{1,0:T(8,128)}, bf16[2,3,256,512]{3,2,1,0:T(8,128)(2,1)S(1)}) custom-call(s32[11]{0:T(128)S(1)} %copy-done.8, bf16[3,256,4096]{2,1,0:T(8,128)(2,1)} %bitcast.25, bf16[3,256,4096]{2,1,0:T(8,128)(2,1)} %collective-permute-done.4.x_oth, ...), custom_call_target="tpu_custom_call", output_to_operand_aliasing={{0}: (7, {})} | custom-call | flops 3221225472 | bytes 8388608 | tf_op jit(solution)/shard_map/pallas_call | solution.py:150
  74.8 3.5 %shard_map.79.refs_0_ = f32[16,1,512]{2,1,0:T(1,128)S(1)} custom-call(s32[11]{0:T(128)S(1)} %copy-done.8, bf16[512,512]{1,0:T(8,128)(2,1)S(1)} %collective-permute-done.11.refs_0_, bf16[512,512]{1,0:T(8,128)(2,1)S(1)} %collective-permute-done.14.refs_1_, bf16[2,3,256,512]{3,2,1,0:T(8,128)(2,1)S(1)} %get-tuple-element.60.refs_2_, ...), custom_call_target="tpu_custom_call" | custom-call | flops 1610612736 | bytes 6291456 | tf_op jit(solution)/shard_map/pallas_call | solution.py:216
  78.3 8.4 %all_to_all.15.got = f32[16,1,512]{2,1,0:T(1,128)S(1)} all-to-all(f32[16,1,512]{2,1,0:T(1,128)S(1)} %shard_map.80), channel_id=1, replica_groups=mesh['xh'=2,'z'=8,'core'=2,'xl'=2,'y'=4] {'core','xl','y'}, dimensions={0} | all-to-all | bytes 65536 | tf_op jit(solution)/shard_map/all_to_all | solution.py:440
  87.3 9.1 %all-to-all-start.2 = ((f32[16,1,512]{2,1,0:T(1,128)}), f32[16,1,512]{2,1,0:T(1,128)S(1)}, u32[]{:S(2)}, u32[]{:S(2)}) async-start(f32[16,1,512]{2,1,0:T(1,128)} %shard_map.81), calls=%async_computation.2 | async-start | bytes 65536 | tf_op jit(solution)/shard_map/all_to_all | solution.py:440
  96.5 8.8 %all-to-all-done.2.fit = f32[16,1,512]{2,1,0:T(1,128)S(1)} async-done(((f32[16,1,512]{2,1,0:T(1,128)}), f32[16,1,512]{2,1,0:T(1,128)S(1)}, u32[]{:S(2)}, u32[]{:S(2)}) %all-to-all-start.2) | async-done | bytes 32800 | tf_op jit(solution)/shard_map/all_to_all | solution.py:440
  105.9 4.7 %shard_map.82 = (f32[2,64,512]{2,1,0:T(8,128)}, f32[2,64,512]{2,1,0:T(8,128)}, f32[1,256]{1,0:T(1,128)}) custom-call(s32[11]{0:T(128)} %stack.47.place.kidx, f32[16,1,512]{2,1,0:T(1,128)} %copy-done.9, bf16[8,256,256]{2,1,0:T(8,128)(2,1)} %copy-done, bf16[8,256,512]{2,1,0:T(8,128)(2,1)} %bitcast.26), custom_call_target="tpu_custom_call" | custom-call | flops 536870912 | bytes 4194304 | tf_op jit(solution)/shard_map/pallas_call | solution.py:421
  110.6 1.9 %collective-permute-start.17 = (f32[2,64,512]{2,1,0:T(8,128)}, f32[2,64,512]{2,1,0:T(8,128)S(1)}, u32[]{:S(2)}, u32[]{:S(2)}) collective-permute-start(f32[2,64,512]{2,1,0:T(8,128)} %get-tuple-element.68), channel_id=1, source_target_pairs={{0,8},{1,9},{2,10},{3,11},{4,12},{5,13},{6,14},{7,15},{8,0},{9,1},... | collective-permute-start | bytes 786440 | tf_op jit(solution)/shard_map/ppermute | solution.py:453
  112.4 1.4 %collective-permute-done.17 = f32[2,64,512]{2,1,0:T(8,128)S(1)} collective-permute-done((f32[2,64,512]{2,1,0:T(8,128)}, f32[2,64,512]{2,1,0:T(8,128)S(1)}, u32[]{:S(2)}, u32[]{:S(2)}) %collective-permute-start.17) | collective-permute-done | bytes 262176 | tf_op jit(solution)/shard_map/ppermute | solution.py:453
  115.3 5.9 %collective-permute-done.18 = f32[64,512]{1,0:T(8,128)S(1)} collective-permute-done((f32[64,512]{1,0:T(8,128)S(1)}, f32[64,512]{1,0:T(8,128)S(1)}, u32[]{:S(2)}, u32[]{:S(2)}) %collective-permute-start.18) | collective-permute-done | bytes 131104 | tf_op jit(solution)/shard_map/ppermute | solution.py:453
  (63 shorter events, 9.0 us)
Async XLA Ops:
  7.2 89.3 %all-gather.3.cloned.1.call-start = ((), (), s32[]{:S(2)}) async-start(), calls=%async_computation.3 | async-start | bytes 2359296 | tf_op jit(solution)/shard_map/all_gather | solution.py:485
  7.2 31.7 %collective-permute-start.4 = (bf16[3,256,4096]{2,1,0:T(8,128)(2,1)}, bf16[3,256,4096]{2,1,0:T(8,128)(2,1)}, u32[]{:S(2)}, u32[]{:S(2)}) collective-permute-start(bf16[3,256,4096]{2,1,0:T(8,128)(2,1)} %bitcast.21), channel_id=1, source_target_pairs={{0,8},{1,9},{2,10},{3,11},{4,12},{5,13},{6,14},{7,15},{8,0},{9,1},... | collective-permute-start | bytes 18874376 | tf_op jit(solution)/shard_map/ppermute | solution.py:453
  14.3 19.5 %collective-permute-start.5 = (bf16[512,512]{1,0:T(8,128)(2,1)}, bf16[512,512]{1,0:T(8,128)(2,1)S(1)}, u32[]{:S(2)}, u32[]{:S(2)}) collective-permute-start(bf16[512,512]{1,0:T(8,128)(2,1)} %get-tuple-element.40.refs_0_), channel_id=1, source_target_pairs={{0,1},{1,2},{2,3},{3,0},{4,5},{5,6},{6,7},{7,4},{8,11},{9,8},{10,9... | collective-permute-start | bytes 1572872 | tf_op jit(solution)/shard_map/ppermute | solution.py:453
  15.4 18.5 %collective-permute-start.6 = (bf16[512,512]{1,0:T(8,128)(2,1)}, bf16[512,512]{1,0:T(8,128)(2,1)}, u32[]{:S(2)}, u32[]{:S(2)}) collective-permute-start(bf16[512,512]{1,0:T(8,128)(2,1)} %get-tuple-element.40.refs_0_), channel_id=1, source_target_pairs={{0,4},{1,5},{2,6},{3,7},{4,0},{5,1},{6,2},{7,3},{8,140},{9,141},{1... | collective-permute-start | bytes 1572872 | tf_op jit(solution)/shard_map/ppermute | solution.py:453
  17.8 20.2 %collective-permute-start = (bf16[512,512]{1,0:T(8,128)(2,1)}, bf16[512,512]{1,0:T(8,128)(2,1)S(1)}, u32[]{:S(2)}, u32[]{:S(2)}) collective-permute-start(bf16[512,512]{1,0:T(8,128)(2,1)} %get-tuple-element.36.refs_0_), channel_id=1, source_target_pairs={{0,1},{1,2},{2,3},{3,0},{4,5},{5,6},{6,7},{7,4},{8,11},{9,8},{10,9... | collective-permute-start | bytes 1572872 | tf_op jit(solution)/shard_map/ppermute | solution.py:453
  18.3 19.7 %collective-permute-start.1 = (bf16[512,512]{1,0:T(8,128)(2,1)}, bf16[512,512]{1,0:T(8,128)(2,1)}, u32[]{:S(2)}, u32[]{:S(2)}) collective-permute-start(bf16[512,512]{1,0:T(8,128)(2,1)} %get-tuple-element.36.refs_0_), channel_id=1, source_target_pairs={{0,4},{1,5},{2,6},{3,7},{4,0},{5,1},{6,2},{7,3},{8,140},{9,141},{1... | collective-permute-start | bytes 1572872 | tf_op jit(solution)/shard_map/ppermute | solution.py:453
  18.5 20.4 %copy-start.8 = (s32[11]{0:T(128)S(1)}, s32[11]{0:T(128)}, u32[]{:S(2)}) copy-start(s32[11]{0:T(128)} %stack.47.place.kidx) | copy-start | bytes 136
  25.6 52.6 %all-to-all-start = ((bf16[8,256,256]{2,1,0:T(8,128)(2,1)}), bf16[8,256,256]{2,1,0:T(8,128)(2,1)S(1)}, u32[]{:S(2)}, u32[]{:S(2)}) async-start(bf16[8,256,256]{2,1,0:T(8,128)(2,1)} %get-tuple-element.65), calls=%async_computation | async-start | bytes 2097152 | tf_op jit(solution)/shard_map/all_to_all | solution.py:486
  34.5 12.8 %collective-permute-start.10 = (bf16[512,512]{1,0:T(8,128)(2,1)S(1)}, bf16[512,512]{1,0:T(8,128)(2,1)S(1)}, u32[]{:S(2)}, u32[]{:S(2)}) collective-permute-start(bf16[512,512]{1,0:T(8,128)(2,1)S(1)} %get-tuple-element.42.refs_3_.refs_0_), channel_id=1, source_target_pairs={{0,4},{1,5},{2,6},{3,7},{4,0},{5,1},{6,2},{7,3},{8,140},{9,141},{1... | collective-permute-start | bytes 1572872 | tf_op jit(solution)/shard_map/ppermute | solution.py:453
  37.0 10.4 %collective-permute-start.9 = (bf16[512,512]{1,0:T(8,128)(2,1)S(1)}, bf16[512,512]{1,0:T(8,128)(2,1)S(1)}, u32[]{:S(2)}, u32[]{:S(2)}) collective-permute-start(bf16[512,512]{1,0:T(8,128)(2,1)S(1)} %get-tuple-element.41.refs_1_), channel_id=1, source_target_pairs={{0,3},{1,0},{2,1},{3,2},{4,7},{5,4},{6,5},{7,6},{8,9},{9,10},{10,1... | collective-permute-start | bytes 1572872 | tf_op jit(solution)/shard_map/ppermute | solution.py:453
  38.7 14.0 %collective-permute-start.2 = (bf16[512,512]{1,0:T(8,128)(2,1)S(1)}, bf16[512,512]{1,0:T(8,128)(2,1)S(1)}, u32[]{:S(2)}, u32[]{:S(2)}) collective-permute-start(bf16[512,512]{1,0:T(8,128)(2,1)S(1)} %get-tuple-element.39.refs_0_), channel_id=1, source_target_pairs={{0,3},{1,0},{2,1},{3,2},{4,7},{5,4},{6,5},{7,6},{8,9},{9,10},{10,1... | collective-permute-start | bytes 1572872 | tf_op jit(solution)/shard_map/ppermute | solution.py:453
  38.7 13.9 %collective-permute-start.3 = (bf16[512,512]{1,0:T(8,128)(2,1)S(1)}, bf16[512,512]{1,0:T(8,128)(2,1)S(1)}, u32[]{:S(2)}, u32[]{:S(2)}) collective-permute-start(bf16[512,512]{1,0:T(8,128)(2,1)S(1)} %get-tuple-element.38.refs_2_.refs_0_), channel_id=1, source_target_pairs={{0,4},{1,5},{2,6},{3,7},{4,0},{5,1},{6,2},{7,3},{8,140},{9,141},{1... | collective-permute-start | bytes 1572872 | tf_op jit(solution)/shard_map/ppermute | solution.py:453
  47.4 11.8 %collective-permute-start.12 = (bf16[512,512]{1,0:T(8,128)(2,1)S(1)}, bf16[512,512]{1,0:T(8,128)(2,1)S(1)}, u32[]{:S(2)}, u32[]{:S(2)}) collective-permute-start(bf16[512,512]{1,0:T(8,128)(2,1)S(1)} %get-tuple-element.54), channel_id=1, source_target_pairs={{0,1},{1,2},{2,3},{3,0},{4,5},{5,6},{6,7},{7,4},{8,11},{9,8},{10,9... | collective-permute-start | bytes 1572872 | tf_op jit(solution)/shard_map/ppermute | solution.py:453
  50.2 9.6 %collective-permute-start.13 = (bf16[512,512]{1,0:T(8,128)(2,1)S(1)}, bf16[512,512]{1,0:T(8,128)(2,1)S(1)}, u32[]{:S(2)}, u32[]{:S(2)}) collective-permute-start(bf16[512,512]{1,0:T(8,128)(2,1)S(1)} %get-tuple-element.49.refs_1_), channel_id=1, source_target_pairs={{0,4},{1,5},{2,6},{3,7},{4,0},{5,1},{6,2},{7,3},{8,140},{9,141},{1... | collective-permute-start | bytes 1572872 | tf_op jit(solution)/shard_map/ppermute | solution.py:453
  52.7 9.2 %collective-permute-start.7 = (bf16[512,512]{1,0:T(8,128)(2,1)S(1)}, bf16[512,512]{1,0:T(8,128)(2,1)S(1)}, u32[]{:S(2)}, u32[]{:S(2)}) collective-permute-start(bf16[512,512]{1,0:T(8,128)(2,1)S(1)} %get-tuple-element.46), channel_id=1, source_target_pairs={{0,1},{1,2},{2,3},{3,0},{4,5},{5,6},{6,7},{7,4},{8,11},{9,8},{10,9... | collective-permute-start | bytes 1572872 | tf_op jit(solution)/shard_map/ppermute | solution.py:453
  53.1 12.2 %collective-permute-start.8 = (bf16[512,512]{1,0:T(8,128)(2,1)S(1)}, bf16[512,512]{1,0:T(8,128)(2,1)S(1)}, u32[]{:S(2)}, u32[]{:S(2)}) collective-permute-start(bf16[512,512]{1,0:T(8,128)(2,1)S(1)} %get-tuple-element.47.refs_0_), channel_id=1, source_target_pairs={{0,4},{1,5},{2,6},{3,7},{4,0},{5,1},{6,2},{7,3},{8,140},{9,141},{1... | collective-permute-start | bytes 1572872 | tf_op jit(solution)/shard_map/ppermute | solution.py:453
  53.3 21.0 %collective-permute-start.16 = (bf16[256,1024]{1,0:T(8,128)(2,1)S(1)}, bf16[256,1024]{1,0:T(8,128)(2,1)S(1)}, u32[]{:S(2)}, u32[]{:S(2)}) collective-permute-start(bf16[256,1024]{1,0:T(8,128)(2,1)S(1)} %copy-done.10), channel_id=1, source_target_pairs={{0,8},{1,9},{2,10},{3,11},{4,12},{5,13},{6,14},{7,15},{8,0},{9,1},... | collective-permute-start | bytes 1572872 | tf_op jit(solution)/shard_map/ppermute | solution.py:453
  59.8 14.6 %collective-permute-start.14 = (bf16[512,512]{1,0:T(8,128)(2,1)S(1)}, bf16[512,512]{1,0:T(8,128)(2,1)S(1)}, u32[]{:S(2)}, u32[]{:S(2)}) collective-permute-start(bf16[512,512]{1,0:T(8,128)(2,1)S(1)} %get-tuple-element.55), channel_id=1, source_target_pairs={{0,1},{1,2},{2,3},{3,0},{4,5},{5,6},{6,7},{7,4},{8,11},{9,8},{10,9... | collective-permute-start | bytes 1572872 | tf_op jit(solution)/shard_map/ppermute | solution.py:453
  65.3 9.5 %collective-permute-start.11 = (bf16[512,512]{1,0:T(8,128)(2,1)S(1)}, bf16[512,512]{1,0:T(8,128)(2,1)S(1)}, u32[]{:S(2)}, u32[]{:S(2)}) collective-permute-start(bf16[512,512]{1,0:T(8,128)(2,1)S(1)} %get-tuple-element.53.refs_2_), channel_id=1, source_target_pairs={{0,4},{1,5},{2,6},{3,7},{4,0},{5,1},{6,2},{7,3},{8,140},{9,141},{1... | collective-permute-start | bytes 1572872 | tf_op jit(solution)/shard_map/ppermute | solution.py:453
  67.9 6.4 %collective-permute-start.15 = (f32[3,256,1]{2,1,0:T(8,128)S(1)}, f32[3,256,1]{2,1,0:T(8,128)S(1)}, u32[]{:S(2)}, u32[]{:S(2)}) collective-permute-start(f32[3,256,1]{2,1,0:T(8,128)S(1)} %copy-done.4), channel_id=1, source_target_pairs={{0,8},{1,9},{2,10},{3,11},{4,12},{5,13},{6,14},{7,15},{8,0},{9,1},... | collective-permute-start | bytes 9224 | tf_op jit(solution)/shard_map/ppermute | solution.py:453
  78.3 27.0 %copy-start = (bf16[8,256,256]{2,1,0:T(8,128)(2,1)}, bf16[8,256,256]{2,1,0:T(8,128)(2,1)S(1)}, u32[]{:S(2)}) copy-start(bf16[8,256,256]{2,1,0:T(8,128)(2,1)S(1)} %all-to-all-done.refs_1_.fout_all) | copy-start | bytes 3145732
  87.3 18.0 %all-to-all-start.2 = ((f32[16,1,512]{2,1,0:T(1,128)}), f32[16,1,512]{2,1,0:T(1,128)S(1)}, u32[]{:S(2)}, u32[]{:S(2)}) async-start(f32[16,1,512]{2,1,0:T(1,128)} %shard_map.81), calls=%async_computation.2 | async-start | bytes 65536 | tf_op jit(solution)/shard_map/all_to_all | solution.py:440
  110.6 3.2 %collective-permute-start.17 = (f32[2,64,512]{2,1,0:T(8,128)}, f32[2,64,512]{2,1,0:T(8,128)S(1)}, u32[]{:S(2)}, u32[]{:S(2)}) collective-permute-start(f32[2,64,512]{2,1,0:T(8,128)} %get-tuple-element.68), channel_id=1, source_target_pairs={{0,8},{1,9},{2,10},{3,11},{4,12},{5,13},{6,14},{7,15},{8,0},{9,1},... | collective-permute-start | bytes 786440 | tf_op jit(solution)/shard_map/ppermute | solution.py:453
  114.8 6.3 %collective-permute-start.18 = (f32[64,512]{1,0:T(8,128)S(1)}, f32[64,512]{1,0:T(8,128)S(1)}, u32[]{:S(2)}, u32[]{:S(2)}) collective-permute-start(f32[64,512]{1,0:T(8,128)S(1)} %slice_bitcast_fusion), channel_id=1, source_target_pairs={{0,128},{1,129},{2,130},{3,131},{4,132},{5,133},{6,134},{7,135},{8... | collective-permute-start | bytes 393224 | tf_op jit(solution)/shard_map/ppermute | solution.py:453
  (9 other events, 83.7 us)
Sparse Core Ops, SparseCore 0:
  14.4 58.6 all-gather.2

commit v7 on v5

--- a/solution.py
+++ b/solution.py
@@ -17,8 +17,8 @@
 WA = XL * Y
 CHAINS = 2
 ROWS_ALL = 24
-VMEM_BYTES = 41 * 1024 * 1024
-LAST_BYTES = 41 * 1024 * 1024
+VMEM_BYTES = 40 * 1024 * 1024
+LAST_BYTES = 40 * 1024 * 1024
 SMALL_BYTES = 1024 * 1024
 LARGE_BYTES = 58 * 1024 * 1024
 
@@ -66,21 +66,18 @@
 
 def fetch(kidx, base, x_own, x_oth, sent, ws, w_sems, buffers, sems):
     count, part, block = len(sent), sent[0][0].shape[0], sent[0][0].shape[1]
-    waits = [[], []]
-
-    def start(source, to, sem, side):
-        copy = pltpu.make_async_copy(source, to, sem)
-        copy.start()
-        waits[side].append(copy)
-
+    copies = [[], []]
     for side, x in ((0, x_own), (1, x_oth)):
         for s in range(count):
+            cols = pl.ds(pl.multiple_of(kidx[base + s] * block, block), block)
+            copies[side].append(
+                pltpu.make_async_copy(x.at[:, :, cols], buffers.at[s, side], sems.at[s, side])
+            )
             if side == 0:
                 for h in range(CHAINS):
-                    start(sent[s][h], ws.at[s, pl.ds(h * part, part), :], w_sems.at[s, h], side)
-            cols = pl.ds(pl.multiple_of(kidx[base + s] * block, block), block)
-            start(x.at[:, :, cols], buffers.at[s, side], sems.at[s, side], side)
-    return waits
+                    to = ws.at[s, pl.ds(h * part, part), :]
+                    copies[side].append(pltpu.make_async_copy(sent[s][h], to, w_sems.at[s, h]))
+    return copies
 
 
 def fetch_scratch(count, members, width, block):
@@ -96,7 +93,8 @@
     return [refs[i : i + CHAINS] for i in range(0, len(refs), CHAINS)]
 
 
-def group_kernel(base, count, has_acc, ahead, kidx, x_own, x_oth, *refs):
+def group_kernel(base, count, has_acc, ahead, extra, kidx, x_own, x_oth, *refs):
+    refs = refs[extra:]
     sent = pairs(refs[: count * CHAINS])
     acc_in = refs[count * CHAINS] if has_acc else None
     if ahead:
@@ -105,18 +103,22 @@
     out, token, ws, w_sems, buffers, sems = refs[-6:]
     members, width = out.shape[2], out.shape[3]
     block = ws.shape[2]
-    waits = fetch(kidx, base, x_own, x_oth, sent, ws, w_sems, buffers, sems)
+    copies = fetch(kidx, base, x_own, x_oth, sent, ws, w_sems, buffers, sems)
+    for copy in copies[0]:
+        copy.start()
     early = []
     if ahead:
         cols = pl.ds(pl.multiple_of(kidx[base + count] * block, block), block)
         for side, x in ((0, x_own), (1, x_oth)):
             early.append(pltpu.make_async_copy(x.at[:, :, cols], x_last.at[side], last_sems.at[side]))
-            early[-1].start()
     token[...] = jnp.zeros_like(token)
     chunk = 512
     for side in range(2):
-        for copy in waits[side]:
+        for copy in copies[side]:
             copy.wait()
+        if side == 0:
+            for copy in copies[1] + early:
+                copy.start()
         for j in range(0, width, chunk):
             cols = pl.ds(j, chunk)
             total = None
@@ -131,7 +133,7 @@
         copy.wait()
 
 
-def group_matmul(base, kidx, x_own, x_oth, sent, acc, ahead=False):
+def group_matmul(base, kidx, x_own, x_oth, sent, acc, ahead=False, extra=()):
     count = len(sent)
     members = x_own.shape[1]
     part, block = sent[0][0].shape
@@ -139,7 +141,7 @@
     smem = pl.BlockSpec(memory_space=pltpu.SMEM)
     vmem = pl.BlockSpec(memory_space=pltpu.VMEM)
     hbm = pl.BlockSpec(memory_space=pl.ANY)
-    args = [x_own, x_oth] + [w for ws in sent for w in ws]
+    args = [x_own, x_oth, *extra] + [w for ws in sent for w in ws]
     specs = [smem] + [hbm] * len(args)
     alias = {}
     if acc is not None:
@@ -148,7 +150,7 @@
         alias = {len(args): 0}
     flops = 2 * 2 * 3 * members * width * block * count
     return pl.pallas_call(
-        functools.partial(group_kernel, base, count, acc is not None, ahead),
+        functools.partial(group_kernel, base, count, acc is not None, ahead, len(extra)),
         out_shape=(
             jax.ShapeDtypeStruct((2, 3, members, width), jnp.float32),
             jax.ShapeDtypeStruct((8, 128), jnp.float32),
@@ -263,37 +265,74 @@
     )(got)
 
 
-def take_kernel(place, weight, fin, *refs):
-    parts, fin_here, sems = refs[:-2], refs[-2], refs[-1]
-    rows, block = parts[0].shape
-    copies = []
-    for h, out in enumerate(parts):
-        at = pl.ds(pl.multiple_of(place[8] * (rows * len(parts)) + h * rows, rows), rows)
-        copies.append(pltpu.make_async_copy(weight.at[at, :], out, sems.at[h]))
-    cols = pl.ds(pl.multiple_of(place[0] * block, block), block)
-    copies.append(pltpu.make_async_copy(fin.at[:, cols], fin_here, sems.at[len(parts)]))
+def cut_kernel(place, fout_all, readout, pieces, mine, theirs, read, fout, sems):
+    half = mine.shape[1]
+    first = pltpu.make_async_copy(fout_all, fout, sems.at[0])
+    first.start()
+    read[...] = readout[:, pl.ds(pl.multiple_of(place[8] * half, half), half)]
+    moves = []
+    run = pieces.shape[2] // XH
+    for h in range(XH):
+        for k in range(Z):
+            cols = pl.ds(h * half + k * run, run)
+            moves.append((fout.at[:, cols], pieces.at[k, :, pl.ds(h * run, run)]))
+    for at, to in ((place[8], mine), (1 - place[8], theirs)):
+        cols = pl.ds(pl.multiple_of(at * half, half), half)
+        moves.append((fout.at[:, cols], to))
+    copies = [pltpu.make_async_copy(x, y, sems.at[i + 1]) for i, (x, y) in enumerate(moves)]
+    first.wait()
     for copy in copies:
         copy.start()
     for copy in copies:
         copy.wait()
 
 
-def take_blocks(place, weight, fin, part):
-    block = weight.shape[1]
-    hbm = pl.BlockSpec(memory_space=pl.ANY)
-    shapes = [jax.ShapeDtypeStruct((part, block), weight.dtype)] * CHAINS
-    shapes.append(jax.ShapeDtypeStruct((fin.shape[0], block), fin.dtype))
-    return pl.pallas_call(
-        take_kernel,
-        out_shape=tuple(shapes),
-        in_specs=[pl.BlockSpec(memory_space=pltpu.SMEM), hbm, hbm],
-        out_specs=(hbm,) * len(shapes),
-        scratch_shapes=[pltpu.SemaphoreType.DMA((len(shapes),))],
+def cut_factors(place, fout, readout):
+    members, out_width = fout.shape
+    half = out_width // CORE
+    hbm = pl.BlockSpec(memory_space=pl.ANY)
+    vmem = pl.BlockSpec(memory_space=pltpu.VMEM)
+    return pl.pallas_call(
+        cut_kernel,
+        out_shape=(
+            jax.ShapeDtypeStruct((Z, members, out_width // Z), fout.dtype),
+            jax.ShapeDtypeStruct((members, half), fout.dtype),
+            jax.ShapeDtypeStruct((members, half), fout.dtype),
+            jax.ShapeDtypeStruct((1, half), readout.dtype),
+        ),
+        in_specs=[pl.BlockSpec(memory_space=pltpu.SMEM), hbm, vmem],
+        out_specs=(hbm, hbm, hbm, vmem),
+        scratch_shapes=[
+            pltpu.VMEM(fout.shape, fout.dtype),
+            pltpu.SemaphoreType.DMA((3 + XH * Z,)),
+        ],
         compiler_params=pltpu.CompilerParams(vmem_limit_bytes=LARGE_BYTES),
-    )(place, weight, fin)
-
-
-def low_kernel(place, x, fin, fout, readout, out, pieces, mine, theirs, read, x_buf, f_buf, sems, out_sems):
+        cost_estimate=pl.CostEstimate(flops=0, bytes_accessed=4 * 1024 * 1024, transcendentals=0),
+    )(place, fout, readout)
+
+
+def block_kernel(place, fin, *refs):
+    out, sem = refs[-2:]
+    block = out.shape[1]
+    cols = pl.ds(pl.multiple_of(place[0] * block, block), block)
+    copy = pltpu.make_async_copy(fin.at[:, cols], out, sem.at[0])
+    copy.start()
+    copy.wait()
+
+
+def cut_block(place, fin, block, *done):
+    hbm = pl.BlockSpec(memory_space=pl.ANY)
+    return pl.pallas_call(
+        block_kernel,
+        out_shape=jax.ShapeDtypeStruct((fin.shape[0], block), fin.dtype),
+        in_specs=[pl.BlockSpec(memory_space=pltpu.SMEM), hbm] + [hbm] * len(done),
+        out_specs=pl.BlockSpec(memory_space=pltpu.VMEM),
+        scratch_shapes=[pltpu.SemaphoreType.DMA((1,))],
+        compiler_params=pltpu.CompilerParams(vmem_limit_bytes=LARGE_BYTES),
+    )(place, fin, *done)
+
+
+def low_kernel(x, fin, out, x_buf, f_buf, sems):
     tiles, rows, tile, width = x_buf.shape
     copies = []
     for t in range(tiles):
@@ -305,20 +344,6 @@
         for copy in pair:
             copy.start()
         copies.append(pair)
-    half = mine.shape[1]
-    moves = []
-    for at, to in ((place[8], mine), (1 - place[8], theirs)):
-        cols = pl.ds(pl.multiple_of(at * half, half), half)
-        moves.append((fout.at[:, cols], to))
-    run = pieces.shape[2] // XH
-    for h in range(XH):
-        for k in range(Z):
-            cols = pl.ds(h * half + k * run, run)
-            moves.append((fout.at[:, cols], pieces.at[k, :, pl.ds(h * run, run)]))
-    moved = [pltpu.make_async_copy(a, b, out_sems.at[i]) for i, (a, b) in enumerate(moves)]
-    for copy in moved:
-        copy.start()
-    read[...] = readout[:, pl.ds(pl.multiple_of(place[8] * half, half), half)]
     chunk = 128
     for t in range(tiles):
         for copy in copies[t]:
@@ -332,40 +357,28 @@
                 totals[r] = term if totals[r] is None else totals[r] + term
         for r in range(rows):
             out[r, pl.ds(t * tile, tile), :] = perturb_scale * jnp.sum(totals[r], axis=1, keepdims=True)
-    for copy in moved:
-        copy.wait()
-
-
-def low_term(place, x, fin, fout, readout):
+
+
+def low_term(x, fin):
     rows, members, width = x.shape
-    out_width = fout.shape[1]
-    half = out_width // CORE
     tile = 64
     tiles = members // tile
     hbm = pl.BlockSpec(memory_space=pl.ANY)
-    vmem = pl.BlockSpec(memory_space=pltpu.VMEM)
     return pl.pallas_call(
         low_kernel,
-        out_shape=(
-            jax.ShapeDtypeStruct((rows, members, 1), jnp.float32),
-            jax.ShapeDtypeStruct((Z, members, out_width // Z), fout.dtype),
-            jax.ShapeDtypeStruct((members, half), fout.dtype),
-            jax.ShapeDtypeStruct((members, half), fout.dtype),
-            jax.ShapeDtypeStruct((1, half), readout.dtype),
-        ),
-        in_specs=[pl.BlockSpec(memory_space=pltpu.SMEM), hbm, hbm, hbm, vmem],
-        out_specs=(vmem, hbm, hbm, hbm, vmem),
+        out_shape=jax.ShapeDtypeStruct((rows, members, 1), jnp.float32),
+        in_specs=[hbm, hbm],
+        out_specs=pl.BlockSpec(memory_space=pltpu.VMEM),
         scratch_shapes=[
             pltpu.VMEM((tiles, rows, tile, width), jnp.bfloat16),
             pltpu.VMEM((tiles, tile, width), jnp.bfloat16),
             pltpu.SemaphoreType.DMA((tiles, 2)),
-            pltpu.SemaphoreType.DMA((2 + XH * Z,)),
         ],
-        compiler_params=pltpu.CompilerParams(vmem_limit_bytes=LARGE_BYTES),
+        compiler_params=pltpu.CompilerParams(vmem_limit_bytes=VMEM_BYTES),
         cost_estimate=pl.CostEstimate(
             flops=2 * rows * members * width, bytes_accessed=9 * 1024 * 1024, transcendentals=0
         ),
-    )(place, x, fin, fout, readout)
+    )(x, fin)
 
 
 def step_kernel(place, fit, fout_all, fin_all, keep, give, util, rows_ref, fout, fin, sems):
@@ -470,22 +483,21 @@
 
     part = half // CHAINS
     chains = range(CHAINS)
-    *own, fin_here = take_blocks(places, weight, factor_in, part)
+    own = [lax.dynamic_slice_in_dim(weight, c * half + h * part, part, 0) for h in chains]
     w_a = [send(w, y_fwd) for w in own]
     w_d = [send(w, x_go) for w in own]
     x_oth = send(x_own, core_go)
 
-    low_own, pieces_here, fout_mine, fout_theirs, read_mine = low_term(
-        places, x_own, factor_in, factor_out, readout[None]
-    )
-    fin_all = lax.all_gather(fin_here, "z", axis=0)
+    fin_all = lax.all_gather(cut_block(places, factor_in, block), "z", axis=0)
+    pieces_here, fout_mine, fout_theirs, read_mine = cut_factors(places, factor_out, readout[None])
     pieces = lax.all_to_all(pieces_here, "z", 0, 0, tiled=True)
+    low_own = low_term(x_own, factor_in)
     low_oth = send(low_own, core_go)
     fout_got = send(fout_theirs, core_go)
 
     w_b, w_e, w_c, w_f, w_g = ([None] * CHAINS for _ in range(5))
     for h in chains:
-        own[h], w_a[h], w_d[h] = after((own[h], w_a[h], w_d[h]), low_own)
+        own[h], w_a[h], w_d[h] = after((own[h], w_a[h], w_d[h]))
         w_b[h] = send(own[h], y_bwd)
         w_e[h] = send(w_a[h], x_go)
     acc, token = group_matmul(0, places, x_own, x_oth, [own, w_a, w_d], None)
@@ -493,7 +505,7 @@
         w_a[h], w_b[h], w_e[h] = after((w_a[h], w_b[h], w_e[h]), token)
         w_c[h] = send(w_a[h], y_fwd)
         w_f[h] = send(w_b[h], x_go)
-    acc, token = group_matmul(3, places, x_own, x_oth, [w_b, w_e], acc)
+    acc, token = group_matmul(3, places, x_own, x_oth, [w_b, w_e], acc, extra=(low_own,))
     for h in chains:
         w_c[h], w_f[h], w_e[h] = after((w_c[h], w_f[h], w_e[h]), token)
         w_g[h] = send(w_c[h], x_go) if h == 0 else send(w_e[h], y_fwd)

time: 227 us -> 127 us (0.56)
  Pallas kernels: 137 us -> 37.9 us
  starting transfers between devices: 40.1 us -> 43.6 us
  waiting for transfers between devices: 21.8 us -> 18.6 us
    pallas_call x2 -> x3, Pallas kernels: 108 us -> 8.99 us  [the longest x1 4.02 us: cut_factors(): pl.pallas_call(cut_kernel, out_shape=(jax.ShapeDtypeStruct((Z, members, o...]
    ppermute x19, waiting for transfers between devices: 12.9 us -> 9.69 us  [send(): return lax.ppermute(v, AXES, pairs)]
  transfers between devices with their start and end apart: 22 -> 22, of which waited for: 7 -> 6; matrix products, arithmetic and copies ran while one was open for 0% -> 2% of each run, Pallas kernels for 58% -> 26%
where the time goes in v7:
time: 127 us
  starting transfers between devices  43.6 us (34%)
  Pallas kernels  37.9 us (30%)
  waiting for transfers between devices  18.6 us (15%)
  between operations  14.3 us (11%)
  blocking collectives  8.18 us (6%)
  local copies, waits for them, and re-layouts  2.6 us (2%)
  other arithmetic  1.67 us (1%)
    ppermute x19, starting transfers between devices, send(): return lax.ppermute(v, AXES, pairs)  24.7 us
    pallas_call x3, Pallas kernels, group_matmul(): pl.pallas_call(functools.partial(group_kernel, base, count, acc is not No...  20.2 us
    all_to_all x1, starting transfers between devices, share(): return lax.all_to_all(x, axes, 0, 0, tiled=True)  10.6 us
    ppermute x19, waiting for transfers between devices, send(): return lax.ppermute(v, AXES, pairs)  9.69 us
    all_to_all x1, waiting for transfers between devices, share(): return lax.all_to_all(x, axes, 0, 0, tiled=True)  8.83 us
    all_to_all x1, starting transfers between devices, shards(): pieces = lax.all_to_all(pieces_here, 'z', 0, 0, tiled=True)  8.2 us
    all_to_all x1, blocking collectives, share(): return lax.all_to_all(x, axes, 0, 0, tiled=True)  8.18 us
    pallas_call x1, Pallas kernels, weight_part(): pl.pallas_call(step_kernel, out_shape=(block, block, jax.ShapeDtypeStruct...  4.62 us
  transfers between devices with their start and end apart: 22, of which 6 were waited for; matrix products, arithmetic and copies ran while one was open for 2% of the time, Pallas kernels for 26%

profile of v7, /device:TPU:1, one launch (start us, length us, event | category | flops | bytes accessed | tf_op | source)
XLA Modules:
  0.0 126.7 jit_solution(15320222547919326058)
XLA Ops:
  7.2 3.3 %collective-permute-start.4 = (bf16[3,256,4096]{2,1,0:T(8,128)(2,1)}, bf16[3,256,4096]{2,1,0:T(8,128)(2,1)}, u32[]{:S(2)}, u32[]{:S(2)}) collective-permute-start(bf16[3,256,4096]{2,1,0:T(8,128)(2,1)} %bitcast.21), channel_id=1, source_target_pairs={{0,8},{1,9},{2,10},{3,11},{4,12},{5,13},{6,14},{7,15},{8,0},{9,1},... | collective-permute-start | bytes 18874376 | tf_op jit(solution)/shard_map/ppermute | solution.py:462
  11.2 2.5 %shard_map.82 = bf16[256,512]{1,0:T(8,128)(2,1)} custom-call(s32[11]{0:T(128)} %stack.47.kidx.place, bf16[256,4096]{1,0:T(8,128)(2,1)} %fin.3), custom_call_target="tpu_custom_call" | custom-call | tf_op jit(solution)/shard_map/pallas_call | solution.py:325
  13.7 1.3 %constant_dynamic-slice_fusion = (bf16[512,512]{1,0:T(8,128)(2,1)S(1)}, bf16[512,512]{1,0:T(8,128)(2,1)S(1)}) fusion(bf16[2048,512]{1,0:T(8,128)(2,1)} %param.6, s32[]{:T(128)S(6)} %select_n.7, s32[]{:T(128)S(6)} %select_n.6), kind=kLoop, calls=%fused_computation.3 | loop fusion | bytes 2097160 | tf_op jit(solution)/shard_map/dynamic_slice | solution.py:486
  16.1 2.5 %collective-permute-start.6 = (bf16[512,512]{1,0:T(8,128)(2,1)S(1)}, bf16[512,512]{1,0:T(8,128)(2,1)}, u32[]{:S(2)}, u32[]{:S(2)}) collective-permute-start(bf16[512,512]{1,0:T(8,128)(2,1)S(1)} %get-tuple-element.62.refs_0_), channel_id=1, source_target_pairs={{0,4},{1,5},{2,6},{3,7},{4,0},{5,1},{6,2},{7,3},{8,140},{9,141},{1... | collective-permute-start | bytes 1572872 | tf_op jit(solution)/shard_map/ppermute | solution.py:462
  19.2 4.0 %shard_map.78 = (bf16[8,256,256]{2,1,0:T(8,128)(2,1)}, bf16[256,1024]{1,0:T(8,128)(2,1)}, bf16[256,1024]{1,0:T(8,128)(2,1)}, f32[1,1024]{1,0:T(1,128)}) custom-call(s32[11]{0:T(128)} %stack.47.kidx.place, bf16[256,2048]{1,0:T(8,128)(2,1)} %fout_all.1, f32[1,2048]{1,0:T(1,128)} %bitcast.29), custom_call_target="tpu_custom_call" | custom-call | bytes 4194304 | tf_op jit(solution)/shard_map/pallas_call | solution.py:295
  23.2 8.2 %all-to-all-start = ((bf16[8,256,256]{2,1,0:T(8,128)(2,1)}), bf16[8,256,256]{2,1,0:T(8,128)(2,1)S(1)}, u32[]{:S(2)}, u32[]{:S(2)}) async-start(bf16[8,256,256]{2,1,0:T(8,128)(2,1)} %get-tuple-element.58), calls=%async_computation | async-start | bytes 2097152 | tf_op jit(solution)/shard_map/all_to_all | solution.py:493
  31.5 2.6 %collective-permute-start.10 = (bf16[512,512]{1,0:T(8,128)(2,1)S(1)}, bf16[512,512]{1,0:T(8,128)(2,1)S(1)}, u32[]{:S(2)}, u32[]{:S(2)}) collective-permute-start(bf16[512,512]{1,0:T(8,128)(2,1)S(1)} %get-tuple-element.35.refs_3_.refs_0_), channel_id=1, source_target_pairs={{0,4},{1,5},{2,6},{3,7},{4,0},{5,1},{6,2},{7,3},{8,140},{9,141},{1... | collective-permute-start | bytes 1572872 | tf_op jit(solution)/shard_map/ppermute | solution.py:462
  35.4 8.2 %shard_map.70 = (f32[2,3,256,1024]{3,2,1,0:T(8,128)S(1)}, f32[8,128]{1,0:T(8,128)S(1)}) custom-call(s32[11]{0:T(128)S(1)} %copy-done.3, bf16[3,256,4096]{2,1,0:T(8,128)(2,1)} %bitcast.22, bf16[3,256,4096]{2,1,0:T(8,128)(2,1)} %collective-permute-done.4.x_oth, bf16[512,512]{1,0:T(8,128)(2,1)S(1)} %get-tuple-element.33.refs_0_, ...), custom_call_target="tpu_custom_call" | custom-call | flops 4831838208 | bytes 8388608 | tf_op jit(solution)/shard_map/pallas_call | solution.py:152
  43.7 2.5 %collective-permute-start.12 = (bf16[512,512]{1,0:T(8,128)(2,1)S(1)}, bf16[512,512]{1,0:T(8,128)(2,1)S(1)}, u32[]{:S(2)}, u32[]{:S(2)}) collective-permute-start(bf16[512,512]{1,0:T(8,128)(2,1)S(1)} %get-tuple-element.47), channel_id=1, source_target_pairs={{0,1},{1,2},{2,3},{3,0},{4,5},{5,6},{6,7},{7,4},{8,11},{9,8},{10,9... | collective-permute-start | bytes 1572872 | tf_op jit(solution)/shard_map/ppermute | solution.py:462
  46.2 2.5 %collective-permute-start.13 = (bf16[512,512]{1,0:T(8,128)(2,1)S(1)}, bf16[512,512]{1,0:T(8,128)(2,1)S(1)}, u32[]{:S(2)}, u32[]{:S(2)}) collective-permute-start(bf16[512,512]{1,0:T(8,128)(2,1)S(1)} %get-tuple-element.42.refs_2_), channel_id=1, source_target_pairs={{0,4},{1,5},{2,6},{3,7},{4,0},{5,1},{6,2},{7,3},{8,140},{9,141},{1... | collective-permute-start | bytes 1572872 | tf_op jit(solution)/shard_map/ppermute | solution.py:462
  48.7 1.7 %collective-permute-done.2.refs_1_ = bf16[512,512]{1,0:T(8,128)(2,1)S(1)} collective-permute-done((bf16[512,512]{1,0:T(8,128)(2,1)S(1)}, bf16[512,512]{1,0:T(8,128)(2,1)S(1)}, u32[]{:S(2)}, u32[]{:S(2)}) %collective-permute-start.2) | collective-permute-done | bytes 524320 | tf_op jit(solution)/shard_map/ppermute | solution.py:462
  51.5 2.5 %shard_map.72.refs_0_.refs_4_ = f32[3,256,1]{2,1,0:T(8,128)S(1)} custom-call(bf16[3,256,4096]{2,1,0:T(8,128)(2,1)S(1)} %bitcast.27, bf16[256,4096]{1,0:T(8,128)(2,1)S(1)} %copy-done.1), custom_call_target="tpu_custom_call" | custom-call | flops 6291456 | bytes 9437184 | tf_op jit(solution)/shard_map/pallas_call | solution.py:367
  54.0 5.7 %shard_map.74 = (f32[2,3,256,1024]{3,2,1,0:T(8,128)S(1)}, f32[8,128]{1,0:T(8,128)S(1)}) custom-call(s32[11]{0:T(128)S(1)} %copy-done.3, bf16[3,256,4096]{2,1,0:T(8,128)(2,1)} %bitcast.23, bf16[3,256,4096]{2,1,0:T(8,128)(2,1)} %collective-permute-done.4.x_oth, f32[3,256,1]{2,1,0:T(8,128)S(1)} %shard_map.72.refs_0_.refs_4_, ...), custom_call_target="tpu_custom_call", output_to_operand_aliasing={{0}: (8, {})} | custom-call | flops 3221225472 | bytes 8388608 | tf_op jit(solution)/shard_map/pallas_call | solution.py:152
  59.7 1.7 %collective-permute-start.14 = (bf16[512,512]{1,0:T(8,128)(2,1)S(1)}, bf16[512,512]{1,0:T(8,128)(2,1)S(1)}, u32[]{:S(2)}, u32[]{:S(2)}) collective-permute-start(bf16[512,512]{1,0:T(8,128)(2,1)S(1)} %get-tuple-element.48), channel_id=1, source_target_pairs={{0,1},{1,2},{2,3},{3,0},{4,5},{5,6},{6,7},{7,4},{8,11},{9,8},{10,9... | collective-permute-start | bytes 1572872 | tf_op jit(solution)/shard_map/ppermute | solution.py:462
  61.4 3.1 %collective-permute-start.11 = (bf16[512,512]{1,0:T(8,128)(2,1)S(1)}, bf16[512,512]{1,0:T(8,128)(2,1)S(1)}, u32[]{:S(2)}, u32[]{:S(2)}) collective-permute-start(bf16[512,512]{1,0:T(8,128)(2,1)S(1)} %get-tuple-element.46.refs_2_), channel_id=1, source_target_pairs={{0,4},{1,5},{2,6},{3,7},{4,0},{5,1},{6,2},{7,3},{8,140},{9,141},{1... | collective-permute-start | bytes 1572872 | tf_op jit(solution)/shard_map/ppermute | solution.py:462
  64.6 6.3 %shard_map.77 = (f32[2,3,256,1024]{3,2,1,0:T(8,128)S(1)}, f32[8,128]{1,0:T(8,128)}, bf16[2,3,256,512]{3,2,1,0:T(8,128)(2,1)S(1)}) custom-call(s32[11]{0:T(128)S(1)} %copy-done.3, bf16[3,256,4096]{2,1,0:T(8,128)(2,1)} %bitcast.24, bf16[3,256,4096]{2,1,0:T(8,128)(2,1)} %collective-permute-done.4.x_oth, ...), custom_call_target="tpu_custom_call", output_to_operand_aliasing={{0}: (7, {})} | custom-call | flops 3221225472 | bytes 8388608 | tf_op jit(solution)/shard_map/pallas_call | solution.py:152
  71.5 3.4 %shard_map.79.refs_0_ = f32[16,1,512]{2,1,0:T(1,128)S(1)} custom-call(s32[11]{0:T(128)S(1)} %copy-done.3, bf16[512,512]{1,0:T(8,128)(2,1)S(1)} %collective-permute-done.11.refs_0_, bf16[512,512]{1,0:T(8,128)(2,1)S(1)} %collective-permute-done.14.refs_1_, bf16[2,3,256,512]{3,2,1,0:T(8,128)(2,1)S(1)} %get-tuple-element.53.refs_2_, ...), custom_call_target="tpu_custom_call" | custom-call | flops 1610612736 | bytes 6291456 | tf_op jit(solution)/shard_map/pallas_call | solution.py:218
  75.0 8.2 %all_to_all.15.got = f32[16,1,512]{2,1,0:T(1,128)S(1)} all-to-all(f32[16,1,512]{2,1,0:T(1,128)S(1)} %shard_map.80), channel_id=1, replica_groups=mesh['xh'=2,'z'=8,'core'=2,'xl'=2,'y'=4] {'core','xl','y'}, dimensions={0} | all-to-all | bytes 65536 | tf_op jit(solution)/shard_map/all_to_all | solution.py:449
  83.8 10.6 %all-to-all-start.2 = ((f32[16,1,512]{2,1,0:T(1,128)}), f32[16,1,512]{2,1,0:T(1,128)S(1)}, u32[]{:S(2)}, u32[]{:S(2)}) async-start(f32[16,1,512]{2,1,0:T(1,128)} %shard_map.81), calls=%async_computation.2 | async-start | bytes 65536 | tf_op jit(solution)/shard_map/all_to_all | solution.py:449
  94.5 8.8 %all-to-all-done.2.fit = f32[16,1,512]{2,1,0:T(1,128)S(1)} async-done(((f32[16,1,512]{2,1,0:T(1,128)}), f32[16,1,512]{2,1,0:T(1,128)S(1)}, u32[]{:S(2)}, u32[]{:S(2)}) %all-to-all-start.2) | async-done | bytes 32800 | tf_op jit(solution)/shard_map/all_to_all | solution.py:449
  104.0 4.6 %shard_map.83 = (f32[2,64,512]{2,1,0:T(8,128)}, f32[2,64,512]{2,1,0:T(8,128)}, f32[1,256]{1,0:T(1,128)}) custom-call(s32[11]{0:T(128)} %stack.47.kidx.place, f32[16,1,512]{2,1,0:T(1,128)} %copy-done.5, bf16[8,256,256]{2,1,0:T(8,128)(2,1)} %copy-done, bf16[8,256,512]{2,1,0:T(8,128)(2,1)} %bitcast.28), custom_call_target="tpu_custom_call" | custom-call | flops 536870912 | bytes 4194304 | tf_op jit(solution)/shard_map/pallas_call | solution.py:430
  108.6 1.9 %collective-permute-start.17 = (f32[2,64,512]{2,1,0:T(8,128)}, f32[2,64,512]{2,1,0:T(8,128)S(1)}, u32[]{:S(2)}, u32[]{:S(2)}) collective-permute-start(f32[2,64,512]{2,1,0:T(8,128)} %get-tuple-element.60), channel_id=1, source_target_pairs={{0,8},{1,9},{2,10},{3,11},{4,12},{5,13},{6,14},{7,15},{8,0},{9,1},... | collective-permute-start | bytes 786440 | tf_op jit(solution)/shard_map/ppermute | solution.py:462
  110.5 1.4 %collective-permute-done.17 = f32[2,64,512]{2,1,0:T(8,128)S(1)} collective-permute-done((f32[2,64,512]{2,1,0:T(8,128)}, f32[2,64,512]{2,1,0:T(8,128)S(1)}, u32[]{:S(2)}, u32[]{:S(2)}) %collective-permute-start.17) | collective-permute-done | bytes 262176 | tf_op jit(solution)/shard_map/ppermute | solution.py:462
  113.4 5.9 %collective-permute-done.18 = f32[64,512]{1,0:T(8,128)S(1)} collective-permute-done((f32[64,512]{1,0:T(8,128)S(1)}, f32[64,512]{1,0:T(8,128)S(1)}, u32[]{:S(2)}, u32[]{:S(2)}) %collective-permute-start.18) | collective-permute-done | bytes 131104 | tf_op jit(solution)/shard_map/ppermute | solution.py:462
  (62 shorter events, 9.0 us)
Async XLA Ops:
  7.2 87.4 %all-gather.3.cloned.1.call-start = ((), (), s32[]{:S(2)}) async-start(), calls=%async_computation.3 | async-start | bytes 2359296 | tf_op jit(solution)/shard_map/all_gather | solution.py:491
  7.2 28.1 %collective-permute-start.4 = (bf16[3,256,4096]{2,1,0:T(8,128)(2,1)}, bf16[3,256,4096]{2,1,0:T(8,128)(2,1)}, u32[]{:S(2)}, u32[]{:S(2)}) collective-permute-start(bf16[3,256,4096]{2,1,0:T(8,128)(2,1)} %bitcast.21), channel_id=1, source_target_pairs={{0,8},{1,9},{2,10},{3,11},{4,12},{5,13},{6,14},{7,15},{8,0},{9,1},... | collective-permute-start | bytes 18874376 | tf_op jit(solution)/shard_map/ppermute | solution.py:462
  11.2 24.1 %copy-start.3 = (s32[11]{0:T(128)S(1)}, s32[11]{0:T(128)}, u32[]{:S(2)}) copy-start(s32[11]{0:T(128)} %stack.47.kidx.place) | copy-start | bytes 136
  15.0 16.5 %collective-permute-start.5 = (bf16[512,512]{1,0:T(8,128)(2,1)S(1)}, bf16[512,512]{1,0:T(8,128)(2,1)S(1)}, u32[]{:S(2)}, u32[]{:S(2)}) collective-permute-start(bf16[512,512]{1,0:T(8,128)(2,1)S(1)} %get-tuple-element.62.refs_0_), channel_id=1, source_target_pairs={{0,1},{1,2},{2,3},{3,0},{4,5},{5,6},{6,7},{7,4},{8,11},{9,8},{10,9... | collective-permute-start | bytes 1572872 | tf_op jit(solution)/shard_map/ppermute | solution.py:462
  16.1 15.4 %collective-permute-start.6 = (bf16[512,512]{1,0:T(8,128)(2,1)S(1)}, bf16[512,512]{1,0:T(8,128)(2,1)}, u32[]{:S(2)}, u32[]{:S(2)}) collective-permute-start(bf16[512,512]{1,0:T(8,128)(2,1)S(1)} %get-tuple-element.62.refs_0_), channel_id=1, source_target_pairs={{0,4},{1,5},{2,6},{3,7},{4,0},{5,1},{6,2},{7,3},{8,140},{9,141},{1... | collective-permute-start | bytes 1572872 | tf_op jit(solution)/shard_map/ppermute | solution.py:462
  18.5 16.5 %collective-permute-start = (bf16[512,512]{1,0:T(8,128)(2,1)S(1)}, bf16[512,512]{1,0:T(8,128)(2,1)S(1)}, u32[]{:S(2)}, u32[]{:S(2)}) collective-permute-start(bf16[512,512]{1,0:T(8,128)(2,1)S(1)} %get-tuple-element.63.refs_0_), channel_id=1, source_target_pairs={{0,1},{1,2},{2,3},{3,0},{4,5},{5,6},{6,7},{7,4},{8,11},{9,8},{10,9... | collective-permute-start | bytes 1572872 | tf_op jit(solution)/shard_map/ppermute | solution.py:462
  19.0 16.0 %collective-permute-start.1 = (bf16[512,512]{1,0:T(8,128)(2,1)S(1)}, bf16[512,512]{1,0:T(8,128)(2,1)}, u32[]{:S(2)}, u32[]{:S(2)}) collective-permute-start(bf16[512,512]{1,0:T(8,128)(2,1)S(1)} %get-tuple-element.63.refs_0_), channel_id=1, source_target_pairs={{0,4},{1,5},{2,6},{3,7},{4,0},{5,1},{6,2},{7,3},{8,140},{9,141},{1... | collective-permute-start | bytes 1572872 | tf_op jit(solution)/shard_map/ppermute | solution.py:462
  23.2 51.7 %all-to-all-start = ((bf16[8,256,256]{2,1,0:T(8,128)(2,1)}), bf16[8,256,256]{2,1,0:T(8,128)(2,1)S(1)}, u32[]{:S(2)}, u32[]{:S(2)}) async-start(bf16[8,256,256]{2,1,0:T(8,128)(2,1)} %get-tuple-element.58), calls=%async_computation | async-start | bytes 2097152 | tf_op jit(solution)/shard_map/all_to_all | solution.py:493
  31.5 12.1 %collective-permute-start.10 = (bf16[512,512]{1,0:T(8,128)(2,1)S(1)}, bf16[512,512]{1,0:T(8,128)(2,1)S(1)}, u32[]{:S(2)}, u32[]{:S(2)}) collective-permute-start(bf16[512,512]{1,0:T(8,128)(2,1)S(1)} %get-tuple-element.35.refs_3_.refs_0_), channel_id=1, source_target_pairs={{0,4},{1,5},{2,6},{3,7},{4,0},{5,1},{6,2},{7,3},{8,140},{9,141},{1... | collective-permute-start | bytes 1572872 | tf_op jit(solution)/shard_map/ppermute | solution.py:462
  34.0 9.6 %collective-permute-start.9 = (bf16[512,512]{1,0:T(8,128)(2,1)S(1)}, bf16[512,512]{1,0:T(8,128)(2,1)S(1)}, u32[]{:S(2)}, u32[]{:S(2)}) collective-permute-start(bf16[512,512]{1,0:T(8,128)(2,1)S(1)} %get-tuple-element.34.refs_1_), channel_id=1, source_target_pairs={{0,3},{1,0},{2,1},{3,2},{4,7},{5,4},{6,5},{7,6},{8,9},{9,10},{10,1... | collective-permute-start | bytes 1572872 | tf_op jit(solution)/shard_map/ppermute | solution.py:462
  35.0 13.7 %collective-permute-start.3 = (bf16[512,512]{1,0:T(8,128)(2,1)S(1)}, bf16[512,512]{1,0:T(8,128)(2,1)S(1)}, u32[]{:S(2)}, u32[]{:S(2)}) collective-permute-start(bf16[512,512]{1,0:T(8,128)(2,1)S(1)} %get-tuple-element.32.refs_2_.refs_0_), channel_id=1, source_target_pairs={{0,4},{1,5},{2,6},{3,7},{4,0},{5,1},{6,2},{7,3},{8,140},{9,141},{1... | collective-permute-start | bytes 1572872 | tf_op jit(solution)/shard_map/ppermute | solution.py:462
  35.2 15.2 %collective-permute-start.2 = (bf16[512,512]{1,0:T(8,128)(2,1)S(1)}, bf16[512,512]{1,0:T(8,128)(2,1)S(1)}, u32[]{:S(2)}, u32[]{:S(2)}) collective-permute-start(bf16[512,512]{1,0:T(8,128)(2,1)S(1)} %get-tuple-element.33.refs_0_), channel_id=1, source_target_pairs={{0,3},{1,0},{2,1},{3,2},{4,7},{5,4},{6,5},{7,6},{8,9},{9,10},{10,1... | collective-permute-start | bytes 1572872 | tf_op jit(solution)/shard_map/ppermute | solution.py:462
  43.7 16.0 %collective-permute-start.12 = (bf16[512,512]{1,0:T(8,128)(2,1)S(1)}, bf16[512,512]{1,0:T(8,128)(2,1)S(1)}, u32[]{:S(2)}, u32[]{:S(2)}) collective-permute-start(bf16[512,512]{1,0:T(8,128)(2,1)S(1)} %get-tuple-element.47), channel_id=1, source_target_pairs={{0,1},{1,2},{2,3},{3,0},{4,5},{5,6},{6,7},{7,4},{8,11},{9,8},{10,9... | collective-permute-start | bytes 1572872 | tf_op jit(solution)/shard_map/ppermute | solution.py:462
  46.2 13.5 %collective-permute-start.13 = (bf16[512,512]{1,0:T(8,128)(2,1)S(1)}, bf16[512,512]{1,0:T(8,128)(2,1)S(1)}, u32[]{:S(2)}, u32[]{:S(2)}) collective-permute-start(bf16[512,512]{1,0:T(8,128)(2,1)S(1)} %get-tuple-element.42.refs_2_), channel_id=1, source_target_pairs={{0,4},{1,5},{2,6},{3,7},{4,0},{5,1},{6,2},{7,3},{8,140},{9,141},{1... | collective-permute-start | bytes 1572872 | tf_op jit(solution)/shard_map/ppermute | solution.py:462
  50.4 11.0 %collective-permute-start.7 = (bf16[512,512]{1,0:T(8,128)(2,1)S(1)}, bf16[512,512]{1,0:T(8,128)(2,1)S(1)}, u32[]{:S(2)}, u32[]{:S(2)}) collective-permute-start(bf16[512,512]{1,0:T(8,128)(2,1)S(1)} %get-tuple-element.39), channel_id=1, source_target_pairs={{0,1},{1,2},{2,3},{3,0},{4,5},{5,6},{6,7},{7,4},{8,11},{9,8},{10,9... | collective-permute-start | bytes 1572872 | tf_op jit(solution)/shard_map/ppermute | solution.py:462
  50.4 11.0 %collective-permute-start.8 = (bf16[512,512]{1,0:T(8,128)(2,1)S(1)}, bf16[512,512]{1,0:T(8,128)(2,1)S(1)}, u32[]{:S(2)}, u32[]{:S(2)}) collective-permute-start(bf16[512,512]{1,0:T(8,128)(2,1)S(1)} %get-tuple-element.40.refs_1_), channel_id=1, source_target_pairs={{0,4},{1,5},{2,6},{3,7},{4,0},{5,1},{6,2},{7,3},{8,140},{9,141},{1... | collective-permute-start | bytes 1572872 | tf_op jit(solution)/shard_map/ppermute | solution.py:462
  50.4 20.5 %collective-permute-start.16 = (bf16[256,1024]{1,0:T(8,128)(2,1)S(1)}, bf16[256,1024]{1,0:T(8,128)(2,1)S(1)}, u32[]{:S(2)}, u32[]{:S(2)}) collective-permute-start(bf16[256,1024]{1,0:T(8,128)(2,1)S(1)} %copy-done.6), channel_id=1, source_target_pairs={{0,8},{1,9},{2,10},{3,11},{4,12},{5,13},{6,14},{7,15},{8,0},{9,1},... | collective-permute-start | bytes 1572872 | tf_op jit(solution)/shard_map/ppermute | solution.py:462
  59.7 11.2 %collective-permute-start.14 = (bf16[512,512]{1,0:T(8,128)(2,1)S(1)}, bf16[512,512]{1,0:T(8,128)(2,1)S(1)}, u32[]{:S(2)}, u32[]{:S(2)}) collective-permute-start(bf16[512,512]{1,0:T(8,128)(2,1)S(1)} %get-tuple-element.48), channel_id=1, source_target_pairs={{0,1},{1,2},{2,3},{3,0},{4,5},{5,6},{6,7},{7,4},{8,11},{9,8},{10,9... | collective-permute-start | bytes 1572872 | tf_op jit(solution)/shard_map/ppermute | solution.py:462
  61.4 10.1 %collective-permute-start.11 = (bf16[512,512]{1,0:T(8,128)(2,1)S(1)}, bf16[512,512]{1,0:T(8,128)(2,1)S(1)}, u32[]{:S(2)}, u32[]{:S(2)}) collective-permute-start(bf16[512,512]{1,0:T(8,128)(2,1)S(1)} %get-tuple-element.46.refs_2_), channel_id=1, source_target_pairs={{0,4},{1,5},{2,6},{3,7},{4,0},{5,1},{6,2},{7,3},{8,140},{9,141},{1... | collective-permute-start | bytes 1572872 | tf_op jit(solution)/shard_map/ppermute | solution.py:462
  64.6 6.3 %collective-permute-start.15 = (f32[3,256,1]{2,1,0:T(8,128)S(1)}, f32[3,256,1]{2,1,0:T(8,128)S(1)}, u32[]{:S(2)}, u32[]{:S(2)}) collective-permute-start(f32[3,256,1]{2,1,0:T(8,128)S(1)} %shard_map.72.refs_0_.refs_4_), channel_id=1, source_target_pairs={{0,8},{1,9},{2,10},{3,11},{4,12},{5,13},{6,14},{7,15},{8,0},{9,1},... | collective-permute-start | bytes 9224 | tf_op jit(solution)/shard_map/ppermute | solution.py:462
  75.0 28.4 %copy-start = (bf16[8,256,256]{2,1,0:T(8,128)(2,1)}, bf16[8,256,256]{2,1,0:T(8,128)(2,1)S(1)}, u32[]{:S(2)}) copy-start(bf16[8,256,256]{2,1,0:T(8,128)(2,1)S(1)} %all-to-all-done.refs_1_.fout_all) | copy-start | bytes 3145732
  83.8 19.5 %all-to-all-start.2 = ((f32[16,1,512]{2,1,0:T(1,128)}), f32[16,1,512]{2,1,0:T(1,128)S(1)}, u32[]{:S(2)}, u32[]{:S(2)}) async-start(f32[16,1,512]{2,1,0:T(1,128)} %shard_map.81), calls=%async_computation.2 | async-start | bytes 65536 | tf_op jit(solution)/shard_map/all_to_all | solution.py:449
  108.6 3.3 %collective-permute-start.17 = (f32[2,64,512]{2,1,0:T(8,128)}, f32[2,64,512]{2,1,0:T(8,128)S(1)}, u32[]{:S(2)}, u32[]{:S(2)}) collective-permute-start(f32[2,64,512]{2,1,0:T(8,128)} %get-tuple-element.60), channel_id=1, source_target_pairs={{0,8},{1,9},{2,10},{3,11},{4,12},{5,13},{6,14},{7,15},{8,0},{9,1},... | collective-permute-start | bytes 786440 | tf_op jit(solution)/shard_map/ppermute | solution.py:462
  112.9 6.3 %collective-permute-start.18 = (f32[64,512]{1,0:T(8,128)S(1)}, f32[64,512]{1,0:T(8,128)S(1)}, u32[]{:S(2)}, u32[]{:S(2)}) collective-permute-start(f32[64,512]{1,0:T(8,128)S(1)} %slice_bitcast_fusion), channel_id=1, source_target_pairs={{0,128},{1,129},{2,130},{3,131},{4,132},{5,133},{6,134},{7,135},{8... | collective-permute-start | bytes 393224 | tf_op jit(solution)/shard_map/ppermute | solution.py:462
  (7 other events, 77.9 us)
Sparse Core Ops, SparseCore 0:
  13.8 59.8 all-gather.2

commit v8 on v7

--- a/solution.py
+++ b/solution.py
@@ -15,7 +15,6 @@
 AXES = ("xh", "z", "core", "xl", "y")
 SIZES = (XH, Z, CORE, XL, Y)
 WA = XL * Y
-CHAINS = 2
 ROWS_ALL = 24
 VMEM_BYTES = 40 * 1024 * 1024
 LAST_BYTES = 40 * 1024 * 1024
@@ -65,53 +64,46 @@
 
 
 def fetch(kidx, base, x_own, x_oth, sent, ws, w_sems, buffers, sems):
-    count, part, block = len(sent), sent[0][0].shape[0], sent[0][0].shape[1]
+    block = ws.shape[2]
     copies = [[], []]
     for side, x in ((0, x_own), (1, x_oth)):
-        for s in range(count):
+        for s, parts in enumerate(sent):
             cols = pl.ds(pl.multiple_of(kidx[base + s] * block, block), block)
             copies[side].append(
                 pltpu.make_async_copy(x.at[:, :, cols], buffers.at[s, side], sems.at[s, side])
             )
             if side == 0:
-                for h in range(CHAINS):
-                    to = ws.at[s, pl.ds(h * part, part), :]
-                    copies[side].append(pltpu.make_async_copy(sent[s][h], to, w_sems.at[s, h]))
+                rows = parts[0].shape[0]
+                for h, part in enumerate(parts):
+                    to = ws.at[s, pl.ds(h * rows, rows), :]
+                    copies[side].append(pltpu.make_async_copy(part, to, w_sems.at[s, h]))
     return copies
 
 
-def fetch_scratch(count, members, width, block):
-    return [
-        pltpu.VMEM((count, width, block), jnp.bfloat16),
-        pltpu.SemaphoreType.DMA((count, CHAINS)),
-        pltpu.VMEM((count, 2, 3, members, block), jnp.bfloat16),
-        pltpu.SemaphoreType.DMA((count, 2)),
-    ]
-
-
-def pairs(refs):
-    return [refs[i : i + CHAINS] for i in range(0, len(refs), CHAINS)]
-
-
-def group_kernel(base, count, has_acc, ahead, extra, kidx, x_own, x_oth, *refs):
-    refs = refs[extra:]
-    sent = pairs(refs[: count * CHAINS])
-    acc_in = refs[count * CHAINS] if has_acc else None
-    if ahead:
-        *refs, x_last, ws, w_sems, buffers, sems, last_sems = refs
-        refs = (*refs, ws, w_sems, buffers, sems)
-    out, token, ws, w_sems, buffers, sems = refs[-6:]
+def group_kernel(base, counts, has_acc, ahead, extra, hand, kidx, x_own, x_oth, *refs):
+    refs = list(refs[extra:])
+    sent = []
+    for n in counts:
+        sent.append(refs[:n])
+        refs = refs[n:]
+    acc_in = refs.pop(0) if has_acc else None
+    out = refs.pop(0)
+    handed = [refs.pop(0) for _ in hand]
+    x_last = refs.pop(0) if ahead else None
+    ws, w_sems, buffers, sems, more_sems = refs
     members, width = out.shape[2], out.shape[3]
     block = ws.shape[2]
     copies = fetch(kidx, base, x_own, x_oth, sent, ws, w_sems, buffers, sems)
     for copy in copies[0]:
         copy.start()
     early = []
+    for i, (s, row) in enumerate(hand):
+        source = ws.at[s, pl.ds(row, handed[i].shape[0]), :]
+        early.append(pltpu.make_async_copy(source, handed[i], more_sems.at[i]))
     if ahead:
-        cols = pl.ds(pl.multiple_of(kidx[base + count] * block, block), block)
+        cols = pl.ds(pl.multiple_of(kidx[base + len(counts)] * block, block), block)
         for side, x in ((0, x_own), (1, x_oth)):
-            early.append(pltpu.make_async_copy(x.at[:, :, cols], x_last.at[side], last_sems.at[side]))
-    token[...] = jnp.zeros_like(token)
+            early.append(pltpu.make_async_copy(x.at[:, :, cols], x_last.at[side], more_sems.at[2 + side]))
     chunk = 512
     for side in range(2):
         for copy in copies[side]:
@@ -122,7 +114,7 @@
         for j in range(0, width, chunk):
             cols = pl.ds(j, chunk)
             total = None
-            for s in range(count):
+            for s in range(len(counts)):
                 part = nt_dot(buffers[s, side].reshape(3 * members, block), ws[s, cols, :])
                 total = part if total is None else total + part
             total = total.reshape(3, members, chunk)
@@ -133,11 +125,11 @@
         copy.wait()
 
 
-def group_matmul(base, kidx, x_own, x_oth, sent, acc, ahead=False, extra=()):
-    count = len(sent)
+def group_matmul(base, kidx, x_own, x_oth, sent, acc, ahead=False, extra=(), hand=(), hand_rows=0):
+    counts = [len(parts) for parts in sent]
     members = x_own.shape[1]
-    part, block = sent[0][0].shape
-    width = part * CHAINS
+    block = sent[0][0].shape[1]
+    width = sent[0][0].shape[0] * counts[0]
     smem = pl.BlockSpec(memory_space=pltpu.SMEM)
     vmem = pl.BlockSpec(memory_space=pltpu.VMEM)
     hbm = pl.BlockSpec(memory_space=pl.ANY)
@@ -148,52 +140,64 @@
         specs.append(vmem)
         args.append(acc)
         alias = {len(args): 0}
-    flops = 2 * 2 * 3 * members * width * block * count
-    return pl.pallas_call(
-        functools.partial(group_kernel, base, count, acc is not None, ahead, len(extra)),
-        out_shape=(
-            jax.ShapeDtypeStruct((2, 3, members, width), jnp.float32),
-            jax.ShapeDtypeStruct((8, 128), jnp.float32),
-        )
-        + ((jax.ShapeDtypeStruct((2, 3, members, block), x_own.dtype),) if ahead else ()),
+    shapes = [jax.ShapeDtypeStruct((2, 3, members, width), jnp.float32)]
+    outs = [vmem]
+    for _ in hand:
+        shapes.append(jax.ShapeDtypeStruct((hand_rows, block), jnp.bfloat16))
+        outs.append(hbm)
+    if ahead:
+        shapes.append(jax.ShapeDtypeStruct((2, 3, members, block), x_own.dtype))
+        outs.append(vmem)
+    flops = 2 * 2 * 3 * members * width * block * len(counts)
+    return pl.pallas_call(
+        functools.partial(group_kernel, base, counts, acc is not None, ahead, len(extra), hand),
+        out_shape=tuple(shapes),
         in_specs=specs,
-        out_specs=(vmem,) * (3 if ahead else 2),
-        scratch_shapes=fetch_scratch(count, members, width, block)
-        + ([pltpu.SemaphoreType.DMA((2,))] if ahead else []),
+        out_specs=tuple(outs),
+        scratch_shapes=[
+            pltpu.VMEM((len(counts), width, block), jnp.bfloat16),
+            pltpu.SemaphoreType.DMA((len(counts), 2)),
+            pltpu.VMEM((len(counts), 2, 3, members, block), jnp.bfloat16),
+            pltpu.SemaphoreType.DMA((len(counts), 2)),
+            pltpu.SemaphoreType.DMA((4,)),
+        ],
         input_output_aliases=alias,
         compiler_params=pltpu.CompilerParams(vmem_limit_bytes=VMEM_BYTES),
         cost_estimate=pl.CostEstimate(flops=flops, bytes_accessed=8 * 1024 * 1024, transcendentals=0),
     )(kidx, *args)
 
 
-def last_kernel(kidx, *refs):
-    sent = refs[:CHAINS]
-    x, acc, low_own, low_oth, fout_own, fout_oth, readout, out, ws, w_sems = refs[CHAINS:]
+def last_kernel(kidx, w_lo, w_hi, fout_mine, fout_theirs, x, acc, low_own, low_oth, readout, out, ws, w_sems, fouts, f_sems):
     members, width = acc.shape[2], acc.shape[3]
     block = ws.shape[1]
-    part_rows = sent[0].shape[0]
+    rows = w_lo.shape[0]
+    first = pl.multiple_of(kidx[8] * width, width)
     copies = []
-    for h in range(CHAINS):
-        to = ws.at[pl.ds(h * part_rows, part_rows), :]
-        copies.append(pltpu.make_async_copy(sent[h], to, w_sems.at[h]))
-        copies[-1].start()
+    for h, part in enumerate((w_lo, w_hi)):
+        copies.append(pltpu.make_async_copy(part, ws.at[pl.ds(h * rows, rows), :], w_sems.at[h]))
+    moves = []
+    for side, fout in ((0, fout_mine), (1, fout_theirs)):
+        moves.append(pltpu.make_async_copy(fout.at[:, pl.ds(first, width)], fouts.at[side], f_sems.at[side]))
+    for copy in copies + moves:
+        copy.start()
     for copy in copies:
         copy.wait()
     chunk = 256
     ones = jnp.ones((8, 128), jnp.float32)
-    for side, low, fout in ((0, low_own, fout_own), (1, low_oth, fout_oth)):
+    for side, low in ((0, low_own), (1, low_oth)):
+        moves[side].wait()
         total = jnp.zeros((members, 128), jnp.float32)
         for j in range(0, width, chunk):
             cols = pl.ds(j, chunk)
             part = nt_dot(x[side].reshape(3 * members, block), ws[cols, :])
             part = part.reshape(3, members, chunk)
-            shift = fout[:, cols].astype(jnp.float32)
+            shift = fouts[side, :, cols].astype(jnp.float32)
             summed = None
             for r in range(3):
                 pert = part[r] + acc[side, r, :, cols] + low[r] * shift
                 term = jnp.tanh(pert)
                 summed = term if summed is None else summed + term
-            summed = summed * readout[:, cols]
+            summed = summed * readout[:, pl.ds(pl.multiple_of(first + j, chunk), chunk)]
             for h in range(0, chunk, 128):
                 total = total + summed[:, h : h + 128]
         row = lax.dot_general(
@@ -208,21 +212,23 @@
             out[k, :, at] = row
 
 
-def last_matmul(kidx, sent, x, acc, low_own, low_oth, fout_own, fout_oth, readout):
+def last_matmul(kidx, w_lo, w_hi, fout_mine, fout_theirs, x, acc, low_own, low_oth, readout):
     members = x.shape[2]
-    part, block = sent[0].shape
-    width = part * CHAINS
+    block = w_lo.shape[1]
+    width = acc.shape[3]
     smem = pl.BlockSpec(memory_space=pltpu.SMEM)
     vmem = pl.BlockSpec(memory_space=pltpu.VMEM)
     hbm = pl.BlockSpec(memory_space=pl.ANY)
     return pl.pallas_call(
         last_kernel,
         out_shape=jax.ShapeDtypeStruct((CORE * WA, 1, 2 * members), jnp.float32),
-        in_specs=[smem] + [hbm] * CHAINS + [vmem] * 7,
+        in_specs=[smem] + [hbm] * 4 + [vmem] * 5,
         out_specs=vmem,
         scratch_shapes=[
             pltpu.VMEM((width, block), jnp.bfloat16),
-            pltpu.SemaphoreType.DMA((CHAINS,)),
+            pltpu.SemaphoreType.DMA((2,)),
+            pltpu.VMEM((2, members, width), jnp.bfloat16),
+            pltpu.SemaphoreType.DMA((2,)),
         ],
         compiler_params=pltpu.CompilerParams(vmem_limit_bytes=LAST_BYTES),
         cost_estimate=pl.CostEstimate(
@@ -230,7 +236,7 @@
             bytes_accessed=6 * 1024 * 1024,
             transcendentals=6 * members * width,
         ),
-    )(kidx, *sent, x, acc, low_own, low_oth, fout_own, fout_oth, readout)
+    )(kidx, w_lo, w_hi, fout_mine, fout_theirs, x, acc, low_own, low_oth, readout)
 
 
 def after_kernel(*refs):
@@ -265,50 +271,30 @@
     )(got)
 
 
-def cut_kernel(place, fout_all, readout, pieces, mine, theirs, read, fout, sems):
-    half = mine.shape[1]
-    first = pltpu.make_async_copy(fout_all, fout, sems.at[0])
-    first.start()
-    read[...] = readout[:, pl.ds(pl.multiple_of(place[8] * half, half), half)]
-    moves = []
-    run = pieces.shape[2] // XH
+def cut_kernel(fout, pieces, token):
+    token[...] = jnp.zeros_like(token)
+    half = fout.shape[1] // XH
+    run = pieces.shape[1] // XH
     for h in range(XH):
         for k in range(Z):
             cols = pl.ds(h * half + k * run, run)
-            moves.append((fout.at[:, cols], pieces.at[k, :, pl.ds(h * run, run)]))
-    for at, to in ((place[8], mine), (1 - place[8], theirs)):
-        cols = pl.ds(pl.multiple_of(at * half, half), half)
-        moves.append((fout.at[:, cols], to))
-    copies = [pltpu.make_async_copy(x, y, sems.at[i + 1]) for i, (x, y) in enumerate(moves)]
-    first.wait()
-    for copy in copies:
-        copy.start()
-    for copy in copies:
-        copy.wait()
-
-
-def cut_factors(place, fout, readout):
+            pieces[k, pl.ds(h * run, run), :] = jnp.transpose(fout[:, cols])
+
+
+def cut_factors(fout):
     members, out_width = fout.shape
-    half = out_width // CORE
-    hbm = pl.BlockSpec(memory_space=pl.ANY)
     vmem = pl.BlockSpec(memory_space=pltpu.VMEM)
     return pl.pallas_call(
         cut_kernel,
         out_shape=(
-            jax.ShapeDtypeStruct((Z, members, out_width // Z), fout.dtype),
-            jax.ShapeDtypeStruct((members, half), fout.dtype),
-            jax.ShapeDtypeStruct((members, half), fout.dtype),
-            jax.ShapeDtypeStruct((1, half), readout.dtype),
+            jax.ShapeDtypeStruct((Z, out_width // Z, members), fout.dtype),
+            jax.ShapeDtypeStruct((8, 128), jnp.float32),
         ),
-        in_specs=[pl.BlockSpec(memory_space=pltpu.SMEM), hbm, vmem],
-        out_specs=(hbm, hbm, hbm, vmem),
-        scratch_shapes=[
-            pltpu.VMEM(fout.shape, fout.dtype),
-            pltpu.SemaphoreType.DMA((3 + XH * Z,)),
-        ],
+        in_specs=[vmem],
+        out_specs=(vmem, vmem),
         compiler_params=pltpu.CompilerParams(vmem_limit_bytes=LARGE_BYTES),
         cost_estimate=pl.CostEstimate(flops=0, bytes_accessed=4 * 1024 * 1024, transcendentals=0),
-    )(place, fout, readout)
+    )(fout)
 
 
 def block_kernel(place, fin, *refs):
@@ -332,7 +318,8 @@
     )(place, fin, *done)
 
 
-def low_kernel(x, fin, out, x_buf, f_buf, sems):
+def low_kernel(x, fin, out, token, x_buf, f_buf, sems):
+    token[...] = jnp.zeros_like(token)
     tiles, rows, tile, width = x_buf.shape
     copies = []
     for t in range(tiles):
@@ -366,22 +353,25 @@
     hbm = pl.BlockSpec(memory_space=pl.ANY)
     return pl.pallas_call(
         low_kernel,
-        out_shape=jax.ShapeDtypeStruct((rows, members, 1), jnp.float32),
+        out_shape=(
+            jax.ShapeDtypeStruct((rows, members, 1), jnp.float32),
+            jax.ShapeDtypeStruct((8, 128), jnp.float32),
+        ),
         in_specs=[hbm, hbm],
-        out_specs=pl.BlockSpec(memory_space=pltpu.VMEM),
+        out_specs=(pl.BlockSpec(memory_space=pltpu.VMEM),) * 2,
         scratch_shapes=[
             pltpu.VMEM((tiles, rows, tile, width), jnp.bfloat16),
             pltpu.VMEM((tiles, tile, width), jnp.bfloat16),
             pltpu.SemaphoreType.DMA((tiles, 2)),
         ],
-        compiler_params=pltpu.CompilerParams(vmem_limit_bytes=VMEM_BYTES),
+        compiler_params=pltpu.CompilerParams(vmem_limit_bytes=LARGE_BYTES),
         cost_estimate=pl.CostEstimate(
             flops=2 * rows * members * width, bytes_accessed=9 * 1024 * 1024, transcendentals=0
         ),
     )(x, fin)
 
 
-def step_kernel(place, fit, fout_all, fin_all, keep, give, util, rows_ref, fout, fin, sems):
+def step_kernel(place, fit, fout_all, fin_all, keep, give, util, fout, fin, sems):
     copies = []
     for k in range(Z):
         pair = (
@@ -400,17 +390,13 @@
     c, xh, z = place[8], place[9], place[10]
     at = pl.ds(pl.multiple_of(c * members, members), members)
     util[...] = (fit[xh * Z + z, :, at] - mean) / root
-    for k in range(Z):
-        rows_ref[k : k + 1, :] = fit[xh * Z + k, :, at]
-    columns = (jnp.transpose(rows_ref[...]) - mean) / root
     total = None
     for k in range(Z):
         for copy in copies[k]:
             copy.wait()
-        scaled = (fout[k].astype(jnp.float32) * columns[:, k : k + 1]).astype(jnp.bfloat16)
-        one = lax.dot_general(
-            scaled, fin[k], (((0,), (0,)), ((), ())), preferred_element_type=jnp.float32
-        )
+        row = (fit[xh * Z + k, :, at] - mean) / root
+        scaled = (fout[k].astype(jnp.float32) * row).astype(jnp.bfloat16)
+        one = jnp.dot(scaled, fin[k], preferred_element_type=jnp.float32)
         total = one if total is None else total + one
     total = total * (1.0 / np.sqrt(float(count)))
     rows = keep.shape[1]
@@ -422,7 +408,7 @@
 
 
 def weight_part(place, fit, fout, fin):
-    members, rows = fout.shape[1], fout.shape[2]
+    rows, members = fout.shape[1], fout.shape[2]
     cols = fin.shape[2]
     vmem = pl.BlockSpec(memory_space=pltpu.VMEM)
     hbm = pl.BlockSpec(memory_space=pl.ANY)
@@ -433,7 +419,6 @@
         in_specs=[pl.BlockSpec(memory_space=pltpu.SMEM), vmem, hbm, hbm],
         out_specs=(vmem, vmem, vmem),
         scratch_shapes=[
-            pltpu.VMEM((Z, members), jnp.float32),
             pltpu.VMEM(fout.shape, fout.dtype),
             pltpu.VMEM(fin.shape, fin.dtype),
             pltpu.SemaphoreType.DMA((Z, 2)),
@@ -481,37 +466,36 @@
 
     places = jnp.stack([k_own, k_a, k_d, k_b, k_e, k_f, k_c, k_g, c, xh, z]).astype(jnp.int32)
 
-    part = half // CHAINS
-    chains = range(CHAINS)
-    own = [lax.dynamic_slice_in_dim(weight, c * half + h * part, part, 0) for h in chains]
-    w_a = [send(w, y_fwd) for w in own]
-    w_d = [send(w, x_go) for w in own]
+    own = lax.dynamic_slice_in_dim(weight, c * half, half, 0)
+    w_a = send(own, y_fwd)
+    w_d = send(own, x_go)
     x_oth = send(x_own, core_go)
+    fout_oth = send(factor_out, core_go)
 
     fin_all = lax.all_gather(cut_block(places, factor_in, block), "z", axis=0)
-    pieces_here, fout_mine, fout_theirs, read_mine = cut_factors(places, factor_out, readout[None])
+    pieces_here, cut_done = cut_factors(factor_out)
     pieces = lax.all_to_all(pieces_here, "z", 0, 0, tiled=True)
-    low_own = low_term(x_own, factor_in)
+    low_own, low_done = low_term(x_own, factor_in)
     low_oth = send(low_own, core_go)
-    fout_got = send(fout_theirs, core_go)
-
-    w_b, w_e, w_c, w_f, w_g = ([None] * CHAINS for _ in range(5))
-    for h in chains:
-        own[h], w_a[h], w_d[h] = after((own[h], w_a[h], w_d[h]))
-        w_b[h] = send(own[h], y_bwd)
-        w_e[h] = send(w_a[h], x_go)
-    acc, token = group_matmul(0, places, x_own, x_oth, [own, w_a, w_d], None)
-    for h in chains:
-        w_a[h], w_b[h], w_e[h] = after((w_a[h], w_b[h], w_e[h]), token)
-        w_c[h] = send(w_a[h], y_fwd)
-        w_f[h] = send(w_b[h], x_go)
-    acc, token = group_matmul(3, places, x_own, x_oth, [w_b, w_e], acc, extra=(low_own,))
-    for h in chains:
-        w_c[h], w_f[h], w_e[h] = after((w_c[h], w_f[h], w_e[h]), token)
-        w_g[h] = send(w_c[h], x_go) if h == 0 else send(w_e[h], y_fwd)
-    acc, token, x_last = group_matmul(5, places, x_own, x_oth, [w_f, w_c], acc, ahead=True)
+
+    part = half // 2
+    own, w_a, w_d = after((own, w_a, w_d), cut_done, low_done)
+    w_b = send(own, y_bwd)
+    w_e = send(w_a, x_go)
+    acc, a_on = group_matmul(
+        0, places, x_own, x_oth, [[own], [w_a], [w_d]], None, hand=((1, 0),), hand_rows=half
+    )
+    w_c = send(a_on, y_fwd)
+    w_b, w_e = after((w_b, w_e), a_on)
+    w_f = send(w_b, x_go)
+    acc, e_hi = group_matmul(
+        3, places, x_own, x_oth, [[w_b], [w_e]], acc, hand=((1, part),), hand_rows=part
+    )
+    g_lo = send(w_c[:part], x_go)
+    g_hi = send(e_hi, y_fwd)
+    acc, x_last = group_matmul(5, places, x_own, x_oth, [[w_f], [w_c]], acc, ahead=True)
     partial = last_matmul(
-        places, w_g, x_last, acc, low_own, low_oth, fout_mine, fout_got, read_mine
+        places, g_lo, g_hi, factor_out, fout_oth, x_last, acc, low_own, low_oth, readout[None]
     )
     (partial,) = after((partial,), pieces)
 

time: 127 us -> 130 us (1.024)
  starting transfers between devices: 43.6 us -> 33.8 us
  waiting for transfers between devices: 18.6 us -> 25.2 us
  blocking collectives: 8.18 us -> 11 us
  local copies, waits for them, and re-layouts: 2.6 us -> 5.29 us
    ppermute x19 -> x13, starting transfers between devices: 24.7 us -> 18.6 us  [send(): return lax.ppermute(v, AXES, pairs)]
    ppermute x19 -> x13, waiting for transfers between devices: 9.69 us -> 15.3 us  [send(): return lax.ppermute(v, AXES, pairs)]
    all_to_all x1, starting transfers between devices: 10.6 us -> 7.01 us  [share(): return lax.all_to_all(x, axes, 0, 0, tiled=True)]
    unnamed x18 -> x22, local copies, waits for them, and re-layouts: 0.65 us -> 3.55 us
    all_to_all x1, blocking collectives: 8.18 us -> 11 us  [share(): return lax.all_to_all(x, axes, 0, 0, tiled=True)]
  transfers between devices with their start and end apart: 22 -> 16, of which waited for: 6 -> 8; matrix products, arithmetic and copies ran while one was open for 2% -> 1% of each run, Pallas kernels for 26% -> 27%
where the time goes in v8:
time: 130 us
  Pallas kernels  38.4 us (30%)
  starting transfers between devices  33.8 us (26%)
  waiting for transfers between devices  25.2 us (19%)
  between operations  14.2 us (11%)
  blocking collectives  11 us (8%)
  local copies, waits for them, and re-layouts  5.29 us (4%)
  other arithmetic  1.67 us (1%)
    pallas_call x3, Pallas kernels, group_matmul(): pl.pallas_call(functools.partial(group_kernel, base, counts, acc is not N...  20.6 us
    ppermute x13, starting transfers between devices, send(): return lax.ppermute(v, AXES, pairs)  18.6 us
    ppermute x13, waiting for transfers between devices, send(): return lax.ppermute(v, AXES, pairs)  15.3 us
    all_to_all x1, blocking collectives, share(): return lax.all_to_all(x, axes, 0, 0, tiled=True)  11 us
    all_to_all x1, waiting for transfers between devices, share(): return lax.all_to_all(x, axes, 0, 0, tiled=True)  8.83 us
    all_to_all x1, starting transfers between devices, shards(): pieces = lax.all_to_all(pieces_here, 'z', 0, 0, tiled=True)  8.19 us
    all_to_all x1, starting transfers between devices, share(): return lax.all_to_all(x, axes, 0, 0, tiled=True)  7.01 us
    pallas_call x1, Pallas kernels, low_term(): pl.pallas_call(low_kernel, out_shape=(jax.ShapeDtypeStruct((rows, members...  4.63 us
  transfers between devices with their start and end apart: 16, of which 8 were waited for; matrix products, arithmetic and copies ran while one was open for 1% of the time, Pallas kernels for 27%

profile of v8, /device:TPU:1, one launch (start us, length us, event | category | flops | bytes accessed | tf_op | source)
XLA Modules:
  0.0 129.6 jit_solution(4115480196983370446)
XLA Ops:
  7.2 3.3 %collective-permute-start = (bf16[3,256,4096]{2,1,0:T(8,128)(2,1)}, bf16[3,256,4096]{2,1,0:T(8,128)(2,1)}, u32[]{:S(2)}, u32[]{:S(2)}) collective-permute-start(bf16[3,256,4096]{2,1,0:T(8,128)(2,1)} %bitcast.22), channel_id=1, source_target_pairs={{0,8},{1,9},{2,10},{3,11},{4,12},{5,13},{6,14},{7,15},{8,0},{9,1},... | collective-permute-start | bytes 18874376 | tf_op jit(solution)/shard_map/ppermute | solution.py:447
  11.6 1.8 %collective-permute-start.1 = (bf16[1024,512]{1,0:T(8,128)(2,1)}, bf16[1024,512]{1,0:T(8,128)(2,1)}, u32[]{:S(2)}, u32[]{:S(2)}) collective-permute-start(bf16[1024,512]{1,0:T(8,128)(2,1)} %constant_dynamic-slice_fusion.refs_0_), channel_id=1, source_target_pairs={{0,1},{1,2},{2,3},{3,0},{4,5},{5,6},{6,7},{7,4},{8,11},{9,8},{10,9... | collective-permute-start | bytes 3145736 | tf_op jit(solution)/shard_map/ppermute | solution.py:447
  13.4 2.5 %collective-permute-start.2 = (bf16[1024,512]{1,0:T(8,128)(2,1)}, bf16[1024,512]{1,0:T(8,128)(2,1)S(1)}, u32[]{:S(2)}, u32[]{:S(2)}) collective-permute-start(bf16[1024,512]{1,0:T(8,128)(2,1)} %constant_dynamic-slice_fusion.refs_0_), channel_id=1, source_target_pairs={{0,4},{1,5},{2,6},{3,7},{4,0},{5,1},{6,2},{7,3},{8,140},{9,141},{1... | collective-permute-start | bytes 3145736 | tf_op jit(solution)/shard_map/ppermute | solution.py:447
  16.5 2.3 %shard_map.78 = bf16[256,512]{1,0:T(8,128)(2,1)} custom-call(s32[11]{0:T(128)} %stack.47.kidx.place, bf16[256,4096]{1,0:T(8,128)(2,1)} %fin.3), custom_call_target="tpu_custom_call" | custom-call | tf_op jit(solution)/shard_map/pallas_call | solution.py:311
  18.9 2.5 %shard_map.68 = (bf16[8,256,256]{2,1,0:T(8,128)(2,1)}, f32[8,128]{1,0:T(8,128)}) custom-call(bf16[256,2048]{1,0:T(8,128)(2,1)} %fout_mine.1), custom_call_target="tpu_custom_call" | custom-call | bytes 4194304 | tf_op jit(solution)/shard_map/pallas_call | solution.py:287
  21.4 4.6 %shard_map.69 = (f32[3,256,1]{2,1,0:T(8,128)}, f32[8,128]{1,0:T(8,128)}) custom-call(bf16[3,256,4096]{2,1,0:T(8,128)(2,1)} %bitcast.23, bf16[256,4096]{1,0:T(8,128)(2,1)} %fin.3), custom_call_target="tpu_custom_call" | custom-call | flops 6291456 | bytes 9437184 | tf_op jit(solution)/shard_map/pallas_call | solution.py:354
  26.1 2.8 %collective-permute-done.2.refs_2_ = bf16[1024,512]{1,0:T(8,128)(2,1)S(1)} collective-permute-done((bf16[1024,512]{1,0:T(8,128)(2,1)}, bf16[1024,512]{1,0:T(8,128)(2,1)S(1)}, u32[]{:S(2)}, u32[]{:S(2)}) %collective-permute-start.2) | collective-permute-done | bytes 1048608 | tf_op jit(solution)/shard_map/ppermute | solution.py:447
  30.6 2.1 %collective-permute-start.6 = (bf16[1024,512]{1,0:T(8,128)(2,1)}, bf16[1024,512]{1,0:T(8,128)(2,1)}, u32[]{:S(2)}, u32[]{:S(2)}) collective-permute-start(bf16[1024,512]{1,0:T(8,128)(2,1)} %get-tuple-element.23.refs_1_), channel_id=1, source_target_pairs={{0,4},{1,5},{2,6},{3,7},{4,0},{5,1},{6,2},{7,3},{8,140},{9,141},{1... | collective-permute-start | bytes 3145736 | tf_op jit(solution)/shard_map/ppermute | solution.py:447
  32.6 8.2 %all-to-all-start = ((bf16[8,256,256]{2,1,0:T(8,128)(2,1)}), bf16[8,256,256]{2,1,0:T(8,128)(2,1)S(1)}, u32[]{:S(2)}, u32[]{:S(2)}) async-start(bf16[8,256,256]{2,1,0:T(8,128)(2,1)} %get-tuple-element.34), calls=%async_computation | async-start | bytes 2097152 | tf_op jit(solution)/shard_map/all_to_all | solution.py:477
  40.8 1.2 copy-done.4
  42.1 8.3 %shard_map.71 = (f32[2,3,256,1024]{3,2,1,0:T(8,128)S(1)}, bf16[1024,512]{1,0:T(8,128)(2,1)S(1)}) custom-call(s32[11]{0:T(128)S(1)} %copy-done.6, bf16[3,256,4096]{2,1,0:T(8,128)(2,1)} %bitcast.24, bf16[3,256,4096]{2,1,0:T(8,128)(2,1)} %collective-permute-done.x_oth, bf16[1024,512]{1,0:T(8,128)(2,1)} %get-tuple-element.22.refs_0_, ...), custom_call_target="tpu_custom_call" | custom-call | flops 4831838208 | bytes 8388608 | tf_op jit(solution)/shard_map/pallas_call | solution.py:152
  50.4 2.7 %collective-permute-start.3 = (bf16[1024,512]{1,0:T(8,128)(2,1)S(1)}, bf16[1024,512]{1,0:T(8,128)(2,1)S(1)}, u32[]{:S(2)}, u32[]{:S(2)}) collective-permute-start(bf16[1024,512]{1,0:T(8,128)(2,1)S(1)} %get-tuple-element.25.refs_2_), channel_id=1, source_target_pairs={{0,1},{1,2},{2,3},{3,0},{4,5},{5,6},{6,7},{7,4},{8,11},{9,8},{10,9... | collective-permute-start | bytes 3145736 | tf_op jit(solution)/shard_map/ppermute | solution.py:447
  53.4 6.5 %shard_map.73 = (f32[2,3,256,1024]{3,2,1,0:T(8,128)S(1)}, bf16[512,512]{1,0:T(8,128)(2,1)S(1)}) custom-call(s32[11]{0:T(128)S(1)} %copy-done.6, bf16[3,256,4096]{2,1,0:T(8,128)(2,1)} %bitcast.25, bf16[3,256,4096]{2,1,0:T(8,128)(2,1)} %collective-permute-done.x_oth, bf16[1024,512]{1,0:T(8,128)(2,1)} %get-tuple-element.26.refs_0_, ...), custom_call_target="tpu_custom_call", output_to_operand_aliasing={{0}: (5, {})} | custom-call | flops 3221225472 | bytes 8388608 | tf_op jit(solution)/shard_map/pallas_call | solution.py:152
  60.9 4.0 %collective-permute-done.3.refs_1_ = bf16[1024,512]{1,0:T(8,128)(2,1)S(1)} collective-permute-done((bf16[1024,512]{1,0:T(8,128)(2,1)S(1)}, bf16[1024,512]{1,0:T(8,128)(2,1)S(1)}, u32[]{:S(2)}, u32[]{:S(2)}) %collective-permute-start.3) | collective-permute-done | bytes 1048608 | tf_op jit(solution)/shard_map/ppermute | solution.py:447
  65.2 2.3 %collective-permute-start.10 = (f32[3,256,1]{2,1,0:T(8,128)S(1)}, f32[3,256,1]{2,1,0:T(8,128)S(1)}, u32[]{:S(2)}, u32[]{:S(2)}) collective-permute-start(f32[3,256,1]{2,1,0:T(8,128)S(1)} %copy-done.5), channel_id=1, source_target_pairs={{0,8},{1,9},{2,10},{3,11},{4,12},{5,13},{6,14},{7,15},{8,0},{9,1},... | collective-permute-start | bytes 9224 | tf_op jit(solution)/shard_map/ppermute | solution.py:447
  68.6 5.8 %shard_map.74 = (f32[2,3,256,1024]{3,2,1,0:T(8,128)S(1)}, bf16[2,3,256,512]{3,2,1,0:T(8,128)(2,1)S(1)}) custom-call(s32[11]{0:T(128)S(1)} %copy-done.6, bf16[3,256,4096]{2,1,0:T(8,128)(2,1)} %bitcast.26, bf16[3,256,4096]{2,1,0:T(8,128)(2,1)} %collective-permute-done.x_oth, ...), custom_call_target="tpu_custom_call", output_to_operand_aliasing={{0}: (5, {})} | custom-call | flops 3221225472 | bytes 8388608 | tf_op jit(solution)/shard_map/pallas_call | solution.py:152
  74.5 3.8 %shard_map.75.refs_0_ = f32[16,1,512]{2,1,0:T(1,128)S(1)} custom-call(s32[11]{0:T(128)S(1)} %copy-done.6, bf16[512,512]{1,0:T(8,128)(2,1)S(1)} %collective-permute-done.4.w_lo, bf16[512,512]{1,0:T(8,128)(2,1)S(1)} %collective-permute-done.7.w_hi, bf16[256,2048]{1,0:T(8,128)(2,1)S(1)} %copy-done.2, bf16[256,2048]{1,0:T(8,128)(2,1)S(1)} %collective-permute-done.8.fout_theirs, ...), custom_call_target="tpu_custom_call" | custom-call | flops 1610612736 | bytes 6291456 | tf_op jit(solution)/shard_map/pallas_call | solution.py:222
  79.5 11.0 %all_to_all.15.got = f32[16,1,512]{2,1,0:T(1,128)S(1)} all-to-all(f32[16,1,512]{2,1,0:T(1,128)S(1)} %shard_map.76), channel_id=1, replica_groups=mesh['xh'=2,'z'=8,'core'=2,'xl'=2,'y'=4] {'core','xl','y'}, dimensions={0} | all-to-all | bytes 65536 | tf_op jit(solution)/shard_map/all_to_all | solution.py:434
  91.1 7.0 %all-to-all-start.2 = ((f32[16,1,512]{2,1,0:T(1,128)}), f32[16,1,512]{2,1,0:T(1,128)S(1)}, u32[]{:S(2)}, u32[]{:S(2)}) async-start(f32[16,1,512]{2,1,0:T(1,128)} %shard_map.77), calls=%async_computation.2 | async-start | bytes 65536 | tf_op jit(solution)/shard_map/all_to_all | solution.py:434
  98.1 8.8 %all-to-all-done.2.fit = f32[16,1,512]{2,1,0:T(1,128)S(1)} async-done(((f32[16,1,512]{2,1,0:T(1,128)}), f32[16,1,512]{2,1,0:T(1,128)S(1)}, u32[]{:S(2)}, u32[]{:S(2)}) %all-to-all-start.2) | async-done | bytes 32800 | tf_op jit(solution)/shard_map/all_to_all | solution.py:434
  107.6 3.9 %shard_map.79 = (f32[2,64,512]{2,1,0:T(8,128)}, f32[2,64,512]{2,1,0:T(8,128)}, f32[1,256]{1,0:T(1,128)}) custom-call(s32[11]{0:T(128)} %stack.47.kidx.place, f32[16,1,512]{2,1,0:T(1,128)} %copy-done.10, bf16[8,256,256]{2,1,0:T(8,128)(2,1)} %copy-done.1, bf16[8,256,512]{2,1,0:T(8,128)(2,1)} %bitcast.27), custom_call_target="tpu_custom_call" | custom-call | flops 536870912 | bytes 4194304 | tf_op jit(solution)/shard_map/pallas_call | solution.py:416
  111.5 1.9 %collective-permute-start.11 = (f32[2,64,512]{2,1,0:T(8,128)}, f32[2,64,512]{2,1,0:T(8,128)S(1)}, u32[]{:S(2)}, u32[]{:S(2)}) collective-permute-start(f32[2,64,512]{2,1,0:T(8,128)} %get-tuple-element.36), channel_id=1, source_target_pairs={{0,8},{1,9},{2,10},{3,11},{4,12},{5,13},{6,14},{7,15},{8,0},{9,1},... | collective-permute-start | bytes 786440 | tf_op jit(solution)/shard_map/ppermute | solution.py:447
  113.4 1.4 %collective-permute-done.11 = f32[2,64,512]{2,1,0:T(8,128)S(1)} collective-permute-done((f32[2,64,512]{2,1,0:T(8,128)}, f32[2,64,512]{2,1,0:T(8,128)S(1)}, u32[]{:S(2)}, u32[]{:S(2)}) %collective-permute-start.11) | collective-permute-done | bytes 262176 | tf_op jit(solution)/shard_map/ppermute | solution.py:447
  116.2 5.9 %collective-permute-done.12 = f32[64,512]{1,0:T(8,128)S(1)} collective-permute-done((f32[64,512]{1,0:T(8,128)S(1)}, f32[64,512]{1,0:T(8,128)S(1)}, u32[]{:S(2)}, u32[]{:S(2)}) %collective-permute-start.12) | collective-permute-done | bytes 131104 | tf_op jit(solution)/shard_map/ppermute | solution.py:447
  (50 shorter events, 10.8 us)
Async XLA Ops:
  7.2 3.4 %copy-start = (bf16[2048,512]{1,0:T(8,128)(2,1)S(1)}, bf16[2048,512]{1,0:T(8,128)(2,1)}, u32[]{:S(2)}) copy-start(bf16[2048,512]{1,0:T(8,128)(2,1)} %param.6) | copy-start | bytes 6291460
  7.2 90.9 %all-gather.3.cloned.1.call-start = ((), (), s32[]{:S(2)}) async-start(), calls=%async_computation.3 | async-start | bytes 2359296 | tf_op jit(solution)/shard_map/all_gather | solution.py:475
  7.2 33.6 %collective-permute-start = (bf16[3,256,4096]{2,1,0:T(8,128)(2,1)}, bf16[3,256,4096]{2,1,0:T(8,128)(2,1)}, u32[]{:S(2)}, u32[]{:S(2)}) collective-permute-start(bf16[3,256,4096]{2,1,0:T(8,128)(2,1)} %bitcast.22), channel_id=1, source_target_pairs={{0,8},{1,9},{2,10},{3,11},{4,12},{5,13},{6,14},{7,15},{8,0},{9,1},... | collective-permute-start | bytes 18874376 | tf_op jit(solution)/shard_map/ppermute | solution.py:447
  11.6 14.4 %collective-permute-start.1 = (bf16[1024,512]{1,0:T(8,128)(2,1)}, bf16[1024,512]{1,0:T(8,128)(2,1)}, u32[]{:S(2)}, u32[]{:S(2)}) collective-permute-start(bf16[1024,512]{1,0:T(8,128)(2,1)} %constant_dynamic-slice_fusion.refs_0_), channel_id=1, source_target_pairs={{0,1},{1,2},{2,3},{3,0},{4,5},{5,6},{6,7},{7,4},{8,11},{9,8},{10,9... | collective-permute-start | bytes 3145736 | tf_op jit(solution)/shard_map/ppermute | solution.py:447
  13.4 15.5 %collective-permute-start.2 = (bf16[1024,512]{1,0:T(8,128)(2,1)}, bf16[1024,512]{1,0:T(8,128)(2,1)S(1)}, u32[]{:S(2)}, u32[]{:S(2)}) collective-permute-start(bf16[1024,512]{1,0:T(8,128)(2,1)} %constant_dynamic-slice_fusion.refs_0_), channel_id=1, source_target_pairs={{0,4},{1,5},{2,6},{3,7},{4,0},{5,1},{6,2},{7,3},{8,140},{9,141},{1... | collective-permute-start | bytes 3145736 | tf_op jit(solution)/shard_map/ppermute | solution.py:447
  21.4 7.5 %copy-start.8 = (f32[8,128]{1,0:T(8,128)S(1)}, f32[8,128]{1,0:T(8,128)}, u32[]{:S(2)}) copy-start(f32[8,128]{1,0:T(8,128)} %get-tuple-element.20.refs_3_) | copy-start | bytes 12292
  21.4 19.4 %copy-start.6 = (s32[11]{0:T(128)S(1)}, s32[11]{0:T(128)}, u32[]{:S(2)}) copy-start(s32[11]{0:T(128)} %stack.47.kidx.place) | copy-start | bytes 136
  30.6 22.6 %collective-permute-start.5 = (bf16[1024,512]{1,0:T(8,128)(2,1)}, bf16[1024,512]{1,0:T(8,128)(2,1)}, u32[]{:S(2)}, u32[]{:S(2)}) collective-permute-start(bf16[1024,512]{1,0:T(8,128)(2,1)} %get-tuple-element.22.refs_0_), channel_id=1, source_target_pairs={{0,3},{1,0},{2,1},{3,2},{4,7},{5,4},{6,5},{7,6},{8,9},{9,10},{10,1... | collective-permute-start | bytes 3145736 | tf_op jit(solution)/shard_map/ppermute | solution.py:447
  30.6 22.6 %collective-permute-start.6 = (bf16[1024,512]{1,0:T(8,128)(2,1)}, bf16[1024,512]{1,0:T(8,128)(2,1)}, u32[]{:S(2)}, u32[]{:S(2)}) collective-permute-start(bf16[1024,512]{1,0:T(8,128)(2,1)} %get-tuple-element.23.refs_1_), channel_id=1, source_target_pairs={{0,4},{1,5},{2,6},{3,7},{4,0},{5,1},{6,2},{7,3},{8,140},{9,141},{1... | collective-permute-start | bytes 3145736 | tf_op jit(solution)/shard_map/ppermute | solution.py:447
  32.6 46.8 %all-to-all-start = ((bf16[8,256,256]{2,1,0:T(8,128)(2,1)}), bf16[8,256,256]{2,1,0:T(8,128)(2,1)S(1)}, u32[]{:S(2)}, u32[]{:S(2)}) async-start(bf16[8,256,256]{2,1,0:T(8,128)(2,1)} %get-tuple-element.34), calls=%async_computation | async-start | bytes 2097152 | tf_op jit(solution)/shard_map/all_to_all | solution.py:477
  40.8 1.2 copy-start.4
  42.1 11.3 %copy-start.2 = (bf16[256,2048]{1,0:T(8,128)(2,1)S(1)}, bf16[256,2048]{1,0:T(8,128)(2,1)}, u32[]{:S(2)}) copy-start(bf16[256,2048]{1,0:T(8,128)(2,1)} %fout_mine.1) | copy-start | bytes 3145732
  50.4 14.5 %collective-permute-start.3 = (bf16[1024,512]{1,0:T(8,128)(2,1)S(1)}, bf16[1024,512]{1,0:T(8,128)(2,1)S(1)}, u32[]{:S(2)}, u32[]{:S(2)}) collective-permute-start(bf16[1024,512]{1,0:T(8,128)(2,1)S(1)} %get-tuple-element.25.refs_2_), channel_id=1, source_target_pairs={{0,1},{1,2},{2,3},{3,0},{4,5},{5,6},{6,7},{7,4},{8,11},{9,8},{10,9... | collective-permute-start | bytes 3145736 | tf_op jit(solution)/shard_map/ppermute | solution.py:447
  53.1 15.5 %collective-permute-start.9 = (bf16[1024,512]{1,0:T(8,128)(2,1)}, bf16[1024,512]{1,0:T(8,128)(2,1)S(1)}, u32[]{:S(2)}, u32[]{:S(2)}) collective-permute-start(bf16[1024,512]{1,0:T(8,128)(2,1)} %get-tuple-element.26.refs_0_), channel_id=1, source_target_pairs={{0,4},{1,5},{2,6},{3,7},{4,0},{5,1},{6,2},{7,3},{8,140},{9,141},{1... | collective-permute-start | bytes 3145736 | tf_op jit(solution)/shard_map/ppermute | solution.py:447
  53.3 21.0 %collective-permute-start.8 = (bf16[256,2048]{1,0:T(8,128)(2,1)S(1)}, bf16[256,2048]{1,0:T(8,128)(2,1)S(1)}, u32[]{:S(2)}, u32[]{:S(2)}) collective-permute-start(bf16[256,2048]{1,0:T(8,128)(2,1)S(1)} %copy-done.2), channel_id=1, source_target_pairs={{0,8},{1,9},{2,10},{3,11},{4,12},{5,13},{6,14},{7,15},{8,0},{9,1},... | collective-permute-start | bytes 3145736 | tf_op jit(solution)/shard_map/ppermute | solution.py:447
  53.4 11.8 %copy-start.5 = (f32[3,256,1]{2,1,0:T(8,128)S(1)}, f32[3,256,1]{2,1,0:T(8,128)}, u32[]{:S(2)}) copy-start(f32[3,256,1]{2,1,0:T(8,128)} %get-tuple-element.33.low_own) | copy-start | bytes 9220
  59.9 14.5 %collective-permute-start.7 = (bf16[512,512]{1,0:T(8,128)(2,1)S(1)}, bf16[512,512]{1,0:T(8,128)(2,1)S(1)}, u32[]{:S(2)}, u32[]{:S(2)}) collective-permute-start(bf16[512,512]{1,0:T(8,128)(2,1)S(1)} %get-tuple-element.29), channel_id=1, source_target_pairs={{0,1},{1,2},{2,3},{3,0},{4,5},{5,6},{6,7},{7,4},{8,11},{9,8},{10,9... | collective-permute-start | bytes 1572872 | tf_op jit(solution)/shard_map/ppermute | solution.py:447
  64.9 9.6 %collective-permute-start.4 = (bf16[512,512]{1,0:T(8,128)(2,1)S(1)}, bf16[512,512]{1,0:T(8,128)(2,1)S(1)}, u32[]{:S(2)}, u32[]{:S(2)}) collective-permute-start(bf16[512,512]{1,0:T(8,128)(2,1)S(1)} %slice.12), channel_id=1, source_target_pairs={{0,4},{1,5},{2,6},{3,7},{4,0},{5,1},{6,2},{7,3},{8,140},{9,141},{1... | collective-permute-start | bytes 1572872 | tf_op jit(solution)/shard_map/ppermute | solution.py:447
  65.2 9.2 %collective-permute-start.10 = (f32[3,256,1]{2,1,0:T(8,128)S(1)}, f32[3,256,1]{2,1,0:T(8,128)S(1)}, u32[]{:S(2)}, u32[]{:S(2)}) collective-permute-start(f32[3,256,1]{2,1,0:T(8,128)S(1)} %copy-done.5), channel_id=1, source_target_pairs={{0,8},{1,9},{2,10},{3,11},{4,12},{5,13},{6,14},{7,15},{8,0},{9,1},... | collective-permute-start | bytes 9224 | tf_op jit(solution)/shard_map/ppermute | solution.py:447
  68.6 5.9 %copy-start.7 = (f32[2048]{0:T(1024)S(1)}, f32[2048]{0:T(1024)}, u32[]{:S(2)}) copy-start(f32[2048]{0:T(1024)} %param.9) | copy-start | bytes 24580
  79.5 27.5 %copy-start.1 = (bf16[8,256,256]{2,1,0:T(8,128)(2,1)}, bf16[8,256,256]{2,1,0:T(8,128)(2,1)S(1)}, u32[]{:S(2)}) copy-start(bf16[8,256,256]{2,1,0:T(8,128)(2,1)S(1)} %all-to-all-done.refs_1_.fout_all) | copy-start | bytes 3145732
  91.1 15.9 %all-to-all-start.2 = ((f32[16,1,512]{2,1,0:T(1,128)}), f32[16,1,512]{2,1,0:T(1,128)S(1)}, u32[]{:S(2)}, u32[]{:S(2)}) async-start(f32[16,1,512]{2,1,0:T(1,128)} %shard_map.77), calls=%async_computation.2 | async-start | bytes 65536 | tf_op jit(solution)/shard_map/all_to_all | solution.py:434
  111.5 3.3 %collective-permute-start.11 = (f32[2,64,512]{2,1,0:T(8,128)}, f32[2,64,512]{2,1,0:T(8,128)S(1)}, u32[]{:S(2)}, u32[]{:S(2)}) collective-permute-start(f32[2,64,512]{2,1,0:T(8,128)} %get-tuple-element.36), channel_id=1, source_target_pairs={{0,8},{1,9},{2,10},{3,11},{4,12},{5,13},{6,14},{7,15},{8,0},{9,1},... | collective-permute-start | bytes 786440 | tf_op jit(solution)/shard_map/ppermute | solution.py:447
  115.8 6.3 %collective-permute-start.12 = (f32[64,512]{1,0:T(8,128)S(1)}, f32[64,512]{1,0:T(8,128)S(1)}, u32[]{:S(2)}, u32[]{:S(2)}) collective-permute-start(f32[64,512]{1,0:T(8,128)S(1)} %slice_bitcast_fusion), channel_id=1, source_target_pairs={{0,128},{1,129},{2,130},{3,131},{4,132},{5,133},{6,134},{7,135},{8... | collective-permute-start | bytes 393224 | tf_op jit(solution)/shard_map/ppermute | solution.py:447
  (3 other events, 2.3 us)
Sparse Core Ops, SparseCore 0:
  19.0 58.2 all-gather.2

commit v9 on v8

--- a/solution.py
+++ b/solution.py
@@ -364,7 +364,7 @@
             pltpu.VMEM((tiles, tile, width), jnp.bfloat16),
             pltpu.SemaphoreType.DMA((tiles, 2)),
         ],
-        compiler_params=pltpu.CompilerParams(vmem_limit_bytes=LARGE_BYTES),
+        compiler_params=pltpu.CompilerParams(vmem_limit_bytes=VMEM_BYTES),
         cost_estimate=pl.CostEstimate(
             flops=2 * rows * members * width, bytes_accessed=9 * 1024 * 1024, transcendentals=0
         ),
@@ -466,33 +466,36 @@
 
     places = jnp.stack([k_own, k_a, k_d, k_b, k_e, k_f, k_c, k_g, c, xh, z]).astype(jnp.int32)
 
+    part = half // 2
     own = lax.dynamic_slice_in_dim(weight, c * half, half, 0)
-    w_a = send(own, y_fwd)
-    w_d = send(own, x_go)
+    own_parts = [lax.dynamic_slice_in_dim(weight, c * half + h * part, part, 0) for h in range(2)]
+    w_a = [send(w, y_fwd) for w in own_parts]
+    w_d = [send(w, x_go) for w in own_parts]
     x_oth = send(x_own, core_go)
     fout_oth = send(factor_out, core_go)
 
-    fin_all = lax.all_gather(cut_block(places, factor_in, block), "z", axis=0)
+    fin_all = lax.all_gather(cut_block(places, factor_in, block, own_parts[0]), "z", axis=0)
     pieces_here, cut_done = cut_factors(factor_out)
     pieces = lax.all_to_all(pieces_here, "z", 0, 0, tiled=True)
     low_own, low_done = low_term(x_own, factor_in)
     low_oth = send(low_own, core_go)
 
-    part = half // 2
-    own, w_a, w_d = after((own, w_a, w_d), cut_done, low_done)
+    w_a[0], w_d[0] = after((w_a[0], w_d[0]))
+    e_lo = send(w_a[0], x_go)
+    w_a[1], w_d[1], own = after((w_a[1], w_d[1], own), cut_done)
     w_b = send(own, y_bwd)
-    w_e = send(w_a, x_go)
+    e_hi = send(w_a[1], x_go)
     acc, a_on = group_matmul(
-        0, places, x_own, x_oth, [[own], [w_a], [w_d]], None, hand=((1, 0),), hand_rows=half
+        0, places, x_own, x_oth, [[own], w_a, w_d], None, hand=((1, 0),), hand_rows=half
     )
     w_c = send(a_on, y_fwd)
-    w_b, w_e = after((w_b, w_e), a_on)
+    w_b, e_lo, e_hi = after((w_b, e_lo, e_hi), a_on)
     w_f = send(w_b, x_go)
-    acc, e_hi = group_matmul(
-        3, places, x_own, x_oth, [[w_b], [w_e]], acc, hand=((1, part),), hand_rows=part
+    acc, e_on = group_matmul(
+        3, places, x_own, x_oth, [[w_b], [e_lo, e_hi]], acc, extra=(low_done,), hand=((1, part),), hand_rows=part
     )
     g_lo = send(w_c[:part], x_go)
-    g_hi = send(e_hi, y_fwd)
+    g_hi = send(e_on, y_fwd)
     acc, x_last = group_matmul(5, places, x_own, x_oth, [[w_f], [w_c]], acc, ahead=True)
     partial = last_matmul(
         places, g_lo, g_hi, factor_out, fout_oth, x_last, acc, low_own, low_oth, readout[None]

time: 130 us -> 130 us (level)
  waiting for transfers between devices: 25.2 us -> 19.3 us
  starting transfers between devices: 33.8 us -> 39.1 us
  local copies, waits for them, and re-layouts: 5.29 us -> 9.03 us
  Pallas kernels: 38.4 us -> 35.8 us
    ppermute x13 -> x16, waiting for transfers between devices: 15.3 us -> 10.4 us  [send(): return lax.ppermute(v, AXES, pairs)]
    ppermute x13 -> x16, starting transfers between devices: 18.6 us -> 21.6 us  [send(): return lax.ppermute(v, AXES, pairs)]
    all_to_all x1, starting transfers between devices: 7.01 us -> 9.42 us  [share(): return lax.all_to_all(x, axes, 0, 0, tiled=True)]
    pallas_call x1, Pallas kernels: 4.63 us -> 2.5 us  [low_term(): pl.pallas_call(low_kernel, out_shape=(jax.ShapeDtypeStruct((rows, members...]
    dynamic_slice x0 -> x1, local copies, waits for them, and re-layouts: none -> 2.09 us  [shards(): lax.dynamic_slice_in_dim(weight, c * half + h * part, part, 0)]
    unnamed x22 -> x28, local copies, waits for them, and re-layouts: 3.55 us -> 3.95 us
  transfers between devices with their start and end apart: 16 -> 19, of which waited for: 8 -> 6; matrix products, arithmetic and copies ran while one was open for 1% -> 4% of each run, Pallas kernels for 27% -> 25%
where the time goes in v9:
time: 130 us; the launch traced here: 129 us
  starting transfers between devices  39.1 us (30%)
  Pallas kernels  35.8 us (28%)
  waiting for transfers between devices  19.3 us (15%)
  between operations  14.3 us (11%)
  blocking collectives  10.2 us (8%)
  local copies, waits for them, and re-layouts  9.03 us (7%)
  other arithmetic  1.67 us (1%)
    ppermute x16, starting transfers between devices, send(): return lax.ppermute(v, AXES, pairs)  21.6 us
    pallas_call x3, Pallas kernels, group_matmul(): pl.pallas_call(functools.partial(group_kernel, base, counts, acc is not N...  20.1 us
    ppermute x16, waiting for transfers between devices, send(): return lax.ppermute(v, AXES, pairs)  10.4 us
    all_to_all x1, blocking collectives, share(): return lax.all_to_all(x, axes, 0, 0, tiled=True)  10.2 us
    all_to_all x1, starting transfers between devices, share(): return lax.all_to_all(x, axes, 0, 0, tiled=True)  9.42 us
    all_to_all x1, waiting for transfers between devices, share(): return lax.all_to_all(x, axes, 0, 0, tiled=True)  8.83 us
    all_to_all x1, starting transfers between devices, shards(): pieces = lax.all_to_all(pieces_here, 'z', 0, 0, tiled=True)  8.04 us
    unnamed x28, local copies, waits for them, and re-layouts  3.95 us
  transfers between devices with their start and end apart: 19, of which 6 were waited for; matrix products, arithmetic and copies ran while one was open for 4% of the time, Pallas kernels for 25%

profile of v9, /device:TPU:1, one launch (start us, length us, event | category | flops | bytes accessed | tf_op | source)
XLA Modules:
  0.0 129.3 jit_solution(5593531844281320562)
XLA Ops:
  7.2 3.3 %collective-permute-start = (bf16[3,256,4096]{2,1,0:T(8,128)(2,1)}, bf16[3,256,4096]{2,1,0:T(8,128)(2,1)}, u32[]{:S(2)}, u32[]{:S(2)}) collective-permute-start(bf16[3,256,4096]{2,1,0:T(8,128)(2,1)} %bitcast.21), channel_id=1, source_target_pairs={{0,8},{1,9},{2,10},{3,11},{4,12},{5,13},{6,14},{7,15},{8,0},{9,1},... | collective-permute-start | bytes 18874376 | tf_op jit(solution)/shard_map/ppermute | solution.py:447
  11.2 2.1 %constant_dynamic-slice_fusion = (bf16[512,512]{1,0:T(8,128)(2,1)}, bf16[512,512]{1,0:T(8,128)(2,1)S(1)}) fusion(bf16[2048,512]{1,0:T(8,128)(2,1)} %param.6, s32[]{:T(128)S(6)} %select_n.8, s32[]{:T(128)S(6)} %select_n.7), kind=kLoop, calls=%fused_computation.3 | loop fusion | bytes 2097160 | tf_op jit(solution)/shard_map/dynamic_slice | solution.py:471
  13.3 2.4 %shard_map.79 = bf16[256,512]{1,0:T(8,128)(2,1)} custom-call(s32[11]{0:T(128)} %stack.47.kidx.place, bf16[256,4096]{1,0:T(8,128)(2,1)} %fin.3, bf16[512,512]{1,0:T(8,128)(2,1)} %get-tuple-element.44.refs_0_), custom_call_target="tpu_custom_call" | custom-call | tf_op jit(solution)/shard_map/pallas_call | solution.py:311
  16.8 2.5 %collective-permute-start.2 = (bf16[512,512]{1,0:T(8,128)(2,1)S(1)}, bf16[512,512]{1,0:T(8,128)(2,1)S(1)}, u32[]{:S(2)}, u32[]{:S(2)}) collective-permute-start(bf16[512,512]{1,0:T(8,128)(2,1)S(1)} %get-tuple-element.45), channel_id=1, source_target_pairs={{0,4},{1,5},{2,6},{3,7},{4,0},{5,1},{6,2},{7,3},{8,140},{9,141},{1... | collective-permute-start | bytes 1572872 | tf_op jit(solution)/shard_map/ppermute | solution.py:447
  20.0 2.5 %shard_map.68 = (bf16[8,256,256]{2,1,0:T(8,128)(2,1)}, f32[8,128]{1,0:T(8,128)}) custom-call(bf16[256,2048]{1,0:T(8,128)(2,1)} %fout_mine.1), custom_call_target="tpu_custom_call" | custom-call | bytes 4194304 | tf_op jit(solution)/shard_map/pallas_call | solution.py:287
  22.5 2.3 %constant_dynamic-slice_fusion.1.refs_2_ = bf16[1024,512]{1,0:T(8,128)(2,1)} fusion(bf16[2048,512]{1,0:T(8,128)(2,1)} %param.6, s32[]{:T(128)S(6)} %select_n.8), kind=kLoop, calls=%fused_computation.4 | loop fusion | bytes 2097156 | tf_op jit(solution)/shard_map/dynamic_slice | solution.py:470
  24.8 1.6 %collective-permute-done.2.refs_1_ = bf16[512,512]{1,0:T(8,128)(2,1)S(1)} collective-permute-done((bf16[512,512]{1,0:T(8,128)(2,1)S(1)}, bf16[512,512]{1,0:T(8,128)(2,1)S(1)}, u32[]{:S(2)}, u32[]{:S(2)}) %collective-permute-start.2) | collective-permute-done | bytes 524320 | tf_op jit(solution)/shard_map/ppermute | solution.py:447
  26.6 8.0 %all-to-all-start = ((bf16[8,256,256]{2,1,0:T(8,128)(2,1)}), bf16[8,256,256]{2,1,0:T(8,128)(2,1)S(1)}, u32[]{:S(2)}, u32[]{:S(2)}) async-start(bf16[8,256,256]{2,1,0:T(8,128)(2,1)} %get-tuple-element.40), calls=%async_computation | async-start | bytes 2097152 | tf_op jit(solution)/shard_map/all_to_all | solution.py:479
  34.7 2.5 %collective-permute-start.9 = (bf16[512,512]{1,0:T(8,128)(2,1)}, bf16[512,512]{1,0:T(8,128)(2,1)S(1)}, u32[]{:S(2)}, u32[]{:S(2)}) collective-permute-start(bf16[512,512]{1,0:T(8,128)(2,1)} %get-tuple-element.26.refs_2_), channel_id=1, source_target_pairs={{0,4},{1,5},{2,6},{3,7},{4,0},{5,1},{6,2},{7,3},{8,140},{9,141},{1... | collective-permute-start | bytes 1572872 | tf_op jit(solution)/shard_map/ppermute | solution.py:447
  40.7 8.2 %shard_map.71 = (f32[2,3,256,1024]{3,2,1,0:T(8,128)S(1)}, bf16[1024,512]{1,0:T(8,128)(2,1)S(1)}) custom-call(s32[11]{0:T(128)S(1)} %copy-done.7, bf16[3,256,4096]{2,1,0:T(8,128)(2,1)} %bitcast.22, bf16[3,256,4096]{2,1,0:T(8,128)(2,1)} %collective-permute-done.x_oth, bf16[1024,512]{1,0:T(8,128)(2,1)} %get-tuple-element.24.refs_0_, ...), custom_call_target="tpu_custom_call" | custom-call | flops 4831838208 | bytes 8388608 | tf_op jit(solution)/shard_map/pallas_call | solution.py:152
  48.9 2.7 %collective-permute-start.5 = (bf16[1024,512]{1,0:T(8,128)(2,1)S(1)}, bf16[1024,512]{1,0:T(8,128)(2,1)S(1)}, u32[]{:S(2)}, u32[]{:S(2)}) collective-permute-start(bf16[1024,512]{1,0:T(8,128)(2,1)S(1)} %get-tuple-element.29.refs_3_), channel_id=1, source_target_pairs={{0,1},{1,2},{2,3},{3,0},{4,5},{5,6},{6,7},{7,4},{8,11},{9,8},{10,9... | collective-permute-start | bytes 3145736 | tf_op jit(solution)/shard_map/ppermute | solution.py:447
  51.7 2.6 %collective-permute-start.12 = (bf16[1024,512]{1,0:T(8,128)(2,1)}, bf16[1024,512]{1,0:T(8,128)(2,1)S(1)}, u32[]{:S(2)}, u32[]{:S(2)}) collective-permute-start(bf16[1024,512]{1,0:T(8,128)(2,1)} %get-tuple-element.31.refs_1_), channel_id=1, source_target_pairs={{0,4},{1,5},{2,6},{3,7},{4,0},{5,1},{6,2},{7,3},{8,140},{9,141},{1... | collective-permute-start | bytes 3145736 | tf_op jit(solution)/shard_map/ppermute | solution.py:447
  54.3 2.5 %shard_map.72 = (f32[3,256,1]{2,1,0:T(8,128)S(1)}, f32[8,128]{1,0:T(8,128)S(1)}) custom-call(bf16[3,256,4096]{2,1,0:T(8,128)(2,1)S(1)} %bitcast.27, bf16[256,4096]{1,0:T(8,128)(2,1)S(1)} %copy-done.1), custom_call_target="tpu_custom_call" | custom-call | flops 6291456 | bytes 9437184 | tf_op jit(solution)/shard_map/pallas_call | solution.py:354
  56.8 6.1 %shard_map.74 = (f32[2,3,256,1024]{3,2,1,0:T(8,128)S(1)}, bf16[512,512]{1,0:T(8,128)(2,1)S(1)}) custom-call(s32[11]{0:T(128)S(1)} %copy-done.7, bf16[3,256,4096]{2,1,0:T(8,128)(2,1)} %bitcast.23, bf16[3,256,4096]{2,1,0:T(8,128)(2,1)} %collective-permute-done.x_oth, f32[8,128]{1,0:T(8,128)S(1)} %get-tuple-element.30.refs_0_, ...), custom_call_target="tpu_custom_call", output_to_operand_aliasing={{0}: (7, {})} | custom-call | flops 3221225472 | bytes 8388608 | tf_op jit(solution)/shard_map/pallas_call | solution.py:152
  64.1 1.9 %collective-permute-start.6 = (bf16[512,512]{1,0:T(8,128)(2,1)S(1)}, bf16[512,512]{1,0:T(8,128)(2,1)S(1)}, u32[]{:S(2)}, u32[]{:S(2)}) collective-permute-start(bf16[512,512]{1,0:T(8,128)(2,1)S(1)} %slice.12), channel_id=1, source_target_pairs={{0,4},{1,5},{2,6},{3,7},{4,0},{5,1},{6,2},{7,3},{8,140},{9,141},{1... | collective-permute-start | bytes 1572872 | tf_op jit(solution)/shard_map/ppermute | solution.py:447
  66.8 5.8 %shard_map.75 = (f32[2,3,256,1024]{3,2,1,0:T(8,128)S(1)}, bf16[2,3,256,512]{3,2,1,0:T(8,128)(2,1)S(1)}) custom-call(s32[11]{0:T(128)S(1)} %copy-done.7, bf16[3,256,4096]{2,1,0:T(8,128)(2,1)} %bitcast.24, bf16[3,256,4096]{2,1,0:T(8,128)(2,1)} %collective-permute-done.x_oth, ...), custom_call_target="tpu_custom_call", output_to_operand_aliasing={{0}: (5, {})} | custom-call | flops 3221225472 | bytes 8388608 | tf_op jit(solution)/shard_map/pallas_call | solution.py:152
  73.8 3.8 %shard_map.76.refs_0_ = f32[16,1,512]{2,1,0:T(1,128)S(1)} custom-call(s32[11]{0:T(128)S(1)} %copy-done.7, bf16[512,512]{1,0:T(8,128)(2,1)S(1)} %collective-permute-done.6.w_lo, bf16[512,512]{1,0:T(8,128)(2,1)S(1)} %collective-permute-done.10.w_hi, bf16[256,2048]{1,0:T(8,128)(2,1)S(1)} %copy-done.2, bf16[256,2048]{1,0:T(8,128)(2,1)} %collective-permute-done.11.fout_theirs, ...), custom_call_target="tpu_custom_call" | custom-call | flops 1610612736 | bytes 6291456 | tf_op jit(solution)/shard_map/pallas_call | solution.py:222
  77.6 10.2 %all_to_all.15.got = f32[16,1,512]{2,1,0:T(1,128)S(1)} all-to-all(f32[16,1,512]{2,1,0:T(1,128)S(1)} %shard_map.77), channel_id=1, replica_groups=mesh['xh'=2,'z'=8,'core'=2,'xl'=2,'y'=4] {'core','xl','y'}, dimensions={0} | all-to-all | bytes 65536 | tf_op jit(solution)/shard_map/all_to_all | solution.py:434
  88.4 9.4 %all-to-all-start.2 = ((f32[16,1,512]{2,1,0:T(1,128)}), f32[16,1,512]{2,1,0:T(1,128)S(1)}, u32[]{:S(2)}, u32[]{:S(2)}) async-start(f32[16,1,512]{2,1,0:T(1,128)} %shard_map.78), calls=%async_computation.2 | async-start | bytes 65536 | tf_op jit(solution)/shard_map/all_to_all | solution.py:434
  97.9 8.8 %all-to-all-done.2.fit = f32[16,1,512]{2,1,0:T(1,128)S(1)} async-done(((f32[16,1,512]{2,1,0:T(1,128)}), f32[16,1,512]{2,1,0:T(1,128)S(1)}, u32[]{:S(2)}, u32[]{:S(2)}) %all-to-all-start.2) | async-done | bytes 32800 | tf_op jit(solution)/shard_map/all_to_all | solution.py:434
  107.3 3.9 %shard_map.80 = (f32[2,64,512]{2,1,0:T(8,128)}, f32[2,64,512]{2,1,0:T(8,128)}, f32[1,256]{1,0:T(1,128)}) custom-call(s32[11]{0:T(128)} %stack.47.kidx.place, f32[16,1,512]{2,1,0:T(1,128)} %copy-done.11, bf16[8,256,256]{2,1,0:T(8,128)(2,1)} %copy-done, bf16[8,256,512]{2,1,0:T(8,128)(2,1)} %bitcast.29), custom_call_target="tpu_custom_call" | custom-call | flops 536870912 | bytes 4194304 | tf_op jit(solution)/shard_map/pallas_call | solution.py:416
  111.2 1.9 %collective-permute-start.14 = (f32[2,64,512]{2,1,0:T(8,128)}, f32[2,64,512]{2,1,0:T(8,128)S(1)}, u32[]{:S(2)}, u32[]{:S(2)}) collective-permute-start(f32[2,64,512]{2,1,0:T(8,128)} %get-tuple-element.42), channel_id=1, source_target_pairs={{0,8},{1,9},{2,10},{3,11},{4,12},{5,13},{6,14},{7,15},{8,0},{9,1},... | collective-permute-start | bytes 786440 | tf_op jit(solution)/shard_map/ppermute | solution.py:447
  113.1 1.4 %collective-permute-done.14 = f32[2,64,512]{2,1,0:T(8,128)S(1)} collective-permute-done((f32[2,64,512]{2,1,0:T(8,128)}, f32[2,64,512]{2,1,0:T(8,128)S(1)}, u32[]{:S(2)}, u32[]{:S(2)}) %collective-permute-start.14) | collective-permute-done | bytes 262176 | tf_op jit(solution)/shard_map/ppermute | solution.py:447
  115.9 5.9 %collective-permute-done.15 = f32[64,512]{1,0:T(8,128)S(1)} collective-permute-done((f32[64,512]{1,0:T(8,128)S(1)}, f32[64,512]{1,0:T(8,128)S(1)}, u32[]{:S(2)}, u32[]{:S(2)}) %collective-permute-start.15) | collective-permute-done | bytes 131104 | tf_op jit(solution)/shard_map/ppermute | solution.py:447
  (65 shorter events, 12.8 us)
Async XLA Ops:
  7.2 90.7 %all-gather.3.cloned.1.call-start = ((), (), s32[]{:S(2)}) async-start(), calls=%async_computation.3 | async-start | bytes 2359296 | tf_op jit(solution)/shard_map/all_gather | solution.py:477
  7.2 31.0 %collective-permute-start = (bf16[3,256,4096]{2,1,0:T(8,128)(2,1)}, bf16[3,256,4096]{2,1,0:T(8,128)(2,1)}, u32[]{:S(2)}, u32[]{:S(2)}) collective-permute-start(bf16[3,256,4096]{2,1,0:T(8,128)(2,1)} %bitcast.21), channel_id=1, source_target_pairs={{0,8},{1,9},{2,10},{3,11},{4,12},{5,13},{6,14},{7,15},{8,0},{9,1},... | collective-permute-start | bytes 18874376 | tf_op jit(solution)/shard_map/ppermute | solution.py:447
  15.8 9.0 %collective-permute-start.1 = (bf16[512,512]{1,0:T(8,128)(2,1)S(1)}, bf16[512,512]{1,0:T(8,128)(2,1)}, u32[]{:S(2)}, u32[]{:S(2)}) collective-permute-start(bf16[512,512]{1,0:T(8,128)(2,1)S(1)} %get-tuple-element.45), channel_id=1, source_target_pairs={{0,1},{1,2},{2,3},{3,0},{4,5},{5,6},{6,7},{7,4},{8,11},{9,8},{10,9... | collective-permute-start | bytes 1572872 | tf_op jit(solution)/shard_map/ppermute | solution.py:447
  16.8 9.5 %collective-permute-start.2 = (bf16[512,512]{1,0:T(8,128)(2,1)S(1)}, bf16[512,512]{1,0:T(8,128)(2,1)S(1)}, u32[]{:S(2)}, u32[]{:S(2)}) collective-permute-start(bf16[512,512]{1,0:T(8,128)(2,1)S(1)} %get-tuple-element.45), channel_id=1, source_target_pairs={{0,4},{1,5},{2,6},{3,7},{4,0},{5,1},{6,2},{7,3},{8,140},{9,141},{1... | collective-permute-start | bytes 1572872 | tf_op jit(solution)/shard_map/ppermute | solution.py:447
  19.3 17.8 %collective-permute-start.3 = (bf16[512,512]{1,0:T(8,128)(2,1)S(1)}, bf16[512,512]{1,0:T(8,128)(2,1)S(1)}, u32[]{:S(2)}, u32[]{:S(2)}) collective-permute-start(bf16[512,512]{1,0:T(8,128)(2,1)S(1)} %copy-done.10), channel_id=1, source_target_pairs={{0,1},{1,2},{2,3},{3,0},{4,5},{5,6},{6,7},{7,4},{8,11},{9,8},{10,9... | collective-permute-start | bytes 1572872 | tf_op jit(solution)/shard_map/ppermute | solution.py:447
  19.8 17.4 %collective-permute-start.4 = (bf16[512,512]{1,0:T(8,128)(2,1)S(1)}, bf16[512,512]{1,0:T(8,128)(2,1)S(1)}, u32[]{:S(2)}, u32[]{:S(2)}) collective-permute-start(bf16[512,512]{1,0:T(8,128)(2,1)S(1)} %copy-done.10), channel_id=1, source_target_pairs={{0,4},{1,5},{2,6},{3,7},{4,0},{5,1},{6,2},{7,3},{8,140},{9,141},{1... | collective-permute-start | bytes 1572872 | tf_op jit(solution)/shard_map/ppermute | solution.py:447
  26.4 11.8 %copy-start.5 = (bf16[512,512]{1,0:T(8,128)(2,1)}, bf16[512,512]{1,0:T(8,128)(2,1)S(1)}, u32[]{:S(2)}) copy-start(bf16[512,512]{1,0:T(8,128)(2,1)S(1)} %get-tuple-element.28.refs_4_) | copy-start | bytes 1572868
  26.4 11.8 %copy-start.7 = (s32[11]{0:T(128)S(1)}, s32[11]{0:T(128)}, u32[]{:S(2)}) copy-start(s32[11]{0:T(128)} %stack.47.kidx.place) | copy-start | bytes 136
  26.4 25.3 %collective-permute-start.7 = (bf16[1024,512]{1,0:T(8,128)(2,1)}, bf16[1024,512]{1,0:T(8,128)(2,1)}, u32[]{:S(2)}, u32[]{:S(2)}) collective-permute-start(bf16[1024,512]{1,0:T(8,128)(2,1)} %get-tuple-element.24.refs_0_), channel_id=1, source_target_pairs={{0,3},{1,0},{2,1},{3,2},{4,7},{5,4},{6,5},{7,6},{8,9},{9,10},{10,1... | collective-permute-start | bytes 3145736 | tf_op jit(solution)/shard_map/ppermute | solution.py:447
  26.6 50.9 %all-to-all-start = ((bf16[8,256,256]{2,1,0:T(8,128)(2,1)}), bf16[8,256,256]{2,1,0:T(8,128)(2,1)S(1)}, u32[]{:S(2)}, u32[]{:S(2)}) async-start(bf16[8,256,256]{2,1,0:T(8,128)(2,1)} %get-tuple-element.40), calls=%async_computation | async-start | bytes 2097152 | tf_op jit(solution)/shard_map/all_to_all | solution.py:479
  34.7 17.0 %collective-permute-start.9 = (bf16[512,512]{1,0:T(8,128)(2,1)}, bf16[512,512]{1,0:T(8,128)(2,1)S(1)}, u32[]{:S(2)}, u32[]{:S(2)}) collective-permute-start(bf16[512,512]{1,0:T(8,128)(2,1)} %get-tuple-element.26.refs_2_), channel_id=1, source_target_pairs={{0,4},{1,5},{2,6},{3,7},{4,0},{5,1},{6,2},{7,3},{8,140},{9,141},{1... | collective-permute-start | bytes 1572872 | tf_op jit(solution)/shard_map/ppermute | solution.py:447
  38.0 13.7 %collective-permute-start.8 = (bf16[512,512]{1,0:T(8,128)(2,1)S(1)}, bf16[512,512]{1,0:T(8,128)(2,1)S(1)}, u32[]{:S(2)}, u32[]{:S(2)}) collective-permute-start(bf16[512,512]{1,0:T(8,128)(2,1)S(1)} %get-tuple-element.25.refs_1_), channel_id=1, source_target_pairs={{0,4},{1,5},{2,6},{3,7},{4,0},{5,1},{6,2},{7,3},{8,140},{9,141},{1... | collective-permute-start | bytes 1572872 | tf_op jit(solution)/shard_map/ppermute | solution.py:447
  38.2 16.1 %slice-start = ((s8[6291456]{0:T(1024)(128)(4,1)}), s8[4194304]{0:T(1024)(128)(4,1)S(1)}, s32[]{:S(2)}) async-start(s8[6291456]{0:T(1024)(128)(4,1)} %bitcast.25), calls=%async_computation.4 | async-start | bytes 8388608
  40.7 13.6 %slice-start.1 = ((s8[6291456]{0:T(1024)(128)(4,1)}), s8[2097152]{0:T(1024)(128)(4,1)S(1)}, s32[]{:S(2)}) async-start(s8[6291456]{0:T(1024)(128)(4,1)} %bitcast.25), calls=%async_computation.5 | async-start | bytes 4194304
  48.9 15.1 %collective-permute-start.5 = (bf16[1024,512]{1,0:T(8,128)(2,1)S(1)}, bf16[1024,512]{1,0:T(8,128)(2,1)S(1)}, u32[]{:S(2)}, u32[]{:S(2)}) collective-permute-start(bf16[1024,512]{1,0:T(8,128)(2,1)S(1)} %get-tuple-element.29.refs_3_), channel_id=1, source_target_pairs={{0,1},{1,2},{2,3},{3,0},{4,5},{5,6},{6,7},{7,4},{8,11},{9,8},{10,9... | collective-permute-start | bytes 3145736 | tf_op jit(solution)/shard_map/ppermute | solution.py:447
  51.7 15.2 %collective-permute-start.12 = (bf16[1024,512]{1,0:T(8,128)(2,1)}, bf16[1024,512]{1,0:T(8,128)(2,1)S(1)}, u32[]{:S(2)}, u32[]{:S(2)}) collective-permute-start(bf16[1024,512]{1,0:T(8,128)(2,1)} %get-tuple-element.31.refs_1_), channel_id=1, source_target_pairs={{0,4},{1,5},{2,6},{3,7},{4,0},{5,1},{6,2},{7,3},{8,140},{9,141},{1... | collective-permute-start | bytes 3145736 | tf_op jit(solution)/shard_map/ppermute | solution.py:447
  54.2 18.4 %collective-permute-start.11 = (bf16[256,2048]{1,0:T(8,128)(2,1)S(1)}, bf16[256,2048]{1,0:T(8,128)(2,1)}, u32[]{:S(2)}, u32[]{:S(2)}) collective-permute-start(bf16[256,2048]{1,0:T(8,128)(2,1)S(1)} %copy-done.2), channel_id=1, source_target_pairs={{0,8},{1,9},{2,10},{3,11},{4,12},{5,13},{6,14},{7,15},{8,0},{9,1},... | collective-permute-start | bytes 3145736 | tf_op jit(solution)/shard_map/ppermute | solution.py:447
  62.9 9.7 %collective-permute-start.10 = (bf16[512,512]{1,0:T(8,128)(2,1)S(1)}, bf16[512,512]{1,0:T(8,128)(2,1)S(1)}, u32[]{:S(2)}, u32[]{:S(2)}) collective-permute-start(bf16[512,512]{1,0:T(8,128)(2,1)S(1)} %get-tuple-element.35), channel_id=1, source_target_pairs={{0,1},{1,2},{2,3},{3,0},{4,5},{5,6},{6,7},{7,4},{8,11},{9,8},{10,9... | collective-permute-start | bytes 1572872 | tf_op jit(solution)/shard_map/ppermute | solution.py:447
  64.1 9.7 %collective-permute-start.6 = (bf16[512,512]{1,0:T(8,128)(2,1)S(1)}, bf16[512,512]{1,0:T(8,128)(2,1)S(1)}, u32[]{:S(2)}, u32[]{:S(2)}) collective-permute-start(bf16[512,512]{1,0:T(8,128)(2,1)S(1)} %slice.12), channel_id=1, source_target_pairs={{0,4},{1,5},{2,6},{3,7},{4,0},{5,1},{6,2},{7,3},{8,140},{9,141},{1... | collective-permute-start | bytes 1572872 | tf_op jit(solution)/shard_map/ppermute | solution.py:447
  66.0 6.6 %collective-permute-start.13 = (f32[3,256,1]{2,1,0:T(8,128)S(1)}, f32[3,256,1]{2,1,0:T(8,128)S(1)}, u32[]{:S(2)}, u32[]{:S(2)}) collective-permute-start(f32[3,256,1]{2,1,0:T(8,128)S(1)} %get-tuple-element.39.low_own), channel_id=1, source_target_pairs={{0,8},{1,9},{2,10},{3,11},{4,12},{5,13},{6,14},{7,15},{8,0},{9,1},... | collective-permute-start | bytes 9224 | tf_op jit(solution)/shard_map/ppermute | solution.py:447
  77.6 29.1 %copy-start = (bf16[8,256,256]{2,1,0:T(8,128)(2,1)}, bf16[8,256,256]{2,1,0:T(8,128)(2,1)S(1)}, u32[]{:S(2)}) copy-start(bf16[8,256,256]{2,1,0:T(8,128)(2,1)S(1)} %all-to-all-done.refs_1_.fout_all) | copy-start | bytes 3145732
  88.4 18.3 %all-to-all-start.2 = ((f32[16,1,512]{2,1,0:T(1,128)}), f32[16,1,512]{2,1,0:T(1,128)S(1)}, u32[]{:S(2)}, u32[]{:S(2)}) async-start(f32[16,1,512]{2,1,0:T(1,128)} %shard_map.78), calls=%async_computation.2 | async-start | bytes 65536 | tf_op jit(solution)/shard_map/all_to_all | solution.py:434
  111.2 3.3 %collective-permute-start.14 = (f32[2,64,512]{2,1,0:T(8,128)}, f32[2,64,512]{2,1,0:T(8,128)S(1)}, u32[]{:S(2)}, u32[]{:S(2)}) collective-permute-start(f32[2,64,512]{2,1,0:T(8,128)} %get-tuple-element.42), channel_id=1, source_target_pairs={{0,8},{1,9},{2,10},{3,11},{4,12},{5,13},{6,14},{7,15},{8,0},{9,1},... | collective-permute-start | bytes 786440 | tf_op jit(solution)/shard_map/ppermute | solution.py:447
  115.5 6.3 %collective-permute-start.15 = (f32[64,512]{1,0:T(8,128)S(1)}, f32[64,512]{1,0:T(8,128)S(1)}, u32[]{:S(2)}, u32[]{:S(2)}) collective-permute-start(f32[64,512]{1,0:T(8,128)S(1)} %slice_bitcast_fusion), channel_id=1, source_target_pairs={{0,128},{1,129},{2,130},{3,131},{4,132},{5,133},{6,134},{7,135},{8... | collective-permute-start | bytes 393224 | tf_op jit(solution)/shard_map/ppermute | solution.py:447
  (9 other events, 31.5 us)
Sparse Core Ops, SparseCore 0:
  15.9 59.4 all-gather.2

commit v10 on v7

--- a/solution.py
+++ b/solution.py
@@ -17,8 +17,8 @@
 WA = XL * Y
 CHAINS = 2
 ROWS_ALL = 24
-VMEM_BYTES = 40 * 1024 * 1024
-LAST_BYTES = 40 * 1024 * 1024
+VMEM_BYTES = 42 * 1024 * 1024
+LAST_BYTES = 42 * 1024 * 1024
 SMALL_BYTES = 1024 * 1024
 LARGE_BYTES = 58 * 1024 * 1024
 
@@ -166,34 +166,37 @@
     )(kidx, *args)
 
 
-def last_kernel(kidx, *refs):
-    sent = refs[:CHAINS]
-    x, acc, low_own, low_oth, fout_own, fout_oth, readout, out, ws, w_sems = refs[CHAINS:]
+def last_kernel(kidx, w_lo, w_hi, fout_mine, fout_theirs, x, acc, low_own, low_oth, readout, out, ws, w_sems, fouts, f_sems):
     members, width = acc.shape[2], acc.shape[3]
     block = ws.shape[1]
-    part_rows = sent[0].shape[0]
+    rows = w_lo.shape[0]
+    first = pl.multiple_of(kidx[8] * width, width)
     copies = []
-    for h in range(CHAINS):
-        to = ws.at[pl.ds(h * part_rows, part_rows), :]
-        copies.append(pltpu.make_async_copy(sent[h], to, w_sems.at[h]))
-        copies[-1].start()
+    for h, part in enumerate((w_lo, w_hi)):
+        copies.append(pltpu.make_async_copy(part, ws.at[pl.ds(h * rows, rows), :], w_sems.at[h]))
+    moves = []
+    for side, fout in ((0, fout_mine), (1, fout_theirs)):
+        moves.append(pltpu.make_async_copy(fout.at[:, pl.ds(first, width)], fouts.at[side], f_sems.at[side]))
+    for copy in copies + moves:
+        copy.start()
     for copy in copies:
         copy.wait()
     chunk = 256
     ones = jnp.ones((8, 128), jnp.float32)
-    for side, low, fout in ((0, low_own, fout_own), (1, low_oth, fout_oth)):
+    for side, low in ((0, low_own), (1, low_oth)):
+        moves[side].wait()
         total = jnp.zeros((members, 128), jnp.float32)
         for j in range(0, width, chunk):
             cols = pl.ds(j, chunk)
             part = nt_dot(x[side].reshape(3 * members, block), ws[cols, :])
             part = part.reshape(3, members, chunk)
-            shift = fout[:, cols].astype(jnp.float32)
+            shift = fouts[side, :, cols].astype(jnp.float32)
             summed = None
             for r in range(3):
                 pert = part[r] + acc[side, r, :, cols] + low[r] * shift
                 term = jnp.tanh(pert)
                 summed = term if summed is None else summed + term
-            summed = summed * readout[:, cols]
+            summed = summed * readout[:, pl.ds(pl.multiple_of(first + j, chunk), chunk)]
             for h in range(0, chunk, 128):
                 total = total + summed[:, h : h + 128]
         row = lax.dot_general(
@@ -208,21 +211,23 @@
             out[k, :, at] = row
 
 
-def last_matmul(kidx, sent, x, acc, low_own, low_oth, fout_own, fout_oth, readout):
+def last_matmul(kidx, w_lo, w_hi, fout_mine, fout_theirs, x, acc, low_own, low_oth, readout):
     members = x.shape[2]
-    part, block = sent[0].shape
-    width = part * CHAINS
+    block = w_lo.shape[1]
+    width = acc.shape[3]
     smem = pl.BlockSpec(memory_space=pltpu.SMEM)
     vmem = pl.BlockSpec(memory_space=pltpu.VMEM)
     hbm = pl.BlockSpec(memory_space=pl.ANY)
     return pl.pallas_call(
         last_kernel,
         out_shape=jax.ShapeDtypeStruct((CORE * WA, 1, 2 * members), jnp.float32),
-        in_specs=[smem] + [hbm] * CHAINS + [vmem] * 7,
+        in_specs=[smem] + [hbm] * 4 + [vmem] * 5,
         out_specs=vmem,
         scratch_shapes=[
             pltpu.VMEM((width, block), jnp.bfloat16),
-            pltpu.SemaphoreType.DMA((CHAINS,)),
+            pltpu.SemaphoreType.DMA((2,)),
+            pltpu.VMEM((2, members, width), jnp.bfloat16),
+            pltpu.SemaphoreType.DMA((2,)),
         ],
         compiler_params=pltpu.CompilerParams(vmem_limit_bytes=LAST_BYTES),
         cost_estimate=pl.CostEstimate(
@@ -230,7 +235,7 @@
             bytes_accessed=6 * 1024 * 1024,
             transcendentals=6 * members * width,
         ),
-    )(kidx, *sent, x, acc, low_own, low_oth, fout_own, fout_oth, readout)
+    )(kidx, w_lo, w_hi, fout_mine, fout_theirs, x, acc, low_own, low_oth, readout)
 
 
 def after_kernel(*refs):
@@ -265,71 +270,30 @@
     )(got)
 
 
-def cut_kernel(place, fout_all, readout, pieces, mine, theirs, read, fout, sems):
-    half = mine.shape[1]
-    first = pltpu.make_async_copy(fout_all, fout, sems.at[0])
-    first.start()
-    read[...] = readout[:, pl.ds(pl.multiple_of(place[8] * half, half), half)]
-    moves = []
-    run = pieces.shape[2] // XH
+def cut_kernel(fout, pieces, token):
+    token[...] = jnp.zeros_like(token)
+    half = fout.shape[1] // XH
+    run = pieces.shape[1] // XH
     for h in range(XH):
         for k in range(Z):
             cols = pl.ds(h * half + k * run, run)
-            moves.append((fout.at[:, cols], pieces.at[k, :, pl.ds(h * run, run)]))
-    for at, to in ((place[8], mine), (1 - place[8], theirs)):
-        cols = pl.ds(pl.multiple_of(at * half, half), half)
-        moves.append((fout.at[:, cols], to))
-    copies = [pltpu.make_async_copy(x, y, sems.at[i + 1]) for i, (x, y) in enumerate(moves)]
-    first.wait()
-    for copy in copies:
-        copy.start()
-    for copy in copies:
-        copy.wait()
-
-
-def cut_factors(place, fout, readout):
+            pieces[k, pl.ds(h * run, run), :] = jnp.transpose(fout[:, cols])
+
+
+def cut_factors(fout):
     members, out_width = fout.shape
-    half = out_width // CORE
-    hbm = pl.BlockSpec(memory_space=pl.ANY)
     vmem = pl.BlockSpec(memory_space=pltpu.VMEM)
     return pl.pallas_call(
         cut_kernel,
         out_shape=(
-            jax.ShapeDtypeStruct((Z, members, out_width // Z), fout.dtype),
-            jax.ShapeDtypeStruct((members, half), fout.dtype),
-            jax.ShapeDtypeStruct((members, half), fout.dtype),
-            jax.ShapeDtypeStruct((1, half), readout.dtype),
+            jax.ShapeDtypeStruct((Z, out_width // Z, members), fout.dtype),
+            jax.ShapeDtypeStruct((8, 128), jnp.float32),
         ),
-        in_specs=[pl.BlockSpec(memory_space=pltpu.SMEM), hbm, vmem],
-        out_specs=(hbm, hbm, hbm, vmem),
-        scratch_shapes=[
-            pltpu.VMEM(fout.shape, fout.dtype),
-            pltpu.SemaphoreType.DMA((3 + XH * Z,)),
-        ],
+        in_specs=[vmem],
+        out_specs=(vmem, vmem),
         compiler_params=pltpu.CompilerParams(vmem_limit_bytes=LARGE_BYTES),
         cost_estimate=pl.CostEstimate(flops=0, bytes_accessed=4 * 1024 * 1024, transcendentals=0),
-    )(place, fout, readout)
-
-
-def block_kernel(place, fin, *refs):
-    out, sem = refs[-2:]
-    block = out.shape[1]
-    cols = pl.ds(pl.multiple_of(place[0] * block, block), block)
-    copy = pltpu.make_async_copy(fin.at[:, cols], out, sem.at[0])
-    copy.start()
-    copy.wait()
-
-
-def cut_block(place, fin, block, *done):
-    hbm = pl.BlockSpec(memory_space=pl.ANY)
-    return pl.pallas_call(
-        block_kernel,
-        out_shape=jax.ShapeDtypeStruct((fin.shape[0], block), fin.dtype),
-        in_specs=[pl.BlockSpec(memory_space=pltpu.SMEM), hbm] + [hbm] * len(done),
-        out_specs=pl.BlockSpec(memory_space=pltpu.VMEM),
-        scratch_shapes=[pltpu.SemaphoreType.DMA((1,))],
-        compiler_params=pltpu.CompilerParams(vmem_limit_bytes=LARGE_BYTES),
-    )(place, fin, *done)
+    )(fout)
 
 
 def low_kernel(x, fin, out, x_buf, f_buf, sems):
@@ -381,7 +345,7 @@
     )(x, fin)
 
 
-def step_kernel(place, fit, fout_all, fin_all, keep, give, util, rows_ref, fout, fin, sems):
+def step_kernel(place, fit, fout_all, fin_all, keep, give, util, fout, fin, sems):
     copies = []
     for k in range(Z):
         pair = (
@@ -400,17 +364,13 @@
     c, xh, z = place[8], place[9], place[10]
     at = pl.ds(pl.multiple_of(c * members, members), members)
     util[...] = (fit[xh * Z + z, :, at] - mean) / root
-    for k in range(Z):
-        rows_ref[k : k + 1, :] = fit[xh * Z + k, :, at]
-    columns = (jnp.transpose(rows_ref[...]) - mean) / root
     total = None
     for k in range(Z):
         for copy in copies[k]:
             copy.wait()
-        scaled = (fout[k].astype(jnp.float32) * columns[:, k : k + 1]).astype(jnp.bfloat16)
-        one = lax.dot_general(
-            scaled, fin[k], (((0,), (0,)), ((), ())), preferred_element_type=jnp.float32
-        )
+        row = (fit[xh * Z + k, :, at] - mean) / root
+        scaled = (fout[k].astype(jnp.float32) * row).astype(jnp.bfloat16)
+        one = jnp.dot(scaled, fin[k], preferred_element_type=jnp.float32)
         total = one if total is None else total + one
     total = total * (1.0 / np.sqrt(float(count)))
     rows = keep.shape[1]
@@ -422,7 +382,7 @@
 
 
 def weight_part(place, fit, fout, fin):
-    members, rows = fout.shape[1], fout.shape[2]
+    rows, members = fout.shape[1], fout.shape[2]
     cols = fin.shape[2]
     vmem = pl.BlockSpec(memory_space=pltpu.VMEM)
     hbm = pl.BlockSpec(memory_space=pl.ANY)
@@ -433,7 +393,6 @@
         in_specs=[pl.BlockSpec(memory_space=pltpu.SMEM), vmem, hbm, hbm],
         out_specs=(vmem, vmem, vmem),
         scratch_shapes=[
-            pltpu.VMEM((Z, members), jnp.float32),
             pltpu.VMEM(fout.shape, fout.dtype),
             pltpu.VMEM(fin.shape, fin.dtype),
             pltpu.SemaphoreType.DMA((Z, 2)),
@@ -488,12 +447,13 @@
     w_d = [send(w, x_go) for w in own]
     x_oth = send(x_own, core_go)
 
-    fin_all = lax.all_gather(cut_block(places, factor_in, block), "z", axis=0)
-    pieces_here, fout_mine, fout_theirs, read_mine = cut_factors(places, factor_out, readout[None])
+    fin_here = lax.dynamic_slice_in_dim(factor_in, wa * block, block, 1)
+    fin_all = lax.all_gather(fin_here, "z", axis=0)
+    pieces_here, cut_done = cut_factors(factor_out)
     pieces = lax.all_to_all(pieces_here, "z", 0, 0, tiled=True)
+    fout_oth = send(factor_out, core_go)
     low_own = low_term(x_own, factor_in)
     low_oth = send(low_own, core_go)
-    fout_got = send(fout_theirs, core_go)
 
     w_b, w_e, w_c, w_f, w_g = ([None] * CHAINS for _ in range(5))
     for h in chains:
@@ -511,7 +471,7 @@
         w_g[h] = send(w_c[h], x_go) if h == 0 else send(w_e[h], y_fwd)
     acc, token, x_last = group_matmul(5, places, x_own, x_oth, [w_f, w_c], acc, ahead=True)
     partial = last_matmul(
-        places, w_g, x_last, acc, low_own, low_oth, fout_mine, fout_got, read_mine
+        places, *w_g, factor_out, fout_oth, x_last, acc, low_own, low_oth, readout[None]
     )
     (partial,) = after((partial,), pieces)
 

time: 127 us -> 127 us (level)
  local copies, waits for them, and re-layouts: 2.6 us -> 8.01 us
  Pallas kernels: 37.9 us -> 34.3 us
  starting transfers between devices: 43.6 us -> 40.2 us
  waiting for transfers between devices: 18.6 us -> 20 us
    pallas_call x2 -> x1, Pallas kernels: 6.49 us -> 2.52 us  [cut_factors(): pl.pallas_call(cut_kernel, out_shape=(jax.ShapeDtypeStruct((Z, out_width...]
    unnamed x18 -> x22, local copies, waits for them, and re-layouts: 0.65 us -> 3.93 us
    ppermute x19, starting transfers between devices: 24.7 us -> 22.5 us  [send(): return lax.ppermute(v, AXES, pairs)]
    dynamic_slice x0 -> x1, local copies, waits for them, and re-layouts: none -> 1.7 us  [shards(): fin_here = lax.dynamic_slice_in_dim(factor_in, wa * block, block, 1)]
    ppermute x19, waiting for transfers between devices: 9.69 us -> 11.1 us  [send(): return lax.ppermute(v, AXES, pairs)]
  transfers between devices with their start and end apart: 22 -> 22, of which waited for: 6 -> 5; matrix products, arithmetic and copies ran while one was open for 2% -> 3% of each run, Pallas kernels for 26% -> 24%
where the time goes in v10:
time: 127 us; the launch traced here: 126 us
  starting transfers between devices  40.2 us (32%)
  Pallas kernels  34.3 us (27%)
  waiting for transfers between devices  20 us (16%)
  between operations  14.3 us (11%)
  local copies, waits for them, and re-layouts  8.01 us (6%)
  blocking collectives  7.75 us (6%)
  other arithmetic  1.67 us (1%)
    ppermute x19, starting transfers between devices, send(): return lax.ppermute(v, AXES, pairs)  22.5 us
    pallas_call x3, Pallas kernels, group_matmul(): pl.pallas_call(functools.partial(group_kernel, base, count, acc is not No...  20.9 us
    ppermute x19, waiting for transfers between devices, send(): return lax.ppermute(v, AXES, pairs)  11.1 us
    all_to_all x1, starting transfers between devices, share(): return lax.all_to_all(x, axes, 0, 0, tiled=True)  9.42 us
    all_to_all x1, waiting for transfers between devices, share(): return lax.all_to_all(x, axes, 0, 0, tiled=True)  8.83 us
    all_to_all x1, starting transfers between devices, shards(): pieces = lax.all_to_all(pieces_here, 'z', 0, 0, tiled=True)  8.19 us
    all_to_all x1, blocking collectives, share(): return lax.all_to_all(x, axes, 0, 0, tiled=True)  7.75 us
    unnamed x22, local copies, waits for them, and re-layouts  3.93 us
  transfers between devices with their start and end apart: 22, of which 5 were waited for; matrix products, arithmetic and copies ran while one was open for 3% of the time, Pallas kernels for 24%

profile of v10, /device:TPU:1, one launch (start us, length us, event | category | flops | bytes accessed | tf_op | source)
XLA Modules:
  0.0 126.2 jit_solution(7517380312250231279)
XLA Ops:
  7.2 3.3 %collective-permute-start.4 = (bf16[3,256,4096]{2,1,0:T(8,128)(2,1)}, bf16[3,256,4096]{2,1,0:T(8,128)(2,1)}, u32[]{:S(2)}, u32[]{:S(2)}) collective-permute-start(bf16[3,256,4096]{2,1,0:T(8,128)(2,1)} %bitcast.21), channel_id=1, source_target_pairs={{0,8},{1,9},{2,10},{3,11},{4,12},{5,13},{6,14},{7,15},{8,0},{9,1},... | collective-permute-start | bytes 18874376 | tf_op jit(solution)/shard_map/ppermute | solution.py:421
  10.5 1.7 %constant_dynamic-slice_fusion = bf16[256,512]{1,0:T(8,128)(2,1)} fusion(bf16[256,4096]{1,0:T(8,128)(2,1)} %fin.1, s32[]{:T(128)S(6)} %select_n.11), kind=kLoop, calls=%fused_computation.3 | loop fusion | bytes 524292 | tf_op jit(solution)/shard_map/dynamic_slice | solution.py:450
  12.3 2.3 %constant_dynamic-slice_fusion.1 = (bf16[512,512]{1,0:T(8,128)(2,1)}, bf16[512,512]{1,0:T(8,128)(2,1)}) fusion(bf16[2048,512]{1,0:T(8,128)(2,1)} %param.6, s32[]{:T(128)S(6)} %select_n.10, s32[]{:T(128)S(6)} %select_n.9), kind=kLoop, calls=%fused_computation.4 | loop fusion | bytes 2097160 | tf_op jit(solution)/shard_map/dynamic_slice | solution.py:445
  15.5 2.5 %collective-permute-start.6 = (bf16[512,512]{1,0:T(8,128)(2,1)}, bf16[512,512]{1,0:T(8,128)(2,1)S(1)}, u32[]{:S(2)}, u32[]{:S(2)}) collective-permute-start(bf16[512,512]{1,0:T(8,128)(2,1)} %get-tuple-element.56.refs_0_), channel_id=1, source_target_pairs={{0,4},{1,5},{2,6},{3,7},{4,0},{5,1},{6,2},{7,3},{8,140},{9,141},{1... | collective-permute-start | bytes 1572872 | tf_op jit(solution)/shard_map/ppermute | solution.py:421
  18.7 2.5 %shard_map.79 = (bf16[8,256,256]{2,1,0:T(8,128)(2,1)}, f32[8,128]{1,0:T(8,128)}) custom-call(bf16[256,2048]{1,0:T(8,128)(2,1)} %fout.1), custom_call_target="tpu_custom_call" | custom-call | bytes 4194304 | tf_op jit(solution)/shard_map/pallas_call | solution.py:286
  21.2 8.2 %all-to-all-start = ((bf16[8,256,256]{2,1,0:T(8,128)(2,1)}), bf16[8,256,256]{2,1,0:T(8,128)(2,1)}, u32[]{:S(2)}, u32[]{:S(2)}) async-start(bf16[8,256,256]{2,1,0:T(8,128)(2,1)} %get-tuple-element.52), calls=%async_computation | async-start | bytes 2097152 | tf_op jit(solution)/shard_map/all_to_all | solution.py:453
  29.4 2.6 %collective-permute-start.10 = (bf16[512,512]{1,0:T(8,128)(2,1)}, bf16[512,512]{1,0:T(8,128)(2,1)}, u32[]{:S(2)}, u32[]{:S(2)}) collective-permute-start(bf16[512,512]{1,0:T(8,128)(2,1)} %get-tuple-element.32.refs_3_.refs_0_), channel_id=1, source_target_pairs={{0,4},{1,5},{2,6},{3,7},{4,0},{5,1},{6,2},{7,3},{8,140},{9,141},{1... | collective-permute-start | bytes 1572872 | tf_op jit(solution)/shard_map/ppermute | solution.py:421
  35.6 1.3 %copy-done.5 = bf16[512,512]{1,0:T(8,128)(2,1)S(1)} copy-done((bf16[512,512]{1,0:T(8,128)(2,1)S(1)}, bf16[512,512]{1,0:T(8,128)(2,1)}, u32[]{:S(2)}) %copy-start.5) | copy-done | bytes 524312
  36.9 8.3 %shard_map.70 = (f32[2,3,256,1024]{3,2,1,0:T(8,128)S(1)}, f32[8,128]{1,0:T(8,128)S(1)}) custom-call(s32[11]{0:T(128)S(1)} %stack.47.kidx.place, bf16[3,256,4096]{2,1,0:T(8,128)(2,1)} %bitcast.22, bf16[3,256,4096]{2,1,0:T(8,128)(2,1)} %collective-permute-done.4.x_oth, bf16[512,512]{1,0:T(8,128)(2,1)} %get-tuple-element.30.refs_0_, ...), custom_call_target="tpu_custom_call" | custom-call | flops 4831838208 | bytes 8388608 | tf_op jit(solution)/shard_map/pallas_call | solution.py:152
  45.2 2.8 %collective-permute-start.12 = (bf16[512,512]{1,0:T(8,128)(2,1)}, bf16[512,512]{1,0:T(8,128)(2,1)S(1)}, u32[]{:S(2)}, u32[]{:S(2)}) collective-permute-start(bf16[512,512]{1,0:T(8,128)(2,1)} %get-tuple-element.44), channel_id=1, source_target_pairs={{0,1},{1,2},{2,3},{3,0},{4,5},{5,6},{6,7},{7,4},{8,11},{9,8},{10,9... | collective-permute-start | bytes 1572872 | tf_op jit(solution)/shard_map/ppermute | solution.py:421
  48.0 2.2 %collective-permute-start.13 = (bf16[512,512]{1,0:T(8,128)(2,1)}, bf16[512,512]{1,0:T(8,128)(2,1)S(1)}, u32[]{:S(2)}, u32[]{:S(2)}) collective-permute-start(bf16[512,512]{1,0:T(8,128)(2,1)} %get-tuple-element.39.refs_2_), channel_id=1, source_target_pairs={{0,4},{1,5},{2,6},{3,7},{4,0},{5,1},{6,2},{7,3},{8,140},{9,141},{1... | collective-permute-start | bytes 1572872 | tf_op jit(solution)/shard_map/ppermute | solution.py:421
  51.0 2.5 %shard_map.72.refs_0_.low_own = f32[3,256,1]{2,1,0:T(8,128)S(1)} custom-call(bf16[3,256,4096]{2,1,0:T(8,128)(2,1)S(1)} %bitcast.27, bf16[256,4096]{1,0:T(8,128)(2,1)S(1)} %copy-done.1), custom_call_target="tpu_custom_call" | custom-call | flops 6291456 | bytes 9437184 | tf_op jit(solution)/shard_map/pallas_call | solution.py:331
  53.5 6.3 %shard_map.74 = (f32[2,3,256,1024]{3,2,1,0:T(8,128)S(1)}, f32[8,128]{1,0:T(8,128)S(1)}) custom-call(s32[11]{0:T(128)S(1)} %stack.47.kidx.place, bf16[3,256,4096]{2,1,0:T(8,128)(2,1)} %bitcast.23, bf16[3,256,4096]{2,1,0:T(8,128)(2,1)} %collective-permute-done.4.x_oth, f32[3,256,1]{2,1,0:T(8,128)S(1)} %shard_map.72.refs_0_.low_own, ...), custom_call_target="tpu_custom_call", output_to_operand_aliasing={{0}: (8, {})} | custom-call | flops 3221225472 | bytes 8388608 | tf_op jit(solution)/shard_map/pallas_call | solution.py:152
  60.6 2.8 %collective-permute-done.8.refs_1_ = bf16[512,512]{1,0:T(8,128)(2,1)S(1)} collective-permute-done((bf16[512,512]{1,0:T(8,128)(2,1)}, bf16[512,512]{1,0:T(8,128)(2,1)S(1)}, u32[]{:S(2)}, u32[]{:S(2)}) %collective-permute-start.8) | collective-permute-done | bytes 524320 | tf_op jit(solution)/shard_map/ppermute | solution.py:421
  63.5 2.2 %collective-permute-start.11 = (bf16[512,512]{1,0:T(8,128)(2,1)S(1)}, bf16[512,512]{1,0:T(8,128)(2,1)S(1)}, u32[]{:S(2)}, u32[]{:S(2)}) collective-permute-start(bf16[512,512]{1,0:T(8,128)(2,1)S(1)} %get-tuple-element.43.refs_2_), channel_id=1, source_target_pairs={{0,4},{1,5},{2,6},{3,7},{4,0},{5,1},{6,2},{7,3},{8,140},{9,141},{1... | collective-permute-start | bytes 1572872 | tf_op jit(solution)/shard_map/ppermute | solution.py:421
  65.7 6.3 %shard_map.77 = (f32[2,3,256,1024]{3,2,1,0:T(8,128)S(1)}, f32[8,128]{1,0:T(8,128)}, bf16[2,3,256,512]{3,2,1,0:T(8,128)(2,1)S(1)}) custom-call(s32[11]{0:T(128)S(1)} %stack.47.kidx.place, bf16[3,256,4096]{2,1,0:T(8,128)(2,1)} %bitcast.24, bf16[3,256,4096]{2,1,0:T(8,128)(2,1)} %collective-permute-done.4.x_oth, ...), custom_call_target="tpu_custom_call", output_to_operand_aliasing={{0}: (7, {})} | custom-call | flops 3221225472 | bytes 8388608 | tf_op jit(solution)/shard_map/pallas_call | solution.py:152
  73.0 3.8 %shard_map.78.refs_0_ = f32[16,1,512]{2,1,0:T(1,128)S(1)} custom-call(s32[11]{0:T(128)S(1)} %stack.47.kidx.place, bf16[512,512]{1,0:T(8,128)(2,1)S(1)} %collective-permute-done.11.w_lo, bf16[512,512]{1,0:T(8,128)(2,1)S(1)} %collective-permute-done.14.w_hi, bf16[256,2048]{1,0:T(8,128)(2,1)S(1)} %copy-done, ...), custom_call_target="tpu_custom_call" | custom-call | flops 1610612736 | bytes 6291456 | tf_op jit(solution)/shard_map/pallas_call | solution.py:221
  76.9 7.7 %all_to_all.15.got = f32[16,1,512]{2,1,0:T(1,128)S(1)} all-to-all(f32[16,1,512]{2,1,0:T(1,128)S(1)} %shard_map.80), channel_id=1, replica_groups=mesh['xh'=2,'z'=8,'core'=2,'xl'=2,'y'=4] {'core','xl','y'}, dimensions={0} | all-to-all | bytes 65536 | tf_op jit(solution)/shard_map/all_to_all | solution.py:408
  85.3 9.4 %all-to-all-start.2 = ((f32[16,1,512]{2,1,0:T(1,128)}), f32[16,1,512]{2,1,0:T(1,128)S(1)}, u32[]{:S(2)}, u32[]{:S(2)}) async-start(f32[16,1,512]{2,1,0:T(1,128)} %shard_map.81), calls=%async_computation.2 | async-start | bytes 65536 | tf_op jit(solution)/shard_map/all_to_all | solution.py:408
  94.7 8.8 %all-to-all-done.2.fit = f32[16,1,512]{2,1,0:T(1,128)S(1)} async-done(((f32[16,1,512]{2,1,0:T(1,128)}), f32[16,1,512]{2,1,0:T(1,128)S(1)}, u32[]{:S(2)}, u32[]{:S(2)}) %all-to-all-start.2) | async-done | bytes 32800 | tf_op jit(solution)/shard_map/all_to_all | solution.py:408
  104.2 3.9 %shard_map.82 = (f32[2,64,512]{2,1,0:T(8,128)}, f32[2,64,512]{2,1,0:T(8,128)}, f32[1,256]{1,0:T(1,128)}) custom-call(s32[11]{0:T(128)} %copy-done.6, f32[16,1,512]{2,1,0:T(1,128)} %copy-done.8, bf16[8,256,256]{2,1,0:T(8,128)(2,1)} %all-to-all-done.refs_1_.fout_all, bf16[8,256,512]{2,1,0:T(8,128)(2,1)} %bitcast.29), custom_call_target="tpu_custom_call" | custom-call | flops 536870912 | bytes 4194304 | tf_op jit(solution)/shard_map/pallas_call | solution.py:390
  108.1 1.9 %collective-permute-start.17 = (f32[2,64,512]{2,1,0:T(8,128)}, f32[2,64,512]{2,1,0:T(8,128)S(1)}, u32[]{:S(2)}, u32[]{:S(2)}) collective-permute-start(f32[2,64,512]{2,1,0:T(8,128)} %get-tuple-element.54), channel_id=1, source_target_pairs={{0,8},{1,9},{2,10},{3,11},{4,12},{5,13},{6,14},{7,15},{8,0},{9,1},... | collective-permute-start | bytes 786440 | tf_op jit(solution)/shard_map/ppermute | solution.py:421
  110.0 1.4 %collective-permute-done.17 = f32[2,64,512]{2,1,0:T(8,128)S(1)} collective-permute-done((f32[2,64,512]{2,1,0:T(8,128)}, f32[2,64,512]{2,1,0:T(8,128)S(1)}, u32[]{:S(2)}, u32[]{:S(2)}) %collective-permute-start.17) | collective-permute-done | bytes 262176 | tf_op jit(solution)/shard_map/ppermute | solution.py:421
  112.8 5.9 %collective-permute-done.18 = f32[64,512]{1,0:T(8,128)S(1)} collective-permute-done((f32[64,512]{1,0:T(8,128)S(1)}, f32[64,512]{1,0:T(8,128)S(1)}, u32[]{:S(2)}, u32[]{:S(2)}) %collective-permute-start.18) | collective-permute-done | bytes 131104 | tf_op jit(solution)/shard_map/ppermute | solution.py:421
  (66 shorter events, 11.3 us)
Async XLA Ops:
  7.2 87.5 %all-gather.3.cloned.1.call-start = ((), (), s32[]{:S(2)}) async-start(), calls=%async_computation.3 | async-start | bytes 2359296 | tf_op jit(solution)/shard_map/all_gather | solution.py:451
  7.2 27.2 %collective-permute-start.4 = (bf16[3,256,4096]{2,1,0:T(8,128)(2,1)}, bf16[3,256,4096]{2,1,0:T(8,128)(2,1)}, u32[]{:S(2)}, u32[]{:S(2)}) collective-permute-start(bf16[3,256,4096]{2,1,0:T(8,128)(2,1)} %bitcast.21), channel_id=1, source_target_pairs={{0,8},{1,9},{2,10},{3,11},{4,12},{5,13},{6,14},{7,15},{8,0},{9,1},... | collective-permute-start | bytes 18874376 | tf_op jit(solution)/shard_map/ppermute | solution.py:421
  14.5 14.9 %collective-permute-start.5 = (bf16[512,512]{1,0:T(8,128)(2,1)}, bf16[512,512]{1,0:T(8,128)(2,1)}, u32[]{:S(2)}, u32[]{:S(2)}) collective-permute-start(bf16[512,512]{1,0:T(8,128)(2,1)} %get-tuple-element.56.refs_0_), channel_id=1, source_target_pairs={{0,1},{1,2},{2,3},{3,0},{4,5},{5,6},{6,7},{7,4},{8,11},{9,8},{10,9... | collective-permute-start | bytes 1572872 | tf_op jit(solution)/shard_map/ppermute | solution.py:421
  15.5 13.9 %collective-permute-start.6 = (bf16[512,512]{1,0:T(8,128)(2,1)}, bf16[512,512]{1,0:T(8,128)(2,1)S(1)}, u32[]{:S(2)}, u32[]{:S(2)}) collective-permute-start(bf16[512,512]{1,0:T(8,128)(2,1)} %get-tuple-element.56.refs_0_), channel_id=1, source_target_pairs={{0,4},{1,5},{2,6},{3,7},{4,0},{5,1},{6,2},{7,3},{8,140},{9,141},{1... | collective-permute-start | bytes 1572872 | tf_op jit(solution)/shard_map/ppermute | solution.py:421
  18.0 15.0 %collective-permute-start = (bf16[512,512]{1,0:T(8,128)(2,1)}, bf16[512,512]{1,0:T(8,128)(2,1)}, u32[]{:S(2)}, u32[]{:S(2)}) collective-permute-start(bf16[512,512]{1,0:T(8,128)(2,1)} %get-tuple-element.57.refs_0_), channel_id=1, source_target_pairs={{0,1},{1,2},{2,3},{3,0},{4,5},{5,6},{6,7},{7,4},{8,11},{9,8},{10,9... | collective-permute-start | bytes 1572872 | tf_op jit(solution)/shard_map/ppermute | solution.py:421
  18.5 14.5 %collective-permute-start.1 = (bf16[512,512]{1,0:T(8,128)(2,1)}, bf16[512,512]{1,0:T(8,128)(2,1)S(1)}, u32[]{:S(2)}, u32[]{:S(2)}) collective-permute-start(bf16[512,512]{1,0:T(8,128)(2,1)} %get-tuple-element.57.refs_0_), channel_id=1, source_target_pairs={{0,4},{1,5},{2,6},{3,7},{4,0},{5,1},{6,2},{7,3},{8,140},{9,141},{1... | collective-permute-start | bytes 1572872 | tf_op jit(solution)/shard_map/ppermute | solution.py:421
  21.2 55.6 %all-to-all-start = ((bf16[8,256,256]{2,1,0:T(8,128)(2,1)}), bf16[8,256,256]{2,1,0:T(8,128)(2,1)}, u32[]{:S(2)}, u32[]{:S(2)}) async-start(bf16[8,256,256]{2,1,0:T(8,128)(2,1)} %get-tuple-element.52), calls=%async_computation | async-start | bytes 2097152 | tf_op jit(solution)/shard_map/all_to_all | solution.py:453
  29.4 15.8 %collective-permute-start.10 = (bf16[512,512]{1,0:T(8,128)(2,1)}, bf16[512,512]{1,0:T(8,128)(2,1)}, u32[]{:S(2)}, u32[]{:S(2)}) collective-permute-start(bf16[512,512]{1,0:T(8,128)(2,1)} %get-tuple-element.32.refs_3_.refs_0_), channel_id=1, source_target_pairs={{0,4},{1,5},{2,6},{3,7},{4,0},{5,1},{6,2},{7,3},{8,140},{9,141},{1... | collective-permute-start | bytes 1572872 | tf_op jit(solution)/shard_map/ppermute | solution.py:421
  32.0 13.2 %collective-permute-start.9 = (bf16[512,512]{1,0:T(8,128)(2,1)}, bf16[512,512]{1,0:T(8,128)(2,1)}, u32[]{:S(2)}, u32[]{:S(2)}) collective-permute-start(bf16[512,512]{1,0:T(8,128)(2,1)} %get-tuple-element.31.refs_1_), channel_id=1, source_target_pairs={{0,3},{1,0},{2,1},{3,2},{4,7},{5,4},{6,5},{7,6},{8,9},{9,10},{10,1... | collective-permute-start | bytes 1572872 | tf_op jit(solution)/shard_map/ppermute | solution.py:421
  33.8 16.4 %collective-permute-start.3 = (bf16[512,512]{1,0:T(8,128)(2,1)}, bf16[512,512]{1,0:T(8,128)(2,1)}, u32[]{:S(2)}, u32[]{:S(2)}) collective-permute-start(bf16[512,512]{1,0:T(8,128)(2,1)} %get-tuple-element.29.refs_2_.refs_0_), channel_id=1, source_target_pairs={{0,4},{1,5},{2,6},{3,7},{4,0},{5,1},{6,2},{7,3},{8,140},{9,141},{1... | collective-permute-start | bytes 1572872 | tf_op jit(solution)/shard_map/ppermute | solution.py:421
  34.3 15.9 %collective-permute-start.2 = (bf16[512,512]{1,0:T(8,128)(2,1)}, bf16[512,512]{1,0:T(8,128)(2,1)}, u32[]{:S(2)}, u32[]{:S(2)}) collective-permute-start(bf16[512,512]{1,0:T(8,128)(2,1)} %get-tuple-element.30.refs_0_), channel_id=1, source_target_pairs={{0,3},{1,0},{2,1},{3,2},{4,7},{5,4},{6,5},{7,6},{8,9},{9,10},{10,1... | collective-permute-start | bytes 1572872 | tf_op jit(solution)/shard_map/ppermute | solution.py:421
  34.4 38.6 %copy-start.6 = (s32[11]{0:T(128)}, s32[11]{0:T(128)S(1)}, u32[]{:S(2)}) copy-start(s32[11]{0:T(128)S(1)} %stack.47.kidx.place) | copy-start | bytes 136
  34.4 16.5 %slice-start = ((s8[6291456]{0:T(1024)(128)(4,1)}), s8[4194304]{0:T(1024)(128)(4,1)S(1)}, s32[]{:S(2)}) async-start(s8[6291456]{0:T(1024)(128)(4,1)} %bitcast.25), calls=%async_computation.4 | async-start | bytes 8388608
  45.2 14.6 %collective-permute-start.12 = (bf16[512,512]{1,0:T(8,128)(2,1)}, bf16[512,512]{1,0:T(8,128)(2,1)S(1)}, u32[]{:S(2)}, u32[]{:S(2)}) collective-permute-start(bf16[512,512]{1,0:T(8,128)(2,1)} %get-tuple-element.44), channel_id=1, source_target_pairs={{0,1},{1,2},{2,3},{3,0},{4,5},{5,6},{6,7},{7,4},{8,11},{9,8},{10,9... | collective-permute-start | bytes 1572872 | tf_op jit(solution)/shard_map/ppermute | solution.py:421
  48.0 11.9 %collective-permute-start.13 = (bf16[512,512]{1,0:T(8,128)(2,1)}, bf16[512,512]{1,0:T(8,128)(2,1)S(1)}, u32[]{:S(2)}, u32[]{:S(2)}) collective-permute-start(bf16[512,512]{1,0:T(8,128)(2,1)} %get-tuple-element.39.refs_2_), channel_id=1, source_target_pairs={{0,4},{1,5},{2,6},{3,7},{4,0},{5,1},{6,2},{7,3},{8,140},{9,141},{1... | collective-permute-start | bytes 1572872 | tf_op jit(solution)/shard_map/ppermute | solution.py:421
  50.2 10.4 %collective-permute-start.7 = (bf16[512,512]{1,0:T(8,128)(2,1)}, bf16[512,512]{1,0:T(8,128)(2,1)S(1)}, u32[]{:S(2)}, u32[]{:S(2)}) collective-permute-start(bf16[512,512]{1,0:T(8,128)(2,1)} %get-tuple-element.36), channel_id=1, source_target_pairs={{0,1},{1,2},{2,3},{3,0},{4,5},{5,6},{6,7},{7,4},{8,11},{9,8},{10,9... | collective-permute-start | bytes 1572872 | tf_op jit(solution)/shard_map/ppermute | solution.py:421
  50.7 12.8 %collective-permute-start.8 = (bf16[512,512]{1,0:T(8,128)(2,1)}, bf16[512,512]{1,0:T(8,128)(2,1)S(1)}, u32[]{:S(2)}, u32[]{:S(2)}) collective-permute-start(bf16[512,512]{1,0:T(8,128)(2,1)} %get-tuple-element.37.refs_1_), channel_id=1, source_target_pairs={{0,4},{1,5},{2,6},{3,7},{4,0},{5,1},{6,2},{7,3},{8,140},{9,141},{1... | collective-permute-start | bytes 1572872 | tf_op jit(solution)/shard_map/ppermute | solution.py:421
  51.0 21.0 %collective-permute-start.15 = (bf16[256,2048]{1,0:T(8,128)(2,1)S(1)}, bf16[256,2048]{1,0:T(8,128)(2,1)S(1)}, u32[]{:S(2)}, u32[]{:S(2)}) collective-permute-start(bf16[256,2048]{1,0:T(8,128)(2,1)S(1)} %copy-done), channel_id=1, source_target_pairs={{0,8},{1,9},{2,10},{3,11},{4,12},{5,13},{6,14},{7,15},{8,0},{9,1},... | collective-permute-start | bytes 3145736 | tf_op jit(solution)/shard_map/ppermute | solution.py:421
  59.9 12.1 %collective-permute-start.14 = (bf16[512,512]{1,0:T(8,128)(2,1)}, bf16[512,512]{1,0:T(8,128)(2,1)S(1)}, u32[]{:S(2)}, u32[]{:S(2)}) collective-permute-start(bf16[512,512]{1,0:T(8,128)(2,1)} %get-tuple-element.45), channel_id=1, source_target_pairs={{0,1},{1,2},{2,3},{3,0},{4,5},{5,6},{6,7},{7,4},{8,11},{9,8},{10,9... | collective-permute-start | bytes 1572872 | tf_op jit(solution)/shard_map/ppermute | solution.py:421
  63.5 9.6 %collective-permute-start.11 = (bf16[512,512]{1,0:T(8,128)(2,1)S(1)}, bf16[512,512]{1,0:T(8,128)(2,1)S(1)}, u32[]{:S(2)}, u32[]{:S(2)}) collective-permute-start(bf16[512,512]{1,0:T(8,128)(2,1)S(1)} %get-tuple-element.43.refs_2_), channel_id=1, source_target_pairs={{0,4},{1,5},{2,6},{3,7},{4,0},{5,1},{6,2},{7,3},{8,140},{9,141},{1... | collective-permute-start | bytes 1572872 | tf_op jit(solution)/shard_map/ppermute | solution.py:421
  65.7 6.3 %collective-permute-start.16 = (f32[3,256,1]{2,1,0:T(8,128)S(1)}, f32[3,256,1]{2,1,0:T(8,128)S(1)}, u32[]{:S(2)}, u32[]{:S(2)}) collective-permute-start(f32[3,256,1]{2,1,0:T(8,128)S(1)} %shard_map.72.refs_0_.low_own), channel_id=1, source_target_pairs={{0,8},{1,9},{2,10},{3,11},{4,12},{5,13},{6,14},{7,15},{8,0},{9,1},... | collective-permute-start | bytes 9224 | tf_op jit(solution)/shard_map/ppermute | solution.py:421
  85.3 18.3 %all-to-all-start.2 = ((f32[16,1,512]{2,1,0:T(1,128)}), f32[16,1,512]{2,1,0:T(1,128)S(1)}, u32[]{:S(2)}, u32[]{:S(2)}) async-start(f32[16,1,512]{2,1,0:T(1,128)} %shard_map.81), calls=%async_computation.2 | async-start | bytes 65536 | tf_op jit(solution)/shard_map/all_to_all | solution.py:408
  108.1 3.3 %collective-permute-start.17 = (f32[2,64,512]{2,1,0:T(8,128)}, f32[2,64,512]{2,1,0:T(8,128)S(1)}, u32[]{:S(2)}, u32[]{:S(2)}) collective-permute-start(f32[2,64,512]{2,1,0:T(8,128)} %get-tuple-element.54), channel_id=1, source_target_pairs={{0,8},{1,9},{2,10},{3,11},{4,12},{5,13},{6,14},{7,15},{8,0},{9,1},... | collective-permute-start | bytes 786440 | tf_op jit(solution)/shard_map/ppermute | solution.py:421
  112.4 6.3 %collective-permute-start.18 = (f32[64,512]{1,0:T(8,128)S(1)}, f32[64,512]{1,0:T(8,128)S(1)}, u32[]{:S(2)}, u32[]{:S(2)}) collective-permute-start(f32[64,512]{1,0:T(8,128)S(1)} %slice_bitcast_fusion), channel_id=1, source_target_pairs={{0,128},{1,129},{2,130},{3,131},{4,132},{5,133},{6,134},{7,135},{8... | collective-permute-start | bytes 393224 | tf_op jit(solution)/shard_map/ppermute | solution.py:421
  (9 other events, 41.9 us)
Sparse Core Ops, SparseCore 0:
  12.4 59.9 all-gather.2

commit v11 on v10

--- a/solution.py
+++ b/solution.py
@@ -17,8 +17,8 @@
 WA = XL * Y
 CHAINS = 2
 ROWS_ALL = 24
-VMEM_BYTES = 42 * 1024 * 1024
-LAST_BYTES = 42 * 1024 * 1024
+VMEM_BYTES = 36 * 1024 * 1024
+LAST_BYTES = 36 * 1024 * 1024
 SMALL_BYTES = 1024 * 1024
 LARGE_BYTES = 58 * 1024 * 1024
 
@@ -397,7 +397,7 @@
             pltpu.VMEM(fin.shape, fin.dtype),
             pltpu.SemaphoreType.DMA((Z, 2)),
         ],
-        compiler_params=pltpu.CompilerParams(vmem_limit_bytes=LARGE_BYTES),
+        compiler_params=pltpu.CompilerParams(vmem_limit_bytes=48 * 1024 * 1024),
         cost_estimate=pl.CostEstimate(
             flops=2 * rows * Z * members * cols, bytes_accessed=4 * 1024 * 1024, transcendentals=0
         ),

time: 127 us -> 126 us (level)
  Pallas kernels: 34.3 us -> 33 us
    pallas_call x3, Pallas kernels: 20.9 us -> 19.6 us  [group_matmul(): pl.pallas_call(functools.partial(group_kernel, base, count, acc is not No...]
    unnamed x22 -> x14, local copies, waits for them, and re-layouts: 3.93 us -> 4.42 us
  transfers between devices with their start and end apart: 22 -> 22, of which waited for: 5 -> 5; matrix products, arithmetic and copies ran while one was open for 3% -> 3% of each run, Pallas kernels for 24% -> 23%
where the time goes in v11:
time: 126 us
  starting transfers between devices  40.7 us (32%)
  Pallas kernels  33 us (26%)
  waiting for transfers between devices  20.7 us (16%)
  between operations  14.3 us (11%)
  local copies, waits for them, and re-layouts  8.44 us (7%)
  blocking collectives  7.72 us (6%)
    ppermute x19, starting transfers between devices, send(): return lax.ppermute(v, AXES, pairs)  22.7 us
    pallas_call x3, Pallas kernels, group_matmul(): pl.pallas_call(functools.partial(group_kernel, base, count, acc is not No...  19.6 us
    ppermute x19, waiting for transfers between devices, send(): return lax.ppermute(v, AXES, pairs)  11.8 us
    all_to_all x1, starting transfers between devices, share(): return lax.all_to_all(x, axes, 0, 0, tiled=True)  9.69 us
    all_to_all x1, waiting for transfers between devices, share(): return lax.all_to_all(x, axes, 0, 0, tiled=True)  8.83 us
    all_to_all x1, starting transfers between devices, shards(): pieces = lax.all_to_all(pieces_here, 'z', 0, 0, tiled=True)  8.32 us
    all_to_all x1, blocking collectives, share(): return lax.all_to_all(x, axes, 0, 0, tiled=True)  7.72 us
    unnamed x14, local copies, waits for them, and re-layouts  4.42 us
  transfers between devices with their start and end apart: 22, of which 5 were waited for; matrix products, arithmetic and copies ran while one was open for 3% of the time, Pallas kernels for 23%

profile of v11, /device:TPU:1, one launch (start us, length us, event | category | flops | bytes accessed | tf_op | source)
XLA Modules:
  0.0 125.6 jit_solution(17977394240131880627)
XLA Ops:
  7.2 3.3 %collective-permute-start.4 = (bf16[3,256,4096]{2,1,0:T(8,128)(2,1)}, bf16[3,256,4096]{2,1,0:T(8,128)(2,1)}, u32[]{:S(2)}, u32[]{:S(2)}) collective-permute-start(bf16[3,256,4096]{2,1,0:T(8,128)(2,1)} %bitcast.21), channel_id=1, source_target_pairs={{0,8},{1,9},{2,10},{3,11},{4,12},{5,13},{6,14},{7,15},{8,0},{9,1},... | collective-permute-start | bytes 18874376 | tf_op jit(solution)/shard_map/ppermute | solution.py:421
  10.5 1.7 %constant_dynamic-slice_fusion = bf16[256,512]{1,0:T(8,128)(2,1)} fusion(bf16[256,4096]{1,0:T(8,128)(2,1)} %fin.1, s32[]{:T(128)S(6)} %select_n.11), kind=kLoop, calls=%fused_computation.3 | loop fusion | bytes 524292 | tf_op jit(solution)/shard_map/dynamic_slice | solution.py:450
  12.2 2.3 %constant_dynamic-slice_fusion.1 = (bf16[512,512]{1,0:T(8,128)(2,1)}, bf16[512,512]{1,0:T(8,128)(2,1)}) fusion(bf16[2048,512]{1,0:T(8,128)(2,1)} %param.6, s32[]{:T(128)S(6)} %select_n.10, s32[]{:T(128)S(6)} %select_n.9), kind=kLoop, calls=%fused_computation.4 | loop fusion | bytes 2097160 | tf_op jit(solution)/shard_map/dynamic_slice | solution.py:445
  15.5 2.5 %collective-permute-start.6 = (bf16[512,512]{1,0:T(8,128)(2,1)}, bf16[512,512]{1,0:T(8,128)(2,1)}, u32[]{:S(2)}, u32[]{:S(2)}) collective-permute-start(bf16[512,512]{1,0:T(8,128)(2,1)} %get-tuple-element.56.refs_0_), channel_id=1, source_target_pairs={{0,4},{1,5},{2,6},{3,7},{4,0},{5,1},{6,2},{7,3},{8,140},{9,141},{1... | collective-permute-start | bytes 1572872 | tf_op jit(solution)/shard_map/ppermute | solution.py:421
  18.6 2.5 %shard_map.79 = (bf16[8,256,256]{2,1,0:T(8,128)(2,1)}, f32[8,128]{1,0:T(8,128)}) custom-call(bf16[256,2048]{1,0:T(8,128)(2,1)} %fout.1), custom_call_target="tpu_custom_call" | custom-call | bytes 4194304 | tf_op jit(solution)/shard_map/pallas_call | solution.py:286
  21.2 8.3 %all-to-all-start = ((bf16[8,256,256]{2,1,0:T(8,128)(2,1)}), bf16[8,256,256]{2,1,0:T(8,128)(2,1)S(1)}, u32[]{:S(2)}, u32[]{:S(2)}) async-start(bf16[8,256,256]{2,1,0:T(8,128)(2,1)} %get-tuple-element.52), calls=%async_computation | async-start | bytes 2097152 | tf_op jit(solution)/shard_map/all_to_all | solution.py:453
  29.5 2.6 %collective-permute-start.10 = (bf16[512,512]{1,0:T(8,128)(2,1)}, bf16[512,512]{1,0:T(8,128)(2,1)}, u32[]{:S(2)}, u32[]{:S(2)}) collective-permute-start(bf16[512,512]{1,0:T(8,128)(2,1)} %get-tuple-element.32.refs_3_.refs_0_), channel_id=1, source_target_pairs={{0,4},{1,5},{2,6},{3,7},{4,0},{5,1},{6,2},{7,3},{8,140},{9,141},{1... | collective-permute-start | bytes 1572872 | tf_op jit(solution)/shard_map/ppermute | solution.py:421
  33.6 2.8 %copy-done = bf16[256,3,4096]{2,0,1:T(8,128)(2,1)S(1)} copy-done((bf16[256,3,4096]{2,0,1:T(8,128)(2,1)S(1)}, bf16[256,3,4096]{2,0,1:T(8,128)(2,1)}, u32[]{:S(2)}) %copy-start) | copy-done | bytes 6291480
  36.4 8.2 %shard_map.70 = (f32[2,3,256,1024]{3,2,1,0:T(8,128)S(1)}, f32[8,128]{1,0:T(8,128)S(1)}) custom-call(s32[11]{0:T(128)S(1)} %stack.47.kidx.place, bf16[3,256,4096]{2,1,0:T(8,128)(2,1)S(1)} %bitcast.22, bf16[3,256,4096]{2,1,0:T(8,128)(2,1)} %collective-permute-done.4.x_oth, bf16[512,512]{1,0:T(8,128)(2,1)} %get-tuple-element.30.refs_0_, ...), custom_call_target="tpu_custom_call" | custom-call | flops 4831838208 | bytes 8388608 | tf_op jit(solution)/shard_map/pallas_call | solution.py:152
  44.6 2.8 %collective-permute-start.12 = (bf16[512,512]{1,0:T(8,128)(2,1)}, bf16[512,512]{1,0:T(8,128)(2,1)S(1)}, u32[]{:S(2)}, u32[]{:S(2)}) collective-permute-start(bf16[512,512]{1,0:T(8,128)(2,1)} %get-tuple-element.44), channel_id=1, source_target_pairs={{0,1},{1,2},{2,3},{3,0},{4,5},{5,6},{6,7},{7,4},{8,11},{9,8},{10,9... | collective-permute-start | bytes 1572872 | tf_op jit(solution)/shard_map/ppermute | solution.py:421
  47.4 2.3 %collective-permute-start.13 = (bf16[512,512]{1,0:T(8,128)(2,1)}, bf16[512,512]{1,0:T(8,128)(2,1)S(1)}, u32[]{:S(2)}, u32[]{:S(2)}) collective-permute-start(bf16[512,512]{1,0:T(8,128)(2,1)} %get-tuple-element.39.refs_2_), channel_id=1, source_target_pairs={{0,4},{1,5},{2,6},{3,7},{4,0},{5,1},{6,2},{7,3},{8,140},{9,141},{1... | collective-permute-start | bytes 1572872 | tf_op jit(solution)/shard_map/ppermute | solution.py:421
  50.4 2.5 %shard_map.72.refs_0_.low_own = f32[3,256,1]{2,1,0:T(8,128)S(1)} custom-call(bf16[3,256,4096]{2,1,0:T(8,128)(2,1)S(1)} %bitcast.25, bf16[256,4096]{1,0:T(8,128)(2,1)S(1)} %copy-done.2), custom_call_target="tpu_custom_call" | custom-call | flops 6291456 | bytes 9437184 | tf_op jit(solution)/shard_map/pallas_call | solution.py:331
  52.9 6.0 %shard_map.74 = (f32[2,3,256,1024]{3,2,1,0:T(8,128)S(1)}, f32[8,128]{1,0:T(8,128)S(1)}) custom-call(s32[11]{0:T(128)S(1)} %stack.47.kidx.place, bf16[3,256,4096]{2,1,0:T(8,128)(2,1)S(1)} %bitcast.26, bf16[3,256,4096]{2,1,0:T(8,128)(2,1)} %collective-permute-done.4.x_oth, ...), custom_call_target="tpu_custom_call", output_to_operand_aliasing={{0}: (8, {})} | custom-call | flops 3221225472 | bytes 8388608 | tf_op jit(solution)/shard_map/pallas_call | solution.py:152
  59.8 3.0 %collective-permute-done.8.refs_1_ = bf16[512,512]{1,0:T(8,128)(2,1)S(1)} collective-permute-done((bf16[512,512]{1,0:T(8,128)(2,1)}, bf16[512,512]{1,0:T(8,128)(2,1)S(1)}, u32[]{:S(2)}, u32[]{:S(2)}) %collective-permute-start.8) | collective-permute-done | bytes 524320 | tf_op jit(solution)/shard_map/ppermute | solution.py:421
  62.9 2.3 %collective-permute-start.11 = (bf16[512,512]{1,0:T(8,128)(2,1)S(1)}, bf16[512,512]{1,0:T(8,128)(2,1)S(1)}, u32[]{:S(2)}, u32[]{:S(2)}) collective-permute-start(bf16[512,512]{1,0:T(8,128)(2,1)S(1)} %get-tuple-element.43.refs_2_), channel_id=1, source_target_pairs={{0,4},{1,5},{2,6},{3,7},{4,0},{5,1},{6,2},{7,3},{8,140},{9,141},{1... | collective-permute-start | bytes 1572872 | tf_op jit(solution)/shard_map/ppermute | solution.py:421
  65.2 5.4 %shard_map.77 = (f32[2,3,256,1024]{3,2,1,0:T(8,128)S(1)}, f32[8,128]{1,0:T(8,128)}, bf16[2,3,256,512]{3,2,1,0:T(8,128)(2,1)S(1)}) custom-call(s32[11]{0:T(128)S(1)} %stack.47.kidx.place, bf16[3,256,4096]{2,1,0:T(8,128)(2,1)S(1)} %bitcast.27, bf16[3,256,4096]{2,1,0:T(8,128)(2,1)} %collective-permute-done.4.x_oth, ...), custom_call_target="tpu_custom_call", output_to_operand_aliasing={{0}: (7, {})} | custom-call | flops 3221225472 | bytes 8388608 | tf_op jit(solution)/shard_map/pallas_call | solution.py:152
  70.7 1.7 %collective-permute-done.11.w_lo = bf16[512,512]{1,0:T(8,128)(2,1)S(1)} collective-permute-done((bf16[512,512]{1,0:T(8,128)(2,1)S(1)}, bf16[512,512]{1,0:T(8,128)(2,1)S(1)}, u32[]{:S(2)}, u32[]{:S(2)}) %collective-permute-start.11) | collective-permute-done | bytes 524320 | tf_op jit(solution)/shard_map/ppermute | solution.py:421
  72.4 3.8 %shard_map.78.refs_0_ = f32[16,1,512]{2,1,0:T(1,128)S(1)} custom-call(s32[11]{0:T(128)S(1)} %stack.47.kidx.place, bf16[512,512]{1,0:T(8,128)(2,1)S(1)} %collective-permute-done.11.w_lo, bf16[512,512]{1,0:T(8,128)(2,1)S(1)} %collective-permute-done.14.w_hi, bf16[256,2048]{1,0:T(8,128)(2,1)S(1)} %copy-done.1, ...), custom_call_target="tpu_custom_call" | custom-call | flops 1610612736 | bytes 6291456 | tf_op jit(solution)/shard_map/pallas_call | solution.py:221
  76.2 7.7 %all_to_all.15.got = f32[16,1,512]{2,1,0:T(1,128)S(1)} all-to-all(f32[16,1,512]{2,1,0:T(1,128)S(1)} %shard_map.80), channel_id=1, replica_groups=mesh['xh'=2,'z'=8,'core'=2,'xl'=2,'y'=4] {'core','xl','y'}, dimensions={0} | all-to-all | bytes 65536 | tf_op jit(solution)/shard_map/all_to_all | solution.py:408
  84.5 9.7 %all-to-all-start.2 = ((f32[16,1,512]{2,1,0:T(1,128)}), f32[16,1,512]{2,1,0:T(1,128)S(1)}, u32[]{:S(2)}, u32[]{:S(2)}) async-start(f32[16,1,512]{2,1,0:T(1,128)} %shard_map.81), calls=%async_computation.2 | async-start | bytes 65536 | tf_op jit(solution)/shard_map/all_to_all | solution.py:408
  94.3 8.8 %all-to-all-done.2.fit = f32[16,1,512]{2,1,0:T(1,128)S(1)} async-done(((f32[16,1,512]{2,1,0:T(1,128)}), f32[16,1,512]{2,1,0:T(1,128)S(1)}, u32[]{:S(2)}, u32[]{:S(2)}) %all-to-all-start.2) | async-done | bytes 32800 | tf_op jit(solution)/shard_map/all_to_all | solution.py:408
  104.7 3.9 %shard_map.82 = (f32[2,64,512]{2,1,0:T(8,128)S(1)}, f32[2,64,512]{2,1,0:T(8,128)S(1)}, f32[1,256]{1,0:T(1,128)}) custom-call(s32[11]{0:T(128)S(1)} %stack.47.kidx.place, f32[16,1,512]{2,1,0:T(1,128)S(1)} %all-to-all-done.2.fit, bf16[8,256,256]{2,1,0:T(8,128)(2,1)S(1)} %all-to-all-done.refs_1_.fout_all, bf16[8,256,512]{2,1,0:T(8,128)(2,1)S(1)} %bitcast.28), custom_call_target="tpu_custom_call" | custom-call | flops 536870912 | bytes 4194304 | tf_op jit(solution)/shard_map/pallas_call | solution.py:390
  108.6 1.9 %collective-permute-start.17 = (f32[2,64,512]{2,1,0:T(8,128)S(1)}, f32[2,64,512]{2,1,0:T(8,128)S(1)}, u32[]{:S(2)}, u32[]{:S(2)}) collective-permute-start(f32[2,64,512]{2,1,0:T(8,128)S(1)} %get-tuple-element.54), channel_id=1, source_target_pairs={{0,8},{1,9},{2,10},{3,11},{4,12},{5,13},{6,14},{7,15},{8,0},{9,1},... | collective-permute-start | bytes 786440 | tf_op jit(solution)/shard_map/ppermute | solution.py:421
  112.2 5.9 %collective-permute-done.18 = f32[64,512]{1,0:T(8,128)S(1)} collective-permute-done((f32[64,512]{1,0:T(8,128)S(1)}, f32[64,512]{1,0:T(8,128)S(1)}, u32[]{:S(2)}, u32[]{:S(2)}) %collective-permute-start.18) | collective-permute-done | bytes 131104 | tf_op jit(solution)/shard_map/ppermute | solution.py:421
  (58 shorter events, 9.4 us)
Async XLA Ops:
  7.2 87.1 %all-gather.3.cloned.1.call-start = ((), (), s32[]{:S(2)}) async-start(), calls=%async_computation.3 | async-start | bytes 2359296 | tf_op jit(solution)/shard_map/all_gather | solution.py:451
  7.2 26.3 %collective-permute-start.4 = (bf16[3,256,4096]{2,1,0:T(8,128)(2,1)}, bf16[3,256,4096]{2,1,0:T(8,128)(2,1)}, u32[]{:S(2)}, u32[]{:S(2)}) collective-permute-start(bf16[3,256,4096]{2,1,0:T(8,128)(2,1)} %bitcast.21), channel_id=1, source_target_pairs={{0,8},{1,9},{2,10},{3,11},{4,12},{5,13},{6,14},{7,15},{8,0},{9,1},... | collective-permute-start | bytes 18874376 | tf_op jit(solution)/shard_map/ppermute | solution.py:421
  14.5 15.0 %collective-permute-start.5 = (bf16[512,512]{1,0:T(8,128)(2,1)}, bf16[512,512]{1,0:T(8,128)(2,1)}, u32[]{:S(2)}, u32[]{:S(2)}) collective-permute-start(bf16[512,512]{1,0:T(8,128)(2,1)} %get-tuple-element.56.refs_0_), channel_id=1, source_target_pairs={{0,1},{1,2},{2,3},{3,0},{4,5},{5,6},{6,7},{7,4},{8,11},{9,8},{10,9... | collective-permute-start | bytes 1572872 | tf_op jit(solution)/shard_map/ppermute | solution.py:421
  15.5 14.0 %collective-permute-start.6 = (bf16[512,512]{1,0:T(8,128)(2,1)}, bf16[512,512]{1,0:T(8,128)(2,1)}, u32[]{:S(2)}, u32[]{:S(2)}) collective-permute-start(bf16[512,512]{1,0:T(8,128)(2,1)} %get-tuple-element.56.refs_0_), channel_id=1, source_target_pairs={{0,4},{1,5},{2,6},{3,7},{4,0},{5,1},{6,2},{7,3},{8,140},{9,141},{1... | collective-permute-start | bytes 1572872 | tf_op jit(solution)/shard_map/ppermute | solution.py:421
  18.0 15.1 %collective-permute-start = (bf16[512,512]{1,0:T(8,128)(2,1)}, bf16[512,512]{1,0:T(8,128)(2,1)}, u32[]{:S(2)}, u32[]{:S(2)}) collective-permute-start(bf16[512,512]{1,0:T(8,128)(2,1)} %get-tuple-element.57.refs_0_), channel_id=1, source_target_pairs={{0,1},{1,2},{2,3},{3,0},{4,5},{5,6},{6,7},{7,4},{8,11},{9,8},{10,9... | collective-permute-start | bytes 1572872 | tf_op jit(solution)/shard_map/ppermute | solution.py:421
  18.4 14.6 %collective-permute-start.1 = (bf16[512,512]{1,0:T(8,128)(2,1)}, bf16[512,512]{1,0:T(8,128)(2,1)}, u32[]{:S(2)}, u32[]{:S(2)}) collective-permute-start(bf16[512,512]{1,0:T(8,128)(2,1)} %get-tuple-element.57.refs_0_), channel_id=1, source_target_pairs={{0,4},{1,5},{2,6},{3,7},{4,0},{5,1},{6,2},{7,3},{8,140},{9,141},{1... | collective-permute-start | bytes 1572872 | tf_op jit(solution)/shard_map/ppermute | solution.py:421
  21.2 29.2 %slice-start = ((s8[6291456]{0:T(1024)(128)(4,1)}), s8[2097152]{0:T(1024)(128)(4,1)S(1)}, s32[]{:S(2)}) async-start(s8[6291456]{0:T(1024)(128)(4,1)} %bitcast.23), calls=%async_computation.4 | async-start | bytes 4194304
  21.2 55.0 %all-to-all-start = ((bf16[8,256,256]{2,1,0:T(8,128)(2,1)}), bf16[8,256,256]{2,1,0:T(8,128)(2,1)S(1)}, u32[]{:S(2)}, u32[]{:S(2)}) async-start(bf16[8,256,256]{2,1,0:T(8,128)(2,1)} %get-tuple-element.52), calls=%async_computation | async-start | bytes 2097152 | tf_op jit(solution)/shard_map/all_to_all | solution.py:453
  29.5 15.1 %collective-permute-start.10 = (bf16[512,512]{1,0:T(8,128)(2,1)}, bf16[512,512]{1,0:T(8,128)(2,1)}, u32[]{:S(2)}, u32[]{:S(2)}) collective-permute-start(bf16[512,512]{1,0:T(8,128)(2,1)} %get-tuple-element.32.refs_3_.refs_0_), channel_id=1, source_target_pairs={{0,4},{1,5},{2,6},{3,7},{4,0},{5,1},{6,2},{7,3},{8,140},{9,141},{1... | collective-permute-start | bytes 1572872 | tf_op jit(solution)/shard_map/ppermute | solution.py:421
  32.1 12.5 %collective-permute-start.9 = (bf16[512,512]{1,0:T(8,128)(2,1)}, bf16[512,512]{1,0:T(8,128)(2,1)}, u32[]{:S(2)}, u32[]{:S(2)}) collective-permute-start(bf16[512,512]{1,0:T(8,128)(2,1)} %get-tuple-element.31.refs_1_), channel_id=1, source_target_pairs={{0,3},{1,0},{2,1},{3,2},{4,7},{5,4},{6,5},{7,6},{8,9},{9,10},{10,1... | collective-permute-start | bytes 1572872 | tf_op jit(solution)/shard_map/ppermute | solution.py:421
  33.1 16.6 %collective-permute-start.3 = (bf16[512,512]{1,0:T(8,128)(2,1)}, bf16[512,512]{1,0:T(8,128)(2,1)}, u32[]{:S(2)}, u32[]{:S(2)}) collective-permute-start(bf16[512,512]{1,0:T(8,128)(2,1)} %get-tuple-element.29.refs_2_.refs_0_), channel_id=1, source_target_pairs={{0,4},{1,5},{2,6},{3,7},{4,0},{5,1},{6,2},{7,3},{8,140},{9,141},{1... | collective-permute-start | bytes 1572872 | tf_op jit(solution)/shard_map/ppermute | solution.py:421
  33.4 16.3 %collective-permute-start.2 = (bf16[512,512]{1,0:T(8,128)(2,1)}, bf16[512,512]{1,0:T(8,128)(2,1)}, u32[]{:S(2)}, u32[]{:S(2)}) collective-permute-start(bf16[512,512]{1,0:T(8,128)(2,1)} %get-tuple-element.30.refs_0_), channel_id=1, source_target_pairs={{0,3},{1,0},{2,1},{3,2},{4,7},{5,4},{6,5},{7,6},{8,9},{9,10},{10,1... | collective-permute-start | bytes 1572872 | tf_op jit(solution)/shard_map/ppermute | solution.py:421
  36.4 14.0 %slice-start.1 = ((s8[6291456]{0:T(1024)(128)(4,1)}), s8[4194304]{0:T(1024)(128)(4,1)S(1)}, s32[]{:S(2)}) async-start(s8[6291456]{0:T(1024)(128)(4,1)} %bitcast.23), calls=%async_computation.5 | async-start | bytes 8388608
  44.6 14.3 %collective-permute-start.12 = (bf16[512,512]{1,0:T(8,128)(2,1)}, bf16[512,512]{1,0:T(8,128)(2,1)S(1)}, u32[]{:S(2)}, u32[]{:S(2)}) collective-permute-start(bf16[512,512]{1,0:T(8,128)(2,1)} %get-tuple-element.44), channel_id=1, source_target_pairs={{0,1},{1,2},{2,3},{3,0},{4,5},{5,6},{6,7},{7,4},{8,11},{9,8},{10,9... | collective-permute-start | bytes 1572872 | tf_op jit(solution)/shard_map/ppermute | solution.py:421
  47.4 11.5 %collective-permute-start.13 = (bf16[512,512]{1,0:T(8,128)(2,1)}, bf16[512,512]{1,0:T(8,128)(2,1)S(1)}, u32[]{:S(2)}, u32[]{:S(2)}) collective-permute-start(bf16[512,512]{1,0:T(8,128)(2,1)} %get-tuple-element.39.refs_2_), channel_id=1, source_target_pairs={{0,4},{1,5},{2,6},{3,7},{4,0},{5,1},{6,2},{7,3},{8,140},{9,141},{1... | collective-permute-start | bytes 1572872 | tf_op jit(solution)/shard_map/ppermute | solution.py:421
  49.7 10.1 %collective-permute-start.7 = (bf16[512,512]{1,0:T(8,128)(2,1)}, bf16[512,512]{1,0:T(8,128)(2,1)S(1)}, u32[]{:S(2)}, u32[]{:S(2)}) collective-permute-start(bf16[512,512]{1,0:T(8,128)(2,1)} %get-tuple-element.36), channel_id=1, source_target_pairs={{0,1},{1,2},{2,3},{3,0},{4,5},{5,6},{6,7},{7,4},{8,11},{9,8},{10,9... | collective-permute-start | bytes 1572872 | tf_op jit(solution)/shard_map/ppermute | solution.py:421
  50.2 12.7 %collective-permute-start.8 = (bf16[512,512]{1,0:T(8,128)(2,1)}, bf16[512,512]{1,0:T(8,128)(2,1)S(1)}, u32[]{:S(2)}, u32[]{:S(2)}) collective-permute-start(bf16[512,512]{1,0:T(8,128)(2,1)} %get-tuple-element.37.refs_1_), channel_id=1, source_target_pairs={{0,4},{1,5},{2,6},{3,7},{4,0},{5,1},{6,2},{7,3},{8,140},{9,141},{1... | collective-permute-start | bytes 1572872 | tf_op jit(solution)/shard_map/ppermute | solution.py:421
  50.4 20.3 %collective-permute-start.15 = (bf16[256,2048]{1,0:T(8,128)(2,1)S(1)}, bf16[256,2048]{1,0:T(8,128)(2,1)S(1)}, u32[]{:S(2)}, u32[]{:S(2)}) collective-permute-start(bf16[256,2048]{1,0:T(8,128)(2,1)S(1)} %copy-done.1), channel_id=1, source_target_pairs={{0,8},{1,9},{2,10},{3,11},{4,12},{5,13},{6,14},{7,15},{8,0},{9,1},... | collective-permute-start | bytes 3145736 | tf_op jit(solution)/shard_map/ppermute | solution.py:421
  58.9 11.7 %collective-permute-start.14 = (bf16[512,512]{1,0:T(8,128)(2,1)}, bf16[512,512]{1,0:T(8,128)(2,1)S(1)}, u32[]{:S(2)}, u32[]{:S(2)}) collective-permute-start(bf16[512,512]{1,0:T(8,128)(2,1)} %get-tuple-element.45), channel_id=1, source_target_pairs={{0,1},{1,2},{2,3},{3,0},{4,5},{5,6},{6,7},{7,4},{8,11},{9,8},{10,9... | collective-permute-start | bytes 1572872 | tf_op jit(solution)/shard_map/ppermute | solution.py:421
  62.9 9.5 %collective-permute-start.11 = (bf16[512,512]{1,0:T(8,128)(2,1)S(1)}, bf16[512,512]{1,0:T(8,128)(2,1)S(1)}, u32[]{:S(2)}, u32[]{:S(2)}) collective-permute-start(bf16[512,512]{1,0:T(8,128)(2,1)S(1)} %get-tuple-element.43.refs_2_), channel_id=1, source_target_pairs={{0,4},{1,5},{2,6},{3,7},{4,0},{5,1},{6,2},{7,3},{8,140},{9,141},{1... | collective-permute-start | bytes 1572872 | tf_op jit(solution)/shard_map/ppermute | solution.py:421
  65.2 5.5 %collective-permute-start.16 = (f32[3,256,1]{2,1,0:T(8,128)S(1)}, f32[3,256,1]{2,1,0:T(8,128)S(1)}, u32[]{:S(2)}, u32[]{:S(2)}) collective-permute-start(f32[3,256,1]{2,1,0:T(8,128)S(1)} %shard_map.72.refs_0_.low_own), channel_id=1, source_target_pairs={{0,8},{1,9},{2,10},{3,11},{4,12},{5,13},{6,14},{7,15},{8,0},{9,1},... | collective-permute-start | bytes 9224 | tf_op jit(solution)/shard_map/ppermute | solution.py:421
  84.5 18.6 %all-to-all-start.2 = ((f32[16,1,512]{2,1,0:T(1,128)}), f32[16,1,512]{2,1,0:T(1,128)S(1)}, u32[]{:S(2)}, u32[]{:S(2)}) async-start(f32[16,1,512]{2,1,0:T(1,128)} %shard_map.81), calls=%async_computation.2 | async-start | bytes 65536 | tf_op jit(solution)/shard_map/all_to_all | solution.py:408
  108.6 3.1 %collective-permute-start.17 = (f32[2,64,512]{2,1,0:T(8,128)S(1)}, f32[2,64,512]{2,1,0:T(8,128)S(1)}, u32[]{:S(2)}, u32[]{:S(2)}) collective-permute-start(f32[2,64,512]{2,1,0:T(8,128)S(1)} %get-tuple-element.54), channel_id=1, source_target_pairs={{0,8},{1,9},{2,10},{3,11},{4,12},{5,13},{6,14},{7,15},{8,0},{9,1},... | collective-permute-start | bytes 786440 | tf_op jit(solution)/shard_map/ppermute | solution.py:421
  111.8 6.3 %collective-permute-start.18 = (f32[64,512]{1,0:T(8,128)S(1)}, f32[64,512]{1,0:T(8,128)S(1)}, u32[]{:S(2)}, u32[]{:S(2)}) collective-permute-start(f32[64,512]{1,0:T(8,128)S(1)} %slice_bitcast_fusion), channel_id=1, source_target_pairs={{0,128},{1,129},{2,130},{3,131},{4,132},{5,133},{6,134},{7,135},{8... | collective-permute-start | bytes 393224 | tf_op jit(solution)/shard_map/ppermute | solution.py:421
  (5 other events, 23.3 us)
Sparse Core Ops, SparseCore 0:
  12.4 59.9 all-gather.2

commit v12 on v11

--- a/solution.py
+++ b/solution.py
@@ -20,6 +20,7 @@
 VMEM_BYTES = 36 * 1024 * 1024
 LAST_BYTES = 36 * 1024 * 1024
 SMALL_BYTES = 1024 * 1024
+STEP_BYTES = 54 * 1024 * 1024
 LARGE_BYTES = 58 * 1024 * 1024
 
 
@@ -397,7 +398,7 @@
             pltpu.VMEM(fin.shape, fin.dtype),
             pltpu.SemaphoreType.DMA((Z, 2)),
         ],
-        compiler_params=pltpu.CompilerParams(vmem_limit_bytes=48 * 1024 * 1024),
+        compiler_params=pltpu.CompilerParams(vmem_limit_bytes=STEP_BYTES),
         cost_estimate=pl.CostEstimate(
             flops=2 * rows * Z * members * cols, bytes_accessed=4 * 1024 * 1024, transcendentals=0
         ),

time: 126 us -> 126 us (level)
    unnamed x14 -> x18, local copies, waits for them, and re-layouts: 4.42 us -> 3.45 us
where the time goes in v12:
time: 126 us
  starting transfers between devices  40.8 us (32%)
  Pallas kernels  32.9 us (26%)
  waiting for transfers between devices  20.9 us (17%)
  between operations  14.3 us (11%)
  blocking collectives  7.71 us (6%)
  local copies, waits for them, and re-layouts  7.47 us (6%)
  other arithmetic  1.67 us (1%)
    ppermute x19, starting transfers between devices, send(): return lax.ppermute(v, AXES, pairs)  22.7 us
    pallas_call x3, Pallas kernels, group_matmul(): pl.pallas_call(functools.partial(group_kernel, base, count, acc is not No...  19.6 us
    ppermute x19, waiting for transfers between devices, send(): return lax.ppermute(v, AXES, pairs)  12 us
    all_to_all x1, starting transfers between devices, share(): return lax.all_to_all(x, axes, 0, 0, tiled=True)  9.69 us
    all_to_all x1, waiting for transfers between devices, share(): return lax.all_to_all(x, axes, 0, 0, tiled=True)  8.83 us
    all_to_all x1, starting transfers between devices, shards(): pieces = lax.all_to_all(pieces_here, 'z', 0, 0, tiled=True)  8.32 us
    all_to_all x1, blocking collectives, share(): return lax.all_to_all(x, axes, 0, 0, tiled=True)  7.71 us
    pallas_call x1, Pallas kernels, weight_part(): pl.pallas_call(step_kernel, out_shape=(block, block, jax.ShapeDtypeStruct...  3.86 us
  transfers between devices with their start and end apart: 22, of which 5 were waited for; matrix products, arithmetic and copies ran while one was open for 3% of the time, Pallas kernels for 23%

profile of v12, /device:TPU:1, one launch (start us, length us, event | category | flops | bytes accessed | tf_op | source)
XLA Modules:
  0.0 125.7 jit_solution(9994100698648018055)
XLA Ops:
  7.2 3.3 %collective-permute-start.4 = (bf16[3,256,4096]{2,1,0:T(8,128)(2,1)}, bf16[3,256,4096]{2,1,0:T(8,128)(2,1)}, u32[]{:S(2)}, u32[]{:S(2)}) collective-permute-start(bf16[3,256,4096]{2,1,0:T(8,128)(2,1)} %bitcast.21), channel_id=1, source_target_pairs={{0,8},{1,9},{2,10},{3,11},{4,12},{5,13},{6,14},{7,15},{8,0},{9,1},... | collective-permute-start | bytes 18874376 | tf_op jit(solution)/shard_map/ppermute | solution.py:422
  10.5 1.7 %constant_dynamic-slice_fusion = bf16[256,512]{1,0:T(8,128)(2,1)} fusion(bf16[256,4096]{1,0:T(8,128)(2,1)} %fin.1, s32[]{:T(128)S(6)} %select_n.11), kind=kLoop, calls=%fused_computation.3 | loop fusion | bytes 524292 | tf_op jit(solution)/shard_map/dynamic_slice | solution.py:451
  12.2 2.3 %constant_dynamic-slice_fusion.1 = (bf16[512,512]{1,0:T(8,128)(2,1)}, bf16[512,512]{1,0:T(8,128)(2,1)}) fusion(bf16[2048,512]{1,0:T(8,128)(2,1)} %param.6, s32[]{:T(128)S(6)} %select_n.10, s32[]{:T(128)S(6)} %select_n.9), kind=kLoop, calls=%fused_computation.4 | loop fusion | bytes 2097160 | tf_op jit(solution)/shard_map/dynamic_slice | solution.py:446
  15.5 2.5 %collective-permute-start.6 = (bf16[512,512]{1,0:T(8,128)(2,1)}, bf16[512,512]{1,0:T(8,128)(2,1)}, u32[]{:S(2)}, u32[]{:S(2)}) collective-permute-start(bf16[512,512]{1,0:T(8,128)(2,1)} %get-tuple-element.56.refs_0_), channel_id=1, source_target_pairs={{0,4},{1,5},{2,6},{3,7},{4,0},{5,1},{6,2},{7,3},{8,140},{9,141},{1... | collective-permute-start | bytes 1572872 | tf_op jit(solution)/shard_map/ppermute | solution.py:422
  18.6 2.5 %shard_map.79 = (bf16[8,256,256]{2,1,0:T(8,128)(2,1)}, f32[8,128]{1,0:T(8,128)}) custom-call(bf16[256,2048]{1,0:T(8,128)(2,1)} %fout.1), custom_call_target="tpu_custom_call" | custom-call | bytes 4194304 | tf_op jit(solution)/shard_map/pallas_call | solution.py:287
  21.2 8.3 %all-to-all-start = ((bf16[8,256,256]{2,1,0:T(8,128)(2,1)}), bf16[8,256,256]{2,1,0:T(8,128)(2,1)S(1)}, u32[]{:S(2)}, u32[]{:S(2)}) async-start(bf16[8,256,256]{2,1,0:T(8,128)(2,1)} %get-tuple-element.52), calls=%async_computation | async-start | bytes 2097152 | tf_op jit(solution)/shard_map/all_to_all | solution.py:454
  29.5 2.6 %collective-permute-start.10 = (bf16[512,512]{1,0:T(8,128)(2,1)}, bf16[512,512]{1,0:T(8,128)(2,1)}, u32[]{:S(2)}, u32[]{:S(2)}) collective-permute-start(bf16[512,512]{1,0:T(8,128)(2,1)} %get-tuple-element.32.refs_3_.refs_0_), channel_id=1, source_target_pairs={{0,4},{1,5},{2,6},{3,7},{4,0},{5,1},{6,2},{7,3},{8,140},{9,141},{1... | collective-permute-start | bytes 1572872 | tf_op jit(solution)/shard_map/ppermute | solution.py:422
  33.6 2.8 %copy-done = bf16[256,3,4096]{2,0,1:T(8,128)(2,1)S(1)} copy-done((bf16[256,3,4096]{2,0,1:T(8,128)(2,1)S(1)}, bf16[256,3,4096]{2,0,1:T(8,128)(2,1)}, u32[]{:S(2)}) %copy-start) | copy-done | bytes 6291480
  36.4 8.2 %shard_map.70 = (f32[2,3,256,1024]{3,2,1,0:T(8,128)S(1)}, f32[8,128]{1,0:T(8,128)S(1)}) custom-call(s32[11]{0:T(128)S(1)} %stack.47.kidx.place, bf16[3,256,4096]{2,1,0:T(8,128)(2,1)S(1)} %bitcast.22, bf16[3,256,4096]{2,1,0:T(8,128)(2,1)} %collective-permute-done.4.x_oth, bf16[512,512]{1,0:T(8,128)(2,1)} %get-tuple-element.30.refs_0_, ...), custom_call_target="tpu_custom_call" | custom-call | flops 4831838208 | bytes 8388608 | tf_op jit(solution)/shard_map/pallas_call | solution.py:153
  44.6 2.8 %collective-permute-start.12 = (bf16[512,512]{1,0:T(8,128)(2,1)}, bf16[512,512]{1,0:T(8,128)(2,1)S(1)}, u32[]{:S(2)}, u32[]{:S(2)}) collective-permute-start(bf16[512,512]{1,0:T(8,128)(2,1)} %get-tuple-element.44), channel_id=1, source_target_pairs={{0,1},{1,2},{2,3},{3,0},{4,5},{5,6},{6,7},{7,4},{8,11},{9,8},{10,9... | collective-permute-start | bytes 1572872 | tf_op jit(solution)/shard_map/ppermute | solution.py:422
  47.4 2.3 %collective-permute-start.13 = (bf16[512,512]{1,0:T(8,128)(2,1)}, bf16[512,512]{1,0:T(8,128)(2,1)S(1)}, u32[]{:S(2)}, u32[]{:S(2)}) collective-permute-start(bf16[512,512]{1,0:T(8,128)(2,1)} %get-tuple-element.39.refs_2_), channel_id=1, source_target_pairs={{0,4},{1,5},{2,6},{3,7},{4,0},{5,1},{6,2},{7,3},{8,140},{9,141},{1... | collective-permute-start | bytes 1572872 | tf_op jit(solution)/shard_map/ppermute | solution.py:422
  50.4 2.5 %shard_map.72.refs_0_.low_own = f32[3,256,1]{2,1,0:T(8,128)S(1)} custom-call(bf16[3,256,4096]{2,1,0:T(8,128)(2,1)S(1)} %bitcast.25, bf16[256,4096]{1,0:T(8,128)(2,1)S(1)} %copy-done.3), custom_call_target="tpu_custom_call" | custom-call | flops 6291456 | bytes 9437184 | tf_op jit(solution)/shard_map/pallas_call | solution.py:332
  52.9 6.0 %shard_map.74 = (f32[2,3,256,1024]{3,2,1,0:T(8,128)S(1)}, f32[8,128]{1,0:T(8,128)S(1)}) custom-call(s32[11]{0:T(128)S(1)} %stack.47.kidx.place, bf16[3,256,4096]{2,1,0:T(8,128)(2,1)S(1)} %bitcast.26, bf16[3,256,4096]{2,1,0:T(8,128)(2,1)} %collective-permute-done.4.x_oth, ...), custom_call_target="tpu_custom_call", output_to_operand_aliasing={{0}: (8, {})} | custom-call | flops 3221225472 | bytes 8388608 | tf_op jit(solution)/shard_map/pallas_call | solution.py:153
  59.8 3.0 %collective-permute-done.8.refs_1_ = bf16[512,512]{1,0:T(8,128)(2,1)S(1)} collective-permute-done((bf16[512,512]{1,0:T(8,128)(2,1)}, bf16[512,512]{1,0:T(8,128)(2,1)S(1)}, u32[]{:S(2)}, u32[]{:S(2)}) %collective-permute-start.8) | collective-permute-done | bytes 524320 | tf_op jit(solution)/shard_map/ppermute | solution.py:422
  62.9 2.3 %collective-permute-start.11 = (bf16[512,512]{1,0:T(8,128)(2,1)S(1)}, bf16[512,512]{1,0:T(8,128)(2,1)S(1)}, u32[]{:S(2)}, u32[]{:S(2)}) collective-permute-start(bf16[512,512]{1,0:T(8,128)(2,1)S(1)} %get-tuple-element.43.refs_2_), channel_id=1, source_target_pairs={{0,4},{1,5},{2,6},{3,7},{4,0},{5,1},{6,2},{7,3},{8,140},{9,141},{1... | collective-permute-start | bytes 1572872 | tf_op jit(solution)/shard_map/ppermute | solution.py:422
  65.2 5.4 %shard_map.77 = (f32[2,3,256,1024]{3,2,1,0:T(8,128)S(1)}, f32[8,128]{1,0:T(8,128)}, bf16[2,3,256,512]{3,2,1,0:T(8,128)(2,1)S(1)}) custom-call(s32[11]{0:T(128)S(1)} %stack.47.kidx.place, bf16[3,256,4096]{2,1,0:T(8,128)(2,1)S(1)} %bitcast.27, bf16[3,256,4096]{2,1,0:T(8,128)(2,1)} %collective-permute-done.4.x_oth, ...), custom_call_target="tpu_custom_call", output_to_operand_aliasing={{0}: (7, {})} | custom-call | flops 3221225472 | bytes 8388608 | tf_op jit(solution)/shard_map/pallas_call | solution.py:153
  70.7 1.7 %collective-permute-done.11.w_lo = bf16[512,512]{1,0:T(8,128)(2,1)S(1)} collective-permute-done((bf16[512,512]{1,0:T(8,128)(2,1)S(1)}, bf16[512,512]{1,0:T(8,128)(2,1)S(1)}, u32[]{:S(2)}, u32[]{:S(2)}) %collective-permute-start.11) | collective-permute-done | bytes 524320 | tf_op jit(solution)/shard_map/ppermute | solution.py:422
  72.4 3.8 %shard_map.78.refs_0_ = f32[16,1,512]{2,1,0:T(1,128)S(1)} custom-call(s32[11]{0:T(128)S(1)} %stack.47.kidx.place, bf16[512,512]{1,0:T(8,128)(2,1)S(1)} %collective-permute-done.11.w_lo, bf16[512,512]{1,0:T(8,128)(2,1)S(1)} %collective-permute-done.14.w_hi, bf16[256,2048]{1,0:T(8,128)(2,1)S(1)} %copy-done.2, ...), custom_call_target="tpu_custom_call" | custom-call | flops 1610612736 | bytes 6291456 | tf_op jit(solution)/shard_map/pallas_call | solution.py:222
  76.2 7.7 %all_to_all.15.got = f32[16,1,512]{2,1,0:T(1,128)S(1)} all-to-all(f32[16,1,512]{2,1,0:T(1,128)S(1)} %shard_map.80), channel_id=1, replica_groups=mesh['xh'=2,'z'=8,'core'=2,'xl'=2,'y'=4] {'core','xl','y'}, dimensions={0} | all-to-all | bytes 65536 | tf_op jit(solution)/shard_map/all_to_all | solution.py:409
  84.5 9.7 %all-to-all-start.2 = ((f32[16,1,512]{2,1,0:T(1,128)}), f32[16,1,512]{2,1,0:T(1,128)S(1)}, u32[]{:S(2)}, u32[]{:S(2)}) async-start(f32[16,1,512]{2,1,0:T(1,128)} %shard_map.81), calls=%async_computation.2 | async-start | bytes 65536 | tf_op jit(solution)/shard_map/all_to_all | solution.py:409
  94.3 8.8 %all-to-all-done.2.fit = f32[16,1,512]{2,1,0:T(1,128)S(1)} async-done(((f32[16,1,512]{2,1,0:T(1,128)}), f32[16,1,512]{2,1,0:T(1,128)S(1)}, u32[]{:S(2)}, u32[]{:S(2)}) %all-to-all-start.2) | async-done | bytes 32800 | tf_op jit(solution)/shard_map/all_to_all | solution.py:409
  103.7 3.9 %shard_map.82 = (f32[2,64,512]{2,1,0:T(8,128)}, f32[2,64,512]{2,1,0:T(8,128)}, f32[1,256]{1,0:T(1,128)}) custom-call(s32[11]{0:T(128)} %copy-done.4, f32[16,1,512]{2,1,0:T(1,128)} %copy-done.6, bf16[8,256,256]{2,1,0:T(8,128)(2,1)} %copy-done.1, bf16[8,256,512]{2,1,0:T(8,128)(2,1)} %bitcast.29), custom_call_target="tpu_custom_call" | custom-call | flops 536870912 | bytes 4194304 | tf_op jit(solution)/shard_map/pallas_call | solution.py:391
  107.6 1.9 %collective-permute-start.17 = (f32[2,64,512]{2,1,0:T(8,128)}, f32[2,64,512]{2,1,0:T(8,128)S(1)}, u32[]{:S(2)}, u32[]{:S(2)}) collective-permute-start(f32[2,64,512]{2,1,0:T(8,128)} %get-tuple-element.54), channel_id=1, source_target_pairs={{0,8},{1,9},{2,10},{3,11},{4,12},{5,13},{6,14},{7,15},{8,0},{9,1},... | collective-permute-start | bytes 786440 | tf_op jit(solution)/shard_map/ppermute | solution.py:422
  112.3 5.9 %collective-permute-done.18 = f32[64,512]{1,0:T(8,128)S(1)} collective-permute-done((f32[64,512]{1,0:T(8,128)S(1)}, f32[64,512]{1,0:T(8,128)S(1)}, u32[]{:S(2)}, u32[]{:S(2)}) %collective-permute-start.18) | collective-permute-done | bytes 131104 | tf_op jit(solution)/shard_map/ppermute | solution.py:422
  (62 shorter events, 9.5 us)
Async XLA Ops:
  7.2 87.1 %all-gather.3.cloned.1.call-start = ((), (), s32[]{:S(2)}) async-start(), calls=%async_computation.3 | async-start | bytes 2359296 | tf_op jit(solution)/shard_map/all_gather | solution.py:452
  7.2 26.3 %collective-permute-start.4 = (bf16[3,256,4096]{2,1,0:T(8,128)(2,1)}, bf16[3,256,4096]{2,1,0:T(8,128)(2,1)}, u32[]{:S(2)}, u32[]{:S(2)}) collective-permute-start(bf16[3,256,4096]{2,1,0:T(8,128)(2,1)} %bitcast.21), channel_id=1, source_target_pairs={{0,8},{1,9},{2,10},{3,11},{4,12},{5,13},{6,14},{7,15},{8,0},{9,1},... | collective-permute-start | bytes 18874376 | tf_op jit(solution)/shard_map/ppermute | solution.py:422
  14.5 15.0 %collective-permute-start.5 = (bf16[512,512]{1,0:T(8,128)(2,1)}, bf16[512,512]{1,0:T(8,128)(2,1)}, u32[]{:S(2)}, u32[]{:S(2)}) collective-permute-start(bf16[512,512]{1,0:T(8,128)(2,1)} %get-tuple-element.56.refs_0_), channel_id=1, source_target_pairs={{0,1},{1,2},{2,3},{3,0},{4,5},{5,6},{6,7},{7,4},{8,11},{9,8},{10,9... | collective-permute-start | bytes 1572872 | tf_op jit(solution)/shard_map/ppermute | solution.py:422
  15.5 14.0 %collective-permute-start.6 = (bf16[512,512]{1,0:T(8,128)(2,1)}, bf16[512,512]{1,0:T(8,128)(2,1)}, u32[]{:S(2)}, u32[]{:S(2)}) collective-permute-start(bf16[512,512]{1,0:T(8,128)(2,1)} %get-tuple-element.56.refs_0_), channel_id=1, source_target_pairs={{0,4},{1,5},{2,6},{3,7},{4,0},{5,1},{6,2},{7,3},{8,140},{9,141},{1... | collective-permute-start | bytes 1572872 | tf_op jit(solution)/shard_map/ppermute | solution.py:422
  18.0 15.1 %collective-permute-start = (bf16[512,512]{1,0:T(8,128)(2,1)}, bf16[512,512]{1,0:T(8,128)(2,1)}, u32[]{:S(2)}, u32[]{:S(2)}) collective-permute-start(bf16[512,512]{1,0:T(8,128)(2,1)} %get-tuple-element.57.refs_0_), channel_id=1, source_target_pairs={{0,1},{1,2},{2,3},{3,0},{4,5},{5,6},{6,7},{7,4},{8,11},{9,8},{10,9... | collective-permute-start | bytes 1572872 | tf_op jit(solution)/shard_map/ppermute | solution.py:422
  18.4 14.7 %collective-permute-start.1 = (bf16[512,512]{1,0:T(8,128)(2,1)}, bf16[512,512]{1,0:T(8,128)(2,1)}, u32[]{:S(2)}, u32[]{:S(2)}) collective-permute-start(bf16[512,512]{1,0:T(8,128)(2,1)} %get-tuple-element.57.refs_0_), channel_id=1, source_target_pairs={{0,4},{1,5},{2,6},{3,7},{4,0},{5,1},{6,2},{7,3},{8,140},{9,141},{1... | collective-permute-start | bytes 1572872 | tf_op jit(solution)/shard_map/ppermute | solution.py:422
  21.2 29.2 %slice-start = ((s8[6291456]{0:T(1024)(128)(4,1)}), s8[2097152]{0:T(1024)(128)(4,1)S(1)}, s32[]{:S(2)}) async-start(s8[6291456]{0:T(1024)(128)(4,1)} %bitcast.23), calls=%async_computation.4 | async-start | bytes 4194304
  21.2 55.0 %all-to-all-start = ((bf16[8,256,256]{2,1,0:T(8,128)(2,1)}), bf16[8,256,256]{2,1,0:T(8,128)(2,1)S(1)}, u32[]{:S(2)}, u32[]{:S(2)}) async-start(bf16[8,256,256]{2,1,0:T(8,128)(2,1)} %get-tuple-element.52), calls=%async_computation | async-start | bytes 2097152 | tf_op jit(solution)/shard_map/all_to_all | solution.py:454
  29.5 15.1 %collective-permute-start.10 = (bf16[512,512]{1,0:T(8,128)(2,1)}, bf16[512,512]{1,0:T(8,128)(2,1)}, u32[]{:S(2)}, u32[]{:S(2)}) collective-permute-start(bf16[512,512]{1,0:T(8,128)(2,1)} %get-tuple-element.32.refs_3_.refs_0_), channel_id=1, source_target_pairs={{0,4},{1,5},{2,6},{3,7},{4,0},{5,1},{6,2},{7,3},{8,140},{9,141},{1... | collective-permute-start | bytes 1572872 | tf_op jit(solution)/shard_map/ppermute | solution.py:422
  32.1 12.5 %collective-permute-start.9 = (bf16[512,512]{1,0:T(8,128)(2,1)}, bf16[512,512]{1,0:T(8,128)(2,1)}, u32[]{:S(2)}, u32[]{:S(2)}) collective-permute-start(bf16[512,512]{1,0:T(8,128)(2,1)} %get-tuple-element.31.refs_1_), channel_id=1, source_target_pairs={{0,3},{1,0},{2,1},{3,2},{4,7},{5,4},{6,5},{7,6},{8,9},{9,10},{10,1... | collective-permute-start | bytes 1572872 | tf_op jit(solution)/shard_map/ppermute | solution.py:422
  33.1 16.6 %collective-permute-start.3 = (bf16[512,512]{1,0:T(8,128)(2,1)}, bf16[512,512]{1,0:T(8,128)(2,1)}, u32[]{:S(2)}, u32[]{:S(2)}) collective-permute-start(bf16[512,512]{1,0:T(8,128)(2,1)} %get-tuple-element.29.refs_2_.refs_0_), channel_id=1, source_target_pairs={{0,4},{1,5},{2,6},{3,7},{4,0},{5,1},{6,2},{7,3},{8,140},{9,141},{1... | collective-permute-start | bytes 1572872 | tf_op jit(solution)/shard_map/ppermute | solution.py:422
  33.4 16.3 %collective-permute-start.2 = (bf16[512,512]{1,0:T(8,128)(2,1)}, bf16[512,512]{1,0:T(8,128)(2,1)}, u32[]{:S(2)}, u32[]{:S(2)}) collective-permute-start(bf16[512,512]{1,0:T(8,128)(2,1)} %get-tuple-element.30.refs_0_), channel_id=1, source_target_pairs={{0,3},{1,0},{2,1},{3,2},{4,7},{5,4},{6,5},{7,6},{8,9},{9,10},{10,1... | collective-permute-start | bytes 1572872 | tf_op jit(solution)/shard_map/ppermute | solution.py:422
  33.5 38.8 %copy-start.4 = (s32[11]{0:T(128)}, s32[11]{0:T(128)S(1)}, u32[]{:S(2)}) copy-start(s32[11]{0:T(128)S(1)} %stack.47.kidx.place) | copy-start | bytes 136
  44.6 14.3 %collective-permute-start.12 = (bf16[512,512]{1,0:T(8,128)(2,1)}, bf16[512,512]{1,0:T(8,128)(2,1)S(1)}, u32[]{:S(2)}, u32[]{:S(2)}) collective-permute-start(bf16[512,512]{1,0:T(8,128)(2,1)} %get-tuple-element.44), channel_id=1, source_target_pairs={{0,1},{1,2},{2,3},{3,0},{4,5},{5,6},{6,7},{7,4},{8,11},{9,8},{10,9... | collective-permute-start | bytes 1572872 | tf_op jit(solution)/shard_map/ppermute | solution.py:422
  47.4 11.5 %collective-permute-start.13 = (bf16[512,512]{1,0:T(8,128)(2,1)}, bf16[512,512]{1,0:T(8,128)(2,1)S(1)}, u32[]{:S(2)}, u32[]{:S(2)}) collective-permute-start(bf16[512,512]{1,0:T(8,128)(2,1)} %get-tuple-element.39.refs_2_), channel_id=1, source_target_pairs={{0,4},{1,5},{2,6},{3,7},{4,0},{5,1},{6,2},{7,3},{8,140},{9,141},{1... | collective-permute-start | bytes 1572872 | tf_op jit(solution)/shard_map/ppermute | solution.py:422
  49.7 10.1 %collective-permute-start.7 = (bf16[512,512]{1,0:T(8,128)(2,1)}, bf16[512,512]{1,0:T(8,128)(2,1)S(1)}, u32[]{:S(2)}, u32[]{:S(2)}) collective-permute-start(bf16[512,512]{1,0:T(8,128)(2,1)} %get-tuple-element.36), channel_id=1, source_target_pairs={{0,1},{1,2},{2,3},{3,0},{4,5},{5,6},{6,7},{7,4},{8,11},{9,8},{10,9... | collective-permute-start | bytes 1572872 | tf_op jit(solution)/shard_map/ppermute | solution.py:422
  50.2 12.7 %collective-permute-start.8 = (bf16[512,512]{1,0:T(8,128)(2,1)}, bf16[512,512]{1,0:T(8,128)(2,1)S(1)}, u32[]{:S(2)}, u32[]{:S(2)}) collective-permute-start(bf16[512,512]{1,0:T(8,128)(2,1)} %get-tuple-element.37.refs_1_), channel_id=1, source_target_pairs={{0,4},{1,5},{2,6},{3,7},{4,0},{5,1},{6,2},{7,3},{8,140},{9,141},{1... | collective-permute-start | bytes 1572872 | tf_op jit(solution)/shard_map/ppermute | solution.py:422
  50.4 20.3 %collective-permute-start.15 = (bf16[256,2048]{1,0:T(8,128)(2,1)S(1)}, bf16[256,2048]{1,0:T(8,128)(2,1)S(1)}, u32[]{:S(2)}, u32[]{:S(2)}) collective-permute-start(bf16[256,2048]{1,0:T(8,128)(2,1)S(1)} %copy-done.2), channel_id=1, source_target_pairs={{0,8},{1,9},{2,10},{3,11},{4,12},{5,13},{6,14},{7,15},{8,0},{9,1},... | collective-permute-start | bytes 3145736 | tf_op jit(solution)/shard_map/ppermute | solution.py:422
  58.9 11.7 %collective-permute-start.14 = (bf16[512,512]{1,0:T(8,128)(2,1)}, bf16[512,512]{1,0:T(8,128)(2,1)S(1)}, u32[]{:S(2)}, u32[]{:S(2)}) collective-permute-start(bf16[512,512]{1,0:T(8,128)(2,1)} %get-tuple-element.45), channel_id=1, source_target_pairs={{0,1},{1,2},{2,3},{3,0},{4,5},{5,6},{6,7},{7,4},{8,11},{9,8},{10,9... | collective-permute-start | bytes 1572872 | tf_op jit(solution)/shard_map/ppermute | solution.py:422
  62.9 9.5 %collective-permute-start.11 = (bf16[512,512]{1,0:T(8,128)(2,1)S(1)}, bf16[512,512]{1,0:T(8,128)(2,1)S(1)}, u32[]{:S(2)}, u32[]{:S(2)}) collective-permute-start(bf16[512,512]{1,0:T(8,128)(2,1)S(1)} %get-tuple-element.43.refs_2_), channel_id=1, source_target_pairs={{0,4},{1,5},{2,6},{3,7},{4,0},{5,1},{6,2},{7,3},{8,140},{9,141},{1... | collective-permute-start | bytes 1572872 | tf_op jit(solution)/shard_map/ppermute | solution.py:422
  65.2 5.5 %collective-permute-start.16 = (f32[3,256,1]{2,1,0:T(8,128)S(1)}, f32[3,256,1]{2,1,0:T(8,128)S(1)}, u32[]{:S(2)}, u32[]{:S(2)}) collective-permute-start(f32[3,256,1]{2,1,0:T(8,128)S(1)} %shard_map.72.refs_0_.low_own), channel_id=1, source_target_pairs={{0,8},{1,9},{2,10},{3,11},{4,12},{5,13},{6,14},{7,15},{8,0},{9,1},... | collective-permute-start | bytes 9224 | tf_op jit(solution)/shard_map/ppermute | solution.py:422
  84.5 18.6 %all-to-all-start.2 = ((f32[16,1,512]{2,1,0:T(1,128)}), f32[16,1,512]{2,1,0:T(1,128)S(1)}, u32[]{:S(2)}, u32[]{:S(2)}) async-start(f32[16,1,512]{2,1,0:T(1,128)} %shard_map.81), calls=%async_computation.2 | async-start | bytes 65536 | tf_op jit(solution)/shard_map/all_to_all | solution.py:409
  107.6 3.3 %collective-permute-start.17 = (f32[2,64,512]{2,1,0:T(8,128)}, f32[2,64,512]{2,1,0:T(8,128)S(1)}, u32[]{:S(2)}, u32[]{:S(2)}) collective-permute-start(f32[2,64,512]{2,1,0:T(8,128)} %get-tuple-element.54), channel_id=1, source_target_pairs={{0,8},{1,9},{2,10},{3,11},{4,12},{5,13},{6,14},{7,15},{8,0},{9,1},... | collective-permute-start | bytes 786440 | tf_op jit(solution)/shard_map/ppermute | solution.py:422
  111.9 6.3 %collective-permute-start.18 = (f32[64,512]{1,0:T(8,128)S(1)}, f32[64,512]{1,0:T(8,128)S(1)}, u32[]{:S(2)}, u32[]{:S(2)}) collective-permute-start(f32[64,512]{1,0:T(8,128)S(1)} %slice_bitcast_fusion), channel_id=1, source_target_pairs={{0,128},{1,129},{2,130},{3,131},{4,132},{5,133},{6,134},{7,135},{8... | collective-permute-start | bytes 393224 | tf_op jit(solution)/shard_map/ppermute | solution.py:422
  (7 other events, 63.2 us)
Sparse Core Ops, SparseCore 0:
  12.4 59.9 all-gather.2
